TPU v7x, 256 devices: a whole 4x4x8 slice. The times are simulated.
256 devices in a mesh: row: 32 (over z, y_hi, core), col: 8 (over x, y_lo).
Axes of the slice: x: 4, y: 4 (y_hi: 2, y_lo: 2; y = y_hi * 2 + y_lo), z: 8, core: 2. Of those that a mesh axis runs over, the one named last changes fastest.
Arguments:
- vectors_in: float32 [1024, 196608], P(('col', 'row')), may hold values from -6 to 6
- householder: float32 [4, 64, 196608], P(None, None, 'row'), may hold values from -0.013671875 to 0.013671875
- tfactors: float32 [4, 64, 64], replicated, as said below
Outputs:
- vectors_out: float32 [1024, 196608], P('col', 'row')
Inputs may be any that keep to these rules, and one draw needn't show every extreme that they name: `tfactors`: every factor is upper triangular with its diagonal between 1 and 2.
All inputs are finite; a program needn't handle non-finite values.
Results may differ from a plain program's by a relative error of at most 0.0001.
Values sent between devices are 32-bit elements; how exact they have to be, the bound alone decides.
No kernel may reach another device: no remote copies, remote signals or barrier semaphores. Data moves between devices by JAX's collectives and lax.ppermute only.
A program may use at most 64 MiB of HBM per device.

v0:
```python
import jax
import jax.numpy as jnp
from jax import lax
from jax.sharding import PartitionSpec as P


def right_product(left, right):
    return lax.dot_general(
        left,
        right,
        (((1,), (1,)), ((), ())),
        precision=lax.Precision.HIGHEST,
        preferred_element_type=jnp.float32,
    )


def apply_block(current, basis, factor):
    partial_sum = right_product(current, basis)
    whole_sum = lax.psum(partial_sum, "row")
    scaled = right_product(whole_sum, factor)
    return current - jnp.dot(
        scaled, basis, precision=lax.Precision.HIGHEST, preferred_element_type=jnp.float32
    )


def shards(vectors_in, householder, tfactors):
    current = lax.all_to_all(vectors_in, "row", split_axis=1, concat_axis=0, tiled=True)
    panels = householder.shape[0]

    def one_panel(step, state):
        index = panels - 1 - step
        return apply_block(state, householder[index], tfactors[index])

    current = lax.fori_loop(0, panels, one_panel, current)
    return current


def solution(mesh):
    in_specs = (P(("col", "row"), None), P(None, None, "row"), P())
    out_specs = P("col", "row")
    return jax.shard_map(shards, mesh=mesh, in_specs=in_specs, out_specs=out_specs, check_vma=False)
```

profile of v0, /device:TPU:4, one launch (start us, length us, event | category | flops | bytes accessed | tf_op | source)
XLA Modules:
  0.0 648.6 jit_solution(6237534079467619508)
XLA Ops:
  0.0 11.5 %all-to-all-start = ((f32[4,32,6144]{2,0,1:T(4,128)}), f32[4,32,6144]{2,0,1:T(4,128)S(1)}, u32[]{:S(2)}, u32[]{:S(2)}) async-start(f32[4,32,6144]{2,0,1:T(4,128)} %bitcast.32), calls=%async_computation | async-start | bytes 6291456 | tf_op jit(solution)/shard_map/all_to_all | solution.py:27
  11.5 74.3 %all-to-all-done = f32[4,32,6144]{2,0,1:T(4,128)S(1)} async-done(((f32[4,32,6144]{2,0,1:T(4,128)}), f32[4,32,6144]{2,0,1:T(4,128)S(1)}, u32[]{:S(2)}, u32[]{:S(2)}) %all-to-all-start) | async-done | bytes 3145760 | tf_op jit(solution)/shard_map/all_to_all | solution.py:27
  85.8 0.0 copy-start.1
  85.8 1.7 copy-done.1
  87.4 3.1 all_to_all.17
  90.5 556.4 %while.15 = (s32[]{:T(128)}, f32[128,6144]{1,0:T(8,128)S(1)}, f32[4,64,6144]{2,1,0:T(8,128)}, f32[4,64,64]{2,1,0:T(8,128)}, s32[]{:T(128)}, /*index=5*/s32[]{:T(128)}, s32[]{:T(128)}, s32[]{:T(128)}) while((s32[]{:T(128)}, f32[128,6144]{1,0:T(8,128)S(1)}, f32[4,64,6144]{2,1,0:T(8,128)}, f32[4,64,64]{2,1,0:T(8,128)}, s32[]{:T(128)}, ...), condition=%wide.region_2.0_spmd, body=%wide.region_0.0_spmd.sunk | while | flops 1215045632 | bytes 12812439 | solution.py:34
  90.6 4.8 fusion.31
  95.4 128.5 %psum.15 = f32[128,64]{0,1:T(8,128)S(1)} all-reduce(f32[128,64]{0,1:T(8,128)S(1)} %fusion.31), channel_id=1, replica_groups=mesh['row'=32,'col'=8] {'row'}, use_global_device_ids=true, to_apply=%region_1.0 | all-reduce | flops 8192 | bytes 65536 | tf_op jit(solution)/shard_map/while/body/eval_jaxpr/psum | solution.py:19
  223.9 1.0 fusion.32
  224.9 4.7 convolution_subtract_fusion.2
  229.7 4.8 fusion.31
  234.5 128.5 %psum.15 = f32[128,64]{0,1:T(8,128)S(1)} all-reduce(f32[128,64]{0,1:T(8,128)S(1)} %fusion.31), channel_id=1, replica_groups=mesh['row'=32,'col'=8] {'row'}, use_global_device_ids=true, to_apply=%region_1.0 | all-reduce | flops 8192 | bytes 65536 | tf_op jit(solution)/shard_map/while/body/eval_jaxpr/psum | solution.py:19
  362.9 1.0 fusion.32
  364.0 4.7 convolution_subtract_fusion.2
  368.8 4.8 fusion.31
  373.5 128.5 %psum.15 = f32[128,64]{0,1:T(8,128)S(1)} all-reduce(f32[128,64]{0,1:T(8,128)S(1)} %fusion.31), channel_id=1, replica_groups=mesh['row'=32,'col'=8] {'row'}, use_global_device_ids=true, to_apply=%region_1.0 | all-reduce | flops 8192 | bytes 65536 | tf_op jit(solution)/shard_map/while/body/eval_jaxpr/psum | solution.py:19
  502.0 1.0 fusion.32
  503.1 4.7 convolution_subtract_fusion.2
  507.8 4.8 fusion.31
  512.6 128.5 %psum.15 = f32[128,64]{0,1:T(8,128)S(1)} all-reduce(f32[128,64]{0,1:T(8,128)S(1)} %fusion.31), channel_id=1, replica_groups=mesh['row'=32,'col'=8] {'row'}, use_global_device_ids=true, to_apply=%region_1.0 | all-reduce | flops 8192 | bytes 65536 | tf_op jit(solution)/shard_map/while/body/eval_jaxpr/psum | solution.py:19
  641.1 1.0 fusion.32
  642.1 4.7 convolution_subtract_fusion.2
  646.9 0.0 copy-start
  646.9 1.7 copy-done
Async XLA Ops:
  0.0 85.8 %all-to-all-start = ((f32[4,32,6144]{2,0,1:T(4,128)}), f32[4,32,6144]{2,0,1:T(4,128)S(1)}, u32[]{:S(2)}, u32[]{:S(2)}) async-start(f32[4,32,6144]{2,0,1:T(4,128)} %bitcast.32), calls=%async_computation | async-start | bytes 6291456 | tf_op jit(solution)/shard_map/all_to_all | solution.py:27
  85.8 1.7 copy-start.1
  646.9 1.7 copy-start
where the time goes:
time: 649 us
  blocking collectives  514 us (79%)
  waiting for transfers between devices  74.3 us (11%)
  matrix products  42.3 us (7%)
  starting transfers between devices  11.5 us (2%)
    psum x4, blocking collectives, apply_block(): whole_sum = lax.psum(partial_sum, 'row')  514 us
    all_to_all x1, waiting for transfers between devices, shards(): lax.all_to_all(vectors_in, 'row', split_axis=1, concat_axis=0, tiled=True)  74.3 us
    dot_general x8, matrix products, right_product(): lax.dot_general(left, right, (((1,), (1,)), ((), ())), precision=lax.Prec...  23.3 us
    dot_general x4, matrix products, apply_block(): jnp.dot(scaled, basis, precision=lax.Precision.HIGHEST, preferred_element...  19 us
  transfers between devices with their start and end apart: 1, of which 1 were waited for; matrix products, arithmetic and copies ran while one was open for 0% of the time, Pallas kernels for 0%

commit v1 on v0

v1 whole, which is shorter than its diff:
```python
import jax
import jax.numpy as jnp
from jax import lax
from jax.sharding import PartitionSpec as P


def product(left, right, contract, precision=lax.Precision.HIGHEST):
    return lax.dot_general(
        left,
        right,
        ((contract[:1], contract[1:]), ((), ())),
        precision=precision,
        preferred_element_type=jnp.float32,
    )


def swap(value, bit, devices):
    return lax.ppermute(value, "row", [(i, i ^ bit) for i in range(devices)])


def halves(value, upper):
    half = value.shape[0] // 2
    parts = value.reshape(2, half, value.shape[1])
    return parts[upper], parts[1 - upper]


def whole_sum(value, devices):
    index = lax.axis_index("row")
    for bit in (1, 2):
        kept, sent = halves(value, (index // bit) % 2)
        value = kept + swap(sent, bit, devices)
    bit = 4
    while bit < devices:
        value = value + swap(value, bit, devices)
        bit *= 2
    for bit in (2, 1):
        other = swap(value, bit, devices)
        upper = (index // bit) % 2 == 1
        value = jnp.concatenate([jnp.where(upper, other, value), jnp.where(upper, value, other)], axis=0)
    return value


def solution(mesh):
    devices = mesh.shape["row"]

    def shards(vectors_in, householder, tfactors):
        panels, width, rows = householder.shape
        basis = householder.reshape(panels * width, rows)
        gram = product(basis, basis, (1, 1))
        current = lax.all_to_all(vectors_in, "row", split_axis=1, concat_axis=0, tiled=True)
        count = current.shape[0]
        proj = product(current, basis, (1, 1))
        total = whole_sum(jnp.concatenate([proj, gram], axis=0), devices)
        proj, gram = total[:count], total[count:]
        scaled = [None] * panels
        for p in range(panels - 1, -1, -1):
            own = proj[:, p * width : (p + 1) * width]
            for q in range(p + 1, panels):
                block = gram[p * width : (p + 1) * width, q * width : (q + 1) * width]
                own = own - product(scaled[q], block, (1, 1))
            scaled[p] = product(own, tfactors[p], (1, 1))
        scaled = jnp.concatenate(scaled, axis=1)
        return current - product(scaled, basis, (1, 0))

    in_specs = (P(("col", "row"), None), P(None, None, "row"), P())
    out_specs = P("col", "row")
    return jax.shard_map(shards, mesh=mesh, in_specs=in_specs, out_specs=out_specs, check_vma=False)
```

time: 649 us -> 157 us (0.24)
  blocking collectives: 514 us -> 0 us
  waiting for transfers between devices: 74.3 us -> 90.6 us
    psum x4 -> x0, blocking collectives: 514 us -> none  [apply_block(): whole_sum = lax.psum(partial_sum, 'row')]
    ppermute x0 -> x7, waiting for transfers between devices: none -> 34.4 us  [swap(): return lax.ppermute(value, 'row', [(i, i ^ bit) for i in range(devices)])]
    all_to_all x1, waiting for transfers between devices: 74.3 us -> 56.2 us  [shards(): lax.all_to_all(vectors_in, 'row', split_axis=1, concat_axis=0, tiled=True)]
    dot_general x12 -> x13, matrix products: 42.3 us -> 41.2 us  [product(): lax.dot_general(left, right, ((contract[:1], contract[1:]), ((), ())), pr...]
  transfers between devices with their start and end apart: 1 -> 8, of which waited for: 1 -> 8; matrix products, arithmetic and copies ran while one was open for 0% -> 12% of each run, Pallas kernels for 0% -> 0%
where the time goes in v1:
time: 157 us; the launch traced here: 156 us
  waiting for transfers between devices  90.6 us (58%)
  matrix products  41.2 us (26%)
  starting transfers between devices  14.4 us (9%)
  local copies, waits for them, and re-layouts  6.16 us (4%)
  other arithmetic  2.91 us (2%)
    all_to_all x1, waiting for transfers between devices, shards(): lax.all_to_all(vectors_in, 'row', split_axis=1, concat_axis=0, tiled=True)  56.2 us
    dot_general x13, matrix products, product(): lax.dot_general(left, right, ((contract[:1], contract[1:]), ((), ())), pr...  41.2 us
    ppermute x7, waiting for transfers between devices, swap(): return lax.ppermute(value, 'row', [(i, i ^ bit) for i in range(devices)])  34.4 us
    all_to_all x1, starting transfers between devices, shards(): lax.all_to_all(vectors_in, 'row', split_axis=1, concat_axis=0, tiled=True)  11.5 us
  transfers between devices with their start and end apart: 8, of which 8 were waited for; matrix products, arithmetic and copies ran while one was open for 12% of the time, Pallas kernels for 0%

profile of v1, /device:TPU:4, one launch (start us, length us, event | category | flops | bytes accessed | tf_op | source)
XLA Modules:
  0.0 155.5 jit_solution(13761920094102305356)
XLA Ops:
  0.0 11.5 %all-to-all-start = ((f32[4,32,6144]{2,0,1:T(4,128)}), f32[4,32,6144]{2,0,1:T(4,128)S(1)}, u32[]{:S(2)}, u32[]{:S(2)}) async-start(f32[4,32,6144]{2,0,1:T(4,128)} %bitcast.40), calls=%async_computation | async-start | bytes 6291456 | tf_op jit(solution)/shard_map/all_to_all | solution.py:50
  11.5 18.0 %fusion.39 = f32[256,256]{1,0:T(8,128)} fusion(f32[256,6144]{1,0:T(8,128)} %bitcast.36), kind=kOutput, calls=%fused_computation.51 | convolution fusion | flops 4831838208 | bytes 6553600 | tf_op jit(solution)/shard_map/dot_general | solution.py:8
  29.5 56.2 %all-to-all-done = f32[4,32,6144]{2,0,1:T(4,128)S(1)} async-done(((f32[4,32,6144]{2,0,1:T(4,128)}), f32[4,32,6144]{2,0,1:T(4,128)S(1)}, u32[]{:S(2)}, u32[]{:S(2)}) %all-to-all-start) | async-done | bytes 3145760 | tf_op jit(solution)/shard_map/all_to_all | solution.py:50
  85.8 0.0 copy-start
  85.8 1.7 %copy-done = f32[4,32,6144]{2,0,1:T(4,128)} copy-done((f32[4,32,6144]{2,0,1:T(4,128)}, f32[4,32,6144]{2,0,1:T(4,128)S(1)}, u32[]{:S(2)}) %copy-start) | copy-done | bytes 3145752
  87.4 3.1 %all_to_all.17 = f32[128,6144]{1,0:T(8,128)S(1)} reshape(f32[32,4,6144]{2,1,0:T(4,128)} %bitcast.39) | data formatting | bytes 6291456 | tf_op jit(solution)/shard_map/all_to_all | solution.py:50
  90.5 0.0 copy-start.1
  90.6 9.2 %fusion.38 = f32[128,256]{1,0:T(8,128)S(1)} fusion(f32[128,6144]{1,0:T(8,128)S(1)} %all_to_all.17, f32[256,6144]{1,0:T(8,128)} %bitcast.37), kind=kOutput, calls=%fused_computation.50 | convolution fusion | flops 2415919104 | bytes 9568256 | tf_op jit(solution)/shard_map/dot_general | solution.py:8
  99.7 0.0 copy-done.1
  99.8 0.7 dynamic-slice_bitcast_fusion
  100.5 0.1 collective-permute-start
  100.6 1.7 %collective-permute-done = f32[192,256]{1,0:T(8,128)} collective-permute-done((f32[192,256]{1,0:T(8,128)}, f32[192,256]{1,0:T(8,128)}, u32[]{:S(2)}, u32[]{:S(2)}) %collective-permute-start) | collective-permute-done | bytes 196640 | tf_op jit(solution)/shard_map/ppermute | solution.py:18
  102.3 1.0 bitcast_add_fusion
  103.2 0.0 copy-start.2
  103.2 0.7 copy-done.2
  103.9 1.4 collective-permute-start.1
  105.3 5.3 %collective-permute-done.1 = f32[96,256]{1,0:T(8,128)S(1)} collective-permute-done((f32[96,256]{1,0:T(8,128)S(1)}, f32[96,256]{1,0:T(8,128)S(1)}, u32[]{:S(2)}, u32[]{:S(2)}) %collective-permute-start.1) | collective-permute-done | bytes 98336 | tf_op jit(solution)/shard_map/ppermute | solution.py:18
  110.5 0.9 bitcast_add_fusion.1
  111.4 0.6 collective-permute-start.2
  112.0 4.1 %collective-permute-done.2 = f32[96,256]{1,0:T(8,128)S(1)} collective-permute-done((f32[96,256]{1,0:T(8,128)S(1)}, f32[96,256]{1,0:T(8,128)S(1)}, u32[]{:S(2)}, u32[]{:S(2)}) %collective-permute-start.2) | collective-permute-done | bytes 98336 | tf_op jit(solution)/shard_map/ppermute | solution.py:18
  116.1 0.6 collective-permute-start.3
  116.8 7.1 %collective-permute-done.3 = f32[96,256]{1,0:T(8,128)S(1)} collective-permute-done((f32[96,256]{1,0:T(8,128)S(1)}, f32[96,256]{1,0:T(8,128)S(1)}, u32[]{:S(2)}, u32[]{:S(2)}) %collective-permute-start.3) | collective-permute-done | bytes 98336 | tf_op jit(solution)/shard_map/ppermute | solution.py:18
  123.9 0.1 collective-permute-start.4
  124.0 8.5 %collective-permute-done.4 = f32[96,256]{1,0:T(8,128)S(1)} collective-permute-done((f32[96,256]{1,0:T(8,128)S(1)}, f32[96,256]{1,0:T(8,128)S(1)}, u32[]{:S(2)}, u32[]{:S(2)}) %collective-permute-start.4) | collective-permute-done | bytes 98336 | tf_op jit(solution)/shard_map/ppermute | solution.py:18
  132.6 0.1 collective-permute-start.5
  132.7 6.1 %collective-permute-done.5 = f32[96,256]{1,0:T(8,128)S(1)} collective-permute-done((f32[96,256]{1,0:T(8,128)S(1)}, f32[96,256]{1,0:T(8,128)S(1)}, u32[]{:S(2)}, u32[]{:S(2)}) %collective-permute-start.5) | collective-permute-done | bytes 98336 | tf_op jit(solution)/shard_map/ppermute | solution.py:18
  138.8 0.1 collective-permute-start.6
  138.9 1.6 collective-permute-done.6
  140.5 1.0 broadcast_select_fusion
  141.4 1.1 fusion.7
  142.5 0.3 fusion.27
  142.8 0.3 fusion.23
  143.2 0.3 fusion.17
  143.5 1.0 fusion.9
  144.5 0.3 fusion.25
  144.8 0.3 fusion.19
  145.1 1.1 fusion.11
  146.2 0.3 fusion.21
  146.5 1.0 fusion.15
  147.5 8.0 %convolution_subtract_fusion = f32[128,6144]{1,0:T(8,128)} fusion(f32[128,6144]{1,0:T(8,128)S(1)} %all_to_all.17, f32[256,6144]{1,0:T(8,128)} %bitcast.38, f32[128,64]{0,1:T(8,128)S(1)} %fusion.7, f32[128,64]{0,1:T(8,128)S(1)} %fusion.9, f32[128,64]{0,1:T(8,128)S(1)} %fusion.11, f32[128,64]{0,1:T(8,128)S(1)} %fusion.15), kind=kOutput, calls=%fused_computation | convolution fusion | flops 2416803840 | bytes 12713984 | tf_op jit(solution)/shard_map/dot_general | solution.py:8
  (7 shorter events, 0.1 us)
Async XLA Ops:
  0.0 85.8 %all-to-all-start = ((f32[4,32,6144]{2,0,1:T(4,128)}), f32[4,32,6144]{2,0,1:T(4,128)S(1)}, u32[]{:S(2)}, u32[]{:S(2)}) async-start(f32[4,32,6144]{2,0,1:T(4,128)} %bitcast.40), calls=%async_computation | async-start | bytes 6291456 | tf_op jit(solution)/shard_map/all_to_all | solution.py:50
  85.8 1.7 %copy-start = (f32[4,32,6144]{2,0,1:T(4,128)}, f32[4,32,6144]{2,0,1:T(4,128)S(1)}, u32[]{:S(2)}) copy-start(f32[4,32,6144]{2,0,1:T(4,128)S(1)} %all-to-all-done) | copy-start | bytes 9437188
  90.5 9.2 %copy-start.1 = (f32[256,256]{1,0:T(8,128)S(1)}, f32[256,256]{1,0:T(8,128)}, u32[]{:S(2)}) copy-start(f32[256,256]{1,0:T(8,128)} %fusion.39) | copy-start | bytes 786436
  100.5 1.8 %collective-permute-start = (f32[192,256]{1,0:T(8,128)}, f32[192,256]{1,0:T(8,128)}, u32[]{:S(2)}, u32[]{:S(2)}) collective-permute-start(f32[192,256]{1,0:T(8,128)} %dynamic-slice_bitcast_fusion), channel_id=1, source_target_pairs={{0,8},{8,0},{16,24},{24,16},{32,40},{40,32},{48,56},{56,48},{64,72... | collective-permute-start | bytes 589832 | tf_op jit(solution)/shard_map/ppermute | solution.py:18
  103.2 0.7 copy-start.2
  103.9 6.6 %collective-permute-start.1 = (f32[96,256]{1,0:T(8,128)S(1)}, f32[96,256]{1,0:T(8,128)S(1)}, u32[]{:S(2)}, u32[]{:S(2)}) collective-permute-start(f32[96,256]{1,0:T(8,128)S(1)} %dynamic-slice_bitcast_fusion.1), channel_id=1, source_target_pairs={{0,16},{8,24},{16,0},{24,8},{32,48},{40,56},{48,32},{56,40},{64,80... | collective-permute-start | bytes 294920 | tf_op jit(solution)/shard_map/ppermute | solution.py:18
  111.4 4.7 %collective-permute-start.2 = (f32[96,256]{1,0:T(8,128)S(1)}, f32[96,256]{1,0:T(8,128)S(1)}, u32[]{:S(2)}, u32[]{:S(2)}) collective-permute-start(f32[96,256]{1,0:T(8,128)S(1)} %bitcast_add_fusion.1), channel_id=1, source_target_pairs={{0,32},{8,40},{16,48},{24,56},{32,0},{40,8},{48,16},{56,24},{64,96... | collective-permute-start | bytes 294920 | tf_op jit(solution)/shard_map/ppermute | solution.py:18
  116.1 7.8 %collective-permute-start.3 = (f32[96,256]{1,0:T(8,128)S(1)}, f32[96,256]{1,0:T(8,128)S(1)}, u32[]{:S(2)}, u32[]{:S(2)}) collective-permute-start(f32[96,256]{1,0:T(8,128)S(1)} %add.48), channel_id=1, source_target_pairs={{0,64},{8,72},{16,80},{24,88},{32,96},{40,104},{48,112},{56,120},{... | collective-permute-start | bytes 294920 | tf_op jit(solution)/shard_map/ppermute | solution.py:18
  123.9 8.6 %collective-permute-start.4 = (f32[96,256]{1,0:T(8,128)S(1)}, f32[96,256]{1,0:T(8,128)S(1)}, u32[]{:S(2)}, u32[]{:S(2)}) collective-permute-start(f32[96,256]{1,0:T(8,128)S(1)} %add.49), channel_id=1, source_target_pairs={{0,128},{8,136},{16,144},{24,152},{32,160},{40,168},{48,176},{56,1... | collective-permute-start | bytes 294920 | tf_op jit(solution)/shard_map/ppermute | solution.py:18
  132.6 6.2 %collective-permute-start.5 = (f32[96,256]{1,0:T(8,128)S(1)}, f32[96,256]{1,0:T(8,128)S(1)}, u32[]{:S(2)}, u32[]{:S(2)}) collective-permute-start(f32[96,256]{1,0:T(8,128)S(1)} %add.50), channel_id=1, source_target_pairs={{0,16},{8,24},{16,0},{24,8},{32,48},{40,56},{48,32},{56,40},{64,80... | collective-permute-start | bytes 294920 | tf_op jit(solution)/shard_map/ppermute | solution.py:18
  138.8 1.7 %collective-permute-start.6 = (f32[192,256]{1,0:T(8,128)S(1)}, f32[192,256]{1,0:T(8,128)}, u32[]{:S(2)}, u32[]{:S(2)}) collective-permute-start(f32[192,256]{1,0:T(8,128)S(1)} %pad_maximum_fusion.1), channel_id=1, source_target_pairs={{0,8},{8,0},{16,24},{24,16},{32,40},{40,32},{48,56},{56,48},{64,72... | collective-permute-start | bytes 589832 | tf_op jit(solution)/shard_map/ppermute | solution.py:18

commit v2 on v0

v2 whole, which is shorter than its diff:
```python
import functools

import jax
import jax.numpy as jnp
from jax import lax
from jax.experimental import pallas as pl
from jax.experimental.pallas import tpu as pltpu
from jax.sharding import PartitionSpec as P

COLUMNS = 1024
LIMIT = 40 * 1024 * 1024
IN_VMEM = pl.BlockSpec(memory_space=pltpu.VMEM)
IN_SMEM = pl.BlockSpec(memory_space=pltpu.SMEM)
IN_HBM = pl.BlockSpec(memory_space=pl.ANY)


def product(left, right, contract, precision=None):
    return lax.dot_general(
        left, right, (contract, ((), ())), precision=precision, preferred_element_type=jnp.float32
    )


def split(value):
    high = value.astype(jnp.bfloat16)
    low = (value - high.astype(jnp.float32)).astype(jnp.bfloat16)
    return high, low


def pairs_of(panels):
    return [(p, q) for p in range(panels) for q in range(p + 1, panels)]


def gram_kernel(householder_ref, basis_ref, gram_ref, total):
    panels, width, rows = householder_ref.shape
    size = panels * width
    total[...] = jnp.zeros_like(total)

    @pl.loop(0, rows // COLUMNS)
    def _(step):
        columns = pl.ds(pl.multiple_of(step * COLUMNS, COLUMNS), COLUMNS)
        block = householder_ref[:, :, columns].reshape(size, COLUMNS)
        high, low = split(block)
        basis_ref[:size, columns] = high
        basis_ref[size:, columns] = low
        total[...] += product(block, block, ((1,), (1,)), lax.Precision.HIGHEST)

    blocks = [
        total[p * width : (p + 1) * width, q * width : (q + 1) * width] for p, q in pairs_of(panels)
    ]
    for i in range(0, len(blocks), 2):
        at = i // 2 * width
        gram_ref[at : at + width, :] = jnp.concatenate(blocks[i : i + 2], axis=1)


def project_kernel(quarter_ref, arrived_ref, basis_ref, gram_ref, current_ref, kept_ref, sent_ref, total, joint):
    count, rows = current_ref.shape
    size = basis_ref.shape[0] // 2
    total[...] = jnp.zeros_like(total)
    for step in range(rows // COLUMNS):
        columns = pl.ds(step * COLUMNS, COLUMNS)
        block = arrived_ref[:, :, columns].reshape(count, COLUMNS)
        current_ref[:, columns] = block
        high, low = split(block)
        both = jnp.concatenate([high, low], axis=0)
        total[...] += product(basis_ref[:, columns], both, ((1,), (1,)))
    joint[:size, :] = (total[:size, :count] + total[:size, count:]) + (total[size:, :count] + total[size:, count:])
    joint[size:, :] = gram_ref[...]
    quarter = quarter_ref[0]
    part = joint.shape[0] // 4
    for k in range(4):
        target = (kept_ref, sent_ref, kept_ref, sent_ref)[k]
        start = pl.multiple_of((quarter ^ k) * part, 8)
        target[k // 2 * part : (k // 2 + 1) * part, :] = joint[pl.ds(start, part), :]


def finish_kernel(quarter_ref, own_ref, across_ref, other_ref, tfactors_ref, current_ref, basis_ref, out_ref, joint, out, sems):
    panels, width, _ = tfactors_ref.shape
    count, rows = current_ref.shape
    size = panels * width
    quarter = quarter_ref[0]
    part = joint.shape[0] // 4
    parts = (own_ref[...], other_ref[:part, :], across_ref[...], other_ref[part:, :])
    for k in range(4):
        joint[pl.ds(pl.multiple_of((quarter ^ k) * part, 8), part), :] = parts[k]
    gram = {}
    for i, pair in enumerate(pairs_of(panels)):
        at = size + i // 2 * width
        gram[pair] = joint[at : at + width, i % 2 * width : (i % 2 + 1) * width]
    exact = functools.partial(product, contract=((1,), (0,)), precision=lax.Precision.HIGHEST)
    scaled = [exact(tfactors_ref[p], joint[p * width : (p + 1) * width, :]) for p in range(panels)]
    links = {(p, q): exact(tfactors_ref[p], gram[p, q]) for p, q in gram}
    for q in range(panels - 1, 0, -1):
        for p in range(q):
            scaled[p] = scaled[p] - exact(links[p, q], scaled[q])
    high, low = split(jnp.concatenate(scaled, axis=0).T)
    both = jnp.concatenate([high, low], axis=0)
    copies = []
    for step in range(rows // COLUMNS):
        columns = pl.ds(step * COLUMNS, COLUMNS)
        first = product(both, basis_ref[:size, columns], ((1,), (0,)))
        second = product(high, basis_ref[size:, columns], ((1,), (0,)))
        out[:, columns] = current_ref[:, columns] - (first[:count] + (first[count:] + second))
        copy = pltpu.make_async_copy(out.at[:, columns], out_ref.at[:, columns], sems.at[step])
        copy.start()
        copies.append(copy)
    for copy in copies:
        copy.wait()


def in_vmem(value):
    return pltpu.with_memory_space_constraint(value, pltpu.VMEM)


def gram_call(householder):
    panels, width, rows = householder.shape
    size = panels * width
    pairs = len(pairs_of(panels))
    return pl.pallas_call(
        gram_kernel,
        out_shape=(
            pltpu.VMEM((2 * size, rows), jnp.bfloat16),
            jax.ShapeDtypeStruct((pairs // 2 * width, 2 * width), jnp.float32),
        ),
        in_specs=[IN_VMEM],
        out_specs=(IN_VMEM, IN_VMEM),
        scratch_shapes=[pltpu.VMEM((size, size), jnp.float32)],
        compiler_params=pltpu.CompilerParams(vmem_limit_bytes=LIMIT),
        cost_estimate=pl.CostEstimate(flops=12 * size * size * rows, bytes_accessed=4 * size * rows, transcendentals=0),
        name="gram",
    )(householder)


def project_call(quarter, arrived, basis, gram):
    sources, each, rows = arrived.shape
    count = sources * each
    size = basis.shape[0] // 2
    height = size + gram.shape[0]
    return pl.pallas_call(
        project_kernel,
        out_shape=(
            pltpu.VMEM((count, rows), jnp.float32),
            pltpu.VMEM((height // 2, count), jnp.float32),
            pltpu.VMEM((height // 2, count), jnp.float32),
        ),
        in_specs=[IN_SMEM, IN_VMEM, IN_VMEM, IN_VMEM],
        out_specs=(IN_VMEM, IN_VMEM, IN_VMEM),
        scratch_shapes=[
            pltpu.VMEM((2 * size, 2 * count), jnp.float32),
            pltpu.VMEM((height, count), jnp.float32),
        ],
        compiler_params=pltpu.CompilerParams(vmem_limit_bytes=LIMIT),
        name="project",
    )(quarter, in_vmem(arrived), in_vmem(basis), gram)


def finish_call(quarter, own, across, other, tfactors, current, basis):
    count, rows = current.shape
    return pl.pallas_call(
        finish_kernel,
        out_shape=jax.ShapeDtypeStruct((count, rows), jnp.float32),
        in_specs=[IN_SMEM] + [IN_VMEM] * 6,
        out_specs=IN_HBM,
        scratch_shapes=[
            pltpu.VMEM((4 * own.shape[0], count), jnp.float32),
            pltpu.VMEM((count, rows), jnp.float32),
            pltpu.SemaphoreType.DMA((rows // COLUMNS,)),
        ],
        compiler_params=pltpu.CompilerParams(vmem_limit_bytes=LIMIT),
        name="finish",
    )(quarter, in_vmem(own), in_vmem(across), in_vmem(other), tfactors, in_vmem(current), in_vmem(basis))


def solution(mesh):
    devices = mesh.shape["row"]

    def swap(value, flip):
        return lax.ppermute(value, "row", [(i, i ^ flip) for i in range(devices)])

    def shards(vectors_in, householder, tfactors):
        quarter = jnp.reshape(lax.axis_index("row") % 4, (1,)).astype(jnp.int32)
        arrived = lax.all_to_all(
            vectors_in.reshape(vectors_in.shape[0], devices, -1), "row", split_axis=1, concat_axis=0
        )
        basis, gram = gram_call(householder)
        current, kept, sent = project_call(quarter, arrived, basis, gram)
        part = kept.shape[0] // 2
        kept = kept + swap(sent, 1)
        value = kept[:part] + swap(kept[part:], 2)
        flip = 4
        while flip < devices:
            value = value + swap(value, 2 * flip - 4)
            flip *= 2
        across = swap(value, 2)
        other = swap(jnp.concatenate([value, across], axis=0), 1)
        return finish_call(quarter, value, across, other, tfactors, current, basis)

    in_specs = (P(("col", "row"), None), P(None, None, "row"), P())
    out_specs = P("col", "row")
    return jax.shard_map(shards, mesh=mesh, in_specs=in_specs, out_specs=out_specs, check_vma=False)
```

time: 649 us -> 125 us (0.19)
  blocking collectives: 514 us -> 0 us
  matrix products: 42.3 us -> 0 us
  waiting for transfers between devices: 74.3 us -> 88.5 us
  Pallas kernels: 0 us -> 11.6 us
    psum x4 -> x0, blocking collectives: 514 us -> none  [apply_block(): whole_sum = lax.psum(partial_sum, 'row')]
    dot_general x12 -> x0, matrix products: 42.3 us -> none  [the longest x8 23.3 us: right_product(): lax.dot_general(left, right, (((1,), (1,)), ((), ())), precision=lax.Prec...]
    ppermute x0 -> x7, waiting for transfers between devices: none -> 26.2 us  [swap(): return lax.ppermute(value, 'row', [(i, i ^ flip) for i in range(devices)])]
    all_to_all x1, waiting for transfers between devices: 74.3 us -> 62.3 us  [shards(): lax.all_to_all(vectors_in.reshape(vectors_in.shape[0], devices, -1), 'row...]
    pallas_call x0 -> x3, Pallas kernels: none -> 11.6 us  [the longest x1 6.52 us: gram_call(): pl.pallas_call(gram_kernel, out_shape=(pltpu.VMEM((2 * size, rows), jnp.b...]
  transfers between devices with their start and end apart: 1 -> 8, of which waited for: 1 -> 8; matrix products, arithmetic and copies ran while one was open for 0% -> 0% of each run, Pallas kernels for 0% -> 5%
where the time goes in v2:
time: 125 us; the launch traced here: 124 us
  waiting for transfers between devices  88.5 us (71%)
  starting transfers between devices  15.4 us (12%)
  Pallas kernels  11.6 us (9%)
  local copies, waits for them, and re-layouts  8.21 us (7%)
    all_to_all x1, waiting for transfers between devices, shards(): lax.all_to_all(vectors_in.reshape(vectors_in.shape[0], devices, -1), 'row...  62.3 us
    ppermute x7, waiting for transfers between devices, swap(): return lax.ppermute(value, 'row', [(i, i ^ flip) for i in range(devices)])  26.2 us
    all_to_all x1, starting transfers between devices, shards(): lax.all_to_all(vectors_in.reshape(vectors_in.shape[0], devices, -1), 'row...  11.5 us
    unnamed x8, local copies, waits for them, and re-layouts  8.2 us
    pallas_call x1, Pallas kernels, gram_call(): pl.pallas_call(gram_kernel, out_shape=(pltpu.VMEM((2 * size, rows), jnp.b...  6.52 us
    ppermute x7, starting transfers between devices, swap(): return lax.ppermute(value, 'row', [(i, i ^ flip) for i in range(devices)])  3.89 us
    pallas_call x1, Pallas kernels, finish_call(): pl.pallas_call(finish_kernel, out_shape=jax.ShapeDtypeStruct((count, rows...  3.21 us
  transfers between devices with their start and end apart: 8, of which 8 were waited for; matrix products, arithmetic and copies ran while one was open for 0% of the time, Pallas kernels for 5%

profile of v2, /device:TPU:4, one launch (start us, length us, event | category | flops | bytes accessed | tf_op | source)
XLA Modules:
  0.0 123.9 jit_solution(1010996972914102586)
XLA Ops:
  0.0 11.5 %all-to-all-start = ((f32[1,4,32,6144]{3,1,0,2:T(4,128)}), f32[1,4,32,6144]{3,1,0,2:T(4,128)S(1)}, u32[]{:S(2)}, u32[]{:S(2)}) async-start(f32[1,4,32,6144]{3,1,0,2:T(4,128)} %bitcast.8), calls=%async_computation | async-start | bytes 6291456 | tf_op jit(solution)/shard_map/all_to_all | solution.py:181
  11.5 0.0 copy-start.3
  11.5 2.8 %copy-done.3 = f32[4,64,6144]{2,1,0:T(8,128)S(1)} copy-done((f32[4,64,6144]{2,1,0:T(8,128)S(1)}, f32[4,64,6144]{2,1,0:T(8,128)}, u32[]{:S(2)}) %copy-start.3) | copy-done | bytes 6291480
  14.3 6.5 %gram.1 = (bf16[512,6144]{1,0:T(8,128)(2,1)S(1)}, f32[192,128]{1,0:T(8,128)S(1)}) custom-call(f32[4,64,6144]{2,1,0:T(8,128)S(1)} %copy-done.3), custom_call_target="tpu_custom_call" | custom-call | flops 4831838208 | bytes 6291456 | tf_op jit(solution)/shard_map/gram/pallas_call | solution.py:118
  20.8 0.0 copy-start
  20.8 2.6 %copy-done = bf16[512,6144]{1,0:T(8,128)(2,1)} copy-done((bf16[512,6144]{1,0:T(8,128)(2,1)}, bf16[512,6144]{1,0:T(8,128)(2,1)S(1)}, u32[]{:S(2)}) %copy-start) | copy-done | bytes 6291480
  23.5 62.3 %all-to-all-done = f32[1,4,32,6144]{3,1,0,2:T(4,128)S(1)} async-done(((f32[1,4,32,6144]{3,1,0,2:T(4,128)}), f32[1,4,32,6144]{3,1,0,2:T(4,128)S(1)}, u32[]{:S(2)}, u32[]{:S(2)}) %all-to-all-start) | async-done | bytes 3145760 | tf_op jit(solution)/shard_map/all_to_all | solution.py:181
  85.8 0.0 copy-start.1
  85.8 2.8 %copy-done.1 = bf16[512,6144]{1,0:T(8,128)(2,1)S(1)} copy-done((bf16[512,6144]{1,0:T(8,128)(2,1)S(1)}, bf16[512,6144]{1,0:T(8,128)(2,1)}, u32[]{:S(2)}) %copy-start.1) | copy-done | bytes 6291480
  88.5 0.0 copy-start.2
  88.5 1.9 %project.1 = (f32[128,6144]{1,0:T(8,128)S(1)}, f32[224,128]{1,0:T(8,128)S(1)}, f32[224,128]{1,0:T(8,128)S(1)}) custom-call(s32[1]{0:T(128)} %bitcast.quarter_ref, f32[32,4,6144]{2,1,0:T(4,128)S(1)} %bitcast.7, bf16[512,6144]{1,0:T(8,128)(2,1)S(1)} %copy-done.1, f32[192,128]{1,0:T(8,128)S(1)} %get-tuple-element.11.gram_ref), custom_call_target="tpu_custom_call" | custom-call | tf_op jit(solution)/shard_map/project/pallas_call | solution.py:138
  90.4 0.2 collective-permute-start
  90.6 1.3 %collective-permute-done = f32[224,128]{1,0:T(8,128)S(1)} collective-permute-done((f32[224,128]{1,0:T(8,128)S(1)}, f32[224,128]{1,0:T(8,128)S(1)}, u32[]{:S(2)}, u32[]{:S(2)}) %collective-permute-start) | collective-permute-done | bytes 114720 | tf_op jit(solution)/shard_map/ppermute | solution.py:177
  91.9 1.2 collective-permute-start.1
  93.0 4.6 %collective-permute-done.1 = f32[112,128]{1,0:T(8,128)S(1)} collective-permute-done((f32[112,128]{1,0:T(8,128)S(1)}, f32[112,128]{1,0:T(8,128)S(1)}, u32[]{:S(2)}, u32[]{:S(2)}) %collective-permute-start.1) | collective-permute-done | bytes 57376 | tf_op jit(solution)/shard_map/ppermute | solution.py:177
  97.6 0.6 collective-permute-start.2
  98.2 3.7 %collective-permute-done.2 = f32[112,128]{1,0:T(8,128)S(1)} collective-permute-done((f32[112,128]{1,0:T(8,128)S(1)}, f32[112,128]{1,0:T(8,128)S(1)}, u32[]{:S(2)}, u32[]{:S(2)}) %collective-permute-start.2) | collective-permute-done | bytes 57376 | tf_op jit(solution)/shard_map/ppermute | solution.py:177
  101.9 0.1 collective-permute-start.3
  102.0 6.0 %collective-permute-done.3 = f32[112,128]{1,0:T(8,128)S(1)} collective-permute-done((f32[112,128]{1,0:T(8,128)S(1)}, f32[112,128]{1,0:T(8,128)S(1)}, u32[]{:S(2)}, u32[]{:S(2)}) %collective-permute-start.3) | collective-permute-done | bytes 57376 | tf_op jit(solution)/shard_map/ppermute | solution.py:177
  108.0 0.1 collective-permute-start.4
  108.1 5.4 %collective-permute-done.4 = f32[112,128]{1,0:T(8,128)S(1)} collective-permute-done((f32[112,128]{1,0:T(8,128)S(1)}, f32[112,128]{1,0:T(8,128)S(1)}, u32[]{:S(2)}, u32[]{:S(2)}) %collective-permute-start.4) | collective-permute-done | bytes 57376 | tf_op jit(solution)/shard_map/ppermute | solution.py:177
  113.5 1.7 %collective-permute-start.5 = (f32[112,128]{1,0:T(8,128)S(1)}, f32[112,128]{1,0:T(8,128)S(1)}, u32[]{:S(2)}, u32[]{:S(2)}) collective-permute-start(f32[112,128]{1,0:T(8,128)S(1)} %add.24.own_ref), channel_id=1, source_target_pairs={{0,16},{8,24},{16,0},{24,8},{32,48},{40,56},{48,32},{56,40},{64,80... | collective-permute-start | bytes 172040 | tf_op jit(solution)/shard_map/ppermute | solution.py:177
  115.2 4.1 %collective-permute-done.5.across_ref = f32[112,128]{1,0:T(8,128)S(1)} collective-permute-done((f32[112,128]{1,0:T(8,128)S(1)}, f32[112,128]{1,0:T(8,128)S(1)}, u32[]{:S(2)}, u32[]{:S(2)}) %collective-permute-start.5) | collective-permute-done | bytes 57376 | tf_op jit(solution)/shard_map/ppermute | solution.py:177
  119.3 0.1 collective-permute-start.6
  119.4 1.3 %collective-permute-done.6.other_ref = f32[224,128]{1,0:T(8,128)S(1)} collective-permute-done((f32[224,128]{1,0:T(8,128)S(1)}, f32[224,128]{1,0:T(8,128)S(1)}, u32[]{:S(2)}, u32[]{:S(2)}) %collective-permute-start.6) | collective-permute-done | bytes 114720 | tf_op jit(solution)/shard_map/ppermute | solution.py:177
  120.7 0.0 copy-done.2
  120.7 3.2 %finish.1 = f32[128,6144]{1,0:T(8,128)} custom-call(s32[1]{0:T(128)} %bitcast.quarter_ref, f32[112,128]{1,0:T(8,128)S(1)} %add.24.own_ref, f32[112,128]{1,0:T(8,128)S(1)} %collective-permute-done.5.across_ref, f32[224,128]{1,0:T(8,128)S(1)} %collective-permute-done.6.other_ref, f32[4,64,64]{2,1,0:T(8,128)S(1)} %copy-done.2, ...), custom_call_target="tpu_custom_call" | custom-call | tf_op jit(solution)/shard_map/finish/pallas_call | solution.py:158
  (7 shorter events, 0.1 us)
Async XLA Ops:
  0.0 85.8 %all-to-all-start = ((f32[1,4,32,6144]{3,1,0,2:T(4,128)}), f32[1,4,32,6144]{3,1,0,2:T(4,128)S(1)}, u32[]{:S(2)}, u32[]{:S(2)}) async-start(f32[1,4,32,6144]{3,1,0,2:T(4,128)} %bitcast.8), calls=%async_computation | async-start | bytes 6291456 | tf_op jit(solution)/shard_map/all_to_all | solution.py:181
  11.5 2.8 %copy-start.3 = (f32[4,64,6144]{2,1,0:T(8,128)S(1)}, f32[4,64,6144]{2,1,0:T(8,128)}, u32[]{:S(2)}) copy-start(f32[4,64,6144]{2,1,0:T(8,128)} %householder_ref.1) | copy-start | bytes 18874372
  20.8 2.6 %copy-start = (bf16[512,6144]{1,0:T(8,128)(2,1)}, bf16[512,6144]{1,0:T(8,128)(2,1)S(1)}, u32[]{:S(2)}) copy-start(bf16[512,6144]{1,0:T(8,128)(2,1)S(1)} %get-tuple-element.10.basis_ref) | copy-start | bytes 18874372
  85.8 2.8 %copy-start.1 = (bf16[512,6144]{1,0:T(8,128)(2,1)S(1)}, bf16[512,6144]{1,0:T(8,128)(2,1)}, u32[]{:S(2)}) copy-start(bf16[512,6144]{1,0:T(8,128)(2,1)} %copy-done) | copy-start | bytes 18874372
  88.5 32.1 %copy-start.2 = (f32[4,64,64]{2,1,0:T(8,128)S(1)}, f32[4,64,64]{2,1,0:T(8,128)}, u32[]{:S(2)}) copy-start(f32[4,64,64]{2,1,0:T(8,128)} %tfactors_ref.1) | copy-start | bytes 196612
  90.4 1.4 %collective-permute-start = (f32[224,128]{1,0:T(8,128)S(1)}, f32[224,128]{1,0:T(8,128)S(1)}, u32[]{:S(2)}, u32[]{:S(2)}) collective-permute-start(f32[224,128]{1,0:T(8,128)S(1)} %get-tuple-element.13), channel_id=1, source_target_pairs={{0,8},{8,0},{16,24},{24,16},{32,40},{40,32},{48,56},{56,48},{64,72... | collective-permute-start | bytes 344072 | tf_op jit(solution)/shard_map/ppermute | solution.py:177
  91.9 5.8 %collective-permute-start.1 = (f32[112,128]{1,0:T(8,128)S(1)}, f32[112,128]{1,0:T(8,128)S(1)}, u32[]{:S(2)}, u32[]{:S(2)}) collective-permute-start(f32[112,128]{1,0:T(8,128)S(1)} %slice.9), channel_id=1, source_target_pairs={{0,16},{8,24},{16,0},{24,8},{32,48},{40,56},{48,32},{56,40},{64,80... | collective-permute-start | bytes 172040 | tf_op jit(solution)/shard_map/ppermute | solution.py:177
  97.6 4.3 %collective-permute-start.2 = (f32[112,128]{1,0:T(8,128)S(1)}, f32[112,128]{1,0:T(8,128)S(1)}, u32[]{:S(2)}, u32[]{:S(2)}) collective-permute-start(f32[112,128]{1,0:T(8,128)S(1)} %slice_add_fusion), channel_id=1, source_target_pairs={{0,32},{8,40},{16,48},{24,56},{32,0},{40,8},{48,16},{56,24},{64,96... | collective-permute-start | bytes 172040 | tf_op jit(solution)/shard_map/ppermute | solution.py:177
  101.9 6.1 %collective-permute-start.3 = (f32[112,128]{1,0:T(8,128)S(1)}, f32[112,128]{1,0:T(8,128)S(1)}, u32[]{:S(2)}, u32[]{:S(2)}) collective-permute-start(f32[112,128]{1,0:T(8,128)S(1)} %add.22), channel_id=1, source_target_pairs={{0,96},{8,104},{16,112},{24,120},{32,64},{40,72},{48,80},{56,88},{... | collective-permute-start | bytes 172040 | tf_op jit(solution)/shard_map/ppermute | solution.py:177
  108.0 5.5 %collective-permute-start.4 = (f32[112,128]{1,0:T(8,128)S(1)}, f32[112,128]{1,0:T(8,128)S(1)}, u32[]{:S(2)}, u32[]{:S(2)}) collective-permute-start(f32[112,128]{1,0:T(8,128)S(1)} %add.23), channel_id=1, source_target_pairs={{0,224},{8,232},{16,240},{24,248},{32,192},{40,200},{48,208},{56,2... | collective-permute-start | bytes 172040 | tf_op jit(solution)/shard_map/ppermute | solution.py:177
  113.5 5.8 %collective-permute-start.5 = (f32[112,128]{1,0:T(8,128)S(1)}, f32[112,128]{1,0:T(8,128)S(1)}, u32[]{:S(2)}, u32[]{:S(2)}) collective-permute-start(f32[112,128]{1,0:T(8,128)S(1)} %add.24.own_ref), channel_id=1, source_target_pairs={{0,16},{8,24},{16,0},{24,8},{32,48},{40,56},{48,32},{56,40},{64,80... | collective-permute-start | bytes 172040 | tf_op jit(solution)/shard_map/ppermute | solution.py:177
  119.3 1.4 %collective-permute-start.6 = (f32[224,128]{1,0:T(8,128)S(1)}, f32[224,128]{1,0:T(8,128)S(1)}, u32[]{:S(2)}, u32[]{:S(2)}) collective-permute-start(f32[224,128]{1,0:T(8,128)S(1)} %pad_maximum_fusion), channel_id=1, source_target_pairs={{0,8},{8,0},{16,24},{24,16},{32,40},{40,32},{48,56},{56,48},{64,72... | collective-permute-start | bytes 344072 | tf_op jit(solution)/shard_map/ppermute | solution.py:177

commit v3 on v2

v3 whole, which is shorter than its diff:
```python
import functools

import jax
import jax.numpy as jnp
from jax import lax
from jax.experimental import pallas as pl
from jax.experimental.pallas import tpu as pltpu
from jax.sharding import Mesh
from jax.sharding import PartitionSpec as P

COLUMNS = 1024
LIMIT = 40 * 1024 * 1024
IN_VMEM = pl.BlockSpec(memory_space=pltpu.VMEM)
IN_SMEM = pl.BlockSpec(memory_space=pltpu.SMEM)
IN_HBM = pl.BlockSpec(memory_space=pl.ANY)


def product(left, right, contract, precision=None):
    return lax.dot_general(
        left, right, (contract, ((), ())), precision=precision, preferred_element_type=jnp.float32
    )


def split(value):
    high = value.astype(jnp.bfloat16)
    low = (value - high.astype(jnp.float32)).astype(jnp.bfloat16)
    return high, low


def pairs_of(panels):
    return [(p, q) for p in range(panels) for q in range(p + 1, panels)]


def gram_kernel(householder_ref, basis_ref, gram_ref, total):
    panels, width, columns = householder_ref.shape
    size = panels * width
    step = pl.program_id(0)

    @pl.when(step == 0)
    def _():
        total[...] = jnp.zeros_like(total)

    high, low = split(householder_ref[...].reshape(size, columns))
    both = jnp.concatenate([high, low], axis=0)
    basis_ref[...] = both
    first = product(both, high, ((1,), (1,)))
    second = product(both, low, ((1,), (1,)))
    total[...] += (first[:size] + first[size:]) + (second[:size] + second[size:])

    @pl.when(step == pl.num_programs(0) - 1)
    def _():
        blocks = [
            total[p * width : (p + 1) * width, q * width : (q + 1) * width] for p, q in pairs_of(panels)
        ]
        for i in range(0, len(blocks), 2):
            at = i // 2 * width
            gram_ref[at : at + width, :] = jnp.concatenate(blocks[i : i + 2], axis=1)


def project_kernel(core_ref, arrived_ref, basis_ref, current_ref, held_ref, kept_ref, sent_ref, total, joint, sems):
    count, rows = current_ref.shape
    size = basis_ref.shape[0] // 2
    copies = []
    for step in range(rows // COLUMNS):
        columns = pl.ds(step * COLUMNS, COLUMNS)
        copy = pltpu.make_async_copy(basis_ref.at[:, columns], held_ref.at[:, columns], sems.at[step])
        copy.start()
        copies.append(copy)
    total[...] = jnp.zeros_like(total)
    for step in range(rows // COLUMNS):
        columns = pl.ds(step * COLUMNS, COLUMNS)
        block = arrived_ref[:, :, columns].reshape(count, COLUMNS)
        current_ref[:, columns] = block
        high, low = split(block)
        both = jnp.concatenate([high, low], axis=0)
        copies[step].wait()
        total[...] += product(held_ref[:, columns], both, ((1,), (1,)))
    joint[...] = (total[:size, :count] + total[:size, count:]) + (total[size:, :count] + total[size:, count:])
    core = core_ref[0]
    half = size // 2
    kept_ref[...] = joint[pl.ds(pl.multiple_of(core * half, 8), half), :]
    sent_ref[...] = joint[pl.ds(pl.multiple_of((1 - core) * half, 8), half), :]


def finish_kernel(core_ref, own_ref, other_ref, gram_ref, tfactors_ref, current_ref, basis_ref, out_ref, joint, out, sems):
    panels, width, _ = tfactors_ref.shape
    count, rows = current_ref.shape
    size = panels * width
    core = core_ref[0]
    half = size // 2
    joint[pl.ds(pl.multiple_of(core * half, 8), half), :] = own_ref[...]
    joint[pl.ds(pl.multiple_of((1 - core) * half, 8), half), :] = other_ref[...]
    gram = {}
    for i, pair in enumerate(pairs_of(panels)):
        at = i // 2 * width
        gram[pair] = gram_ref[at : at + width, i % 2 * width : (i % 2 + 1) * width]
    exact = functools.partial(product, contract=((1,), (0,)), precision=lax.Precision.HIGHEST)
    scaled = [exact(tfactors_ref[p], joint[p * width : (p + 1) * width, :]) for p in range(panels)]
    links = {(p, q): exact(tfactors_ref[p], gram[p, q]) for p, q in gram}
    for q in range(panels - 1, 0, -1):
        for p in range(q):
            scaled[p] = scaled[p] - exact(links[p, q], scaled[q])
    high, low = split(jnp.concatenate(scaled, axis=0).T)
    both = jnp.concatenate([high, low], axis=0)
    copies = []
    for step in range(rows // COLUMNS):
        columns = pl.ds(step * COLUMNS, COLUMNS)
        first = product(both, basis_ref[:size, columns], ((1,), (0,)))
        second = product(high, basis_ref[size:, columns], ((1,), (0,)))
        out[:, columns] = current_ref[:, columns] - (first[:count] + (first[count:] + second))
        copy = pltpu.make_async_copy(out.at[:, columns], out_ref.at[:, columns], sems.at[step])
        copy.start()
        copies.append(copy)
    for copy in copies:
        copy.wait()


def in_vmem(value):
    return pltpu.with_memory_space_constraint(value, pltpu.VMEM)


def in_hbm(value):
    return pltpu.with_memory_space_constraint(value, pltpu.HBM)


def gram_call(householder):
    panels, width, rows = householder.shape
    size = panels * width
    height = len(pairs_of(panels)) // 2 * width
    return pl.pallas_call(
        gram_kernel,
        out_shape=(
            pltpu.HBM((2 * size, rows), jnp.bfloat16),
            jax.ShapeDtypeStruct((height, 2 * width), jnp.float32),
        ),
        grid=(rows // COLUMNS,),
        in_specs=[pl.BlockSpec((panels, width, COLUMNS), lambda i: (0, 0, i))],
        out_specs=(
            pl.BlockSpec((2 * size, COLUMNS), lambda i: (0, i)),
            pl.BlockSpec((height, 2 * width), lambda i: (0, 0)),
        ),
        scratch_shapes=[pltpu.VMEM((size, size), jnp.float32)],
        compiler_params=pltpu.CompilerParams(vmem_limit_bytes=LIMIT),
        cost_estimate=pl.CostEstimate(flops=8 * size * size * rows, bytes_accessed=8 * size * rows, transcendentals=0),
        name="gram",
    )(in_hbm(householder))


def project_call(core, arrived, basis):
    sources, each, rows = arrived.shape
    count = sources * each
    size = basis.shape[0] // 2
    return pl.pallas_call(
        project_kernel,
        out_shape=(
            pltpu.VMEM((count, rows), jnp.float32),
            pltpu.VMEM((2 * size, rows), jnp.bfloat16),
            pltpu.VMEM((size // 2, count), jnp.float32),
            pltpu.VMEM((size // 2, count), jnp.float32),
        ),
        in_specs=[IN_SMEM, IN_VMEM, pl.BlockSpec(memory_space=pltpu.HBM)],
        out_specs=(IN_VMEM, IN_VMEM, IN_VMEM, IN_VMEM),
        scratch_shapes=[
            pltpu.VMEM((2 * size, 2 * count), jnp.float32),
            pltpu.VMEM((size, count), jnp.float32),
            pltpu.SemaphoreType.DMA((rows // COLUMNS,)),
        ],
        compiler_params=pltpu.CompilerParams(vmem_limit_bytes=LIMIT),
        name="project",
    )(core, in_vmem(arrived), in_hbm(basis))


def finish_call(core, own, other, gram, tfactors, current, basis):
    count, rows = current.shape
    return pl.pallas_call(
        finish_kernel,
        out_shape=jax.ShapeDtypeStruct((count, rows), jnp.float32),
        in_specs=[IN_SMEM] + [IN_VMEM] * 6,
        out_specs=IN_HBM,
        scratch_shapes=[
            pltpu.VMEM((2 * own.shape[0], count), jnp.float32),
            pltpu.VMEM((count, rows), jnp.float32),
            pltpu.SemaphoreType.DMA((rows // COLUMNS,)),
        ],
        compiler_params=pltpu.CompilerParams(vmem_limit_bytes=LIMIT),
        name="finish",
    )(core, in_vmem(own), in_vmem(other), gram, tfactors, in_vmem(current), in_vmem(basis))


def solution(mesh):
    devices, columns = mesh.shape["row"], mesh.shape["col"]
    planes = devices // 4
    row = ("z", "y", "core")
    parts = Mesh(mesh.devices.reshape(planes, 2, 2, columns), row + ("col",))

    def swap(value, flip):
        return lax.ppermute(value, row, [(i, i ^ flip) for i in range(devices)])

    def shards(vectors_in, householder, tfactors):
        core = jnp.reshape(lax.axis_index("core"), (1,)).astype(jnp.int32)
        arrived = lax.all_to_all(
            vectors_in.reshape(vectors_in.shape[0], devices, -1), row, split_axis=1, concat_axis=0
        )
        basis, gram = gram_call(householder)
        gram = gram + swap(gram, 1)
        gram = gram + swap(gram, 2)
        gram = lax.psum(gram, "z")
        current, held, kept, sent = project_call(core, arrived, basis)
        value = kept + swap(sent, 1)
        value = value + swap(value, 2)
        first, second, third = swap(value, 4), swap(value, 8), swap(value, 12)
        value = (value + first) + (second + third)
        value = value + swap(value, 24)
        other = swap(value, 1)
        return finish_call(core, value, other, gram, tfactors, current, held)

    in_specs = (P(("col",) + row, None), P(None, None, row), P())
    out_specs = P("col", row)
    return jax.shard_map(shards, mesh=parts, in_specs=in_specs, out_specs=out_specs, check_vma=False)
```

time: 125 us -> 205 us (1.64)
  waiting for transfers between devices: 88.5 us -> 144 us
  between operations: 0.11 us -> 13.5 us
  Pallas kernels: 11.6 us -> 17.9 us
  starting transfers between devices: 15.4 us -> 18.6 us
    psum x0 -> x1, waiting for transfers between devices: none -> 65.3 us  [shards(): gram = lax.psum(gram, 'z')]
    ppermute x7 -> x9, waiting for transfers between devices: 26.2 us -> 13.7 us  [swap(): return lax.ppermute(value, row, [(i, i ^ flip) for i in range(devices)])]
    pallas_call x1, Pallas kernels: 1.86 us -> 5.87 us  [project_call(): pl.pallas_call(project_kernel, out_shape=(pltpu.VMEM((count, rows), jnp.f...]
    ppermute x7 -> x9, starting transfers between devices: 3.89 us -> 7.06 us  [swap(): return lax.ppermute(value, row, [(i, i ^ flip) for i in range(devices)])]
    all_to_all x1, waiting for transfers between devices: 62.3 us -> 65.4 us  [shards(): lax.all_to_all(vectors_in.reshape(vectors_in.shape[0], devices, -1), row,...]
    pallas_call x1, Pallas kernels: 6.52 us -> 8.83 us  [gram_call(): pl.pallas_call(gram_kernel, out_shape=(pltpu.HBM((2 * size, rows), jnp.bf...]
    unnamed x8 -> x12, local copies, waits for them, and re-layouts: 8.2 us -> 9.9 us
  transfers between devices with their start and end apart: 8 -> 11, of which waited for: 8 -> 8; matrix products, arithmetic and copies ran while one was open for 0% -> 0% of each run, Pallas kernels for 5% -> 4%
where the time goes in v3:
time: 205 us
  waiting for transfers between devices  144 us (70%)
  starting transfers between devices  18.6 us (9%)
  Pallas kernels  17.9 us (9%)
  between operations  13.5 us (7%)
  local copies, waits for them, and re-layouts  9.9 us (5%)
    all_to_all x1, waiting for transfers between devices, shards(): lax.all_to_all(vectors_in.reshape(vectors_in.shape[0], devices, -1), row,...  65.4 us
    psum x1, waiting for transfers between devices, shards(): gram = lax.psum(gram, 'z')  65.3 us
    ppermute x9, waiting for transfers between devices, swap(): return lax.ppermute(value, row, [(i, i ^ flip) for i in range(devices)])  13.7 us
    all_to_all x1, starting transfers between devices, shards(): lax.all_to_all(vectors_in.reshape(vectors_in.shape[0], devices, -1), row,...  11.5 us
    unnamed x12, local copies, waits for them, and re-layouts  9.9 us
    pallas_call x1, Pallas kernels, gram_call(): pl.pallas_call(gram_kernel, out_shape=(pltpu.HBM((2 * size, rows), jnp.bf...  8.83 us
    ppermute x9, starting transfers between devices, swap(): return lax.ppermute(value, row, [(i, i ^ flip) for i in range(devices)])  7.06 us
    pallas_call x1, Pallas kernels, project_call(): pl.pallas_call(project_kernel, out_shape=(pltpu.VMEM((count, rows), jnp.f...  5.87 us
  transfers between devices with their start and end apart: 11, of which 8 were waited for; matrix products, arithmetic and copies ran while one was open for 0% of the time, Pallas kernels for 4%

profile of v3, /device:TPU:4, one launch (start us, length us, event | category | flops | bytes accessed | tf_op | source)
XLA Modules:
  0.0 205.0 jit_solution(622057068010675983)
XLA Ops:
  6.5 11.5 %all-to-all-start = ((f32[1,4,32,6144]{3,1,0,2:T(4,128)}), f32[1,4,32,6144]{3,1,0,2:T(4,128)S(1)}, u32[]{:S(2)}, u32[]{:S(2)}) async-start(f32[1,4,32,6144]{3,1,0,2:T(4,128)} %bitcast.8), calls=%async_computation | async-start | bytes 6291456 | tf_op jit(solution)/shard_map/all_to_all | solution.py:201
  18.0 0.0 all-reduce.2.cloned.1.call-start
  18.1 8.8 %gram.1 = (bf16[512,6144]{1,0:T(8,128)(2,1)}, f32[192,128]{1,0:T(8,128)S(1)}) custom-call(f32[4,64,6144]{2,1,0:T(8,128)} %householder_ref.1), custom_call_target="tpu_custom_call" | custom-call | flops 3221225472 | bytes 12582912 | tf_op jit(solution)/shard_map/gram/pallas_call | solution.py:130
  26.9 65.4 %all-to-all-done = f32[1,4,32,6144]{3,1,0,2:T(4,128)S(1)} async-done(((f32[1,4,32,6144]{3,1,0,2:T(4,128)}), f32[1,4,32,6144]{3,1,0,2:T(4,128)S(1)}, u32[]{:S(2)}, u32[]{:S(2)}) %all-to-all-start) | async-done | bytes 3145760 | tf_op jit(solution)/shard_map/all_to_all | solution.py:201
  92.3 0.0 copy-start.4
  92.3 5.9 %project.1 = (f32[128,6144]{1,0:T(8,128)S(1)}, bf16[512,6144]{1,0:T(8,128)(2,1)S(1)}, f32[128,128]{1,0:T(8,128)S(1)}, f32[128,128]{1,0:T(8,128)S(1)}) custom-call(s32[1]{0:T(128)} %bitcast.core_ref, f32[32,4,6144]{2,1,0:T(4,128)S(1)} %bitcast.7, bf16[512,6144]{1,0:T(8,128)(2,1)} %get-tuple-element.11.basis_ref), custom_call_target="tpu_custom_call" | custom-call | tf_op jit(solution)/shard_map/project/pallas_call | solution.py:153
  98.2 0.0 copy-start
  98.2 2.7 %copy-done = bf16[512,6144]{1,0:T(8,128)(2,1)} copy-done((bf16[512,6144]{1,0:T(8,128)(2,1)}, bf16[512,6144]{1,0:T(8,128)(2,1)S(1)}, u32[]{:S(2)}) %copy-start) | copy-done | bytes 6291480
  100.8 0.0 copy-start.2
  100.8 1.7 copy-done.2
  102.5 0.1 collective-permute-start
  102.6 1.2 collective-permute-done
  103.8 1.2 collective-permute-start.1
  105.0 0.0 collective-permute-start.7
  105.0 4.7 %collective-permute-done.1 = f32[128,128]{1,0:T(8,128)S(1)} collective-permute-done((f32[128,128]{1,0:T(8,128)S(1)}, f32[128,128]{1,0:T(8,128)S(1)}, u32[]{:S(2)}, u32[]{:S(2)}) %collective-permute-start.1) | collective-permute-done | bytes 65568 | tf_op jit(solution)/shard_map/ppermute | solution.py:197
  109.7 0.1 collective-permute-start.4
  109.8 2.0 collective-permute-start.3
  111.7 2.4 %collective-permute-start.2 = (f32[128,128]{1,0:T(8,128)S(1)}, f32[128,128]{1,0:T(8,128)S(1)}, u32[]{:S(2)}, u32[]{:S(2)}) collective-permute-start(f32[128,128]{1,0:T(8,128)S(1)} %add.27), channel_id=1, source_target_pairs={{0,32},{8,40},{16,48},{24,56},{32,0},{40,8},{48,16},{56,24},{64,96... | collective-permute-start | bytes 196616 | tf_op jit(solution)/shard_map/ppermute | solution.py:197
  114.1 0.0 collective-permute-done.7
  114.1 1.2 collective-permute-start.8
  115.3 0.8 collective-permute-done.4
  116.1 1.3 collective-permute-done.3
  117.4 0.0 collective-permute-done.2
  117.4 0.1 collective-permute-start.5
  117.5 2.9 %collective-permute-done.8 = f32[192,128]{1,0:T(8,128)S(1)} collective-permute-done((f32[192,128]{1,0:T(8,128)S(1)}, f32[192,128]{1,0:T(8,128)S(1)}, u32[]{:S(2)}, u32[]{:S(2)}) %collective-permute-start.8) | collective-permute-done | bytes 98336 | tf_op jit(solution)/shard_map/ppermute | solution.py:197
  120.4 0.7 add.33
  121.0 0.0 all-reduce.2.cloned.1.call-update
  121.0 2.9 %collective-permute-done.5 = f32[128,128]{1,0:T(8,128)S(1)} collective-permute-done((f32[128,128]{1,0:T(8,128)S(1)}, f32[128,128]{1,0:T(8,128)S(1)}, u32[]{:S(2)}, u32[]{:S(2)}) %collective-permute-start.5) | collective-permute-done | bytes 65568 | tf_op jit(solution)/shard_map/ppermute | solution.py:197
  124.0 0.1 collective-permute-start.6
  124.1 65.3 %all-reduce.2.cloned.1.call-done.gram_ref = f32[192,128]{1,0:T(8,128)} async-done(((f32[192,128]{1,0:T(8,128)}), f32[192,128]{1,0:T(8,128)}) %all-reduce.2.cloned.1.call-update) | async-done | bytes 98320 | tf_op jit(solution)/shard_map/psum | solution.py:207
  189.4 0.0 collective-permute-done.6.other_ref
  189.4 0.0 copy-done.4
  189.4 0.0 copy-start.1
  189.4 2.8 %copy-done.1 = bf16[512,6144]{1,0:T(8,128)(2,1)S(1)} copy-done((bf16[512,6144]{1,0:T(8,128)(2,1)S(1)}, bf16[512,6144]{1,0:T(8,128)(2,1)}, u32[]{:S(2)}) %copy-start.1) | copy-done | bytes 6291480
  192.1 0.0 copy-start.3
  192.1 1.9 copy-done.3
  194.0 0.0 copy-start.5
  194.0 0.9 copy-done.5
  194.9 3.2 %finish.1 = f32[128,6144]{1,0:T(8,128)} custom-call(s32[1]{0:T(128)} %bitcast.core_ref, f32[128,128]{1,0:T(8,128)S(1)} %add.31.own_ref, f32[128,128]{1,0:T(8,128)S(1)} %collective-permute-done.6.other_ref, f32[192,128]{1,0:T(8,128)S(1)} %copy-done.5, f32[4,64,64]{2,1,0:T(8,128)S(1)} %copy-done.4, f32[128,6144]{1,0:T(8,128)S(1)} %copy-done.3, ...), custom_call_target="tpu_custom_call" | custom-call | tf_op jit(solution)/shard_map/finish/pallas_call | solution.py:175
  (5 shorter events, 0.1 us)
Async XLA Ops:
  6.5 85.8 %all-to-all-start = ((f32[1,4,32,6144]{3,1,0,2:T(4,128)}), f32[1,4,32,6144]{3,1,0,2:T(4,128)S(1)}, u32[]{:S(2)}, u32[]{:S(2)}) async-start(f32[1,4,32,6144]{3,1,0,2:T(4,128)} %bitcast.8), calls=%async_computation | async-start | bytes 6291456 | tf_op jit(solution)/shard_map/all_to_all | solution.py:201
  18.0 171.3 %all-reduce.2.cloned.1.call-start = ((), (), s32[]{:S(2)}) async-start(), calls=%async_computation.1 | async-start | bytes 196608 | tf_op jit(solution)/shard_map/psum | solution.py:207
  92.3 97.1 %copy-start.4 = (f32[4,64,64]{2,1,0:T(8,128)S(1)}, f32[4,64,64]{2,1,0:T(8,128)}, u32[]{:S(2)}) copy-start(f32[4,64,64]{2,1,0:T(8,128)} %tfactors_ref.1) | copy-start | bytes 196612
  98.2 2.7 %copy-start = (bf16[512,6144]{1,0:T(8,128)(2,1)}, bf16[512,6144]{1,0:T(8,128)(2,1)S(1)}, u32[]{:S(2)}) copy-start(bf16[512,6144]{1,0:T(8,128)(2,1)S(1)} %get-tuple-element.16.basis_ref) | copy-start | bytes 18874372
  100.8 1.7 copy-start.2
  102.5 1.3 collective-permute-start
  103.8 5.9 %collective-permute-start.1 = (f32[128,128]{1,0:T(8,128)S(1)}, f32[128,128]{1,0:T(8,128)S(1)}, u32[]{:S(2)}, u32[]{:S(2)}) collective-permute-start(f32[128,128]{1,0:T(8,128)S(1)} %add.26), channel_id=1, source_target_pairs={{0,16},{8,24},{16,0},{24,8},{32,48},{40,56},{48,32},{56,40},{64,80... | collective-permute-start | bytes 196616 | tf_op jit(solution)/shard_map/ppermute | solution.py:197
  105.0 9.2 %collective-permute-start.7 = (f32[192,128]{1,0:T(8,128)S(1)}, f32[192,128]{1,0:T(8,128)S(1)}, u32[]{:S(2)}, u32[]{:S(2)}) collective-permute-start(f32[192,128]{1,0:T(8,128)S(1)} %get-tuple-element.14), channel_id=1, source_target_pairs={{0,8},{8,0},{16,24},{24,16},{32,40},{40,32},{48,56},{56,48},{64,72... | collective-permute-start | bytes 294920 | tf_op jit(solution)/shard_map/ppermute | solution.py:197
  109.7 6.4 %collective-permute-start.4 = (f32[128,128]{1,0:T(8,128)S(1)}, f32[128,128]{1,0:T(8,128)S(1)}, u32[]{:S(2)}, u32[]{:S(2)}) collective-permute-start(f32[128,128]{1,0:T(8,128)S(1)} %add.27), channel_id=1, source_target_pairs={{0,96},{8,104},{16,112},{24,120},{32,64},{40,72},{48,80},{56,88},{... | collective-permute-start | bytes 196616 | tf_op jit(solution)/shard_map/ppermute | solution.py:197
  109.8 7.6 %collective-permute-start.3 = (f32[128,128]{1,0:T(8,128)S(1)}, f32[128,128]{1,0:T(8,128)S(1)}, u32[]{:S(2)}, u32[]{:S(2)}) collective-permute-start(f32[128,128]{1,0:T(8,128)S(1)} %add.27), channel_id=1, source_target_pairs={{0,64},{8,72},{16,80},{24,88},{32,96},{40,104},{48,112},{56,120},{... | collective-permute-start | bytes 196616 | tf_op jit(solution)/shard_map/ppermute | solution.py:197
  111.7 5.6 %collective-permute-start.2 = (f32[128,128]{1,0:T(8,128)S(1)}, f32[128,128]{1,0:T(8,128)S(1)}, u32[]{:S(2)}, u32[]{:S(2)}) collective-permute-start(f32[128,128]{1,0:T(8,128)S(1)} %add.27), channel_id=1, source_target_pairs={{0,32},{8,40},{16,48},{24,56},{32,0},{40,8},{48,16},{56,24},{64,96... | collective-permute-start | bytes 196616 | tf_op jit(solution)/shard_map/ppermute | solution.py:197
  114.1 6.2 %collective-permute-start.8 = (f32[192,128]{1,0:T(8,128)S(1)}, f32[192,128]{1,0:T(8,128)S(1)}, u32[]{:S(2)}, u32[]{:S(2)}) collective-permute-start(f32[192,128]{1,0:T(8,128)S(1)} %add.32), channel_id=1, source_target_pairs={{0,16},{8,24},{16,0},{24,8},{32,48},{40,56},{48,32},{56,40},{64,80... | collective-permute-start | bytes 294920 | tf_op jit(solution)/shard_map/ppermute | solution.py:197
  117.4 6.6 %collective-permute-start.5 = (f32[128,128]{1,0:T(8,128)S(1)}, f32[128,128]{1,0:T(8,128)S(1)}, u32[]{:S(2)}, u32[]{:S(2)}) collective-permute-start(f32[128,128]{1,0:T(8,128)S(1)} %add_add_fusion), channel_id=1, source_target_pairs={{0,192},{8,200},{16,208},{24,216},{32,224},{40,232},{48,240},{56,2... | collective-permute-start | bytes 196616 | tf_op jit(solution)/shard_map/ppermute | solution.py:197
  124.0 65.4 %collective-permute-start.6 = (f32[128,128]{1,0:T(8,128)S(1)}, f32[128,128]{1,0:T(8,128)S(1)}, u32[]{:S(2)}, u32[]{:S(2)}) collective-permute-start(f32[128,128]{1,0:T(8,128)S(1)} %add.31.own_ref), channel_id=1, source_target_pairs={{0,8},{8,0},{16,24},{24,16},{32,40},{40,32},{48,56},{56,48},{64,72... | collective-permute-start | bytes 196616 | tf_op jit(solution)/shard_map/ppermute | solution.py:197
  189.4 2.8 %copy-start.1 = (bf16[512,6144]{1,0:T(8,128)(2,1)S(1)}, bf16[512,6144]{1,0:T(8,128)(2,1)}, u32[]{:S(2)}) copy-start(bf16[512,6144]{1,0:T(8,128)(2,1)} %copy-done) | copy-start | bytes 18874372
  192.1 1.9 copy-start.3
  194.0 0.9 copy-start.5
Sparse Core Ops, SparseCore 0:
  121.2 68.1 all-reduce.1

commit v4 on v3

v4 whole, which is shorter than its diff:
```python
import functools

import jax
import jax.numpy as jnp
from jax import lax
from jax.experimental import pallas as pl
from jax.experimental.pallas import tpu as pltpu
from jax.sharding import PartitionSpec as P

COLUMNS = 1024
LIMIT = 40 * 1024 * 1024
IN_VMEM = pl.BlockSpec(memory_space=pltpu.VMEM)
IN_SMEM = pl.BlockSpec(memory_space=pltpu.SMEM)
IN_HBM = pl.BlockSpec(memory_space=pl.ANY)


def product(left, right, contract, precision=None):
    return lax.dot_general(
        left, right, (contract, ((), ())), precision=precision, preferred_element_type=jnp.float32
    )


def split(value):
    high = value.astype(jnp.bfloat16)
    low = (value - high.astype(jnp.float32)).astype(jnp.bfloat16)
    return high, low


def pairs_of(panels):
    return [(p, q) for p in range(panels) for q in range(p + 1, panels)]


def halves(core, whole, own_ref, other_ref):
    half = whole.shape[0] // 2
    own_ref[...] = whole[pl.ds(pl.multiple_of(core * half, 8), half), :]
    other_ref[...] = whole[pl.ds(pl.multiple_of((1 - core) * half, 8), half), :]


def gram_kernel(core_ref, householder_ref, high_ref, low_ref, kept_ref, sent_ref, total, packed):
    panels, width, columns = householder_ref.shape
    size = panels * width
    step = pl.program_id(0)

    @pl.when(step == 0)
    def _():
        total[...] = jnp.zeros_like(total)

    high, low = split(householder_ref[...].reshape(size, columns))
    high_ref[...] = high
    low_ref[...] = low
    both = jnp.concatenate([high, low], axis=0)
    first = product(both, high, ((1,), (1,)))
    second = product(both, low, ((1,), (1,)))
    total[...] += (first[:size] + first[size:]) + (second[:size] + second[size:])

    @pl.when(step == pl.num_programs(0) - 1)
    def _():
        blocks = [
            total[p * width : (p + 1) * width, q * width : (q + 1) * width] for p, q in pairs_of(panels)
        ]
        for i in range(0, len(blocks), 2):
            at = i // 2 * width
            packed[at : at + width, :] = jnp.concatenate(blocks[i : i + 2], axis=1)
        halves(core_ref[0], packed, kept_ref, sent_ref)


def project_high_kernel(arrived_ref, high_ref, current_ref, rounded_ref, total_ref):
    count, rows = current_ref.shape
    total_ref[...] = jnp.zeros_like(total_ref)
    for step in range(rows // COLUMNS):
        columns = pl.ds(step * COLUMNS, COLUMNS)
        block = arrived_ref[:, :, columns].reshape(count, COLUMNS)
        current_ref[:, columns] = block
        high, low = split(block)
        rounded_ref[:, columns] = high
        both = jnp.concatenate([high, low], axis=0)
        total_ref[...] += product(high_ref[:, columns], both, ((1,), (1,)))


def project_low_kernel(core_ref, total_ref, rounded_ref, low_ref, before_ref, kept_ref, sent_ref, whole):
    del before_ref
    count = rounded_ref.shape[0]
    whole[...] = total_ref[:, :count] + (
        total_ref[:, count:] + product(low_ref[...], rounded_ref[...], ((1,), (1,)))
    )
    halves(core_ref[0], whole, kept_ref, sent_ref)


def finish_kernel(core_ref, own_ref, other_ref, tfactors_ref, current_ref, high_ref, low_ref, out_ref, joint, packed, out, sems):
    panels, width, _ = tfactors_ref.shape
    count, rows = current_ref.shape
    core = core_ref[0]
    half, rest = joint.shape[0] // 2, packed.shape[0] // 2
    for side, part_ref in ((core, own_ref), (1 - core, other_ref)):
        joint[pl.ds(pl.multiple_of(side * half, 8), half), :] = part_ref[:half, :]
        packed[pl.ds(pl.multiple_of(side * rest, 8), rest), :] = part_ref[half:, :]
    gram = {}
    for i, pair in enumerate(pairs_of(panels)):
        at = i // 2 * width
        gram[pair] = packed[at : at + width, i % 2 * width : (i % 2 + 1) * width]
    exact = functools.partial(product, contract=((1,), (0,)), precision=lax.Precision.HIGHEST)
    scaled = [exact(tfactors_ref[p], joint[p * width : (p + 1) * width, :]) for p in range(panels)]
    links = {(p, q): exact(tfactors_ref[p], gram[p, q]) for p, q in gram}
    for q in range(panels - 1, 0, -1):
        for p in range(q):
            scaled[p] = scaled[p] - exact(links[p, q], scaled[q])
    high, low = split(jnp.concatenate(scaled, axis=0).T)
    both = jnp.concatenate([high, low], axis=0)
    copies = []
    for step in range(rows // COLUMNS):
        columns = pl.ds(step * COLUMNS, COLUMNS)
        first = product(both, high_ref[:, columns], ((1,), (0,)))
        second = product(high, low_ref[:, columns], ((1,), (0,)))
        out[:, columns] = current_ref[:, columns] - (first[:count] + (first[count:] + second))
        copy = pltpu.make_async_copy(out.at[:, columns], out_ref.at[:, columns], sems.at[step])
        copy.start()
        copies.append(copy)
    for copy in copies:
        copy.wait()


def in_vmem(value):
    return pltpu.with_memory_space_constraint(value, pltpu.VMEM)


def in_hbm(value):
    return pltpu.with_memory_space_constraint(value, pltpu.HBM)


def gram_call(core, householder):
    panels, width, rows = householder.shape
    size = panels * width
    height = len(pairs_of(panels)) // 2 * width
    return pl.pallas_call(
        gram_kernel,
        out_shape=(
            pltpu.HBM((size, rows), jnp.bfloat16),
            pltpu.HBM((size, rows), jnp.bfloat16),
            jax.ShapeDtypeStruct((height // 2, 2 * width), jnp.float32),
            jax.ShapeDtypeStruct((height // 2, 2 * width), jnp.float32),
        ),
        grid=(rows // COLUMNS,),
        in_specs=[IN_SMEM, pl.BlockSpec((panels, width, COLUMNS), lambda i: (0, 0, i))],
        out_specs=(
            pl.BlockSpec((size, COLUMNS), lambda i: (0, i)),
            pl.BlockSpec((size, COLUMNS), lambda i: (0, i)),
            pl.BlockSpec((height // 2, 2 * width), lambda i: (0, 0)),
            pl.BlockSpec((height // 2, 2 * width), lambda i: (0, 0)),
        ),
        scratch_shapes=[pltpu.VMEM((size, size), jnp.float32), pltpu.VMEM((height, 2 * width), jnp.float32)],
        compiler_params=pltpu.CompilerParams(vmem_limit_bytes=LIMIT),
        cost_estimate=pl.CostEstimate(flops=8 * size * size * rows, bytes_accessed=8 * size * rows, transcendentals=0),
        name="gram",
    )(core, in_hbm(householder))


def project_call(core, arrived, high, low, before):
    sources, each, rows = arrived.shape
    count = sources * each
    size = high.shape[0]
    current, rounded, total = pl.pallas_call(
        project_high_kernel,
        out_shape=(
            pltpu.VMEM((count, rows), jnp.float32),
            pltpu.VMEM((count, rows), jnp.bfloat16),
            pltpu.VMEM((size, 2 * count), jnp.float32),
        ),
        in_specs=[IN_VMEM, IN_VMEM],
        out_specs=(IN_VMEM, IN_VMEM, IN_VMEM),
        compiler_params=pltpu.CompilerParams(vmem_limit_bytes=LIMIT),
        name="project_high",
    )(in_vmem(arrived), in_vmem(high))
    kept, sent = pl.pallas_call(
        project_low_kernel,
        out_shape=(
            pltpu.VMEM((size // 2, count), jnp.float32),
            pltpu.VMEM((size // 2, count), jnp.float32),
        ),
        in_specs=[IN_SMEM, IN_VMEM, IN_VMEM, IN_VMEM, IN_HBM],
        out_specs=(IN_VMEM, IN_VMEM),
        scratch_shapes=[pltpu.VMEM((size, count), jnp.float32)],
        compiler_params=pltpu.CompilerParams(vmem_limit_bytes=LIMIT),
        name="project_low",
    )(core, in_vmem(total), in_vmem(rounded), in_vmem(low), before)
    return current, kept, sent


def finish_call(core, own, other, tfactors, current, high, low):
    count, rows = current.shape
    size = high.shape[0]
    return pl.pallas_call(
        finish_kernel,
        out_shape=jax.ShapeDtypeStruct((count, rows), jnp.float32),
        in_specs=[IN_SMEM] + [IN_VMEM] * 6,
        out_specs=IN_HBM,
        scratch_shapes=[
            pltpu.VMEM((size, count), jnp.float32),
            pltpu.VMEM((2 * own.shape[0] - size, count), jnp.float32),
            pltpu.VMEM((count, rows), jnp.float32),
            pltpu.SemaphoreType.DMA((rows // COLUMNS,)),
        ],
        compiler_params=pltpu.CompilerParams(vmem_limit_bytes=LIMIT),
        name="finish",
    )(core, in_vmem(own), in_vmem(other), tfactors, in_vmem(current), in_vmem(high), in_vmem(low))


def solution(mesh):
    devices = mesh.shape["row"]

    def swap(value, flip):
        return lax.ppermute(value, "row", [(i, i ^ flip) for i in range(devices)])

    def shards(vectors_in, householder, tfactors):
        core = jnp.reshape(lax.axis_index("row") % 2, (1,)).astype(jnp.int32)
        arrived = lax.all_to_all(
            vectors_in.reshape(vectors_in.shape[0], devices, -1), "row", split_axis=1, concat_axis=0
        )
        high, low, gram, sent = gram_call(core, householder)
        gram = gram + swap(sent, 1)
        gram = gram + swap(gram, 2)
        gram = gram + swap(gram, 4)
        current, value, sent = project_call(core, arrived, high, low, gram)
        value = value + swap(sent, 1)
        across = swap(value, 2)
        gram = gram + swap(gram, 24)
        value = value + across
        first, third = swap(value, 4), swap(value, 12)
        second = swap(jnp.concatenate([value, gram], axis=0), 8)
        half = value.shape[0]
        value = (value + first) + (second[:half] + third)
        gram = gram + second[half:]
        value = value + swap(value, 24)
        own = jnp.concatenate([value, gram], axis=0)
        other = swap(own, 1)
        return finish_call(core, own, other, tfactors, current, high, low)

    in_specs = (P(("col", "row"), None), P(None, None, "row"), P())
    out_specs = P("col", "row")
    return jax.shard_map(shards, mesh=mesh, in_specs=in_specs, out_specs=out_specs, check_vma=False)
```

time: 205 us -> 123 us (0.60)
  waiting for transfers between devices: 144 us -> 81.3 us
  between operations: 13.5 us -> 0.1 us
  local copies, waits for them, and re-layouts: 9.9 us -> 2.3 us
  starting transfers between devices: 18.6 us -> 23.6 us
  Pallas kernels: 17.9 us -> 14.5 us
    psum x1 -> x0, waiting for transfers between devices: 65.3 us -> none  [shards(): gram = lax.psum(gram, 'z')]
    ppermute x9 -> x11, waiting for transfers between devices: 13.7 us -> 78.3 us  [swap(): return lax.ppermute(value, 'row', [(i, i ^ flip) for i in range(devices)])]
    all_to_all x1, waiting for transfers between devices: 65.4 us -> 2.95 us  [shards(): lax.all_to_all(vectors_in.reshape(vectors_in.shape[0], devices, -1), 'row...]
    unnamed x12 -> x8, local copies, waits for them, and re-layouts: 9.9 us -> 2.3 us
    ppermute x9 -> x11, starting transfers between devices: 7.06 us -> 12.1 us  [swap(): return lax.ppermute(value, 'row', [(i, i ^ flip) for i in range(devices)])]
    pallas_call x2 -> x3, Pallas kernels: 14.7 us -> 11.2 us  [the longest x1 8.78 us: gram_call(): pl.pallas_call(gram_kernel, out_shape=(pltpu.HBM((size, rows), jnp.bfloat...]
  transfers between devices with their start and end apart: 11 -> 12, of which waited for: 8 -> 10; matrix products, arithmetic and copies ran while one was open for 0% -> 0% of each run, Pallas kernels for 4% -> 7%
where the time goes in v4:
time: 123 us; the launch traced here: 122 us
  waiting for transfers between devices  81.3 us (66%)
  starting transfers between devices  23.6 us (19%)
  Pallas kernels  14.5 us (12%)
  local copies, waits for them, and re-layouts  2.3 us (2%)
    ppermute x11, waiting for transfers between devices, swap(): return lax.ppermute(value, 'row', [(i, i ^ flip) for i in range(devices)])  78.3 us
    ppermute x11, starting transfers between devices, swap(): return lax.ppermute(value, 'row', [(i, i ^ flip) for i in range(devices)])  12.1 us
    all_to_all x1, starting transfers between devices, shards(): lax.all_to_all(vectors_in.reshape(vectors_in.shape[0], devices, -1), 'row...  11.5 us
    pallas_call x1, Pallas kernels, gram_call(): pl.pallas_call(gram_kernel, out_shape=(pltpu.HBM((size, rows), jnp.bfloat...  8.78 us
    pallas_call x1, Pallas kernels, finish_call(): pl.pallas_call(finish_kernel, out_shape=jax.ShapeDtypeStruct((count, rows...  3.21 us
    all_to_all x1, waiting for transfers between devices, shards(): lax.all_to_all(vectors_in.reshape(vectors_in.shape[0], devices, -1), 'row...  2.95 us
  transfers between devices with their start and end apart: 12, of which 10 were waited for; matrix products, arithmetic and copies ran while one was open for 0% of the time, Pallas kernels for 7%

profile of v4, /device:TPU:4, one launch (start us, length us, event | category | flops | bytes accessed | tf_op | source)
XLA Modules:
  0.0 121.9 jit_solution(6774266943618913181)
XLA Ops:
  0.0 11.5 %all-to-all-start = ((f32[1,4,32,6144]{3,1,0,2:T(4,128)}), f32[1,4,32,6144]{3,1,0,2:T(4,128)S(1)}, u32[]{:S(2)}, u32[]{:S(2)}) async-start(f32[1,4,32,6144]{3,1,0,2:T(4,128)} %bitcast.8), calls=%async_computation | async-start | bytes 6291456 | tf_op jit(solution)/shard_map/all_to_all | solution.py:215
  11.5 8.8 %gram.1 = (bf16[256,6144]{1,0:T(8,128)(2,1)}, bf16[256,6144]{1,0:T(8,128)(2,1)}, f32[96,128]{1,0:T(8,128)S(1)}, f32[96,128]{1,0:T(8,128)S(1)}) custom-call(s32[1]{0:T(128)} %bitcast.core_ref, f32[4,64,6144]{2,1,0:T(8,128)} %householder_ref.1), custom_call_target="tpu_custom_call" | custom-call | flops 3221225472 | bytes 12582912 | tf_op jit(solution)/shard_map/gram/pallas_call | solution.py:134
  20.3 0.3 collective-permute-start
  20.6 1.0 collective-permute-done
  21.5 3.4 %collective-permute-start.1 = (f32[96,128]{1,0:T(8,128)S(1)}, f32[96,128]{1,0:T(8,128)S(1)}, u32[]{:S(2)}, u32[]{:S(2)}) collective-permute-start(f32[96,128]{1,0:T(8,128)S(1)} %add.38), channel_id=1, source_target_pairs={{0,16},{8,24},{16,0},{24,8},{32,48},{40,56},{48,32},{56,40},{64,80... | collective-permute-start | bytes 147464 | tf_op jit(solution)/shard_map/ppermute | solution.py:211
  24.9 5.3 %collective-permute-done.1 = f32[96,128]{1,0:T(8,128)S(1)} collective-permute-done((f32[96,128]{1,0:T(8,128)S(1)}, f32[96,128]{1,0:T(8,128)S(1)}, u32[]{:S(2)}, u32[]{:S(2)}) %collective-permute-start.1) | collective-permute-done | bytes 49184 | tf_op jit(solution)/shard_map/ppermute | solution.py:211
  30.2 0.3 collective-permute-start.2
  30.5 52.3 %collective-permute-done.2 = f32[96,128]{1,0:T(8,128)S(1)} collective-permute-done((f32[96,128]{1,0:T(8,128)S(1)}, f32[96,128]{1,0:T(8,128)S(1)}, u32[]{:S(2)}, u32[]{:S(2)}) %collective-permute-start.2) | collective-permute-done | bytes 49184 | tf_op jit(solution)/shard_map/ppermute | solution.py:211
  82.9 3.0 %all-to-all-done = f32[1,4,32,6144]{3,1,0,2:T(4,128)S(1)} async-done(((f32[1,4,32,6144]{3,1,0,2:T(4,128)}), f32[1,4,32,6144]{3,1,0,2:T(4,128)S(1)}, u32[]{:S(2)}, u32[]{:S(2)}) %all-to-all-start) | async-done | bytes 3145760 | tf_op jit(solution)/shard_map/all_to_all | solution.py:215
  85.8 0.0 copy-start
  85.8 1.9 %copy-done = bf16[256,6144]{1,0:T(8,128)(2,1)S(1)} copy-done((bf16[256,6144]{1,0:T(8,128)(2,1)S(1)}, bf16[256,6144]{1,0:T(8,128)(2,1)}, u32[]{:S(2)}) %copy-start) | copy-done | bytes 3145752
  87.7 0.0 copy-start.2
  87.7 1.5 %project_high.1 = (f32[128,6144]{1,0:T(8,128)S(1)}, bf16[128,6144]{1,0:T(8,128)(2,1)S(1)}, f32[256,256]{1,0:T(8,128)S(1)}) custom-call(f32[32,4,6144]{2,1,0:T(4,128)S(1)} %bitcast.7, bf16[256,6144]{1,0:T(8,128)(2,1)S(1)} %copy-done), custom_call_target="tpu_custom_call" | custom-call | tf_op jit(solution)/shard_map/project_high/pallas_call | solution.py:161
  89.2 0.4 copy-done.2
  89.6 0.0 copy-start.1
  89.6 0.0 copy-start.3
  89.6 1.0 project_low.1
  90.6 0.1 collective-permute-start.3
  90.7 1.2 %collective-permute-done.3 = f32[128,128]{1,0:T(8,128)S(1)} collective-permute-done((f32[128,128]{1,0:T(8,128)S(1)}, f32[128,128]{1,0:T(8,128)S(1)}, u32[]{:S(2)}, u32[]{:S(2)}) %collective-permute-start.3) | collective-permute-done | bytes 65568 | tf_op jit(solution)/shard_map/ppermute | solution.py:211
  91.9 3.1 %collective-permute-start.4 = (f32[128,128]{1,0:T(8,128)S(1)}, f32[128,128]{1,0:T(8,128)S(1)}, u32[]{:S(2)}, u32[]{:S(2)}) collective-permute-start(f32[128,128]{1,0:T(8,128)S(1)} %add.41), channel_id=1, source_target_pairs={{0,16},{8,24},{16,0},{24,8},{32,48},{40,56},{48,32},{56,40},{64,80... | collective-permute-start | bytes 196616 | tf_op jit(solution)/shard_map/ppermute | solution.py:211
  95.0 0.5 collective-permute-start.6
  95.5 5.7 %collective-permute-done.6 = f32[96,128]{1,0:T(8,128)S(1)} collective-permute-done((f32[96,128]{1,0:T(8,128)S(1)}, f32[96,128]{1,0:T(8,128)S(1)}, u32[]{:S(2)}, u32[]{:S(2)}) %collective-permute-start.6) | collective-permute-done | bytes 49184 | tf_op jit(solution)/shard_map/ppermute | solution.py:211
  101.2 0.0 collective-permute-done.4
  101.2 1.1 collective-permute-start.7
  102.3 2.2 %collective-permute-start.8 = (f32[128,128]{1,0:T(8,128)S(1)}, f32[128,128]{1,0:T(8,128)S(1)}, u32[]{:S(2)}, u32[]{:S(2)}) collective-permute-start(f32[128,128]{1,0:T(8,128)S(1)} %add.42), channel_id=1, source_target_pairs={{0,96},{8,104},{16,112},{24,120},{32,64},{40,72},{48,80},{56,88},{... | collective-permute-start | bytes 196616 | tf_op jit(solution)/shard_map/ppermute | solution.py:211
  104.6 0.2 collective-permute-start.5
  104.8 3.9 %collective-permute-done.8 = f32[128,128]{1,0:T(8,128)S(1)} collective-permute-done((f32[128,128]{1,0:T(8,128)S(1)}, f32[128,128]{1,0:T(8,128)S(1)}, u32[]{:S(2)}, u32[]{:S(2)}) %collective-permute-start.8) | collective-permute-done | bytes 65568 | tf_op jit(solution)/shard_map/ppermute | solution.py:211
  108.8 1.8 %collective-permute-done.5 = f32[128,128]{1,0:T(8,128)S(1)} collective-permute-done((f32[128,128]{1,0:T(8,128)S(1)}, f32[128,128]{1,0:T(8,128)S(1)}, u32[]{:S(2)}, u32[]{:S(2)}) %collective-permute-start.5) | collective-permute-done | bytes 65568 | tf_op jit(solution)/shard_map/ppermute | solution.py:211
  110.6 0.0 collective-permute-done.7
  110.6 0.8 collective-permute-start.9
  111.4 5.8 %collective-permute-done.9 = f32[128,128]{1,0:T(8,128)S(1)} collective-permute-done((f32[128,128]{1,0:T(8,128)S(1)}, f32[128,128]{1,0:T(8,128)S(1)}, u32[]{:S(2)}, u32[]{:S(2)}) %collective-permute-start.9) | collective-permute-done | bytes 65568 | tf_op jit(solution)/shard_map/ppermute | solution.py:211
  117.2 0.1 collective-permute-start.10
  117.3 1.3 %collective-permute-done.10.other_ref = f32[224,128]{1,0:T(8,128)S(1)} collective-permute-done((f32[224,128]{1,0:T(8,128)S(1)}, f32[224,128]{1,0:T(8,128)S(1)}, u32[]{:S(2)}, u32[]{:S(2)}) %collective-permute-start.10) | collective-permute-done | bytes 114720 | tf_op jit(solution)/shard_map/ppermute | solution.py:211
  118.6 0.0 copy-done.1
  118.6 0.0 copy-done.3
  118.6 3.2 %finish.1 = f32[128,6144]{1,0:T(8,128)} custom-call(s32[1]{0:T(128)} %bitcast.core_ref, f32[224,128]{1,0:T(8,128)S(1)} %pad_maximum_fusion.1.own_ref, f32[224,128]{1,0:T(8,128)S(1)} %collective-permute-done.10.other_ref, f32[4,64,64]{2,1,0:T(8,128)S(1)} %copy-done.3, f32[128,6144]{1,0:T(8,128)S(1)} %get-tuple-element.22.current_ref, ...), custom_call_target="tpu_custom_call" | custom-call | tf_op jit(solution)/shard_map/finish/pallas_call | solution.py:191
  (11 shorter events, 0.1 us)
Async XLA Ops:
  0.0 85.8 %all-to-all-start = ((f32[1,4,32,6144]{3,1,0,2:T(4,128)}), f32[1,4,32,6144]{3,1,0,2:T(4,128)S(1)}, u32[]{:S(2)}, u32[]{:S(2)}) async-start(f32[1,4,32,6144]{3,1,0,2:T(4,128)} %bitcast.8), calls=%async_computation | async-start | bytes 6291456 | tf_op jit(solution)/shard_map/all_to_all | solution.py:215
  20.3 1.2 %collective-permute-start = (f32[96,128]{1,0:T(8,128)S(1)}, f32[96,128]{1,0:T(8,128)S(1)}, u32[]{:S(2)}, u32[]{:S(2)}) collective-permute-start(f32[96,128]{1,0:T(8,128)S(1)} %get-tuple-element.19), channel_id=1, source_target_pairs={{0,8},{8,0},{16,24},{24,16},{32,40},{40,32},{48,56},{56,48},{64,72... | collective-permute-start | bytes 147464 | tf_op jit(solution)/shard_map/ppermute | solution.py:211
  21.5 8.7 %collective-permute-start.1 = (f32[96,128]{1,0:T(8,128)S(1)}, f32[96,128]{1,0:T(8,128)S(1)}, u32[]{:S(2)}, u32[]{:S(2)}) collective-permute-start(f32[96,128]{1,0:T(8,128)S(1)} %add.38), channel_id=1, source_target_pairs={{0,16},{8,24},{16,0},{24,8},{32,48},{40,56},{48,32},{56,40},{64,80... | collective-permute-start | bytes 147464 | tf_op jit(solution)/shard_map/ppermute | solution.py:211
  30.2 52.7 %collective-permute-start.2 = (f32[96,128]{1,0:T(8,128)S(1)}, f32[96,128]{1,0:T(8,128)S(1)}, u32[]{:S(2)}, u32[]{:S(2)}) collective-permute-start(f32[96,128]{1,0:T(8,128)S(1)} %add.39), channel_id=1, source_target_pairs={{0,32},{8,40},{16,48},{24,56},{32,0},{40,8},{48,16},{56,24},{64,96... | collective-permute-start | bytes 147464 | tf_op jit(solution)/shard_map/ppermute | solution.py:211
  85.8 1.9 %copy-start = (bf16[256,6144]{1,0:T(8,128)(2,1)S(1)}, bf16[256,6144]{1,0:T(8,128)(2,1)}, u32[]{:S(2)}) copy-start(bf16[256,6144]{1,0:T(8,128)(2,1)} %get-tuple-element.14.high_ref) | copy-start | bytes 9437188
  87.7 1.9 %copy-start.2 = (bf16[256,6144]{1,0:T(8,128)(2,1)S(1)}, bf16[256,6144]{1,0:T(8,128)(2,1)}, u32[]{:S(2)}) copy-start(bf16[256,6144]{1,0:T(8,128)(2,1)} %get-tuple-element.17.low_ref) | copy-start | bytes 9437188
  89.6 29.1 %copy-start.1 = (bf16[256,6144]{1,0:T(8,128)(2,1)S(1)}, bf16[256,6144]{1,0:T(8,128)(2,1)}, u32[]{:S(2)}) copy-start(bf16[256,6144]{1,0:T(8,128)(2,1)} %get-tuple-element.14.high_ref) | copy-start | bytes 9437188
  89.6 29.1 %copy-start.3 = (f32[4,64,64]{2,1,0:T(8,128)S(1)}, f32[4,64,64]{2,1,0:T(8,128)}, u32[]{:S(2)}) copy-start(f32[4,64,64]{2,1,0:T(8,128)} %tfactors_ref.1) | copy-start | bytes 196612
  90.6 1.3 %collective-permute-start.3 = (f32[128,128]{1,0:T(8,128)S(1)}, f32[128,128]{1,0:T(8,128)S(1)}, u32[]{:S(2)}, u32[]{:S(2)}) collective-permute-start(f32[128,128]{1,0:T(8,128)S(1)} %get-tuple-element.21), channel_id=1, source_target_pairs={{0,8},{8,0},{16,24},{24,16},{32,40},{40,32},{48,56},{56,48},{64,72... | collective-permute-start | bytes 196616 | tf_op jit(solution)/shard_map/ppermute | solution.py:211
  91.9 9.3 %collective-permute-start.4 = (f32[128,128]{1,0:T(8,128)S(1)}, f32[128,128]{1,0:T(8,128)S(1)}, u32[]{:S(2)}, u32[]{:S(2)}) collective-permute-start(f32[128,128]{1,0:T(8,128)S(1)} %add.41), channel_id=1, source_target_pairs={{0,16},{8,24},{16,0},{24,8},{32,48},{40,56},{48,32},{56,40},{64,80... | collective-permute-start | bytes 196616 | tf_op jit(solution)/shard_map/ppermute | solution.py:211
  95.0 6.2 %collective-permute-start.6 = (f32[96,128]{1,0:T(8,128)S(1)}, f32[96,128]{1,0:T(8,128)S(1)}, u32[]{:S(2)}, u32[]{:S(2)}) collective-permute-start(f32[96,128]{1,0:T(8,128)S(1)} %add.40.before_ref), channel_id=1, source_target_pairs={{0,192},{8,200},{16,208},{24,216},{32,224},{40,232},{48,240},{56,2... | collective-permute-start | bytes 147464 | tf_op jit(solution)/shard_map/ppermute | solution.py:211
  101.2 9.4 %collective-permute-start.7 = (f32[224,128]{1,0:T(8,128)S(1)}, f32[224,128]{1,0:T(8,128)S(1)}, u32[]{:S(2)}, u32[]{:S(2)}) collective-permute-start(f32[224,128]{1,0:T(8,128)S(1)} %pad_maximum_fusion), channel_id=1, source_target_pairs={{0,64},{8,72},{16,80},{24,88},{32,96},{40,104},{48,112},{56,120},{... | collective-permute-start | bytes 344072 | tf_op jit(solution)/shard_map/ppermute | solution.py:211
  102.3 6.4 %collective-permute-start.8 = (f32[128,128]{1,0:T(8,128)S(1)}, f32[128,128]{1,0:T(8,128)S(1)}, u32[]{:S(2)}, u32[]{:S(2)}) collective-permute-start(f32[128,128]{1,0:T(8,128)S(1)} %add.42), channel_id=1, source_target_pairs={{0,96},{8,104},{16,112},{24,120},{32,64},{40,72},{48,80},{56,88},{... | collective-permute-start | bytes 196616 | tf_op jit(solution)/shard_map/ppermute | solution.py:211
  104.6 6.0 %collective-permute-start.5 = (f32[128,128]{1,0:T(8,128)S(1)}, f32[128,128]{1,0:T(8,128)S(1)}, u32[]{:S(2)}, u32[]{:S(2)}) collective-permute-start(f32[128,128]{1,0:T(8,128)S(1)} %add.42), channel_id=1, source_target_pairs={{0,32},{8,40},{16,48},{24,56},{32,0},{40,8},{48,16},{56,24},{64,96... | collective-permute-start | bytes 196616 | tf_op jit(solution)/shard_map/ppermute | solution.py:211
  110.6 6.6 %collective-permute-start.9 = (f32[128,128]{1,0:T(8,128)S(1)}, f32[128,128]{1,0:T(8,128)S(1)}, u32[]{:S(2)}, u32[]{:S(2)}) collective-permute-start(f32[128,128]{1,0:T(8,128)S(1)} %fusion), channel_id=1, source_target_pairs={{0,192},{8,200},{16,208},{24,216},{32,224},{40,232},{48,240},{56,2... | collective-permute-start | bytes 196616 | tf_op jit(solution)/shard_map/ppermute | solution.py:211
  117.2 1.4 %collective-permute-start.10 = (f32[224,128]{1,0:T(8,128)S(1)}, f32[224,128]{1,0:T(8,128)S(1)}, u32[]{:S(2)}, u32[]{:S(2)}) collective-permute-start(f32[224,128]{1,0:T(8,128)S(1)} %pad_maximum_fusion.1.own_ref), channel_id=1, source_target_pairs={{0,8},{8,0},{16,24},{24,16},{32,40},{40,32},{48,56},{56,48},{64,72... | collective-permute-start | bytes 344072 | tf_op jit(solution)/shard_map/ppermute | solution.py:211

commit v5 on v4

--- a/solution.py
+++ b/solution.py
@@ -8,6 +8,7 @@
 from jax.sharding import PartitionSpec as P
 
 COLUMNS = 1024
+OUT_COLUMNS = 2048
 LIMIT = 40 * 1024 * 1024
 IN_VMEM = pl.BlockSpec(memory_space=pltpu.VMEM)
 IN_SMEM = pl.BlockSpec(memory_space=pltpu.SMEM)
@@ -77,8 +78,8 @@
         total_ref[...] += product(high_ref[:, columns], both, ((1,), (1,)))
 
 
-def project_low_kernel(core_ref, total_ref, rounded_ref, low_ref, before_ref, kept_ref, sent_ref, whole):
-    del before_ref
+def project_low_kernel(core_ref, total_ref, rounded_ref, low_ref, gram_ref, more_ref, kept_ref, sent_ref, sum_ref, whole):
+    sum_ref[...] = gram_ref[...] + more_ref[...]
     count = rounded_ref.shape[0]
     whole[...] = total_ref[:, :count] + (
         total_ref[:, count:] + product(low_ref[...], rounded_ref[...], ((1,), (1,)))
@@ -107,8 +108,8 @@
     high, low = split(jnp.concatenate(scaled, axis=0).T)
     both = jnp.concatenate([high, low], axis=0)
     copies = []
-    for step in range(rows // COLUMNS):
-        columns = pl.ds(step * COLUMNS, COLUMNS)
+    for step in range(rows // OUT_COLUMNS):
+        columns = pl.ds(step * OUT_COLUMNS, OUT_COLUMNS)
         first = product(both, high_ref[:, columns], ((1,), (0,)))
         second = product(high, low_ref[:, columns], ((1,), (0,)))
         out[:, columns] = current_ref[:, columns] - (first[:count] + (first[count:] + second))
@@ -154,7 +155,7 @@
     )(core, in_hbm(householder))
 
 
-def project_call(core, arrived, high, low, before):
+def project_call(core, arrived, high, low, gram, more):
     sources, each, rows = arrived.shape
     count = sources * each
     size = high.shape[0]
@@ -170,19 +171,20 @@
         compiler_params=pltpu.CompilerParams(vmem_limit_bytes=LIMIT),
         name="project_high",
     )(in_vmem(arrived), in_vmem(high))
-    kept, sent = pl.pallas_call(
+    kept, sent, gram = pl.pallas_call(
         project_low_kernel,
         out_shape=(
             pltpu.VMEM((size // 2, count), jnp.float32),
             pltpu.VMEM((size // 2, count), jnp.float32),
-        ),
-        in_specs=[IN_SMEM, IN_VMEM, IN_VMEM, IN_VMEM, IN_HBM],
-        out_specs=(IN_VMEM, IN_VMEM),
+            pltpu.VMEM(gram.shape, jnp.float32),
+        ),
+        in_specs=[IN_SMEM] + [IN_VMEM] * 5,
+        out_specs=(IN_VMEM, IN_VMEM, IN_VMEM),
         scratch_shapes=[pltpu.VMEM((size, count), jnp.float32)],
         compiler_params=pltpu.CompilerParams(vmem_limit_bytes=LIMIT),
         name="project_low",
-    )(core, in_vmem(total), in_vmem(rounded), in_vmem(low), before)
-    return current, kept, sent
+    )(core, in_vmem(total), in_vmem(rounded), in_vmem(low), in_vmem(gram), in_vmem(more))
+    return current, kept, sent, gram
 
 
 def finish_call(core, own, other, tfactors, current, high, low):
@@ -197,7 +199,7 @@
             pltpu.VMEM((size, count), jnp.float32),
             pltpu.VMEM((2 * own.shape[0] - size, count), jnp.float32),
             pltpu.VMEM((count, rows), jnp.float32),
-            pltpu.SemaphoreType.DMA((rows // COLUMNS,)),
+            pltpu.SemaphoreType.DMA((rows // OUT_COLUMNS,)),
         ],
         compiler_params=pltpu.CompilerParams(vmem_limit_bytes=LIMIT),
         name="finish",
@@ -219,11 +221,9 @@
         gram = gram + swap(sent, 1)
         gram = gram + swap(gram, 2)
         gram = gram + swap(gram, 4)
-        current, value, sent = project_call(core, arrived, high, low, gram)
+        current, value, sent, gram = project_call(core, arrived, high, low, gram, swap(gram, 24))
         value = value + swap(sent, 1)
-        across = swap(value, 2)
-        gram = gram + swap(gram, 24)
-        value = value + across
+        value = value + swap(value, 2)
         first, third = swap(value, 4), swap(value, 12)
         second = swap(jnp.concatenate([value, gram], axis=0), 8)
         half = value.shape[0]

time: 123 us -> 120 us (0.976)
  waiting for transfers between devices: 81.3 us -> 73.1 us
  starting transfers between devices: 23.6 us -> 28.6 us
    ppermute x11, waiting for transfers between devices: 78.3 us -> 72.8 us  [swap(): return lax.ppermute(value, 'row', [(i, i ^ flip) for i in range(devices)])]
    ppermute x11, starting transfers between devices: 12.1 us -> 17.2 us  [swap(): return lax.ppermute(value, 'row', [(i, i ^ flip) for i in range(devices)])]
    all_to_all x1, waiting for transfers between devices: 2.95 us -> 0.29 us  [shards(): lax.all_to_all(vectors_in.reshape(vectors_in.shape[0], devices, -1), 'row...]
  transfers between devices with their start and end apart: 12 -> 12, of which waited for: 10 -> 11; matrix products, arithmetic and copies ran while one was open for 0% -> 0% of each run, Pallas kernels for 7% -> 9%
where the time goes in v5:
time: 120 us; the launch traced here: 119 us
  waiting for transfers between devices  73.1 us (61%)
  starting transfers between devices  28.6 us (24%)
  Pallas kernels  14.6 us (12%)
  local copies, waits for them, and re-layouts  2.31 us (2%)
    ppermute x11, waiting for transfers between devices, swap(): return lax.ppermute(value, 'row', [(i, i ^ flip) for i in range(devices)])  72.8 us
    ppermute x11, starting transfers between devices, swap(): return lax.ppermute(value, 'row', [(i, i ^ flip) for i in range(devices)])  17.2 us
    all_to_all x1, starting transfers between devices, shards(): lax.all_to_all(vectors_in.reshape(vectors_in.shape[0], devices, -1), 'row...  11.5 us
    pallas_call x1, Pallas kernels, gram_call(): pl.pallas_call(gram_kernel, out_shape=(pltpu.HBM((size, rows), jnp.bfloat...  8.78 us
    pallas_call x1, Pallas kernels, finish_call(): pl.pallas_call(finish_kernel, out_shape=jax.ShapeDtypeStruct((count, rows...  3.36 us
  transfers between devices with their start and end apart: 12, of which 11 were waited for; matrix products, arithmetic and copies ran while one was open for 0% of the time, Pallas kernels for 9%

profile of v5, /device:TPU:4, one launch (start us, length us, event | category | flops | bytes accessed | tf_op | source)
XLA Modules:
  0.0 118.8 jit_solution(14307509288118741253)
XLA Ops:
  0.0 11.5 %all-to-all-start = ((f32[1,4,32,6144]{3,1,0,2:T(4,128)}), f32[1,4,32,6144]{3,1,0,2:T(4,128)S(1)}, u32[]{:S(2)}, u32[]{:S(2)}) async-start(f32[1,4,32,6144]{3,1,0,2:T(4,128)} %bitcast.8), calls=%async_computation | async-start | bytes 6291456 | tf_op jit(solution)/shard_map/all_to_all | solution.py:217
  11.5 8.8 %gram.1 = (bf16[256,6144]{1,0:T(8,128)(2,1)}, bf16[256,6144]{1,0:T(8,128)(2,1)}, f32[96,128]{1,0:T(8,128)S(1)}, f32[96,128]{1,0:T(8,128)S(1)}) custom-call(s32[1]{0:T(128)} %bitcast.core_ref, f32[4,64,6144]{2,1,0:T(8,128)} %householder_ref.1), custom_call_target="tpu_custom_call" | custom-call | flops 3221225472 | bytes 12582912 | tf_op jit(solution)/shard_map/gram/pallas_call | solution.py:135
  20.3 0.3 collective-permute-start
  20.6 1.0 collective-permute-done
  21.5 3.4 %collective-permute-start.1 = (f32[96,128]{1,0:T(8,128)S(1)}, f32[96,128]{1,0:T(8,128)S(1)}, u32[]{:S(2)}, u32[]{:S(2)}) collective-permute-start(f32[96,128]{1,0:T(8,128)S(1)} %add.35), channel_id=1, source_target_pairs={{0,16},{8,24},{16,0},{24,8},{32,48},{40,56},{48,32},{56,40},{64,80... | collective-permute-start | bytes 147464 | tf_op jit(solution)/shard_map/ppermute | solution.py:213
  24.9 5.3 %collective-permute-done.1 = f32[96,128]{1,0:T(8,128)S(1)} collective-permute-done((f32[96,128]{1,0:T(8,128)S(1)}, f32[96,128]{1,0:T(8,128)S(1)}, u32[]{:S(2)}, u32[]{:S(2)}) %collective-permute-start.1) | collective-permute-done | bytes 49184 | tf_op jit(solution)/shard_map/ppermute | solution.py:213
  30.2 0.3 collective-permute-start.2
  30.5 52.3 %collective-permute-done.2 = f32[96,128]{1,0:T(8,128)S(1)} collective-permute-done((f32[96,128]{1,0:T(8,128)S(1)}, f32[96,128]{1,0:T(8,128)S(1)}, u32[]{:S(2)}, u32[]{:S(2)}) %collective-permute-start.2) | collective-permute-done | bytes 49184 | tf_op jit(solution)/shard_map/ppermute | solution.py:213
  82.9 2.7 %collective-permute-start.3 = (f32[96,128]{1,0:T(8,128)S(1)}, f32[96,128]{1,0:T(8,128)S(1)}, u32[]{:S(2)}, u32[]{:S(2)}) collective-permute-start(f32[96,128]{1,0:T(8,128)S(1)} %add.37.gram_ref), channel_id=1, source_target_pairs={{0,192},{8,200},{16,208},{24,216},{32,224},{40,232},{48,240},{56,2... | collective-permute-start | bytes 147464 | tf_op jit(solution)/shard_map/ppermute | solution.py:213
  85.5 0.3 all-to-all-done
  85.8 0.0 copy-start
  85.8 1.9 %copy-done = bf16[256,6144]{1,0:T(8,128)(2,1)S(1)} copy-done((bf16[256,6144]{1,0:T(8,128)(2,1)S(1)}, bf16[256,6144]{1,0:T(8,128)(2,1)}, u32[]{:S(2)}) %copy-start) | copy-done | bytes 3145752
  87.7 0.0 copy-start.2
  87.7 1.5 %project_high.1 = (f32[128,6144]{1,0:T(8,128)S(1)}, bf16[128,6144]{1,0:T(8,128)(2,1)S(1)}, f32[256,256]{1,0:T(8,128)S(1)}) custom-call(f32[32,4,6144]{2,1,0:T(4,128)S(1)} %bitcast.7, bf16[256,6144]{1,0:T(8,128)(2,1)S(1)} %copy-done), custom_call_target="tpu_custom_call" | custom-call | tf_op jit(solution)/shard_map/project_high/pallas_call | solution.py:162
  89.2 0.0 collective-permute-done.3.more_ref
  89.2 0.4 copy-done.2
  89.6 0.0 copy-start.1
  89.6 0.0 copy-start.3
  89.6 1.0 project_low.1
  90.6 0.1 collective-permute-start.4
  90.7 1.2 %collective-permute-done.4 = f32[128,128]{1,0:T(8,128)S(1)} collective-permute-done((f32[128,128]{1,0:T(8,128)S(1)}, f32[128,128]{1,0:T(8,128)S(1)}, u32[]{:S(2)}, u32[]{:S(2)}) %collective-permute-start.4) | collective-permute-done | bytes 65568 | tf_op jit(solution)/shard_map/ppermute | solution.py:213
  91.9 3.2 %collective-permute-start.5 = (f32[128,128]{1,0:T(8,128)S(1)}, f32[128,128]{1,0:T(8,128)S(1)}, u32[]{:S(2)}, u32[]{:S(2)}) collective-permute-start(f32[128,128]{1,0:T(8,128)S(1)} %add.38), channel_id=1, source_target_pairs={{0,16},{8,24},{16,0},{24,8},{32,48},{40,56},{48,32},{56,40},{64,80... | collective-permute-start | bytes 196616 | tf_op jit(solution)/shard_map/ppermute | solution.py:213
  95.2 2.6 %collective-permute-done.5 = f32[128,128]{1,0:T(8,128)S(1)} collective-permute-done((f32[128,128]{1,0:T(8,128)S(1)}, f32[128,128]{1,0:T(8,128)S(1)}, u32[]{:S(2)}, u32[]{:S(2)}) %collective-permute-start.5) | collective-permute-done | bytes 65568 | tf_op jit(solution)/shard_map/ppermute | solution.py:213
  97.8 2.3 %collective-permute-start.7 = (f32[224,128]{1,0:T(8,128)S(1)}, f32[224,128]{1,0:T(8,128)S(1)}, u32[]{:S(2)}, u32[]{:S(2)}) collective-permute-start(f32[224,128]{1,0:T(8,128)S(1)} %pad_maximum_fusion), channel_id=1, source_target_pairs={{0,64},{8,72},{16,80},{24,88},{32,96},{40,104},{48,112},{56,120},{... | collective-permute-start | bytes 344072 | tf_op jit(solution)/shard_map/ppermute | solution.py:213
  100.1 1.5 %collective-permute-start.8 = (f32[128,128]{1,0:T(8,128)S(1)}, f32[128,128]{1,0:T(8,128)S(1)}, u32[]{:S(2)}, u32[]{:S(2)}) collective-permute-start(f32[128,128]{1,0:T(8,128)S(1)} %add.39), channel_id=1, source_target_pairs={{0,96},{8,104},{16,112},{24,120},{32,64},{40,72},{48,80},{56,88},{... | collective-permute-start | bytes 196616 | tf_op jit(solution)/shard_map/ppermute | solution.py:213
  101.6 0.0 collective-permute-start.6
  101.6 4.9 %collective-permute-done.8 = f32[128,128]{1,0:T(8,128)S(1)} collective-permute-done((f32[128,128]{1,0:T(8,128)S(1)}, f32[128,128]{1,0:T(8,128)S(1)}, u32[]{:S(2)}, u32[]{:S(2)}) %collective-permute-start.8) | collective-permute-done | bytes 65568 | tf_op jit(solution)/shard_map/ppermute | solution.py:213
  106.5 0.5 collective-permute-done.6
  107.1 0.4 collective-permute-done.7
  107.5 3.3 %collective-permute-start.9 = (f32[128,128]{1,0:T(8,128)S(1)}, f32[128,128]{1,0:T(8,128)S(1)}, u32[]{:S(2)}, u32[]{:S(2)}) collective-permute-start(f32[128,128]{1,0:T(8,128)S(1)} %fusion), channel_id=1, source_target_pairs={{0,192},{8,200},{16,208},{24,216},{32,224},{40,232},{48,240},{56,2... | collective-permute-start | bytes 196616 | tf_op jit(solution)/shard_map/ppermute | solution.py:213
  110.8 3.3 %collective-permute-done.9 = f32[128,128]{1,0:T(8,128)S(1)} collective-permute-done((f32[128,128]{1,0:T(8,128)S(1)}, f32[128,128]{1,0:T(8,128)S(1)}, u32[]{:S(2)}, u32[]{:S(2)}) %collective-permute-start.9) | collective-permute-done | bytes 65568 | tf_op jit(solution)/shard_map/ppermute | solution.py:213
  114.1 0.1 collective-permute-start.10
  114.2 1.3 %collective-permute-done.10.other_ref = f32[224,128]{1,0:T(8,128)S(1)} collective-permute-done((f32[224,128]{1,0:T(8,128)S(1)}, f32[224,128]{1,0:T(8,128)S(1)}, u32[]{:S(2)}, u32[]{:S(2)}) %collective-permute-start.10) | collective-permute-done | bytes 114720 | tf_op jit(solution)/shard_map/ppermute | solution.py:213
  115.5 0.0 copy-done.1
  115.5 0.0 copy-done.3
  115.5 3.4 %finish.1 = f32[128,6144]{1,0:T(8,128)} custom-call(s32[1]{0:T(128)} %bitcast.core_ref, f32[224,128]{1,0:T(8,128)S(1)} %pad_maximum_fusion.1.own_ref, f32[224,128]{1,0:T(8,128)S(1)} %collective-permute-done.10.other_ref, f32[4,64,64]{2,1,0:T(8,128)S(1)} %copy-done.3, f32[128,6144]{1,0:T(8,128)S(1)} %get-tuple-element.24.current_ref, ...), custom_call_target="tpu_custom_call" | custom-call | tf_op jit(solution)/shard_map/finish/pallas_call | solution.py:193
  (10 shorter events, 0.1 us)
Async XLA Ops:
  0.0 85.8 %all-to-all-start = ((f32[1,4,32,6144]{3,1,0,2:T(4,128)}), f32[1,4,32,6144]{3,1,0,2:T(4,128)S(1)}, u32[]{:S(2)}, u32[]{:S(2)}) async-start(f32[1,4,32,6144]{3,1,0,2:T(4,128)} %bitcast.8), calls=%async_computation | async-start | bytes 6291456 | tf_op jit(solution)/shard_map/all_to_all | solution.py:217
  20.3 1.2 %collective-permute-start = (f32[96,128]{1,0:T(8,128)S(1)}, f32[96,128]{1,0:T(8,128)S(1)}, u32[]{:S(2)}, u32[]{:S(2)}) collective-permute-start(f32[96,128]{1,0:T(8,128)S(1)} %get-tuple-element.20), channel_id=1, source_target_pairs={{0,8},{8,0},{16,24},{24,16},{32,40},{40,32},{48,56},{56,48},{64,72... | collective-permute-start | bytes 147464 | tf_op jit(solution)/shard_map/ppermute | solution.py:213
  21.5 8.7 %collective-permute-start.1 = (f32[96,128]{1,0:T(8,128)S(1)}, f32[96,128]{1,0:T(8,128)S(1)}, u32[]{:S(2)}, u32[]{:S(2)}) collective-permute-start(f32[96,128]{1,0:T(8,128)S(1)} %add.35), channel_id=1, source_target_pairs={{0,16},{8,24},{16,0},{24,8},{32,48},{40,56},{48,32},{56,40},{64,80... | collective-permute-start | bytes 147464 | tf_op jit(solution)/shard_map/ppermute | solution.py:213
  30.2 52.7 %collective-permute-start.2 = (f32[96,128]{1,0:T(8,128)S(1)}, f32[96,128]{1,0:T(8,128)S(1)}, u32[]{:S(2)}, u32[]{:S(2)}) collective-permute-start(f32[96,128]{1,0:T(8,128)S(1)} %add.36), channel_id=1, source_target_pairs={{0,32},{8,40},{16,48},{24,56},{32,0},{40,8},{48,16},{56,24},{64,96... | collective-permute-start | bytes 147464 | tf_op jit(solution)/shard_map/ppermute | solution.py:213
  82.9 6.3 %collective-permute-start.3 = (f32[96,128]{1,0:T(8,128)S(1)}, f32[96,128]{1,0:T(8,128)S(1)}, u32[]{:S(2)}, u32[]{:S(2)}) collective-permute-start(f32[96,128]{1,0:T(8,128)S(1)} %add.37.gram_ref), channel_id=1, source_target_pairs={{0,192},{8,200},{16,208},{24,216},{32,224},{40,232},{48,240},{56,2... | collective-permute-start | bytes 147464 | tf_op jit(solution)/shard_map/ppermute | solution.py:213
  85.8 1.9 %copy-start = (bf16[256,6144]{1,0:T(8,128)(2,1)S(1)}, bf16[256,6144]{1,0:T(8,128)(2,1)}, u32[]{:S(2)}) copy-start(bf16[256,6144]{1,0:T(8,128)(2,1)} %get-tuple-element.15.high_ref) | copy-start | bytes 9437188
  87.7 1.9 %copy-start.2 = (bf16[256,6144]{1,0:T(8,128)(2,1)S(1)}, bf16[256,6144]{1,0:T(8,128)(2,1)}, u32[]{:S(2)}) copy-start(bf16[256,6144]{1,0:T(8,128)(2,1)} %get-tuple-element.18.low_ref) | copy-start | bytes 9437188
  89.6 25.9 %copy-start.1 = (bf16[256,6144]{1,0:T(8,128)(2,1)S(1)}, bf16[256,6144]{1,0:T(8,128)(2,1)}, u32[]{:S(2)}) copy-start(bf16[256,6144]{1,0:T(8,128)(2,1)} %get-tuple-element.15.high_ref) | copy-start | bytes 9437188
  89.6 25.9 %copy-start.3 = (f32[4,64,64]{2,1,0:T(8,128)S(1)}, f32[4,64,64]{2,1,0:T(8,128)}, u32[]{:S(2)}) copy-start(f32[4,64,64]{2,1,0:T(8,128)} %tfactors_ref.1) | copy-start | bytes 196612
  90.6 1.3 %collective-permute-start.4 = (f32[128,128]{1,0:T(8,128)S(1)}, f32[128,128]{1,0:T(8,128)S(1)}, u32[]{:S(2)}, u32[]{:S(2)}) collective-permute-start(f32[128,128]{1,0:T(8,128)S(1)} %get-tuple-element.22), channel_id=1, source_target_pairs={{0,8},{8,0},{16,24},{24,16},{32,40},{40,32},{48,56},{56,48},{64,72... | collective-permute-start | bytes 196616 | tf_op jit(solution)/shard_map/ppermute | solution.py:213
  91.9 5.9 %collective-permute-start.5 = (f32[128,128]{1,0:T(8,128)S(1)}, f32[128,128]{1,0:T(8,128)S(1)}, u32[]{:S(2)}, u32[]{:S(2)}) collective-permute-start(f32[128,128]{1,0:T(8,128)S(1)} %add.38), channel_id=1, source_target_pairs={{0,16},{8,24},{16,0},{24,8},{32,48},{40,56},{48,32},{56,40},{64,80... | collective-permute-start | bytes 196616 | tf_op jit(solution)/shard_map/ppermute | solution.py:213
  97.8 9.6 %collective-permute-start.7 = (f32[224,128]{1,0:T(8,128)S(1)}, f32[224,128]{1,0:T(8,128)S(1)}, u32[]{:S(2)}, u32[]{:S(2)}) collective-permute-start(f32[224,128]{1,0:T(8,128)S(1)} %pad_maximum_fusion), channel_id=1, source_target_pairs={{0,64},{8,72},{16,80},{24,88},{32,96},{40,104},{48,112},{56,120},{... | collective-permute-start | bytes 344072 | tf_op jit(solution)/shard_map/ppermute | solution.py:213
  100.1 6.4 %collective-permute-start.8 = (f32[128,128]{1,0:T(8,128)S(1)}, f32[128,128]{1,0:T(8,128)S(1)}, u32[]{:S(2)}, u32[]{:S(2)}) collective-permute-start(f32[128,128]{1,0:T(8,128)S(1)} %add.39), channel_id=1, source_target_pairs={{0,96},{8,104},{16,112},{24,120},{32,64},{40,72},{48,80},{56,88},{... | collective-permute-start | bytes 196616 | tf_op jit(solution)/shard_map/ppermute | solution.py:213
  101.6 5.5 %collective-permute-start.6 = (f32[128,128]{1,0:T(8,128)S(1)}, f32[128,128]{1,0:T(8,128)S(1)}, u32[]{:S(2)}, u32[]{:S(2)}) collective-permute-start(f32[128,128]{1,0:T(8,128)S(1)} %add.39), channel_id=1, source_target_pairs={{0,32},{8,40},{16,48},{24,56},{32,0},{40,8},{48,16},{56,24},{64,96... | collective-permute-start | bytes 196616 | tf_op jit(solution)/shard_map/ppermute | solution.py:213
  107.5 6.6 %collective-permute-start.9 = (f32[128,128]{1,0:T(8,128)S(1)}, f32[128,128]{1,0:T(8,128)S(1)}, u32[]{:S(2)}, u32[]{:S(2)}) collective-permute-start(f32[128,128]{1,0:T(8,128)S(1)} %fusion), channel_id=1, source_target_pairs={{0,192},{8,200},{16,208},{24,216},{32,224},{40,232},{48,240},{56,2... | collective-permute-start | bytes 196616 | tf_op jit(solution)/shard_map/ppermute | solution.py:213
  114.1 1.4 %collective-permute-start.10 = (f32[224,128]{1,0:T(8,128)S(1)}, f32[224,128]{1,0:T(8,128)S(1)}, u32[]{:S(2)}, u32[]{:S(2)}) collective-permute-start(f32[224,128]{1,0:T(8,128)S(1)} %pad_maximum_fusion.1.own_ref), channel_id=1, source_target_pairs={{0,8},{8,0},{16,24},{24,16},{32,40},{40,32},{48,56},{56,48},{64,72... | collective-permute-start | bytes 344072 | tf_op jit(solution)/shard_map/ppermute | solution.py:213

commit v6 on v5

--- a/solution.py
+++ b/solution.py
@@ -5,14 +5,17 @@
 from jax import lax
 from jax.experimental import pallas as pl
 from jax.experimental.pallas import tpu as pltpu
+from jax.sharding import Mesh
 from jax.sharding import PartitionSpec as P
 
 COLUMNS = 1024
 OUT_COLUMNS = 2048
+SHIFTS = (1, -1, 3, -3)
 LIMIT = 40 * 1024 * 1024
 IN_VMEM = pl.BlockSpec(memory_space=pltpu.VMEM)
 IN_SMEM = pl.BlockSpec(memory_space=pltpu.SMEM)
-IN_HBM = pl.BlockSpec(memory_space=pl.ANY)
+IN_ANY = pl.BlockSpec(memory_space=pl.ANY)
+IN_HBM = pl.BlockSpec(memory_space=pltpu.HBM)
 
 
 def product(left, right, contract, precision=None):
@@ -37,7 +40,8 @@
     other_ref[...] = whole[pl.ds(pl.multiple_of((1 - core) * half, 8), half), :]
 
 
-def gram_kernel(core_ref, householder_ref, high_ref, low_ref, kept_ref, sent_ref, total, packed):
+def gram_kernel(core_ref, householder_ref, before_ref, high_ref, low_ref, kept_ref, sent_ref, total, packed):
+    del before_ref
     panels, width, columns = householder_ref.shape
     size = panels * width
     step = pl.program_id(0)
@@ -65,14 +69,74 @@
         halves(core_ref[0], packed, kept_ref, sent_ref)
 
 
-def project_high_kernel(arrived_ref, high_ref, current_ref, rounded_ref, total_ref):
+def cut_kernel(place_ref, vectors_ref, *refs):
+    outs, sems = refs[:-1], refs[-1]
+    wide = outs[0].shape[1]
+    planes = vectors_ref.shape[1] // wide
+    copies = []
+    for i, shift in enumerate(SHIFTS):
+        plane = (place_ref[0] + shift + planes) % planes
+        columns = pl.ds(pl.multiple_of(plane * wide, 128), wide)
+        copies.append(pltpu.make_async_copy(vectors_ref.at[:, columns], outs[i], sems.at[i]))
+        copies[i].start()
+    for copy in copies:
+        copy.wait()
+
+
+def even_kernel(place_ref, vectors_ref, before_ref, out_ref, sems):
+    del before_ref
+    number, _, wide = out_ref.shape
+    copies = []
+    for i in range(number):
+        block = (i // 4 * 2 + place_ref[0] % 2) * 4 + i % 4
+        columns = pl.ds(pl.multiple_of(block * wide, 128), wide)
+        copies.append(pltpu.make_async_copy(vectors_ref.at[:, columns], out_ref.at[i], sems.at[i]))
+        copies[i].start()
+    for copy in copies:
+        copy.wait()
+
+
+def side_kernel(place_ref, up_ref, down_ref, before_ref, kept_ref, sent_ref):
+    del before_ref
+    wide = kept_ref.shape[2]
+    y = place_ref[1]
+    for i, part_ref in enumerate((up_ref, down_ref)):
+        kept_ref[i] = part_ref[:, pl.ds(pl.multiple_of(y * wide, 128), wide)]
+        sent_ref[i] = part_ref[:, pl.ds(pl.multiple_of((1 - y) * wide, 128), wide)]
+
+
+def core_kernel(place_ref, own_ref, got_ref, kept_ref, sent_ref):
+    wide = kept_ref.shape[3]
+    core = place_ref[2]
+    for i, part_ref in enumerate((own_ref, got_ref)):
+        kept_ref[i] = part_ref[:, :, pl.ds(pl.multiple_of(core * wide, 128), wide)]
+        sent_ref[i] = part_ref[:, :, pl.ds(pl.multiple_of((1 - core) * wide, 128), wide)]
+
+
+def project_high_kernel(place_ref, even_ref, kept_one_ref, got_one_ref, kept_three_ref, got_three_ref, high_ref, current_ref, rounded_ref, total_ref):
     count, rows = current_ref.shape
+    planes = count // (4 * even_ref.shape[1])
+    z, y, core = place_ref[0], place_ref[1], place_ref[2]
+    pair = 2 * even_ref.shape[1]
     total_ref[...] = jnp.zeros_like(total_ref)
     for step in range(rows // COLUMNS):
         columns = pl.ds(step * COLUMNS, COLUMNS)
-        block = arrived_ref[:, :, columns].reshape(count, COLUMNS)
-        current_ref[:, columns] = block
-        high, low = split(block)
+
+        def put(plane, side, block):
+            at = pl.multiple_of((plane * 2 + side) * pair, 8)
+            current_ref[pl.ds(at, pair), columns] = block
+
+        for k in range(planes // 2):
+            for side in range(2):
+                at = (2 * k + side) * 2
+                put(2 * k + z % 2, side, even_ref[at : at + 2, :, columns].reshape(pair, COLUMNS))
+        for shift, kept_ref, got_ref in ((1, kept_one_ref, got_one_ref), (3, kept_three_ref, got_three_ref)):
+            for other in range(2):
+                for i, by in enumerate((shift, -shift)):
+                    kept, got = kept_ref[other, i, :, columns], got_ref[other, i, :, columns]
+                    block = jnp.concatenate([jnp.where(core == 0, kept, got), jnp.where(core == 0, got, kept)], axis=0)
+                    put((z - by + planes) % planes, y ^ other, block)
+        high, low = split(current_ref[:, columns])
         rounded_ref[:, columns] = high
         both = jnp.concatenate([high, low], axis=0)
         total_ref[...] += product(high_ref[:, columns], both, ((1,), (1,)))
@@ -128,7 +192,7 @@
     return pltpu.with_memory_space_constraint(value, pltpu.HBM)
 
 
-def gram_call(core, householder):
+def gram_call(core, householder, before):
     panels, width, rows = householder.shape
     size = panels * width
     height = len(pairs_of(panels)) // 2 * width
@@ -141,7 +205,7 @@
             jax.ShapeDtypeStruct((height // 2, 2 * width), jnp.float32),
         ),
         grid=(rows // COLUMNS,),
-        in_specs=[IN_SMEM, pl.BlockSpec((panels, width, COLUMNS), lambda i: (0, 0, i))],
+        in_specs=[IN_SMEM, pl.BlockSpec((panels, width, COLUMNS), lambda i: (0, 0, i)), IN_ANY],
         out_specs=(
             pl.BlockSpec((size, COLUMNS), lambda i: (0, i)),
             pl.BlockSpec((size, COLUMNS), lambda i: (0, i)),
@@ -150,14 +214,26 @@
         ),
         scratch_shapes=[pltpu.VMEM((size, size), jnp.float32), pltpu.VMEM((height, 2 * width), jnp.float32)],
         compiler_params=pltpu.CompilerParams(vmem_limit_bytes=LIMIT),
-        cost_estimate=pl.CostEstimate(flops=8 * size * size * rows, bytes_accessed=8 * size * rows, transcendentals=0),
+        cost_estimate=pl.CostEstimate(flops=10 * 8 * size * size * rows, bytes_accessed=8 * size * rows, transcendentals=0),
         name="gram",
-    )(core, in_hbm(householder))
-
-
-def project_call(core, arrived, high, low, gram, more):
-    sources, each, rows = arrived.shape
-    count = sources * each
+    )(core, in_hbm(householder), before)
+
+
+def local_call(kernel, outs, specs, operands, copies=0):
+    return pl.pallas_call(
+        kernel,
+        out_shape=outs,
+        in_specs=[IN_SMEM] + specs,
+        out_specs=tuple(IN_HBM if out.memory_space == pltpu.HBM else IN_VMEM for out in outs),
+        scratch_shapes=[pltpu.SemaphoreType.DMA((copies,))] if copies else [],
+        compiler_params=pltpu.CompilerParams(vmem_limit_bytes=LIMIT),
+        name=kernel.__name__,
+    )(*operands)
+
+
+def project_call(core, place, even, odd, high, low, gram, more):
+    sources, each, rows = even.shape
+    count = 2 * sources * each
     size = high.shape[0]
     current, rounded, total = pl.pallas_call(
         project_high_kernel,
@@ -166,11 +242,11 @@
             pltpu.VMEM((count, rows), jnp.bfloat16),
             pltpu.VMEM((size, 2 * count), jnp.float32),
         ),
-        in_specs=[IN_VMEM, IN_VMEM],
+        in_specs=[IN_SMEM] + [IN_VMEM] * 6,
         out_specs=(IN_VMEM, IN_VMEM, IN_VMEM),
         compiler_params=pltpu.CompilerParams(vmem_limit_bytes=LIMIT),
         name="project_high",
-    )(in_vmem(arrived), in_vmem(high))
+    )(place, in_vmem(even), *[in_vmem(part) for part in odd], in_vmem(high))
     kept, sent, gram = pl.pallas_call(
         project_low_kernel,
         out_shape=(
@@ -194,7 +270,7 @@
         finish_kernel,
         out_shape=jax.ShapeDtypeStruct((count, rows), jnp.float32),
         in_specs=[IN_SMEM] + [IN_VMEM] * 6,
-        out_specs=IN_HBM,
+        out_specs=IN_ANY,
         scratch_shapes=[
             pltpu.VMEM((size, count), jnp.float32),
             pltpu.VMEM((2 * own.shape[0] - size, count), jnp.float32),
@@ -207,21 +283,44 @@
 
 
 def solution(mesh):
-    devices = mesh.shape["row"]
+    devices, columns = mesh.shape["row"], mesh.shape["col"]
+    planes = devices // 4
+    row = ("half", "odd", "y", "core")
+    parts = Mesh(mesh.devices.reshape(planes // 2, 2, 2, 2, columns), row + ("col",))
 
     def swap(value, flip):
-        return lax.ppermute(value, "row", [(i, i ^ flip) for i in range(devices)])
+        return lax.ppermute(value, row, [(i, i ^ flip) for i in range(devices)])
 
     def shards(vectors_in, householder, tfactors):
-        core = jnp.reshape(lax.axis_index("row") % 2, (1,)).astype(jnp.int32)
-        arrived = lax.all_to_all(
-            vectors_in.reshape(vectors_in.shape[0], devices, -1), "row", split_axis=1, concat_axis=0
-        )
-        high, low, gram, sent = gram_call(core, householder)
+        odd, y, core = lax.axis_index("odd"), lax.axis_index("y"), lax.axis_index("core")
+        z = lax.axis_index("half") * 2 + odd
+        place = jnp.stack([z, y, core]).astype(jnp.int32)
+        core = jnp.reshape(core, (1,)).astype(jnp.int32)
+        each, length = vectors_in.shape
+        wide = length // planes
+
+        def moved(part, shift):
+            return lax.ppermute(part, ("half", "odd"), [(i, (i + shift) % planes) for i in range(planes)])
+
+        def spread(up, down, before):
+            block = pltpu.VMEM((2, each, wide // 2), jnp.float32)
+            kept, sent = local_call(side_kernel, (block, block), [IN_VMEM, IN_VMEM, IN_ANY], (place, up, down, before))
+            block = pltpu.VMEM((2, 2, each, wide // 4), jnp.float32)
+            kept, sent = local_call(core_kernel, (block, block), [IN_VMEM, IN_VMEM], (place, kept, swap(sent, 2)))
+            return kept, swap(sent, 1)
+
+        block = pltpu.VMEM((each, wide), jnp.float32)
+        cut = local_call(cut_kernel, (block,) * len(SHIFTS), [IN_HBM], (place, in_hbm(vectors_in)), len(SHIFTS))
+        came = [moved(part, shift) for part, shift in zip(cut, SHIFTS)]
+        block = pltpu.HBM((devices // 2, each, wide // 4), jnp.float32)
+        (even,) = local_call(even_kernel, (block,), [IN_HBM, IN_ANY], (place, in_hbm(vectors_in), came[0]), devices // 2)
+        even = lax.all_to_all(even, ("half", "y", "core"), split_axis=0, concat_axis=0, tiled=True)
+        high, low, gram, sent = gram_call(core, householder, came[0])
+        scattered = spread(came[0], came[1], came[0]) + spread(came[2], came[3], gram)
         gram = gram + swap(sent, 1)
         gram = gram + swap(gram, 2)
         gram = gram + swap(gram, 4)
-        current, value, sent, gram = project_call(core, arrived, high, low, gram, swap(gram, 24))
+        current, value, sent, gram = project_call(core, place, even, scattered, high, low, gram, swap(gram, 24))
         value = value + swap(sent, 1)
         value = value + swap(value, 2)
         first, third = swap(value, 4), swap(value, 12)
@@ -234,6 +333,6 @@
         other = swap(own, 1)
         return finish_call(core, own, other, tfactors, current, high, low)
 
-    in_specs = (P(("col", "row"), None), P(None, None, "row"), P())
-    out_specs = P("col", "row")
-    return jax.shard_map(shards, mesh=mesh, in_specs=in_specs, out_specs=out_specs, check_vma=False)
+    in_specs = (P(("col",) + row, None), P(None, None, row), P())
+    out_specs = P("col", row)
+    return jax.shard_map(shards, mesh=parts, in_specs=in_specs, out_specs=out_specs, check_vma=False)

time: 120 us -> 167 us (1.39)
  Pallas kernels: 14.6 us -> 70.6 us
  waiting for transfers between devices: 73.1 us -> 49.7 us
  starting transfers between devices: 28.6 us -> 42.9 us
    pallas_call x0 -> x6, Pallas kernels: none -> 55.4 us  [local_call(): pl.pallas_call(kernel, out_shape=outs, in_specs=[IN_SMEM] + specs, out_sp...]
    ppermute x11 -> x19, waiting for transfers between devices: 72.8 us -> 49.7 us  [the longest x15 39.7 us: swap(): return lax.ppermute(value, row, [(i, i ^ flip) for i in range(devices)])]
    ppermute x11 -> x19, starting transfers between devices: 17.2 us -> 35.2 us  [the longest x15 24.1 us: swap(): return lax.ppermute(value, row, [(i, i ^ flip) for i in range(devices)])]
    all_to_all x1, starting transfers between devices: 11.5 us -> 7.67 us  [shards(): lax.all_to_all(even, ('half', 'y', 'core'), split_axis=0, concat_axis=0,...]
  transfers between devices with their start and end apart: 12 -> 20, of which waited for: 11 -> 13; matrix products, arithmetic and copies ran while one was open for 0% -> 0% of each run, Pallas kernels for 9% -> 38%
where the time goes in v6:
time: 167 us; the launch traced here: 166 us
  Pallas kernels  70.6 us (42%)
  waiting for transfers between devices  49.7 us (30%)
  starting transfers between devices  42.9 us (26%)
  local copies, waits for them, and re-layouts  1.9 us (1%)
    pallas_call x6, Pallas kernels, local_call(): pl.pallas_call(kernel, out_shape=outs, in_specs=[IN_SMEM] + specs, out_sp...  55.4 us
    ppermute x15, waiting for transfers between devices, swap(): return lax.ppermute(value, row, [(i, i ^ flip) for i in range(devices)])  39.7 us
    ppermute x15, starting transfers between devices, swap(): return lax.ppermute(value, row, [(i, i ^ flip) for i in range(devices)])  24.1 us
    ppermute x4, starting transfers between devices, moved(): lax.ppermute(part, ('half', 'odd'), [(i, (i + shift) % planes) for i in r...  11.1 us
    ppermute x4, waiting for transfers between devices, moved(): lax.ppermute(part, ('half', 'odd'), [(i, (i + shift) % planes) for i in r...  10 us
    pallas_call x1, Pallas kernels, gram_call(): pl.pallas_call(gram_kernel, out_shape=(pltpu.HBM((size, rows), jnp.bfloat...  8.8 us
    all_to_all x1, starting transfers between devices, shards(): lax.all_to_all(even, ('half', 'y', 'core'), split_axis=0, concat_axis=0,...  7.67 us
    pallas_call x1, Pallas kernels, finish_call(): pl.pallas_call(finish_kernel, out_shape=jax.ShapeDtypeStruct((count, rows...  3.36 us
  transfers between devices with their start and end apart: 20, of which 13 were waited for; matrix products, arithmetic and copies ran while one was open for 0% of the time, Pallas kernels for 38%

profile of v6, /device:TPU:4, one launch (start us, length us, event | category | flops | bytes accessed | tf_op | source)
XLA Modules:
  0.0 165.6 jit_solution(16293374425174515968)
XLA Ops:
  0.0 0.1 pad_add_fusion.place_ref
  0.1 2.8 %cut_kernel.1 = (f32[4,24576]{1,0:T(4,128)S(1)}, f32[4,24576]{1,0:T(4,128)S(1)}, f32[4,24576]{1,0:T(4,128)}, f32[4,24576]{1,0:T(4,128)}) custom-call(s32[3]{0:T(128)S(1)} %pad_add_fusion.place_ref, f32[4,196608]{1,0:T(4,128)} %vectors_ref.3), custom_call_target="tpu_custom_call" | custom-call | tf_op jit(solution)/shard_map/cut_kernel/pallas_call | solution.py:223
  2.9 2.0 %collective-permute-start = (f32[4,24576]{1,0:T(4,128)S(1)}, f32[4,24576]{1,0:T(4,128)S(1)}, u32[]{:S(2)}, u32[]{:S(2)}) collective-permute-start(f32[4,24576]{1,0:T(4,128)S(1)} %get-tuple-element.27), channel_id=1, source_target_pairs={{0,32},{32,64},{64,96},{96,128},{128,160},{160,192},{192,224},{224... | collective-permute-start | bytes 1179656 | tf_op jit(solution)/shard_map/ppermute | solution.py:303
  4.9 4.0 %collective-permute-start.1 = (f32[4,24576]{1,0:T(4,128)S(1)}, f32[4,24576]{1,0:T(4,128)S(1)}, u32[]{:S(2)}, u32[]{:S(2)}) collective-permute-start(f32[4,24576]{1,0:T(4,128)S(1)} %get-tuple-element.28), channel_id=1, source_target_pairs={{0,224},{32,0},{64,32},{96,64},{128,96},{160,128},{192,160},{224,1... | collective-permute-start | bytes 1179656 | tf_op jit(solution)/shard_map/ppermute | solution.py:303
  9.0 1.8 %collective-permute-start.4 = (f32[4,24576]{1,0:T(4,128)}, f32[4,24576]{1,0:T(4,128)S(1)}, u32[]{:S(2)}, u32[]{:S(2)}) collective-permute-start(f32[4,24576]{1,0:T(4,128)} %get-tuple-element.33), channel_id=1, source_target_pairs={{0,96},{32,128},{64,160},{96,192},{128,224},{160,0},{192,32},{224,... | collective-permute-start | bytes 1179656 | tf_op jit(solution)/shard_map/ppermute | solution.py:303
  10.8 3.2 %collective-permute-start.5 = (f32[4,24576]{1,0:T(4,128)}, f32[4,24576]{1,0:T(4,128)S(1)}, u32[]{:S(2)}, u32[]{:S(2)}) collective-permute-start(f32[4,24576]{1,0:T(4,128)} %get-tuple-element.34), channel_id=1, source_target_pairs={{0,160},{32,192},{64,224},{96,0},{128,32},{160,64},{192,96},{224,1... | collective-permute-start | bytes 1179656 | tf_op jit(solution)/shard_map/ppermute | solution.py:303
  14.0 5.7 %collective-permute-done.before_ref.up_ref = f32[4,24576]{1,0:T(4,128)S(1)} collective-permute-done((f32[4,24576]{1,0:T(4,128)S(1)}, f32[4,24576]{1,0:T(4,128)S(1)}, u32[]{:S(2)}, u32[]{:S(2)}) %collective-permute-start) | collective-permute-done | bytes 393248 | tf_op jit(solution)/shard_map/ppermute | solution.py:303
  19.6 4.3 %collective-permute-done.1.down_ref = f32[4,24576]{1,0:T(4,128)S(1)} collective-permute-done((f32[4,24576]{1,0:T(4,128)S(1)}, f32[4,24576]{1,0:T(4,128)S(1)}, u32[]{:S(2)}, u32[]{:S(2)}) %collective-permute-start.1) | collective-permute-done | bytes 393248 | tf_op jit(solution)/shard_map/ppermute | solution.py:303
  24.0 1.3 side_kernel.2
  25.3 3.2 %collective-permute-start.2 = (f32[2,4,12288]{2,1,0:T(4,128)}, f32[2,4,12288]{2,1,0:T(4,128)S(1)}, u32[]{:S(2)}, u32[]{:S(2)}) collective-permute-start(f32[2,4,12288]{2,1,0:T(4,128)} %get-tuple-element.30), channel_id=1, source_target_pairs={{0,16},{8,24},{16,0},{24,8},{32,48},{40,56},{48,32},{56,40},{64,80... | collective-permute-start | bytes 1179656 | tf_op jit(solution)/shard_map/ppermute | solution.py:292
  28.5 49.4 %even_kernel.1 = f32[16,4,6144]{2,1,0:T(4,128)} custom-call(s32[3]{0:T(128)S(1)} %pad_add_fusion.place_ref, f32[4,196608]{1,0:T(4,128)} %vectors_ref.3, f32[4,24576]{1,0:T(4,128)S(1)} %collective-permute-done.before_ref.up_ref), custom_call_target="tpu_custom_call" | custom-call | tf_op jit(solution)/shard_map/even_kernel/pallas_call | solution.py:223
  78.0 7.7 %all-to-all-start = ((f32[16,4,6144]{2,1,0:T(4,128)}), f32[16,4,6144]{2,1,0:T(4,128)S(1)}, u32[]{:S(2)}, u32[]{:S(2)}) async-start(f32[16,4,6144]{2,1,0:T(4,128)} %even_kernel.1), calls=%async_computation | async-start | bytes 3145728 | tf_op jit(solution)/shard_map/all_to_all | solution.py:317
  85.6 8.8 %gram.1 = (bf16[256,6144]{1,0:T(8,128)(2,1)}, bf16[256,6144]{1,0:T(8,128)(2,1)}, f32[96,128]{1,0:T(8,128)S(1)}, f32[96,128]{1,0:T(8,128)S(1)}) custom-call(s32[1]{0:T(128)} %bitcast.core_ref, f32[4,64,6144]{2,1,0:T(8,128)} %householder_ref.1, f32[4,24576]{1,0:T(4,128)S(1)} %collective-permute-done.before_ref.up_ref), custom_call_target="tpu_custom_call" | custom-call | flops 32212254720 | bytes 12582912 | tf_op jit(solution)/shard_map/gram/pallas_call | solution.py:199
  94.4 0.0 collective-permute-done.4.up_ref
  94.4 0.0 collective-permute-done.5.down_ref
  94.4 0.6 side_kernel.3
  95.1 3.5 %collective-permute-start.6 = (f32[2,4,12288]{2,1,0:T(4,128)S(1)}, f32[2,4,12288]{2,1,0:T(4,128)S(1)}, u32[]{:S(2)}, u32[]{:S(2)}) collective-permute-start(f32[2,4,12288]{2,1,0:T(4,128)S(1)} %get-tuple-element.37), channel_id=1, source_target_pairs={{0,16},{8,24},{16,0},{24,8},{32,48},{40,56},{48,32},{56,40},{64,80... | collective-permute-start | bytes 1179656 | tf_op jit(solution)/shard_map/ppermute | solution.py:292
  98.6 0.0 collective-permute-done.2.got_ref
  98.6 0.6 core_kernel.2
  99.2 0.1 collective-permute-start.3
  99.3 13.0 %collective-permute-done.6.got_ref = f32[2,4,12288]{2,1,0:T(4,128)S(1)} collective-permute-done((f32[2,4,12288]{2,1,0:T(4,128)S(1)}, f32[2,4,12288]{2,1,0:T(4,128)S(1)}, u32[]{:S(2)}, u32[]{:S(2)}) %collective-permute-start.6) | collective-permute-done | bytes 393248 | tf_op jit(solution)/shard_map/ppermute | solution.py:292
  112.3 0.6 core_kernel.3
  112.9 0.1 collective-permute-start.7
  113.0 0.5 collective-permute-start.8
  113.5 1.3 collective-permute-done.8
  114.8 4.1 %collective-permute-start.9 = (f32[96,128]{1,0:T(8,128)S(1)}, f32[96,128]{1,0:T(8,128)S(1)}, u32[]{:S(2)}, u32[]{:S(2)}) collective-permute-start(f32[96,128]{1,0:T(8,128)S(1)} %add.34), channel_id=1, source_target_pairs={{0,16},{8,24},{16,0},{24,8},{32,48},{40,56},{48,32},{56,40},{64,80... | collective-permute-start | bytes 147464 | tf_op jit(solution)/shard_map/ppermute | solution.py:292
  118.9 5.4 %collective-permute-done.9 = f32[96,128]{1,0:T(8,128)S(1)} collective-permute-done((f32[96,128]{1,0:T(8,128)S(1)}, f32[96,128]{1,0:T(8,128)S(1)}, u32[]{:S(2)}, u32[]{:S(2)}) %collective-permute-start.9) | collective-permute-done | bytes 49184 | tf_op jit(solution)/shard_map/ppermute | solution.py:292
  124.2 0.1 collective-permute-start.10
  124.3 4.1 %collective-permute-done.10 = f32[96,128]{1,0:T(8,128)S(1)} collective-permute-done((f32[96,128]{1,0:T(8,128)S(1)}, f32[96,128]{1,0:T(8,128)S(1)}, u32[]{:S(2)}, u32[]{:S(2)}) %collective-permute-start.10) | collective-permute-done | bytes 49184 | tf_op jit(solution)/shard_map/ppermute | solution.py:292
  128.4 4.1 %collective-permute-start.11 = (f32[96,128]{1,0:T(8,128)S(1)}, f32[96,128]{1,0:T(8,128)S(1)}, u32[]{:S(2)}, u32[]{:S(2)}) collective-permute-start(f32[96,128]{1,0:T(8,128)S(1)} %add.36.gram_ref), channel_id=1, source_target_pairs={{0,192},{8,200},{16,208},{24,216},{32,224},{40,232},{48,240},{56,2... | collective-permute-start | bytes 147464 | tf_op jit(solution)/shard_map/ppermute | solution.py:292
  132.6 0.0 collective-permute-done.3.got_one_ref
  132.6 0.0 collective-permute-done.7.got_three_ref
  132.6 0.0 all-to-all-done.even_ref
  132.6 0.0 copy-start
  132.6 1.9 %copy-done = bf16[256,6144]{1,0:T(8,128)(2,1)S(1)} copy-done((bf16[256,6144]{1,0:T(8,128)(2,1)S(1)}, bf16[256,6144]{1,0:T(8,128)(2,1)}, u32[]{:S(2)}) %copy-start) | copy-done | bytes 3145752
  134.5 0.0 copy-start.2
  134.5 2.0 %project_high.1 = (f32[128,6144]{1,0:T(8,128)S(1)}, bf16[128,6144]{1,0:T(8,128)(2,1)S(1)}, f32[256,256]{1,0:T(8,128)S(1)}) custom-call(s32[3]{0:T(128)S(1)} %pad_add_fusion.place_ref, f32[16,4,6144]{2,1,0:T(4,128)S(1)} %all-to-all-done.even_ref, f32[2,2,4,6144]{3,2,1,0:T(4,128)S(1)} %get-tuple-element.31.kept_one_ref, ...), custom_call_target="tpu_custom_call" | custom-call | tf_op jit(solution)/shard_map/project_high/pallas_call | solution.py:238
  136.5 0.0 collective-permute-done.11.more_ref
  136.5 0.0 copy-done.2
  136.5 0.0 copy-start.1
  136.5 0.0 copy-start.3
  136.5 1.0 project_low.1
  137.5 0.1 collective-permute-start.12
  137.6 1.2 collective-permute-done.12
  138.9 2.4 %collective-permute-start.13 = (f32[128,128]{1,0:T(8,128)S(1)}, f32[128,128]{1,0:T(8,128)S(1)}, u32[]{:S(2)}, u32[]{:S(2)}) collective-permute-start(f32[128,128]{1,0:T(8,128)S(1)} %add.37), channel_id=1, source_target_pairs={{0,16},{8,24},{16,0},{24,8},{32,48},{40,56},{48,32},{56,40},{64,80... | collective-permute-start | bytes 196616 | tf_op jit(solution)/shard_map/ppermute | solution.py:292
  141.3 3.7 %collective-permute-done.13 = f32[128,128]{1,0:T(8,128)S(1)} collective-permute-done((f32[128,128]{1,0:T(8,128)S(1)}, f32[128,128]{1,0:T(8,128)S(1)}, u32[]{:S(2)}, u32[]{:S(2)}) %collective-permute-start.13) | collective-permute-done | bytes 65568 | tf_op jit(solution)/shard_map/ppermute | solution.py:292
  145.0 1.9 %collective-permute-start.15 = (f32[224,128]{1,0:T(8,128)S(1)}, f32[224,128]{1,0:T(8,128)S(1)}, u32[]{:S(2)}, u32[]{:S(2)}) collective-permute-start(f32[224,128]{1,0:T(8,128)S(1)} %pad_maximum_fusion), channel_id=1, source_target_pairs={{0,64},{8,72},{16,80},{24,88},{32,96},{40,104},{48,112},{56,120},{... | collective-permute-start | bytes 344072 | tf_op jit(solution)/shard_map/ppermute | solution.py:292
  146.9 0.6 collective-permute-start.16
  147.4 1.1 collective-permute-start.14
  148.5 4.5 %collective-permute-done.16 = f32[128,128]{1,0:T(8,128)S(1)} collective-permute-done((f32[128,128]{1,0:T(8,128)S(1)}, f32[128,128]{1,0:T(8,128)S(1)}, u32[]{:S(2)}, u32[]{:S(2)}) %collective-permute-start.16) | collective-permute-done | bytes 65568 | tf_op jit(solution)/shard_map/ppermute | solution.py:292
  153.1 0.7 collective-permute-done.14
  153.8 0.2 collective-permute-done.15
  154.0 2.3 %collective-permute-start.17 = (f32[128,128]{1,0:T(8,128)S(1)}, f32[128,128]{1,0:T(8,128)S(1)}, u32[]{:S(2)}, u32[]{:S(2)}) collective-permute-start(f32[128,128]{1,0:T(8,128)S(1)} %fusion), channel_id=1, source_target_pairs={{0,192},{8,200},{16,208},{24,216},{32,224},{40,232},{48,240},{56,2... | collective-permute-start | bytes 196616 | tf_op jit(solution)/shard_map/ppermute | solution.py:292
  156.4 4.2 %collective-permute-done.17 = f32[128,128]{1,0:T(8,128)S(1)} collective-permute-done((f32[128,128]{1,0:T(8,128)S(1)}, f32[128,128]{1,0:T(8,128)S(1)}, u32[]{:S(2)}, u32[]{:S(2)}) %collective-permute-start.17) | collective-permute-done | bytes 65568 | tf_op jit(solution)/shard_map/ppermute | solution.py:292
  160.6 0.1 collective-permute-start.18
  160.7 1.3 collective-permute-done.18.other_ref
  162.0 0.0 copy-done.1
  162.0 0.0 copy-done.3
  162.1 3.4 %finish.1 = f32[128,6144]{1,0:T(8,128)} custom-call(s32[1]{0:T(128)} %bitcast.core_ref, f32[224,128]{1,0:T(8,128)S(1)} %pad_maximum_fusion.1.own_ref, f32[224,128]{1,0:T(8,128)S(1)} %collective-permute-done.18.other_ref, f32[4,64,64]{2,1,0:T(8,128)S(1)} %copy-done.3, f32[128,6144]{1,0:T(8,128)S(1)} %get-tuple-element.48.current_ref, ...), custom_call_target="tpu_custom_call" | custom-call | tf_op jit(solution)/shard_map/finish/pallas_call | solution.py:269
  (10 shorter events, 0.1 us)
Async XLA Ops:
  2.9 16.7 %collective-permute-start = (f32[4,24576]{1,0:T(4,128)S(1)}, f32[4,24576]{1,0:T(4,128)S(1)}, u32[]{:S(2)}, u32[]{:S(2)}) collective-permute-start(f32[4,24576]{1,0:T(4,128)S(1)} %get-tuple-element.27), channel_id=1, source_target_pairs={{0,32},{32,64},{64,96},{96,128},{128,160},{160,192},{192,224},{224... | collective-permute-start | bytes 1179656 | tf_op jit(solution)/shard_map/ppermute | solution.py:303
  4.9 19.1 %collective-permute-start.1 = (f32[4,24576]{1,0:T(4,128)S(1)}, f32[4,24576]{1,0:T(4,128)S(1)}, u32[]{:S(2)}, u32[]{:S(2)}) collective-permute-start(f32[4,24576]{1,0:T(4,128)S(1)} %get-tuple-element.28), channel_id=1, source_target_pairs={{0,224},{32,0},{64,32},{96,64},{128,96},{160,128},{192,160},{224,1... | collective-permute-start | bytes 1179656 | tf_op jit(solution)/shard_map/ppermute | solution.py:303
  9.0 85.5 %collective-permute-start.4 = (f32[4,24576]{1,0:T(4,128)}, f32[4,24576]{1,0:T(4,128)S(1)}, u32[]{:S(2)}, u32[]{:S(2)}) collective-permute-start(f32[4,24576]{1,0:T(4,128)} %get-tuple-element.33), channel_id=1, source_target_pairs={{0,96},{32,128},{64,160},{96,192},{128,224},{160,0},{192,32},{224,... | collective-permute-start | bytes 1179656 | tf_op jit(solution)/shard_map/ppermute | solution.py:303
  10.8 83.7 %collective-permute-start.5 = (f32[4,24576]{1,0:T(4,128)}, f32[4,24576]{1,0:T(4,128)S(1)}, u32[]{:S(2)}, u32[]{:S(2)}) collective-permute-start(f32[4,24576]{1,0:T(4,128)} %get-tuple-element.34), channel_id=1, source_target_pairs={{0,160},{32,192},{64,224},{96,0},{128,32},{160,64},{192,96},{224,1... | collective-permute-start | bytes 1179656 | tf_op jit(solution)/shard_map/ppermute | solution.py:303
  25.3 73.2 %collective-permute-start.2 = (f32[2,4,12288]{2,1,0:T(4,128)}, f32[2,4,12288]{2,1,0:T(4,128)S(1)}, u32[]{:S(2)}, u32[]{:S(2)}) collective-permute-start(f32[2,4,12288]{2,1,0:T(4,128)} %get-tuple-element.30), channel_id=1, source_target_pairs={{0,16},{8,24},{16,0},{24,8},{32,48},{40,56},{48,32},{56,40},{64,80... | collective-permute-start | bytes 1179656 | tf_op jit(solution)/shard_map/ppermute | solution.py:292
  78.0 54.6 %all-to-all-start = ((f32[16,4,6144]{2,1,0:T(4,128)}), f32[16,4,6144]{2,1,0:T(4,128)S(1)}, u32[]{:S(2)}, u32[]{:S(2)}) async-start(f32[16,4,6144]{2,1,0:T(4,128)} %even_kernel.1), calls=%async_computation | async-start | bytes 3145728 | tf_op jit(solution)/shard_map/all_to_all | solution.py:317
  95.1 17.2 %collective-permute-start.6 = (f32[2,4,12288]{2,1,0:T(4,128)S(1)}, f32[2,4,12288]{2,1,0:T(4,128)S(1)}, u32[]{:S(2)}, u32[]{:S(2)}) collective-permute-start(f32[2,4,12288]{2,1,0:T(4,128)S(1)} %get-tuple-element.37), channel_id=1, source_target_pairs={{0,16},{8,24},{16,0},{24,8},{32,48},{40,56},{48,32},{56,40},{64,80... | collective-permute-start | bytes 1179656 | tf_op jit(solution)/shard_map/ppermute | solution.py:292
  99.2 33.4 %collective-permute-start.3 = (f32[2,2,4,6144]{3,2,1,0:T(4,128)S(1)}, f32[2,2,4,6144]{3,2,1,0:T(4,128)S(1)}, u32[]{:S(2)}, u32[]{:S(2)}) collective-permute-start(f32[2,2,4,6144]{3,2,1,0:T(4,128)S(1)} %get-tuple-element.32), channel_id=1, source_target_pairs={{0,8},{8,0},{16,24},{24,16},{32,40},{40,32},{48,56},{56,48},{64,72... | collective-permute-start | bytes 1179656 | tf_op jit(solution)/shard_map/ppermute | solution.py:292
  112.9 19.7 %collective-permute-start.7 = (f32[2,2,4,6144]{3,2,1,0:T(4,128)S(1)}, f32[2,2,4,6144]{3,2,1,0:T(4,128)S(1)}, u32[]{:S(2)}, u32[]{:S(2)}) collective-permute-start(f32[2,2,4,6144]{3,2,1,0:T(4,128)S(1)} %get-tuple-element.39), channel_id=1, source_target_pairs={{0,8},{8,0},{16,24},{24,16},{32,40},{40,32},{48,56},{56,48},{64,72... | collective-permute-start | bytes 1179656 | tf_op jit(solution)/shard_map/ppermute | solution.py:292
  113.0 1.8 %collective-permute-start.8 = (f32[96,128]{1,0:T(8,128)S(1)}, f32[96,128]{1,0:T(8,128)S(1)}, u32[]{:S(2)}, u32[]{:S(2)}) collective-permute-start(f32[96,128]{1,0:T(8,128)S(1)} %get-tuple-element.44), channel_id=1, source_target_pairs={{0,8},{8,0},{16,24},{24,16},{32,40},{40,32},{48,56},{56,48},{64,72... | collective-permute-start | bytes 147464 | tf_op jit(solution)/shard_map/ppermute | solution.py:292
  114.8 9.4 %collective-permute-start.9 = (f32[96,128]{1,0:T(8,128)S(1)}, f32[96,128]{1,0:T(8,128)S(1)}, u32[]{:S(2)}, u32[]{:S(2)}) collective-permute-start(f32[96,128]{1,0:T(8,128)S(1)} %add.34), channel_id=1, source_target_pairs={{0,16},{8,24},{16,0},{24,8},{32,48},{40,56},{48,32},{56,40},{64,80... | collective-permute-start | bytes 147464 | tf_op jit(solution)/shard_map/ppermute | solution.py:292
  124.2 4.2 %collective-permute-start.10 = (f32[96,128]{1,0:T(8,128)S(1)}, f32[96,128]{1,0:T(8,128)S(1)}, u32[]{:S(2)}, u32[]{:S(2)}) collective-permute-start(f32[96,128]{1,0:T(8,128)S(1)} %add.35), channel_id=1, source_target_pairs={{0,32},{8,40},{16,48},{24,56},{32,0},{40,8},{48,16},{56,24},{64,96... | collective-permute-start | bytes 147464 | tf_op jit(solution)/shard_map/ppermute | solution.py:292
  128.4 8.1 %collective-permute-start.11 = (f32[96,128]{1,0:T(8,128)S(1)}, f32[96,128]{1,0:T(8,128)S(1)}, u32[]{:S(2)}, u32[]{:S(2)}) collective-permute-start(f32[96,128]{1,0:T(8,128)S(1)} %add.36.gram_ref), channel_id=1, source_target_pairs={{0,192},{8,200},{16,208},{24,216},{32,224},{40,232},{48,240},{56,2... | collective-permute-start | bytes 147464 | tf_op jit(solution)/shard_map/ppermute | solution.py:292
  132.6 1.9 %copy-start = (bf16[256,6144]{1,0:T(8,128)(2,1)S(1)}, bf16[256,6144]{1,0:T(8,128)(2,1)}, u32[]{:S(2)}) copy-start(bf16[256,6144]{1,0:T(8,128)(2,1)} %get-tuple-element.40.high_ref) | copy-start | bytes 9437188
  134.5 2.0 %copy-start.2 = (bf16[256,6144]{1,0:T(8,128)(2,1)S(1)}, bf16[256,6144]{1,0:T(8,128)(2,1)}, u32[]{:S(2)}) copy-start(bf16[256,6144]{1,0:T(8,128)(2,1)} %get-tuple-element.43.low_ref) | copy-start | bytes 9437188
  136.5 25.5 %copy-start.1 = (bf16[256,6144]{1,0:T(8,128)(2,1)S(1)}, bf16[256,6144]{1,0:T(8,128)(2,1)}, u32[]{:S(2)}) copy-start(bf16[256,6144]{1,0:T(8,128)(2,1)} %get-tuple-element.40.high_ref) | copy-start | bytes 9437188
  136.5 25.5 %copy-start.3 = (f32[4,64,64]{2,1,0:T(8,128)S(1)}, f32[4,64,64]{2,1,0:T(8,128)}, u32[]{:S(2)}) copy-start(f32[4,64,64]{2,1,0:T(8,128)} %tfactors_ref.1) | copy-start | bytes 196612
  137.5 1.3 collective-permute-start.12
  138.9 6.0 %collective-permute-start.13 = (f32[128,128]{1,0:T(8,128)S(1)}, f32[128,128]{1,0:T(8,128)S(1)}, u32[]{:S(2)}, u32[]{:S(2)}) collective-permute-start(f32[128,128]{1,0:T(8,128)S(1)} %add.37), channel_id=1, source_target_pairs={{0,16},{8,24},{16,0},{24,8},{32,48},{40,56},{48,32},{56,40},{64,80... | collective-permute-start | bytes 196616 | tf_op jit(solution)/shard_map/ppermute | solution.py:292
  145.0 9.1 %collective-permute-start.15 = (f32[224,128]{1,0:T(8,128)S(1)}, f32[224,128]{1,0:T(8,128)S(1)}, u32[]{:S(2)}, u32[]{:S(2)}) collective-permute-start(f32[224,128]{1,0:T(8,128)S(1)} %pad_maximum_fusion), channel_id=1, source_target_pairs={{0,64},{8,72},{16,80},{24,88},{32,96},{40,104},{48,112},{56,120},{... | collective-permute-start | bytes 344072 | tf_op jit(solution)/shard_map/ppermute | solution.py:292
  146.9 6.2 %collective-permute-start.16 = (f32[128,128]{1,0:T(8,128)S(1)}, f32[128,128]{1,0:T(8,128)S(1)}, u32[]{:S(2)}, u32[]{:S(2)}) collective-permute-start(f32[128,128]{1,0:T(8,128)S(1)} %add.38), channel_id=1, source_target_pairs={{0,96},{8,104},{16,112},{24,120},{32,64},{40,72},{48,80},{56,88},{... | collective-permute-start | bytes 196616 | tf_op jit(solution)/shard_map/ppermute | solution.py:292
  147.4 6.4 %collective-permute-start.14 = (f32[128,128]{1,0:T(8,128)S(1)}, f32[128,128]{1,0:T(8,128)S(1)}, u32[]{:S(2)}, u32[]{:S(2)}) collective-permute-start(f32[128,128]{1,0:T(8,128)S(1)} %add.38), channel_id=1, source_target_pairs={{0,32},{8,40},{16,48},{24,56},{32,0},{40,8},{48,16},{56,24},{64,96... | collective-permute-start | bytes 196616 | tf_op jit(solution)/shard_map/ppermute | solution.py:292
  154.0 6.6 %collective-permute-start.17 = (f32[128,128]{1,0:T(8,128)S(1)}, f32[128,128]{1,0:T(8,128)S(1)}, u32[]{:S(2)}, u32[]{:S(2)}) collective-permute-start(f32[128,128]{1,0:T(8,128)S(1)} %fusion), channel_id=1, source_target_pairs={{0,192},{8,200},{16,208},{24,216},{32,224},{40,232},{48,240},{56,2... | collective-permute-start | bytes 196616 | tf_op jit(solution)/shard_map/ppermute | solution.py:292
  160.6 1.4 collective-permute-start.18

commit v7 on v6

--- a/solution.py
+++ b/solution.py
@@ -40,8 +40,7 @@
     other_ref[...] = whole[pl.ds(pl.multiple_of((1 - core) * half, 8), half), :]
 
 
-def gram_kernel(core_ref, householder_ref, before_ref, high_ref, low_ref, kept_ref, sent_ref, total, packed):
-    del before_ref
+def gram_kernel(core_ref, householder_ref, high_ref, low_ref, kept_ref, sent_ref, total, packed):
     panels, width, columns = householder_ref.shape
     size = panels * width
     step = pl.program_id(0)
@@ -83,17 +82,11 @@
         copy.wait()
 
 
-def even_kernel(place_ref, vectors_ref, before_ref, out_ref, sems):
-    del before_ref
+def even_kernel(place_ref, block_ref, out_ref):
+    del place_ref
     number, _, wide = out_ref.shape
-    copies = []
     for i in range(number):
-        block = (i // 4 * 2 + place_ref[0] % 2) * 4 + i % 4
-        columns = pl.ds(pl.multiple_of(block * wide, 128), wide)
-        copies.append(pltpu.make_async_copy(vectors_ref.at[:, columns], out_ref.at[i], sems.at[i]))
-        copies[i].start()
-    for copy in copies:
-        copy.wait()
+        out_ref[i] = block_ref[:, i * wide : (i + 1) * wide]
 
 
 def side_kernel(place_ref, up_ref, down_ref, before_ref, kept_ref, sent_ref):
@@ -192,7 +185,7 @@
     return pltpu.with_memory_space_constraint(value, pltpu.HBM)
 
 
-def gram_call(core, householder, before):
+def gram_call(core, householder):
     panels, width, rows = householder.shape
     size = panels * width
     height = len(pairs_of(panels)) // 2 * width
@@ -205,7 +198,7 @@
             jax.ShapeDtypeStruct((height // 2, 2 * width), jnp.float32),
         ),
         grid=(rows // COLUMNS,),
-        in_specs=[IN_SMEM, pl.BlockSpec((panels, width, COLUMNS), lambda i: (0, 0, i)), IN_ANY],
+        in_specs=[IN_SMEM, pl.BlockSpec((panels, width, COLUMNS), lambda i: (0, 0, i))],
         out_specs=(
             pl.BlockSpec((size, COLUMNS), lambda i: (0, i)),
             pl.BlockSpec((size, COLUMNS), lambda i: (0, i)),
@@ -216,7 +209,7 @@
         compiler_params=pltpu.CompilerParams(vmem_limit_bytes=LIMIT),
         cost_estimate=pl.CostEstimate(flops=10 * 8 * size * size * rows, bytes_accessed=8 * size * rows, transcendentals=0),
         name="gram",
-    )(core, in_hbm(householder), before)
+    )(core, in_hbm(householder))
 
 
 def local_call(kernel, outs, specs, operands, copies=0):
@@ -229,6 +222,23 @@
         compiler_params=pltpu.CompilerParams(vmem_limit_bytes=LIMIT),
         name=kernel.__name__,
     )(*operands)
+
+
+def even_call(place, vectors, planes):
+    each, length = vectors.shape
+    wide = length // planes
+    return pl.pallas_call(
+        even_kernel,
+        out_shape=pltpu.HBM((planes * 2, each, wide // 4), jnp.float32),
+        grid_spec=pltpu.PrefetchScalarGridSpec(
+            num_scalar_prefetch=1,
+            grid=(planes // 2,),
+            in_specs=[pl.BlockSpec((each, wide), lambda k, place_ref: (0, 2 * k + place_ref[0] % 2))],
+            out_specs=pl.BlockSpec((4, each, wide // 4), lambda k, place_ref: (k, 0, 0)),
+        ),
+        compiler_params=pltpu.CompilerParams(vmem_limit_bytes=LIMIT),
+        name="even",
+    )(place, in_hbm(vectors))
 
 
 def project_call(core, place, even, odd, high, low, gram, more):
@@ -312,13 +322,12 @@
         block = pltpu.VMEM((each, wide), jnp.float32)
         cut = local_call(cut_kernel, (block,) * len(SHIFTS), [IN_HBM], (place, in_hbm(vectors_in)), len(SHIFTS))
         came = [moved(part, shift) for part, shift in zip(cut, SHIFTS)]
-        block = pltpu.HBM((devices // 2, each, wide // 4), jnp.float32)
-        (even,) = local_call(even_kernel, (block,), [IN_HBM, IN_ANY], (place, in_hbm(vectors_in), came[0]), devices // 2)
+        even = even_call(place, vectors_in, planes)
         even = lax.all_to_all(even, ("half", "y", "core"), split_axis=0, concat_axis=0, tiled=True)
-        high, low, gram, sent = gram_call(core, householder, came[0])
-        scattered = spread(came[0], came[1], came[0]) + spread(came[2], came[3], gram)
-        gram = gram + swap(sent, 1)
+        high, low, kept, sent = gram_call(core, householder)
+        gram = kept + swap(sent, 1)
         gram = gram + swap(gram, 2)
+        scattered = spread(came[0], came[1], kept) + spread(came[2], came[3], gram)
         gram = gram + swap(gram, 4)
         current, value, sent, gram = project_call(core, place, even, scattered, high, low, gram, swap(gram, 24))
         value = value + swap(sent, 1)

time: 167 us -> 126 us (0.75)
  Pallas kernels: 70.6 us -> 27.7 us
  local copies, waits for them, and re-layouts: 1.9 us -> 5.26 us
  waiting for transfers between devices: 49.7 us -> 46.6 us
    pallas_call x6 -> x5, Pallas kernels: 55.4 us -> 6.54 us  [local_call(): pl.pallas_call(kernel, out_shape=outs, in_specs=[IN_SMEM] + specs, out_sp...]
    ppermute x4, waiting for transfers between devices: 10 us -> 2.1 us  [moved(): lax.ppermute(part, ('half', 'odd'), [(i, (i + shift) % planes) for i in r...]
    ppermute x15, waiting for transfers between devices: 39.7 us -> 44.5 us  [swap(): return lax.ppermute(value, row, [(i, i ^ flip) for i in range(devices)])]
    pallas_call x0 -> x1, Pallas kernels: none -> 4.14 us  [even_call(): pl.pallas_call(even_kernel, out_shape=pltpu.HBM((planes * 2, each, wide /...]
    unnamed x8 -> x18, local copies, waits for them, and re-layouts: 1.9 us -> 5.26 us
    all_to_all x1, starting transfers between devices: 7.67 us -> 9.44 us  [shards(): lax.all_to_all(even, ('half', 'y', 'core'), split_axis=0, concat_axis=0,...]
  transfers between devices with their start and end apart: 20 -> 20, of which waited for: 13 -> 11; matrix products, arithmetic and copies ran while one was open for 0% -> 1% of each run, Pallas kernels for 38% -> 16%
where the time goes in v7:
time: 126 us; the launch traced here: 124 us
  waiting for transfers between devices  46.6 us (37%)
  starting transfers between devices  43.1 us (34%)
  Pallas kernels  27.7 us (22%)
  local copies, waits for them, and re-layouts  5.26 us (4%)
    ppermute x15, waiting for transfers between devices, swap(): return lax.ppermute(value, row, [(i, i ^ flip) for i in range(devices)])  44.5 us
    ppermute x15, starting transfers between devices, swap(): return lax.ppermute(value, row, [(i, i ^ flip) for i in range(devices)])  23.5 us
    ppermute x4, starting transfers between devices, moved(): lax.ppermute(part, ('half', 'odd'), [(i, (i + shift) % planes) for i in r...  10.1 us
    all_to_all x1, starting transfers between devices, shards(): lax.all_to_all(even, ('half', 'y', 'core'), split_axis=0, concat_axis=0,...  9.44 us
    pallas_call x1, Pallas kernels, gram_call(): pl.pallas_call(gram_kernel, out_shape=(pltpu.HBM((size, rows), jnp.bfloat...  8.8 us
    pallas_call x5, Pallas kernels, local_call(): pl.pallas_call(kernel, out_shape=outs, in_specs=[IN_SMEM] + specs, out_sp...  6.54 us
    unnamed x18, local copies, waits for them, and re-layouts  5.26 us
    pallas_call x1, Pallas kernels, even_call(): pl.pallas_call(even_kernel, out_shape=pltpu.HBM((planes * 2, each, wide /...  4.14 us
  transfers between devices with their start and end apart: 20, of which 11 were waited for; matrix products, arithmetic and copies ran while one was open for 1% of the time, Pallas kernels for 16%

profile of v7, /device:TPU:4, one launch (start us, length us, event | category | flops | bytes accessed | tf_op | source)
XLA Modules:
  0.0 123.9 jit_solution(16078267912786511981)
XLA Ops:
  0.0 0.1 pad_add_fusion.place_ref
  0.1 3.1 %cut_kernel.1 = (f32[4,24576]{1,0:T(4,128)}, f32[4,24576]{1,0:T(4,128)}, f32[4,24576]{1,0:T(4,128)}, f32[4,24576]{1,0:T(4,128)}) custom-call(s32[3]{0:T(128)S(1)} %pad_add_fusion.place_ref, f32[4,196608]{1,0:T(4,128)} %vectors_ref.1), custom_call_target="tpu_custom_call" | custom-call | tf_op jit(solution)/shard_map/cut_kernel/pallas_call | solution.py:216
  3.2 4.7 %collective-permute-start.4 = (f32[4,24576]{1,0:T(4,128)}, f32[4,24576]{1,0:T(4,128)}, u32[]{:S(2)}, u32[]{:S(2)}) collective-permute-start(f32[4,24576]{1,0:T(4,128)} %get-tuple-element.34), channel_id=1, source_target_pairs={{0,96},{32,128},{64,160},{96,192},{128,224},{160,0},{192,32},{224,... | collective-permute-start | bytes 1179656 | tf_op jit(solution)/shard_map/ppermute | solution.py:313
  7.9 2.2 %collective-permute-start.5 = (f32[4,24576]{1,0:T(4,128)}, f32[4,24576]{1,0:T(4,128)}, u32[]{:S(2)}, u32[]{:S(2)}) collective-permute-start(f32[4,24576]{1,0:T(4,128)} %get-tuple-element.35), channel_id=1, source_target_pairs={{0,160},{32,192},{64,224},{96,0},{128,32},{160,64},{192,96},{224,1... | collective-permute-start | bytes 1179656 | tf_op jit(solution)/shard_map/ppermute | solution.py:313
  10.1 1.0 collective-permute-start
  11.1 2.2 %collective-permute-start.1 = (f32[4,24576]{1,0:T(4,128)}, f32[4,24576]{1,0:T(4,128)}, u32[]{:S(2)}, u32[]{:S(2)}) collective-permute-start(f32[4,24576]{1,0:T(4,128)} %get-tuple-element.28), channel_id=1, source_target_pairs={{0,224},{32,0},{64,32},{96,64},{128,96},{160,128},{192,160},{224,1... | collective-permute-start | bytes 1179656 | tf_op jit(solution)/shard_map/ppermute | solution.py:313
  13.3 4.1 %even.1 = f32[16,4,6144]{2,1,0:T(4,128)} custom-call(s32[3]{0:T(128)S(1)} %pad_add_fusion.place_ref, f32[4,196608]{1,0:T(4,128)} %vectors_ref.1), custom_call_target="tpu_custom_call" | custom-call | tf_op jit(solution)/shard_map/even/pallas_call | solution.py:230
  17.5 9.4 %all-to-all-start = ((f32[16,4,6144]{2,1,0:T(4,128)}), f32[16,4,6144]{2,1,0:T(4,128)}, u32[]{:S(2)}, u32[]{:S(2)}) async-start(f32[16,4,6144]{2,1,0:T(4,128)} %even.1), calls=%async_computation | async-start | bytes 3145728 | tf_op jit(solution)/shard_map/all_to_all | solution.py:326
  26.9 8.8 %gram.1 = (bf16[256,6144]{1,0:T(8,128)(2,1)}, bf16[256,6144]{1,0:T(8,128)(2,1)}, f32[96,128]{1,0:T(8,128)S(1)}, f32[96,128]{1,0:T(8,128)S(1)}) custom-call(s32[1]{0:T(128)} %bitcast.core_ref, f32[4,64,6144]{2,1,0:T(8,128)} %householder_ref.1), custom_call_target="tpu_custom_call" | custom-call | flops 32212254720 | bytes 12582912 | tf_op jit(solution)/shard_map/gram/pallas_call | solution.py:192
  35.7 0.0 copy-start
  35.7 0.4 collective-permute-start.6
  36.1 0.9 collective-permute-done.6
  37.0 3.4 %collective-permute-start.7 = (f32[96,128]{1,0:T(8,128)S(1)}, f32[96,128]{1,0:T(8,128)S(1)}, u32[]{:S(2)}, u32[]{:S(2)}) collective-permute-start(f32[96,128]{1,0:T(8,128)S(1)} %add.34), channel_id=1, source_target_pairs={{0,16},{8,24},{16,0},{24,8},{32,48},{40,56},{48,32},{56,40},{64,80... | collective-permute-start | bytes 147464 | tf_op jit(solution)/shard_map/ppermute | solution.py:302
  40.4 2.2 %collective-permute-done.7 = f32[96,128]{1,0:T(8,128)S(1)} collective-permute-done((f32[96,128]{1,0:T(8,128)S(1)}, f32[96,128]{1,0:T(8,128)S(1)}, u32[]{:S(2)}, u32[]{:S(2)}) %collective-permute-start.7) | collective-permute-done | bytes 49184 | tf_op jit(solution)/shard_map/ppermute | solution.py:302
  42.7 0.0 collective-permute-done.4.up_ref
  42.7 0.0 collective-permute-done.5.down_ref
  42.7 1.2 side_kernel.3
  43.9 3.5 %collective-permute-start.8 = (f32[2,4,12288]{2,1,0:T(4,128)S(1)}, f32[2,4,12288]{2,1,0:T(4,128)S(1)}, u32[]{:S(2)}, u32[]{:S(2)}) collective-permute-start(f32[2,4,12288]{2,1,0:T(4,128)S(1)} %get-tuple-element.38), channel_id=1, source_target_pairs={{0,16},{8,24},{16,0},{24,8},{32,48},{40,56},{48,32},{56,40},{64,80... | collective-permute-start | bytes 1179656 | tf_op jit(solution)/shard_map/ppermute | solution.py:302
  47.3 0.0 collective-permute-done.up_ref
  47.3 2.1 %collective-permute-done.1.down_ref = f32[4,24576]{1,0:T(4,128)} collective-permute-done((f32[4,24576]{1,0:T(4,128)}, f32[4,24576]{1,0:T(4,128)}, u32[]{:S(2)}, u32[]{:S(2)}) %collective-permute-start.1) | collective-permute-done | bytes 393248 | tf_op jit(solution)/shard_map/ppermute | solution.py:313
  49.4 1.1 side_kernel.2
  50.5 3.3 %collective-permute-start.2 = (f32[2,4,12288]{2,1,0:T(4,128)S(1)}, f32[2,4,12288]{2,1,0:T(4,128)S(1)}, u32[]{:S(2)}, u32[]{:S(2)}) collective-permute-start(f32[2,4,12288]{2,1,0:T(4,128)S(1)} %get-tuple-element.31), channel_id=1, source_target_pairs={{0,16},{8,24},{16,0},{24,8},{32,48},{40,56},{48,32},{56,40},{64,80... | collective-permute-start | bytes 1179656 | tf_op jit(solution)/shard_map/ppermute | solution.py:302
  53.8 8.1 %collective-permute-done.8.got_ref = f32[2,4,12288]{2,1,0:T(4,128)S(1)} collective-permute-done((f32[2,4,12288]{2,1,0:T(4,128)S(1)}, f32[2,4,12288]{2,1,0:T(4,128)S(1)}, u32[]{:S(2)}, u32[]{:S(2)}) %collective-permute-start.8) | collective-permute-done | bytes 393248 | tf_op jit(solution)/shard_map/ppermute | solution.py:302
  61.9 0.6 core_kernel.3
  62.5 0.1 collective-permute-start.9
  62.6 11.2 %collective-permute-done.2.got_ref = f32[2,4,12288]{2,1,0:T(4,128)S(1)} collective-permute-done((f32[2,4,12288]{2,1,0:T(4,128)S(1)}, f32[2,4,12288]{2,1,0:T(4,128)S(1)}, u32[]{:S(2)}, u32[]{:S(2)}) %collective-permute-start.2) | collective-permute-done | bytes 393248 | tf_op jit(solution)/shard_map/ppermute | solution.py:302
  73.8 0.6 core_kernel.2
  74.4 0.0 copy-start.4
  74.4 0.7 copy-done.4
  75.2 0.0 collective-permute-start.3
  75.2 0.5 collective-permute-start.10
  75.7 4.6 %collective-permute-done.10 = f32[96,128]{1,0:T(8,128)S(1)} collective-permute-done((f32[96,128]{1,0:T(8,128)S(1)}, f32[96,128]{1,0:T(8,128)S(1)}, u32[]{:S(2)}, u32[]{:S(2)}) %collective-permute-start.10) | collective-permute-done | bytes 49184 | tf_op jit(solution)/shard_map/ppermute | solution.py:302
  80.3 0.6 add.36.gram_ref
  81.0 3.4 %collective-permute-start.11 = (f32[96,128]{1,0:T(8,128)}, f32[96,128]{1,0:T(8,128)}, u32[]{:S(2)}, u32[]{:S(2)}) collective-permute-start(f32[96,128]{1,0:T(8,128)} %add.36.gram_ref), channel_id=1, source_target_pairs={{0,192},{8,200},{16,208},{24,216},{32,224},{40,232},{48,240},{56,2... | collective-permute-start | bytes 147464 | tf_op jit(solution)/shard_map/ppermute | solution.py:302
  84.3 0.0 collective-permute-done.9.got_three_ref
  84.3 0.7 copy-done.2
  85.1 0.0 collective-permute-done.3.got_one_ref
  85.1 0.8 copy-done.6
  85.9 0.0 all-to-all-done.even_ref
  85.9 0.0 copy-done
  85.9 1.0 copy-done.3
  86.9 1.0 copy-done.5
  87.9 1.0 copy-done.7
  88.9 3.0 %project_high.1 = (f32[128,6144]{1,0:T(8,128)S(1)}, bf16[128,6144]{1,0:T(8,128)(2,1)S(1)}, f32[256,256]{1,0:T(8,128)S(1)}) custom-call(s32[3]{0:T(128)S(1)} %pad_add_fusion.place_ref, f32[16,4,6144]{2,1,0:T(4,128)} %all-to-all-done.even_ref, f32[2,2,4,6144]{3,2,1,0:T(4,128)S(1)} %copy-done.5, f32[2,2,4,6144]{3,2,1,0:T(4,128)S(1)} %copy-done.7, ...), custom_call_target="tpu_custom_call" | custom-call | tf_op jit(solution)/shard_map/project_high/pallas_call | solution.py:248
  91.9 0.0 collective-permute-done.11.more_ref
  91.9 0.0 copy-done.1
  91.9 0.0 copy-start.8
  91.9 1.9 %project_low.1 = (f32[128,128]{1,0:T(8,128)S(1)}, f32[128,128]{1,0:T(8,128)S(1)}, f32[96,128]{1,0:T(8,128)S(1)}) custom-call(s32[1]{0:T(128)} %bitcast.core_ref, f32[256,256]{1,0:T(8,128)S(1)} %get-tuple-element.42.total_ref, bf16[128,6144]{1,0:T(8,128)(2,1)S(1)} %get-tuple-element.43.rounded_ref, bf16[256,6144]{1,0:T(8,128)(2,1)S(1)} %copy-done.1, ...), custom_call_target="tpu_custom_call" | custom-call | tf_op jit(solution)/shard_map/project_low/pallas_call | solution.py:260
  93.8 0.1 collective-permute-start.12
  93.9 1.2 %collective-permute-done.12 = f32[128,128]{1,0:T(8,128)S(1)} collective-permute-done((f32[128,128]{1,0:T(8,128)S(1)}, f32[128,128]{1,0:T(8,128)S(1)}, u32[]{:S(2)}, u32[]{:S(2)}) %collective-permute-start.12) | collective-permute-done | bytes 65568 | tf_op jit(solution)/shard_map/ppermute | solution.py:302
  95.1 3.1 %collective-permute-start.13 = (f32[128,128]{1,0:T(8,128)S(1)}, f32[128,128]{1,0:T(8,128)S(1)}, u32[]{:S(2)}, u32[]{:S(2)}) collective-permute-start(f32[128,128]{1,0:T(8,128)S(1)} %add.37), channel_id=1, source_target_pairs={{0,16},{8,24},{16,0},{24,8},{32,48},{40,56},{48,32},{56,40},{64,80... | collective-permute-start | bytes 196616 | tf_op jit(solution)/shard_map/ppermute | solution.py:302
  98.3 2.9 %collective-permute-done.13 = f32[128,128]{1,0:T(8,128)S(1)} collective-permute-done((f32[128,128]{1,0:T(8,128)S(1)}, f32[128,128]{1,0:T(8,128)S(1)}, u32[]{:S(2)}, u32[]{:S(2)}) %collective-permute-start.13) | collective-permute-done | bytes 65568 | tf_op jit(solution)/shard_map/ppermute | solution.py:302
  101.2 4.0 %collective-permute-start.15 = (f32[224,128]{1,0:T(8,128)S(1)}, f32[224,128]{1,0:T(8,128)S(1)}, u32[]{:S(2)}, u32[]{:S(2)}) collective-permute-start(f32[224,128]{1,0:T(8,128)S(1)} %pad_maximum_fusion), channel_id=1, source_target_pairs={{0,64},{8,72},{16,80},{24,88},{32,96},{40,104},{48,112},{56,120},{... | collective-permute-start | bytes 344072 | tf_op jit(solution)/shard_map/ppermute | solution.py:302
  105.2 0.3 collective-permute-start.14
  105.5 1.3 %collective-permute-start.16 = (f32[128,128]{1,0:T(8,128)S(1)}, f32[128,128]{1,0:T(8,128)S(1)}, u32[]{:S(2)}, u32[]{:S(2)}) collective-permute-start(f32[128,128]{1,0:T(8,128)S(1)} %add.38), channel_id=1, source_target_pairs={{0,96},{8,104},{16,112},{24,120},{32,64},{40,72},{48,80},{56,88},{... | collective-permute-start | bytes 196616 | tf_op jit(solution)/shard_map/ppermute | solution.py:302
  106.7 5.7 %collective-permute-done.14 = f32[128,128]{1,0:T(8,128)S(1)} collective-permute-done((f32[128,128]{1,0:T(8,128)S(1)}, f32[128,128]{1,0:T(8,128)S(1)}, u32[]{:S(2)}, u32[]{:S(2)}) %collective-permute-start.14) | collective-permute-done | bytes 65568 | tf_op jit(solution)/shard_map/ppermute | solution.py:302
  112.4 0.0 collective-permute-done.16
  112.4 0.0 collective-permute-done.15
  112.4 0.1 collective-permute-start.17
  112.6 6.3 %collective-permute-done.17 = f32[128,128]{1,0:T(8,128)S(1)} collective-permute-done((f32[128,128]{1,0:T(8,128)S(1)}, f32[128,128]{1,0:T(8,128)S(1)}, u32[]{:S(2)}, u32[]{:S(2)}) %collective-permute-start.17) | collective-permute-done | bytes 65568 | tf_op jit(solution)/shard_map/ppermute | solution.py:302
  118.9 0.1 collective-permute-start.18
  119.0 1.3 %collective-permute-done.18.other_ref = f32[224,128]{1,0:T(8,128)S(1)} collective-permute-done((f32[224,128]{1,0:T(8,128)S(1)}, f32[224,128]{1,0:T(8,128)S(1)}, u32[]{:S(2)}, u32[]{:S(2)}) %collective-permute-start.18) | collective-permute-done | bytes 114720 | tf_op jit(solution)/shard_map/ppermute | solution.py:302
  120.4 0.0 copy-done.8
  120.4 3.4 %finish.1 = f32[128,6144]{1,0:T(8,128)} custom-call(s32[1]{0:T(128)} %bitcast.core_ref, f32[224,128]{1,0:T(8,128)S(1)} %pad_maximum_fusion.1.own_ref, f32[224,128]{1,0:T(8,128)S(1)} %collective-permute-done.18.other_ref, f32[4,64,64]{2,1,0:T(8,128)S(1)} %copy-done.8, f32[128,6144]{1,0:T(8,128)S(1)} %get-tuple-element.48.current_ref, ...), custom_call_target="tpu_custom_call" | custom-call | tf_op jit(solution)/shard_map/finish/pallas_call | solution.py:279
  (15 shorter events, 0.1 us)
Async XLA Ops:
  3.2 39.5 %collective-permute-start.4 = (f32[4,24576]{1,0:T(4,128)}, f32[4,24576]{1,0:T(4,128)}, u32[]{:S(2)}, u32[]{:S(2)}) collective-permute-start(f32[4,24576]{1,0:T(4,128)} %get-tuple-element.34), channel_id=1, source_target_pairs={{0,96},{32,128},{64,160},{96,192},{128,224},{160,0},{192,32},{224,... | collective-permute-start | bytes 1179656 | tf_op jit(solution)/shard_map/ppermute | solution.py:313
  7.9 34.8 %collective-permute-start.5 = (f32[4,24576]{1,0:T(4,128)}, f32[4,24576]{1,0:T(4,128)}, u32[]{:S(2)}, u32[]{:S(2)}) collective-permute-start(f32[4,24576]{1,0:T(4,128)} %get-tuple-element.35), channel_id=1, source_target_pairs={{0,160},{32,192},{64,224},{96,0},{128,32},{160,64},{192,96},{224,1... | collective-permute-start | bytes 1179656 | tf_op jit(solution)/shard_map/ppermute | solution.py:313
  10.1 37.2 %collective-permute-start = (f32[4,24576]{1,0:T(4,128)}, f32[4,24576]{1,0:T(4,128)S(1)}, u32[]{:S(2)}, u32[]{:S(2)}) collective-permute-start(f32[4,24576]{1,0:T(4,128)} %get-tuple-element.27), channel_id=1, source_target_pairs={{0,32},{32,64},{64,96},{96,128},{128,160},{160,192},{192,224},{224... | collective-permute-start | bytes 1179656 | tf_op jit(solution)/shard_map/ppermute | solution.py:313
  11.1 38.3 %collective-permute-start.1 = (f32[4,24576]{1,0:T(4,128)}, f32[4,24576]{1,0:T(4,128)}, u32[]{:S(2)}, u32[]{:S(2)}) collective-permute-start(f32[4,24576]{1,0:T(4,128)} %get-tuple-element.28), channel_id=1, source_target_pairs={{0,224},{32,0},{64,32},{96,64},{128,96},{160,128},{192,160},{224,1... | collective-permute-start | bytes 1179656 | tf_op jit(solution)/shard_map/ppermute | solution.py:313
  17.5 68.4 %all-to-all-start = ((f32[16,4,6144]{2,1,0:T(4,128)}), f32[16,4,6144]{2,1,0:T(4,128)}, u32[]{:S(2)}, u32[]{:S(2)}) async-start(f32[16,4,6144]{2,1,0:T(4,128)} %even.1), calls=%async_computation | async-start | bytes 3145728 | tf_op jit(solution)/shard_map/all_to_all | solution.py:326
  35.7 50.1 %copy-start = (bf16[256,6144]{1,0:T(8,128)(2,1)S(1)}, bf16[256,6144]{1,0:T(8,128)(2,1)}, u32[]{:S(2)}) copy-start(bf16[256,6144]{1,0:T(8,128)(2,1)} %get-tuple-element.41.high_ref) | copy-start | bytes 9437188
  35.7 1.2 %collective-permute-start.6 = (f32[96,128]{1,0:T(8,128)S(1)}, f32[96,128]{1,0:T(8,128)S(1)}, u32[]{:S(2)}, u32[]{:S(2)}) collective-permute-start(f32[96,128]{1,0:T(8,128)S(1)} %get-tuple-element.36), channel_id=1, source_target_pairs={{0,8},{8,0},{16,24},{24,16},{32,40},{40,32},{48,56},{56,48},{64,72... | collective-permute-start | bytes 147464 | tf_op jit(solution)/shard_map/ppermute | solution.py:302
  37.0 5.7 %collective-permute-start.7 = (f32[96,128]{1,0:T(8,128)S(1)}, f32[96,128]{1,0:T(8,128)S(1)}, u32[]{:S(2)}, u32[]{:S(2)}) collective-permute-start(f32[96,128]{1,0:T(8,128)S(1)} %add.34), channel_id=1, source_target_pairs={{0,16},{8,24},{16,0},{24,8},{32,48},{40,56},{48,32},{56,40},{64,80... | collective-permute-start | bytes 147464 | tf_op jit(solution)/shard_map/ppermute | solution.py:302
  43.9 18.0 %collective-permute-start.8 = (f32[2,4,12288]{2,1,0:T(4,128)S(1)}, f32[2,4,12288]{2,1,0:T(4,128)S(1)}, u32[]{:S(2)}, u32[]{:S(2)}) collective-permute-start(f32[2,4,12288]{2,1,0:T(4,128)S(1)} %get-tuple-element.38), channel_id=1, source_target_pairs={{0,16},{8,24},{16,0},{24,8},{32,48},{40,56},{48,32},{56,40},{64,80... | collective-permute-start | bytes 1179656 | tf_op jit(solution)/shard_map/ppermute | solution.py:302
  50.5 23.3 %collective-permute-start.2 = (f32[2,4,12288]{2,1,0:T(4,128)S(1)}, f32[2,4,12288]{2,1,0:T(4,128)S(1)}, u32[]{:S(2)}, u32[]{:S(2)}) collective-permute-start(f32[2,4,12288]{2,1,0:T(4,128)S(1)} %get-tuple-element.31), channel_id=1, source_target_pairs={{0,16},{8,24},{16,0},{24,8},{32,48},{40,56},{48,32},{56,40},{64,80... | collective-permute-start | bytes 1179656 | tf_op jit(solution)/shard_map/ppermute | solution.py:302
  62.5 21.9 %collective-permute-start.9 = (f32[2,2,4,6144]{3,2,1,0:T(4,128)S(1)}, f32[2,2,4,6144]{3,2,1,0:T(4,128)S(1)}, u32[]{:S(2)}, u32[]{:S(2)}) collective-permute-start(f32[2,2,4,6144]{3,2,1,0:T(4,128)S(1)} %get-tuple-element.40), channel_id=1, source_target_pairs={{0,8},{8,0},{16,24},{24,16},{32,40},{40,32},{48,56},{56,48},{64,72... | collective-permute-start | bytes 1179656 | tf_op jit(solution)/shard_map/ppermute | solution.py:302
  74.4 0.8 copy-start.4
  75.2 9.9 %collective-permute-start.3 = (f32[2,2,4,6144]{3,2,1,0:T(4,128)S(1)}, f32[2,2,4,6144]{3,2,1,0:T(4,128)S(1)}, u32[]{:S(2)}, u32[]{:S(2)}) collective-permute-start(f32[2,2,4,6144]{3,2,1,0:T(4,128)S(1)} %get-tuple-element.33), channel_id=1, source_target_pairs={{0,8},{8,0},{16,24},{24,16},{32,40},{40,32},{48,56},{56,48},{64,72... | collective-permute-start | bytes 1179656 | tf_op jit(solution)/shard_map/ppermute | solution.py:302
  75.2 5.2 %collective-permute-start.10 = (f32[96,128]{1,0:T(8,128)S(1)}, f32[96,128]{1,0:T(8,128)S(1)}, u32[]{:S(2)}, u32[]{:S(2)}) collective-permute-start(f32[96,128]{1,0:T(8,128)S(1)} %add.35.before_ref), channel_id=1, source_target_pairs={{0,32},{8,40},{16,48},{24,56},{32,0},{40,8},{48,16},{56,24},{64,96... | collective-permute-start | bytes 147464 | tf_op jit(solution)/shard_map/ppermute | solution.py:302
  81.0 10.9 %collective-permute-start.11 = (f32[96,128]{1,0:T(8,128)}, f32[96,128]{1,0:T(8,128)}, u32[]{:S(2)}, u32[]{:S(2)}) collective-permute-start(f32[96,128]{1,0:T(8,128)} %add.36.gram_ref), channel_id=1, source_target_pairs={{0,192},{8,200},{16,208},{24,216},{32,224},{40,232},{48,240},{56,2... | collective-permute-start | bytes 147464 | tf_op jit(solution)/shard_map/ppermute | solution.py:302
  84.3 0.7 copy-start.2
  85.1 0.8 copy-start.6
  85.9 1.0 copy-start.3
  86.9 1.0 copy-start.5
  87.9 1.0 copy-start.7
  88.8 3.0 %copy-start.1 = (bf16[256,6144]{1,0:T(8,128)(2,1)S(1)}, bf16[256,6144]{1,0:T(8,128)(2,1)}, u32[]{:S(2)}) copy-start(bf16[256,6144]{1,0:T(8,128)(2,1)} %get-tuple-element.44.low_ref) | copy-start | bytes 9437188
  91.9 28.5 %copy-start.8 = (f32[4,64,64]{2,1,0:T(8,128)S(1)}, f32[4,64,64]{2,1,0:T(8,128)}, u32[]{:S(2)}) copy-start(f32[4,64,64]{2,1,0:T(8,128)} %tfactors_ref.1) | copy-start | bytes 196612
  93.8 1.3 %collective-permute-start.12 = (f32[128,128]{1,0:T(8,128)S(1)}, f32[128,128]{1,0:T(8,128)S(1)}, u32[]{:S(2)}, u32[]{:S(2)}) collective-permute-start(f32[128,128]{1,0:T(8,128)S(1)} %get-tuple-element.46), channel_id=1, source_target_pairs={{0,8},{8,0},{16,24},{24,16},{32,40},{40,32},{48,56},{56,48},{64,72... | collective-permute-start | bytes 196616 | tf_op jit(solution)/shard_map/ppermute | solution.py:302
  95.1 6.0 %collective-permute-start.13 = (f32[128,128]{1,0:T(8,128)S(1)}, f32[128,128]{1,0:T(8,128)S(1)}, u32[]{:S(2)}, u32[]{:S(2)}) collective-permute-start(f32[128,128]{1,0:T(8,128)S(1)} %add.37), channel_id=1, source_target_pairs={{0,16},{8,24},{16,0},{24,8},{32,48},{40,56},{48,32},{56,40},{64,80... | collective-permute-start | bytes 196616 | tf_op jit(solution)/shard_map/ppermute | solution.py:302
  101.2 11.2 %collective-permute-start.15 = (f32[224,128]{1,0:T(8,128)S(1)}, f32[224,128]{1,0:T(8,128)S(1)}, u32[]{:S(2)}, u32[]{:S(2)}) collective-permute-start(f32[224,128]{1,0:T(8,128)S(1)} %pad_maximum_fusion), channel_id=1, source_target_pairs={{0,64},{8,72},{16,80},{24,88},{32,96},{40,104},{48,112},{56,120},{... | collective-permute-start | bytes 344072 | tf_op jit(solution)/shard_map/ppermute | solution.py:302
  105.2 7.2 %collective-permute-start.14 = (f32[128,128]{1,0:T(8,128)S(1)}, f32[128,128]{1,0:T(8,128)S(1)}, u32[]{:S(2)}, u32[]{:S(2)}) collective-permute-start(f32[128,128]{1,0:T(8,128)S(1)} %add.38), channel_id=1, source_target_pairs={{0,32},{8,40},{16,48},{24,56},{32,0},{40,8},{48,16},{56,24},{64,96... | collective-permute-start | bytes 196616 | tf_op jit(solution)/shard_map/ppermute | solution.py:302
  105.5 7.0 %collective-permute-start.16 = (f32[128,128]{1,0:T(8,128)S(1)}, f32[128,128]{1,0:T(8,128)S(1)}, u32[]{:S(2)}, u32[]{:S(2)}) collective-permute-start(f32[128,128]{1,0:T(8,128)S(1)} %add.38), channel_id=1, source_target_pairs={{0,96},{8,104},{16,112},{24,120},{32,64},{40,72},{48,80},{56,88},{... | collective-permute-start | bytes 196616 | tf_op jit(solution)/shard_map/ppermute | solution.py:302
  112.4 6.5 %collective-permute-start.17 = (f32[128,128]{1,0:T(8,128)S(1)}, f32[128,128]{1,0:T(8,128)S(1)}, u32[]{:S(2)}, u32[]{:S(2)}) collective-permute-start(f32[128,128]{1,0:T(8,128)S(1)} %fusion), channel_id=1, source_target_pairs={{0,192},{8,200},{16,208},{24,216},{32,224},{40,232},{48,240},{56,2... | collective-permute-start | bytes 196616 | tf_op jit(solution)/shard_map/ppermute | solution.py:302
  118.9 1.4 %collective-permute-start.18 = (f32[224,128]{1,0:T(8,128)S(1)}, f32[224,128]{1,0:T(8,128)S(1)}, u32[]{:S(2)}, u32[]{:S(2)}) collective-permute-start(f32[224,128]{1,0:T(8,128)S(1)} %pad_maximum_fusion.1.own_ref), channel_id=1, source_target_pairs={{0,8},{8,0},{16,24},{24,16},{32,40},{40,32},{48,56},{56,48},{64,72... | collective-permute-start | bytes 344072 | tf_op jit(solution)/shard_map/ppermute | solution.py:302

commit v8 on v7

--- a/solution.py
+++ b/solution.py
@@ -40,7 +40,8 @@
     other_ref[...] = whole[pl.ds(pl.multiple_of((1 - core) * half, 8), half), :]
 
 
-def gram_kernel(core_ref, householder_ref, high_ref, low_ref, kept_ref, sent_ref, total, packed):
+def gram_kernel(core_ref, householder_ref, before_ref, high_ref, low_ref, kept_ref, sent_ref, total, packed):
+    del before_ref
     panels, width, columns = householder_ref.shape
     size = panels * width
     step = pl.program_id(0)
@@ -82,8 +83,8 @@
         copy.wait()
 
 
-def even_kernel(place_ref, block_ref, out_ref):
-    del place_ref
+def even_kernel(place_ref, block_ref, before_ref, out_ref):
+    del place_ref, before_ref
     number, _, wide = out_ref.shape
     for i in range(number):
         out_ref[i] = block_ref[:, i * wide : (i + 1) * wide]
@@ -133,6 +134,10 @@
         rounded_ref[:, columns] = high
         both = jnp.concatenate([high, low], axis=0)
         total_ref[...] += product(high_ref[:, columns], both, ((1,), (1,)))
+
+
+def after_kernel(held_ref, before_ref, same_ref):
+    del held_ref, before_ref, same_ref
 
 
 def project_low_kernel(core_ref, total_ref, rounded_ref, low_ref, gram_ref, more_ref, kept_ref, sent_ref, sum_ref, whole):
@@ -185,7 +190,7 @@
     return pltpu.with_memory_space_constraint(value, pltpu.HBM)
 
 
-def gram_call(core, householder):
+def gram_call(core, householder, before):
     panels, width, rows = householder.shape
     size = panels * width
     height = len(pairs_of(panels)) // 2 * width
@@ -198,7 +203,7 @@
             jax.ShapeDtypeStruct((height // 2, 2 * width), jnp.float32),
         ),
         grid=(rows // COLUMNS,),
-        in_specs=[IN_SMEM, pl.BlockSpec((panels, width, COLUMNS), lambda i: (0, 0, i))],
+        in_specs=[IN_SMEM, pl.BlockSpec((panels, width, COLUMNS), lambda i: (0, 0, i)), IN_ANY],
         out_specs=(
             pl.BlockSpec((size, COLUMNS), lambda i: (0, i)),
             pl.BlockSpec((size, COLUMNS), lambda i: (0, i)),
@@ -209,7 +214,7 @@
         compiler_params=pltpu.CompilerParams(vmem_limit_bytes=LIMIT),
         cost_estimate=pl.CostEstimate(flops=10 * 8 * size * size * rows, bytes_accessed=8 * size * rows, transcendentals=0),
         name="gram",
-    )(core, in_hbm(householder))
+    )(core, in_hbm(householder), before)
 
 
 def local_call(kernel, outs, specs, operands, copies=0):
@@ -224,7 +229,7 @@
     )(*operands)
 
 
-def even_call(place, vectors, planes):
+def even_call(place, vectors, before, planes):
     each, length = vectors.shape
     wide = length // planes
     return pl.pallas_call(
@@ -233,12 +238,24 @@
         grid_spec=pltpu.PrefetchScalarGridSpec(
             num_scalar_prefetch=1,
             grid=(planes // 2,),
-            in_specs=[pl.BlockSpec((each, wide), lambda k, place_ref: (0, 2 * k + place_ref[0] % 2))],
+            in_specs=[pl.BlockSpec((each, wide), lambda k, place_ref: (0, 2 * k + place_ref[0] % 2)), IN_ANY],
             out_specs=pl.BlockSpec((4, each, wide // 4), lambda k, place_ref: (k, 0, 0)),
         ),
         compiler_params=pltpu.CompilerParams(vmem_limit_bytes=LIMIT),
         name="even",
-    )(place, in_hbm(vectors))
+    )(place, in_hbm(vectors), before)
+
+
+def after(held, before):
+    return pl.pallas_call(
+        after_kernel,
+        out_shape=pltpu.HBM(held.shape, held.dtype),
+        in_specs=[IN_HBM, IN_ANY],
+        out_specs=IN_HBM,
+        input_output_aliases={0: 0},
+        compiler_params=pltpu.CompilerParams(vmem_limit_bytes=1024 * 1024),
+        name="after",
+    )(in_hbm(held), before)
 
 
 def project_call(core, place, even, odd, high, low, gram, more):
@@ -322,23 +339,21 @@
         block = pltpu.VMEM((each, wide), jnp.float32)
         cut = local_call(cut_kernel, (block,) * len(SHIFTS), [IN_HBM], (place, in_hbm(vectors_in)), len(SHIFTS))
         came = [moved(part, shift) for part, shift in zip(cut, SHIFTS)]
-        even = even_call(place, vectors_in, planes)
+        even = even_call(place, vectors_in, came[0], planes)
         even = lax.all_to_all(even, ("half", "y", "core"), split_axis=0, concat_axis=0, tiled=True)
-        high, low, kept, sent = gram_call(core, householder)
+        high, low, kept, sent = gram_call(core, householder, came[0])
         gram = kept + swap(sent, 1)
         gram = gram + swap(gram, 2)
-        scattered = spread(came[0], came[1], kept) + spread(came[2], came[3], gram)
-        gram = gram + swap(gram, 4)
-        current, value, sent, gram = project_call(core, place, even, scattered, high, low, gram, swap(gram, 24))
+        scattered = spread(came[0], came[1], came[0]) + spread(came[2], came[3], gram)
+        high = after(high, even)
+        current, value, sent, gram = project_call(core, place, even, scattered, high, low, gram, swap(gram, 4))
         value = value + swap(sent, 1)
         value = value + swap(value, 2)
+        half = value.shape[0]
         first, third = swap(value, 4), swap(value, 12)
         second = swap(jnp.concatenate([value, gram], axis=0), 8)
-        half = value.shape[0]
-        value = (value + first) + (second[:half] + third)
-        gram = gram + second[half:]
-        value = value + swap(value, 24)
-        own = jnp.concatenate([value, gram], axis=0)
+        own = jnp.concatenate([(value + first) + (second[:half] + third), gram + second[half:]], axis=0)
+        own = own + swap(own, 24)
         other = swap(own, 1)
         return finish_call(core, own, other, tfactors, current, high, low)
 

time: 126 us -> 119 us (0.944)
  starting transfers between devices: 43.1 us -> 39 us
  waiting for transfers between devices: 46.6 us -> 50.3 us
  local copies, waits for them, and re-layouts: 5.26 us -> 1.91 us
  Pallas kernels: 27.7 us -> 26.2 us
    ppermute x4, waiting for transfers between devices: 2.1 us -> 9.16 us  [moved(): lax.ppermute(part, ('half', 'odd'), [(i, (i + shift) % planes) for i in r...]
    ppermute x15 -> x14, starting transfers between devices: 23.5 us -> 18.5 us  [swap(): return lax.ppermute(value, row, [(i, i ^ flip) for i in range(devices)])]
    ppermute x15 -> x14, waiting for transfers between devices: 44.5 us -> 41.1 us  [swap(): return lax.ppermute(value, row, [(i, i ^ flip) for i in range(devices)])]
    unnamed x18 -> x8, local copies, waits for them, and re-layouts: 5.26 us -> 1.91 us
  transfers between devices with their start and end apart: 20 -> 19, of which waited for: 11 -> 12; matrix products, arithmetic and copies ran while one was open for 1% -> 0% of each run, Pallas kernels for 16% -> 16%
where the time goes in v8:
time: 119 us; the launch traced here: 118 us
  waiting for transfers between devices  50.3 us (42%)
  starting transfers between devices  39 us (33%)
  Pallas kernels  26.2 us (22%)
  local copies, waits for them, and re-layouts  1.91 us (2%)
    ppermute x14, waiting for transfers between devices, swap(): return lax.ppermute(value, row, [(i, i ^ flip) for i in range(devices)])  41.1 us
    ppermute x14, starting transfers between devices, swap(): return lax.ppermute(value, row, [(i, i ^ flip) for i in range(devices)])  18.5 us
    all_to_all x1, starting transfers between devices, shards(): lax.all_to_all(even, ('half', 'y', 'core'), split_axis=0, concat_axis=0,...  10.7 us
    ppermute x4, starting transfers between devices, moved(): lax.ppermute(part, ('half', 'odd'), [(i, (i + shift) % planes) for i in r...  9.85 us
    ppermute x4, waiting for transfers between devices, moved(): lax.ppermute(part, ('half', 'odd'), [(i, (i + shift) % planes) for i in r...  9.16 us
    pallas_call x1, Pallas kernels, gram_call(): pl.pallas_call(gram_kernel, out_shape=(pltpu.HBM((size, rows), jnp.bfloat...  8.78 us
    pallas_call x5, Pallas kernels, local_call(): pl.pallas_call(kernel, out_shape=outs, in_specs=[IN_SMEM] + specs, out_sp...  6.84 us
    pallas_call x1, Pallas kernels, even_call(): pl.pallas_call(even_kernel, out_shape=pltpu.HBM((planes * 2, each, wide /...  4.14 us
  transfers between devices with their start and end apart: 19, of which 12 were waited for; matrix products, arithmetic and copies ran while one was open for 0% of the time, Pallas kernels for 16%

profile of v8, /device:TPU:4, one launch (start us, length us, event | category | flops | bytes accessed | tf_op | source)
XLA Modules:
  0.0 117.9 jit_solution(3064701058502825234)
XLA Ops:
  0.0 0.1 pad_add_fusion.place_ref
  0.1 3.0 %cut_kernel.1 = (f32[4,24576]{1,0:T(4,128)S(1)}, f32[4,24576]{1,0:T(4,128)}, f32[4,24576]{1,0:T(4,128)}, f32[4,24576]{1,0:T(4,128)}) custom-call(s32[3]{0:T(128)S(1)} %pad_add_fusion.place_ref, f32[4,196608]{1,0:T(4,128)} %block_ref.1), custom_call_target="tpu_custom_call" | custom-call | tf_op jit(solution)/shard_map/cut_kernel/pallas_call | solution.py:221
  3.0 2.0 %collective-permute-start = (f32[4,24576]{1,0:T(4,128)S(1)}, f32[4,24576]{1,0:T(4,128)S(1)}, u32[]{:S(2)}, u32[]{:S(2)}) collective-permute-start(f32[4,24576]{1,0:T(4,128)S(1)} %get-tuple-element.27), channel_id=1, source_target_pairs={{0,32},{32,64},{64,96},{96,128},{128,160},{160,192},{192,224},{224... | collective-permute-start | bytes 1179656 | tf_op jit(solution)/shard_map/ppermute | solution.py:330
  5.0 5.8 %collective-permute-start.4 = (f32[4,24576]{1,0:T(4,128)}, f32[4,24576]{1,0:T(4,128)S(1)}, u32[]{:S(2)}, u32[]{:S(2)}) collective-permute-start(f32[4,24576]{1,0:T(4,128)} %get-tuple-element.33), channel_id=1, source_target_pairs={{0,96},{32,128},{64,160},{96,192},{128,224},{160,0},{192,32},{224,... | collective-permute-start | bytes 1179656 | tf_op jit(solution)/shard_map/ppermute | solution.py:330
  10.9 0.0 collective-permute-start.5
  10.9 2.0 %collective-permute-start.1 = (f32[4,24576]{1,0:T(4,128)}, f32[4,24576]{1,0:T(4,128)S(1)}, u32[]{:S(2)}, u32[]{:S(2)}) collective-permute-start(f32[4,24576]{1,0:T(4,128)} %get-tuple-element.28), channel_id=1, source_target_pairs={{0,224},{32,0},{64,32},{96,64},{128,96},{160,128},{192,160},{224,1... | collective-permute-start | bytes 1179656 | tf_op jit(solution)/shard_map/ppermute | solution.py:330
  12.9 6.9 %collective-permute-done.before_ref.up_ref = f32[4,24576]{1,0:T(4,128)S(1)} collective-permute-done((f32[4,24576]{1,0:T(4,128)S(1)}, f32[4,24576]{1,0:T(4,128)S(1)}, u32[]{:S(2)}, u32[]{:S(2)}) %collective-permute-start) | collective-permute-done | bytes 393248 | tf_op jit(solution)/shard_map/ppermute | solution.py:330
  19.7 4.1 %even.1 = f32[16,4,6144]{2,1,0:T(4,128)} custom-call(s32[3]{0:T(128)S(1)} %pad_add_fusion.place_ref, f32[4,196608]{1,0:T(4,128)} %block_ref.1, f32[4,24576]{1,0:T(4,128)S(1)} %collective-permute-done.before_ref.up_ref), custom_call_target="tpu_custom_call" | custom-call | tf_op jit(solution)/shard_map/even/pallas_call | solution.py:235
  23.9 10.7 %all-to-all-start = ((f32[16,4,6144]{2,1,0:T(4,128)}), f32[16,4,6144]{2,1,0:T(4,128)S(1)}, u32[]{:S(2)}, u32[]{:S(2)}) async-start(f32[16,4,6144]{2,1,0:T(4,128)} %even.1), calls=%async_computation | async-start | bytes 3145728 | tf_op jit(solution)/shard_map/all_to_all | solution.py:343
  34.6 8.8 %gram.1 = (bf16[256,6144]{1,0:T(8,128)(2,1)}, bf16[256,6144]{1,0:T(8,128)(2,1)}, f32[96,128]{1,0:T(8,128)S(1)}, f32[96,128]{1,0:T(8,128)S(1)}) custom-call(s32[1]{0:T(128)} %bitcast.core_ref, f32[4,64,6144]{2,1,0:T(8,128)} %householder_ref.1, f32[4,24576]{1,0:T(4,128)S(1)} %collective-permute-done.before_ref.up_ref), custom_call_target="tpu_custom_call" | custom-call | flops 32212254720 | bytes 12582912 | tf_op jit(solution)/shard_map/gram/pallas_call | solution.py:197
  43.3 0.4 collective-permute-start.6
  43.7 0.9 collective-permute-done.6
  44.6 3.4 %collective-permute-start.7 = (f32[96,128]{1,0:T(8,128)S(1)}, f32[96,128]{1,0:T(8,128)S(1)}, u32[]{:S(2)}, u32[]{:S(2)}) collective-permute-start(f32[96,128]{1,0:T(8,128)S(1)} %add.31), channel_id=1, source_target_pairs={{0,16},{8,24},{16,0},{24,8},{32,48},{40,56},{48,32},{56,40},{64,80... | collective-permute-start | bytes 147464 | tf_op jit(solution)/shard_map/ppermute | solution.py:319
  48.1 2.3 %collective-permute-done.1.down_ref = f32[4,24576]{1,0:T(4,128)S(1)} collective-permute-done((f32[4,24576]{1,0:T(4,128)}, f32[4,24576]{1,0:T(4,128)S(1)}, u32[]{:S(2)}, u32[]{:S(2)}) %collective-permute-start.1) | collective-permute-done | bytes 393248 | tf_op jit(solution)/shard_map/ppermute | solution.py:330
  50.4 0.6 side_kernel.2
  51.0 3.3 %collective-permute-start.2 = (f32[2,4,12288]{2,1,0:T(4,128)S(1)}, f32[2,4,12288]{2,1,0:T(4,128)S(1)}, u32[]{:S(2)}, u32[]{:S(2)}) collective-permute-start(f32[2,4,12288]{2,1,0:T(4,128)S(1)} %get-tuple-element.30), channel_id=1, source_target_pairs={{0,16},{8,24},{16,0},{24,8},{32,48},{40,56},{48,32},{56,40},{64,80... | collective-permute-start | bytes 1179656 | tf_op jit(solution)/shard_map/ppermute | solution.py:319
  54.3 0.0 collective-permute-done.7
  54.3 0.0 collective-permute-done.4.up_ref
  54.3 0.0 collective-permute-done.5.down_ref
  54.3 0.6 side_kernel.3
  54.9 0.6 collective-permute-start.8
  55.5 16.1 %collective-permute-done.2.got_ref = f32[2,4,12288]{2,1,0:T(4,128)S(1)} collective-permute-done((f32[2,4,12288]{2,1,0:T(4,128)S(1)}, f32[2,4,12288]{2,1,0:T(4,128)S(1)}, u32[]{:S(2)}, u32[]{:S(2)}) %collective-permute-start.2) | collective-permute-done | bytes 393248 | tf_op jit(solution)/shard_map/ppermute | solution.py:319
  71.6 1.3 %core_kernel.2 = (f32[2,2,4,6144]{3,2,1,0:T(4,128)S(1)}, f32[2,2,4,6144]{3,2,1,0:T(4,128)}) custom-call(s32[3]{0:T(128)S(1)} %pad_add_fusion.place_ref, f32[2,4,12288]{2,1,0:T(4,128)S(1)} %get-tuple-element.29.own_ref, f32[2,4,12288]{2,1,0:T(4,128)S(1)} %collective-permute-done.2.got_ref), custom_call_target="tpu_custom_call" | custom-call | tf_op jit(solution)/shard_map/core_kernel/pallas_call | solution.py:221
  72.9 0.0 collective-permute-start.3
  72.9 6.4 %collective-permute-done.8.got_ref = f32[2,4,12288]{2,1,0:T(4,128)S(1)} collective-permute-done((f32[2,4,12288]{2,1,0:T(4,128)S(1)}, f32[2,4,12288]{2,1,0:T(4,128)S(1)}, u32[]{:S(2)}, u32[]{:S(2)}) %collective-permute-start.8) | collective-permute-done | bytes 393248 | tf_op jit(solution)/shard_map/ppermute | solution.py:319
  79.3 1.4 %core_kernel.3 = (f32[2,2,4,6144]{3,2,1,0:T(4,128)S(1)}, f32[2,2,4,6144]{3,2,1,0:T(4,128)}) custom-call(s32[3]{0:T(128)S(1)} %pad_add_fusion.place_ref, f32[2,4,12288]{2,1,0:T(4,128)S(1)} %get-tuple-element.37.own_ref, f32[2,4,12288]{2,1,0:T(4,128)S(1)} %collective-permute-done.8.got_ref), custom_call_target="tpu_custom_call" | custom-call | tf_op jit(solution)/shard_map/core_kernel/pallas_call | solution.py:221
  80.7 0.0 collective-permute-start.9
  80.7 0.0 collective-permute-start.10
  80.7 0.0 all-to-all-done.before_ref.even_ref
  80.7 0.0 collective-permute-done.3.got_one_ref
  80.7 1.9 %collective-permute-done.9.got_three_ref = f32[2,2,4,6144]{3,2,1,0:T(4,128)S(1)} collective-permute-done((f32[2,2,4,6144]{3,2,1,0:T(4,128)}, f32[2,2,4,6144]{3,2,1,0:T(4,128)S(1)}, u32[]{:S(2)}, u32[]{:S(2)}) %collective-permute-start.9) | collective-permute-done | bytes 393248 | tf_op jit(solution)/shard_map/ppermute | solution.py:319
  82.6 0.0 copy-start
  82.6 1.9 %copy-done = bf16[256,6144]{1,0:T(8,128)(2,1)S(1)} copy-done((bf16[256,6144]{1,0:T(8,128)(2,1)S(1)}, bf16[256,6144]{1,0:T(8,128)(2,1)}, u32[]{:S(2)}) %copy-start) | copy-done | bytes 3145752
  84.5 0.0 copy-start.2
  84.5 2.0 %project_high.1 = (f32[128,6144]{1,0:T(8,128)S(1)}, bf16[128,6144]{1,0:T(8,128)(2,1)S(1)}, f32[256,256]{1,0:T(8,128)S(1)}) custom-call(s32[3]{0:T(128)S(1)} %pad_add_fusion.place_ref, f32[16,4,6144]{2,1,0:T(4,128)S(1)} %all-to-all-done.before_ref.even_ref, f32[2,2,4,6144]{3,2,1,0:T(4,128)S(1)} %get-tuple-element.31.kept_one_ref, ...), custom_call_target="tpu_custom_call" | custom-call | tf_op jit(solution)/shard_map/project_high/pallas_call | solution.py:265
  86.5 0.0 collective-permute-done.10.more_ref
  86.5 0.0 copy-done.2
  86.5 0.0 copy-start.1
  86.5 0.0 copy-start.3
  86.6 1.0 project_low.1
  87.6 0.2 collective-permute-start.11
  87.8 1.1 collective-permute-done.11
  88.9 2.3 %collective-permute-start.12 = (f32[128,128]{1,0:T(8,128)S(1)}, f32[128,128]{1,0:T(8,128)S(1)}, u32[]{:S(2)}, u32[]{:S(2)}) collective-permute-start(f32[128,128]{1,0:T(8,128)S(1)} %add.33), channel_id=1, source_target_pairs={{0,16},{8,24},{16,0},{24,8},{32,48},{40,56},{48,32},{56,40},{64,80... | collective-permute-start | bytes 196616 | tf_op jit(solution)/shard_map/ppermute | solution.py:319
  91.2 3.6 %collective-permute-done.12 = f32[128,128]{1,0:T(8,128)S(1)} collective-permute-done((f32[128,128]{1,0:T(8,128)S(1)}, f32[128,128]{1,0:T(8,128)S(1)}, u32[]{:S(2)}, u32[]{:S(2)}) %collective-permute-start.12) | collective-permute-done | bytes 65568 | tf_op jit(solution)/shard_map/ppermute | solution.py:319
  94.8 4.1 %collective-permute-start.14 = (f32[224,128]{1,0:T(8,128)S(1)}, f32[224,128]{1,0:T(8,128)S(1)}, u32[]{:S(2)}, u32[]{:S(2)}) collective-permute-start(f32[224,128]{1,0:T(8,128)S(1)} %pad_maximum_fusion), channel_id=1, source_target_pairs={{0,64},{8,72},{16,80},{24,88},{32,96},{40,104},{48,112},{56,120},{... | collective-permute-start | bytes 344072 | tf_op jit(solution)/shard_map/ppermute | solution.py:319
  98.9 0.3 collective-permute-start.13
  99.2 1.3 %collective-permute-start.15 = (f32[128,128]{1,0:T(8,128)S(1)}, f32[128,128]{1,0:T(8,128)S(1)}, u32[]{:S(2)}, u32[]{:S(2)}) collective-permute-start(f32[128,128]{1,0:T(8,128)S(1)} %add.34), channel_id=1, source_target_pairs={{0,96},{8,104},{16,112},{24,120},{32,64},{40,72},{48,80},{56,88},{... | collective-permute-start | bytes 196616 | tf_op jit(solution)/shard_map/ppermute | solution.py:319
  100.5 5.1 %collective-permute-done.14 = f32[224,128]{1,0:T(8,128)S(1)} collective-permute-done((f32[224,128]{1,0:T(8,128)S(1)}, f32[224,128]{1,0:T(8,128)S(1)}, u32[]{:S(2)}, u32[]{:S(2)}) %collective-permute-start.14) | collective-permute-done | bytes 114720 | tf_op jit(solution)/shard_map/ppermute | solution.py:319
  105.5 0.2 collective-permute-done.13
  105.8 0.0 collective-permute-done.15
  105.8 2.5 %collective-permute-start.16 = (f32[224,128]{1,0:T(8,128)S(1)}, f32[224,128]{1,0:T(8,128)S(1)}, u32[]{:S(2)}, u32[]{:S(2)}) collective-permute-start(f32[224,128]{1,0:T(8,128)S(1)} %pad_maximum_fusion.1), channel_id=1, source_target_pairs={{0,192},{8,200},{16,208},{24,216},{32,224},{40,232},{48,240},{56,2... | collective-permute-start | bytes 344072 | tf_op jit(solution)/shard_map/ppermute | solution.py:319
  108.3 4.6 %collective-permute-done.16 = f32[224,128]{1,0:T(8,128)S(1)} collective-permute-done((f32[224,128]{1,0:T(8,128)S(1)}, f32[224,128]{1,0:T(8,128)S(1)}, u32[]{:S(2)}, u32[]{:S(2)}) %collective-permute-start.16) | collective-permute-done | bytes 114720 | tf_op jit(solution)/shard_map/ppermute | solution.py:319
  112.9 0.1 collective-permute-start.17
  113.0 1.3 %collective-permute-done.17.other_ref = f32[224,128]{1,0:T(8,128)S(1)} collective-permute-done((f32[224,128]{1,0:T(8,128)S(1)}, f32[224,128]{1,0:T(8,128)S(1)}, u32[]{:S(2)}, u32[]{:S(2)}) %collective-permute-start.17) | collective-permute-done | bytes 114720 | tf_op jit(solution)/shard_map/ppermute | solution.py:319
  114.3 0.0 copy-done.1
  114.3 0.0 copy-done.3
  114.3 3.4 %finish.1 = f32[128,6144]{1,0:T(8,128)} custom-call(s32[1]{0:T(128)} %bitcast.core_ref, f32[224,128]{1,0:T(8,128)S(1)} %fusion.1.own_ref, f32[224,128]{1,0:T(8,128)S(1)} %collective-permute-done.17.other_ref, f32[4,64,64]{2,1,0:T(8,128)S(1)} %copy-done.3, f32[128,6144]{1,0:T(8,128)S(1)} %get-tuple-element.48.current_ref, bf16[256,6144]{1,0:T(8,128)(2,1)S(1)} %copy-done.1, ...), custom_call_target="tpu_custom_call" | custom-call | tf_op jit(solution)/shard_map/finish/pallas_call | solution.py:296
  (10 shorter events, 0.1 us)
Async XLA Ops:
  3.0 16.7 %collective-permute-start = (f32[4,24576]{1,0:T(4,128)S(1)}, f32[4,24576]{1,0:T(4,128)S(1)}, u32[]{:S(2)}, u32[]{:S(2)}) collective-permute-start(f32[4,24576]{1,0:T(4,128)S(1)} %get-tuple-element.27), channel_id=1, source_target_pairs={{0,32},{32,64},{64,96},{96,128},{128,160},{160,192},{192,224},{224... | collective-permute-start | bytes 1179656 | tf_op jit(solution)/shard_map/ppermute | solution.py:330
  5.0 49.2 %collective-permute-start.4 = (f32[4,24576]{1,0:T(4,128)}, f32[4,24576]{1,0:T(4,128)S(1)}, u32[]{:S(2)}, u32[]{:S(2)}) collective-permute-start(f32[4,24576]{1,0:T(4,128)} %get-tuple-element.33), channel_id=1, source_target_pairs={{0,96},{32,128},{64,160},{96,192},{128,224},{160,0},{192,32},{224,... | collective-permute-start | bytes 1179656 | tf_op jit(solution)/shard_map/ppermute | solution.py:330
  10.9 43.4 %collective-permute-start.5 = (f32[4,24576]{1,0:T(4,128)}, f32[4,24576]{1,0:T(4,128)S(1)}, u32[]{:S(2)}, u32[]{:S(2)}) collective-permute-start(f32[4,24576]{1,0:T(4,128)} %get-tuple-element.34), channel_id=1, source_target_pairs={{0,160},{32,192},{64,224},{96,0},{128,32},{160,64},{192,96},{224,1... | collective-permute-start | bytes 1179656 | tf_op jit(solution)/shard_map/ppermute | solution.py:330
  10.9 39.5 %collective-permute-start.1 = (f32[4,24576]{1,0:T(4,128)}, f32[4,24576]{1,0:T(4,128)S(1)}, u32[]{:S(2)}, u32[]{:S(2)}) collective-permute-start(f32[4,24576]{1,0:T(4,128)} %get-tuple-element.28), channel_id=1, source_target_pairs={{0,224},{32,0},{64,32},{96,64},{128,96},{160,128},{192,160},{224,1... | collective-permute-start | bytes 1179656 | tf_op jit(solution)/shard_map/ppermute | solution.py:330
  23.9 56.8 %all-to-all-start = ((f32[16,4,6144]{2,1,0:T(4,128)}), f32[16,4,6144]{2,1,0:T(4,128)S(1)}, u32[]{:S(2)}, u32[]{:S(2)}) async-start(f32[16,4,6144]{2,1,0:T(4,128)} %even.1), calls=%async_computation | async-start | bytes 3145728 | tf_op jit(solution)/shard_map/all_to_all | solution.py:343
  43.3 1.3 %collective-permute-start.6 = (f32[96,128]{1,0:T(8,128)S(1)}, f32[96,128]{1,0:T(8,128)S(1)}, u32[]{:S(2)}, u32[]{:S(2)}) collective-permute-start(f32[96,128]{1,0:T(8,128)S(1)} %get-tuple-element.36), channel_id=1, source_target_pairs={{0,8},{8,0},{16,24},{24,16},{32,40},{40,32},{48,56},{56,48},{64,72... | collective-permute-start | bytes 147464 | tf_op jit(solution)/shard_map/ppermute | solution.py:319
  44.6 9.6 %collective-permute-start.7 = (f32[96,128]{1,0:T(8,128)S(1)}, f32[96,128]{1,0:T(8,128)S(1)}, u32[]{:S(2)}, u32[]{:S(2)}) collective-permute-start(f32[96,128]{1,0:T(8,128)S(1)} %add.31), channel_id=1, source_target_pairs={{0,16},{8,24},{16,0},{24,8},{32,48},{40,56},{48,32},{56,40},{64,80... | collective-permute-start | bytes 147464 | tf_op jit(solution)/shard_map/ppermute | solution.py:319
  51.0 20.6 %collective-permute-start.2 = (f32[2,4,12288]{2,1,0:T(4,128)S(1)}, f32[2,4,12288]{2,1,0:T(4,128)S(1)}, u32[]{:S(2)}, u32[]{:S(2)}) collective-permute-start(f32[2,4,12288]{2,1,0:T(4,128)S(1)} %get-tuple-element.30), channel_id=1, source_target_pairs={{0,16},{8,24},{16,0},{24,8},{32,48},{40,56},{48,32},{56,40},{64,80... | collective-permute-start | bytes 1179656 | tf_op jit(solution)/shard_map/ppermute | solution.py:319
  54.9 24.4 %collective-permute-start.8 = (f32[2,4,12288]{2,1,0:T(4,128)S(1)}, f32[2,4,12288]{2,1,0:T(4,128)S(1)}, u32[]{:S(2)}, u32[]{:S(2)}) collective-permute-start(f32[2,4,12288]{2,1,0:T(4,128)S(1)} %get-tuple-element.38), channel_id=1, source_target_pairs={{0,16},{8,24},{16,0},{24,8},{32,48},{40,56},{48,32},{56,40},{64,80... | collective-permute-start | bytes 1179656 | tf_op jit(solution)/shard_map/ppermute | solution.py:319
  72.9 7.7 %collective-permute-start.3 = (f32[2,2,4,6144]{3,2,1,0:T(4,128)}, f32[2,2,4,6144]{3,2,1,0:T(4,128)S(1)}, u32[]{:S(2)}, u32[]{:S(2)}) collective-permute-start(f32[2,2,4,6144]{3,2,1,0:T(4,128)} %get-tuple-element.32), channel_id=1, source_target_pairs={{0,8},{8,0},{16,24},{24,16},{32,40},{40,32},{48,56},{56,48},{64,72... | collective-permute-start | bytes 1179656 | tf_op jit(solution)/shard_map/ppermute | solution.py:319
  80.7 1.9 %collective-permute-start.9 = (f32[2,2,4,6144]{3,2,1,0:T(4,128)}, f32[2,2,4,6144]{3,2,1,0:T(4,128)S(1)}, u32[]{:S(2)}, u32[]{:S(2)}) collective-permute-start(f32[2,2,4,6144]{3,2,1,0:T(4,128)} %get-tuple-element.40), channel_id=1, source_target_pairs={{0,8},{8,0},{16,24},{24,16},{32,40},{40,32},{48,56},{56,48},{64,72... | collective-permute-start | bytes 1179656 | tf_op jit(solution)/shard_map/ppermute | solution.py:319
  80.7 5.9 %collective-permute-start.10 = (f32[96,128]{1,0:T(8,128)S(1)}, f32[96,128]{1,0:T(8,128)S(1)}, u32[]{:S(2)}, u32[]{:S(2)}) collective-permute-start(f32[96,128]{1,0:T(8,128)S(1)} %add.32.before_ref.gram_ref), channel_id=1, source_target_pairs={{0,32},{8,40},{16,48},{24,56},{32,0},{40,8},{48,16},{56,24},{64,96... | collective-permute-start | bytes 147464 | tf_op jit(solution)/shard_map/ppermute | solution.py:319
  82.6 1.9 %copy-start = (bf16[256,6144]{1,0:T(8,128)(2,1)S(1)}, bf16[256,6144]{1,0:T(8,128)(2,1)}, u32[]{:S(2)}) copy-start(bf16[256,6144]{1,0:T(8,128)(2,1)} %after.1.high_ref) | copy-start | bytes 9437188
  84.5 2.0 %copy-start.2 = (bf16[256,6144]{1,0:T(8,128)(2,1)S(1)}, bf16[256,6144]{1,0:T(8,128)(2,1)}, u32[]{:S(2)}) copy-start(bf16[256,6144]{1,0:T(8,128)(2,1)} %get-tuple-element.44.low_ref) | copy-start | bytes 9437188
  86.5 27.8 %copy-start.1 = (bf16[256,6144]{1,0:T(8,128)(2,1)S(1)}, bf16[256,6144]{1,0:T(8,128)(2,1)}, u32[]{:S(2)}) copy-start(bf16[256,6144]{1,0:T(8,128)(2,1)} %after.1.high_ref) | copy-start | bytes 9437188
  86.5 27.8 %copy-start.3 = (f32[4,64,64]{2,1,0:T(8,128)S(1)}, f32[4,64,64]{2,1,0:T(8,128)}, u32[]{:S(2)}) copy-start(f32[4,64,64]{2,1,0:T(8,128)} %tfactors_ref.1) | copy-start | bytes 196612
  87.6 1.3 %collective-permute-start.11 = (f32[128,128]{1,0:T(8,128)S(1)}, f32[128,128]{1,0:T(8,128)S(1)}, u32[]{:S(2)}, u32[]{:S(2)}) collective-permute-start(f32[128,128]{1,0:T(8,128)S(1)} %get-tuple-element.46), channel_id=1, source_target_pairs={{0,8},{8,0},{16,24},{24,16},{32,40},{40,32},{48,56},{56,48},{64,72... | collective-permute-start | bytes 196616 | tf_op jit(solution)/shard_map/ppermute | solution.py:319
  88.9 5.9 %collective-permute-start.12 = (f32[128,128]{1,0:T(8,128)S(1)}, f32[128,128]{1,0:T(8,128)S(1)}, u32[]{:S(2)}, u32[]{:S(2)}) collective-permute-start(f32[128,128]{1,0:T(8,128)S(1)} %add.33), channel_id=1, source_target_pairs={{0,16},{8,24},{16,0},{24,8},{32,48},{40,56},{48,32},{56,40},{64,80... | collective-permute-start | bytes 196616 | tf_op jit(solution)/shard_map/ppermute | solution.py:319
  94.8 10.7 %collective-permute-start.14 = (f32[224,128]{1,0:T(8,128)S(1)}, f32[224,128]{1,0:T(8,128)S(1)}, u32[]{:S(2)}, u32[]{:S(2)}) collective-permute-start(f32[224,128]{1,0:T(8,128)S(1)} %pad_maximum_fusion), channel_id=1, source_target_pairs={{0,64},{8,72},{16,80},{24,88},{32,96},{40,104},{48,112},{56,120},{... | collective-permute-start | bytes 344072 | tf_op jit(solution)/shard_map/ppermute | solution.py:319
  98.9 6.9 %collective-permute-start.13 = (f32[128,128]{1,0:T(8,128)S(1)}, f32[128,128]{1,0:T(8,128)S(1)}, u32[]{:S(2)}, u32[]{:S(2)}) collective-permute-start(f32[128,128]{1,0:T(8,128)S(1)} %add.34), channel_id=1, source_target_pairs={{0,32},{8,40},{16,48},{24,56},{32,0},{40,8},{48,16},{56,24},{64,96... | collective-permute-start | bytes 196616 | tf_op jit(solution)/shard_map/ppermute | solution.py:319
  99.2 6.6 %collective-permute-start.15 = (f32[128,128]{1,0:T(8,128)S(1)}, f32[128,128]{1,0:T(8,128)S(1)}, u32[]{:S(2)}, u32[]{:S(2)}) collective-permute-start(f32[128,128]{1,0:T(8,128)S(1)} %add.34), channel_id=1, source_target_pairs={{0,96},{8,104},{16,112},{24,120},{32,64},{40,72},{48,80},{56,88},{... | collective-permute-start | bytes 196616 | tf_op jit(solution)/shard_map/ppermute | solution.py:319
  105.8 7.1 %collective-permute-start.16 = (f32[224,128]{1,0:T(8,128)S(1)}, f32[224,128]{1,0:T(8,128)S(1)}, u32[]{:S(2)}, u32[]{:S(2)}) collective-permute-start(f32[224,128]{1,0:T(8,128)S(1)} %pad_maximum_fusion.1), channel_id=1, source_target_pairs={{0,192},{8,200},{16,208},{24,216},{32,224},{40,232},{48,240},{56,2... | collective-permute-start | bytes 344072 | tf_op jit(solution)/shard_map/ppermute | solution.py:319
  112.9 1.4 %collective-permute-start.17 = (f32[224,128]{1,0:T(8,128)S(1)}, f32[224,128]{1,0:T(8,128)S(1)}, u32[]{:S(2)}, u32[]{:S(2)}) collective-permute-start(f32[224,128]{1,0:T(8,128)S(1)} %fusion.1.own_ref), channel_id=1, source_target_pairs={{0,8},{8,0},{16,24},{24,16},{32,40},{40,32},{48,56},{56,48},{64,72... | collective-permute-start | bytes 344072 | tf_op jit(solution)/shard_map/ppermute | solution.py:319

commit v9 on v8

--- a/solution.py
+++ b/solution.py
@@ -329,22 +329,28 @@
         def moved(part, shift):
             return lax.ppermute(part, ("half", "odd"), [(i, (i + shift) % planes) for i in range(planes)])
 
-        def spread(up, down, before):
+        def sides(up, down, before):
             block = pltpu.VMEM((2, each, wide // 2), jnp.float32)
-            kept, sent = local_call(side_kernel, (block, block), [IN_VMEM, IN_VMEM, IN_ANY], (place, up, down, before))
+            return local_call(side_kernel, (block, block), [IN_VMEM, IN_VMEM, IN_ANY], (place, up, down, before))
+
+        def spread(kept, got):
             block = pltpu.VMEM((2, 2, each, wide // 4), jnp.float32)
-            kept, sent = local_call(core_kernel, (block, block), [IN_VMEM, IN_VMEM], (place, kept, swap(sent, 2)))
+            kept, sent = local_call(core_kernel, (block, block), [IN_VMEM, IN_VMEM], (place, kept, got))
             return kept, swap(sent, 1)
 
         block = pltpu.VMEM((each, wide), jnp.float32)
         cut = local_call(cut_kernel, (block,) * len(SHIFTS), [IN_HBM], (place, in_hbm(vectors_in)), len(SHIFTS))
         came = [moved(part, shift) for part, shift in zip(cut, SHIFTS)]
-        even = even_call(place, vectors_in, came[0], planes)
-        even = lax.all_to_all(even, ("half", "y", "core"), split_axis=0, concat_axis=0, tiled=True)
+        packed = even_call(place, vectors_in, came[0], planes)
+        even = lax.all_to_all(packed, ("half", "y", "core"), split_axis=0, concat_axis=0, tiled=True)
+        one_kept, one_sent = sides(came[0], came[1], came[0])
+        one_got = swap(one_sent, 2)
         high, low, kept, sent = gram_call(core, householder, came[0])
         gram = kept + swap(sent, 1)
         gram = gram + swap(gram, 2)
-        scattered = spread(came[0], came[1], came[0]) + spread(came[2], came[3], gram)
+        three_kept, three_sent = sides(came[2], came[3], kept)
+        three_got = swap(three_sent, 2)
+        scattered = spread(one_kept, one_got) + spread(three_kept, three_got)
         high = after(high, even)
         current, value, sent, gram = project_call(core, place, even, scattered, high, low, gram, swap(gram, 4))
         value = value + swap(sent, 1)

time: 119 us -> 129 us (1.084)
  waiting for transfers between devices: 50.3 us -> 55.2 us
  starting transfers between devices: 39 us -> 43.3 us
    ppermute x4, waiting for transfers between devices: 9.16 us -> 23 us  [moved(): lax.ppermute(part, ('half', 'odd'), [(i, (i + shift) % planes) for i in r...]
    ppermute x14, waiting for transfers between devices: 41.1 us -> 32.2 us  [swap(): return lax.ppermute(value, row, [(i, i ^ flip) for i in range(devices)])]
    ppermute x14, starting transfers between devices: 18.5 us -> 24.6 us  [swap(): return lax.ppermute(value, row, [(i, i ^ flip) for i in range(devices)])]
    all_to_all x1, starting transfers between devices: 10.7 us -> 7.66 us  [shards(): lax.all_to_all(packed, ('half', 'y', 'core'), split_axis=0, concat_axis=0...]
  transfers between devices with their start and end apart: 19 -> 19, of which waited for: 12 -> 13; matrix products, arithmetic and copies ran while one was open for 0% -> 0% of each run, Pallas kernels for 16% -> 15%
where the time goes in v9:
time: 129 us; the launch traced here: 128 us
  waiting for transfers between devices  55.2 us (43%)
  starting transfers between devices  43.3 us (34%)
  Pallas kernels  26.8 us (21%)
  local copies, waits for them, and re-layouts  1.9 us (1%)
    ppermute x14, waiting for transfers between devices, swap(): return lax.ppermute(value, row, [(i, i ^ flip) for i in range(devices)])  32.2 us
    ppermute x14, starting transfers between devices, swap(): return lax.ppermute(value, row, [(i, i ^ flip) for i in range(devices)])  24.6 us
    ppermute x4, waiting for transfers between devices, moved(): lax.ppermute(part, ('half', 'odd'), [(i, (i + shift) % planes) for i in r...  23 us
    ppermute x4, starting transfers between devices, moved(): lax.ppermute(part, ('half', 'odd'), [(i, (i + shift) % planes) for i in r...  11.1 us
    pallas_call x1, Pallas kernels, gram_call(): pl.pallas_call(gram_kernel, out_shape=(pltpu.HBM((size, rows), jnp.bfloat...  8.78 us
    all_to_all x1, starting transfers between devices, shards(): lax.all_to_all(packed, ('half', 'y', 'core'), split_axis=0, concat_axis=0...  7.66 us
    pallas_call x5, Pallas kernels, local_call(): pl.pallas_call(kernel, out_shape=outs, in_specs=[IN_SMEM] + specs, out_sp...  7.49 us
    pallas_call x1, Pallas kernels, even_call(): pl.pallas_call(even_kernel, out_shape=pltpu.HBM((planes * 2, each, wide /...  4.14 us
  transfers between devices with their start and end apart: 19, of which 13 were waited for; matrix products, arithmetic and copies ran while one was open for 0% of the time, Pallas kernels for 15%

profile of v9, /device:TPU:4, one launch (start us, length us, event | category | flops | bytes accessed | tf_op | source)
XLA Modules:
  0.0 127.7 jit_solution(1955046692635409126)
XLA Ops:
  0.0 0.1 pad_add_fusion.place_ref
  0.1 2.8 %cut_kernel.1 = (f32[4,24576]{1,0:T(4,128)S(1)}, f32[4,24576]{1,0:T(4,128)S(1)}, f32[4,24576]{1,0:T(4,128)}, f32[4,24576]{1,0:T(4,128)}) custom-call(s32[3]{0:T(128)S(1)} %pad_add_fusion.place_ref, f32[4,196608]{1,0:T(4,128)} %block_ref.1), custom_call_target="tpu_custom_call" | custom-call | tf_op jit(solution)/shard_map/cut_kernel/pallas_call | solution.py:221
  2.9 2.0 %collective-permute-start = (f32[4,24576]{1,0:T(4,128)S(1)}, f32[4,24576]{1,0:T(4,128)S(1)}, u32[]{:S(2)}, u32[]{:S(2)}) collective-permute-start(f32[4,24576]{1,0:T(4,128)S(1)} %get-tuple-element.27), channel_id=1, source_target_pairs={{0,32},{32,64},{64,96},{96,128},{128,160},{160,192},{192,224},{224... | collective-permute-start | bytes 1179656 | tf_op jit(solution)/shard_map/ppermute | solution.py:330
  4.9 4.0 %collective-permute-start.1 = (f32[4,24576]{1,0:T(4,128)S(1)}, f32[4,24576]{1,0:T(4,128)S(1)}, u32[]{:S(2)}, u32[]{:S(2)}) collective-permute-start(f32[4,24576]{1,0:T(4,128)S(1)} %get-tuple-element.28), channel_id=1, source_target_pairs={{0,224},{32,0},{64,32},{96,64},{128,96},{160,128},{192,160},{224,1... | collective-permute-start | bytes 1179656 | tf_op jit(solution)/shard_map/ppermute | solution.py:330
  9.0 1.8 %collective-permute-start.4 = (f32[4,24576]{1,0:T(4,128)}, f32[4,24576]{1,0:T(4,128)S(1)}, u32[]{:S(2)}, u32[]{:S(2)}) collective-permute-start(f32[4,24576]{1,0:T(4,128)} %get-tuple-element.33), channel_id=1, source_target_pairs={{0,96},{32,128},{64,160},{96,192},{128,224},{160,0},{192,32},{224,... | collective-permute-start | bytes 1179656 | tf_op jit(solution)/shard_map/ppermute | solution.py:330
  10.8 3.2 %collective-permute-start.5 = (f32[4,24576]{1,0:T(4,128)}, f32[4,24576]{1,0:T(4,128)S(1)}, u32[]{:S(2)}, u32[]{:S(2)}) collective-permute-start(f32[4,24576]{1,0:T(4,128)} %get-tuple-element.34), channel_id=1, source_target_pairs={{0,160},{32,192},{64,224},{96,0},{128,32},{160,64},{192,96},{224,1... | collective-permute-start | bytes 1179656 | tf_op jit(solution)/shard_map/ppermute | solution.py:330
  14.0 5.7 %collective-permute-done.before_ref.up_ref = f32[4,24576]{1,0:T(4,128)S(1)} collective-permute-done((f32[4,24576]{1,0:T(4,128)S(1)}, f32[4,24576]{1,0:T(4,128)S(1)}, u32[]{:S(2)}, u32[]{:S(2)}) %collective-permute-start) | collective-permute-done | bytes 393248 | tf_op jit(solution)/shard_map/ppermute | solution.py:330
  19.6 4.3 %collective-permute-done.1.down_ref = f32[4,24576]{1,0:T(4,128)S(1)} collective-permute-done((f32[4,24576]{1,0:T(4,128)S(1)}, f32[4,24576]{1,0:T(4,128)S(1)}, u32[]{:S(2)}, u32[]{:S(2)}) %collective-permute-start.1) | collective-permute-done | bytes 393248 | tf_op jit(solution)/shard_map/ppermute | solution.py:330
  24.0 1.3 %side_kernel.2 = (f32[2,4,12288]{2,1,0:T(4,128)S(1)}, f32[2,4,12288]{2,1,0:T(4,128)}) custom-call(s32[3]{0:T(128)S(1)} %pad_add_fusion.place_ref, f32[4,24576]{1,0:T(4,128)S(1)} %collective-permute-done.before_ref.up_ref, f32[4,24576]{1,0:T(4,128)S(1)} %collective-permute-done.1.down_ref, f32[4,24576]{1,0:T(4,128)S(1)} %collective-permute-done.before_ref.up_ref), custom_call_target="tpu_custom_call" | custom-call | tf_op jit(solution)/shard_map/side_kernel/pallas_call | solution.py:221
  25.3 3.2 %collective-permute-start.2 = (f32[2,4,12288]{2,1,0:T(4,128)}, f32[2,4,12288]{2,1,0:T(4,128)S(1)}, u32[]{:S(2)}, u32[]{:S(2)}) collective-permute-start(f32[2,4,12288]{2,1,0:T(4,128)} %get-tuple-element.30), channel_id=1, source_target_pairs={{0,16},{8,24},{16,0},{24,8},{32,48},{40,56},{48,32},{56,40},{64,80... | collective-permute-start | bytes 1179656 | tf_op jit(solution)/shard_map/ppermute | solution.py:319
  28.5 4.1 %even.1 = f32[16,4,6144]{2,1,0:T(4,128)} custom-call(s32[3]{0:T(128)S(1)} %pad_add_fusion.place_ref, f32[4,196608]{1,0:T(4,128)} %block_ref.1, f32[4,24576]{1,0:T(4,128)S(1)} %collective-permute-done.before_ref.up_ref), custom_call_target="tpu_custom_call" | custom-call | tf_op jit(solution)/shard_map/even/pallas_call | solution.py:235
  32.7 7.7 %all-to-all-start = ((f32[16,4,6144]{2,1,0:T(4,128)}), f32[16,4,6144]{2,1,0:T(4,128)S(1)}, u32[]{:S(2)}, u32[]{:S(2)}) async-start(f32[16,4,6144]{2,1,0:T(4,128)} %even.1), calls=%async_computation | async-start | bytes 3145728 | tf_op jit(solution)/shard_map/all_to_all | solution.py:345
  40.3 8.8 %gram.1 = (bf16[256,6144]{1,0:T(8,128)(2,1)}, bf16[256,6144]{1,0:T(8,128)(2,1)}, f32[96,128]{1,0:T(8,128)S(1)}, f32[96,128]{1,0:T(8,128)S(1)}) custom-call(s32[1]{0:T(128)} %bitcast.core_ref, f32[4,64,6144]{2,1,0:T(8,128)} %householder_ref.1, f32[4,24576]{1,0:T(4,128)S(1)} %collective-permute-done.before_ref.up_ref), custom_call_target="tpu_custom_call" | custom-call | flops 32212254720 | bytes 12582912 | tf_op jit(solution)/shard_map/gram/pallas_call | solution.py:197
  49.1 0.0 collective-permute-done.4.up_ref
  49.1 13.0 %collective-permute-done.5.down_ref = f32[4,24576]{1,0:T(4,128)S(1)} collective-permute-done((f32[4,24576]{1,0:T(4,128)}, f32[4,24576]{1,0:T(4,128)S(1)}, u32[]{:S(2)}, u32[]{:S(2)}) %collective-permute-start.5) | collective-permute-done | bytes 393248 | tf_op jit(solution)/shard_map/ppermute | solution.py:330
  62.2 0.6 side_kernel.3
  62.8 10.1 %collective-permute-start.6 = (f32[2,4,12288]{2,1,0:T(4,128)S(1)}, f32[2,4,12288]{2,1,0:T(4,128)S(1)}, u32[]{:S(2)}, u32[]{:S(2)}) collective-permute-start(f32[2,4,12288]{2,1,0:T(4,128)S(1)} %get-tuple-element.37), channel_id=1, source_target_pairs={{0,16},{8,24},{16,0},{24,8},{32,48},{40,56},{48,32},{56,40},{64,80... | collective-permute-start | bytes 1179656 | tf_op jit(solution)/shard_map/ppermute | solution.py:319
  72.9 0.0 collective-permute-done.2.got_ref
  72.9 1.3 %core_kernel.2 = (f32[2,2,4,6144]{3,2,1,0:T(4,128)S(1)}, f32[2,2,4,6144]{3,2,1,0:T(4,128)}) custom-call(s32[3]{0:T(128)S(1)} %pad_add_fusion.place_ref, f32[2,4,12288]{2,1,0:T(4,128)S(1)} %get-tuple-element.29.own_ref, f32[2,4,12288]{2,1,0:T(4,128)S(1)} %collective-permute-done.2.got_ref), custom_call_target="tpu_custom_call" | custom-call | tf_op jit(solution)/shard_map/core_kernel/pallas_call | solution.py:221
  74.2 0.0 collective-permute-start.3
  74.2 10.2 %collective-permute-done.6.got_ref = f32[2,4,12288]{2,1,0:T(4,128)S(1)} collective-permute-done((f32[2,4,12288]{2,1,0:T(4,128)S(1)}, f32[2,4,12288]{2,1,0:T(4,128)S(1)}, u32[]{:S(2)}, u32[]{:S(2)}) %collective-permute-start.6) | collective-permute-done | bytes 393248 | tf_op jit(solution)/shard_map/ppermute | solution.py:319
  84.4 1.4 %core_kernel.3 = (f32[2,2,4,6144]{3,2,1,0:T(4,128)S(1)}, f32[2,2,4,6144]{3,2,1,0:T(4,128)}) custom-call(s32[3]{0:T(128)S(1)} %pad_add_fusion.place_ref, f32[2,4,12288]{2,1,0:T(4,128)S(1)} %get-tuple-element.36.own_ref, f32[2,4,12288]{2,1,0:T(4,128)S(1)} %collective-permute-done.6.got_ref), custom_call_target="tpu_custom_call" | custom-call | tf_op jit(solution)/shard_map/core_kernel/pallas_call | solution.py:221
  85.8 0.0 collective-permute-start.7
  85.8 0.5 collective-permute-start.8
  86.3 0.9 collective-permute-done.8
  87.2 2.0 %collective-permute-start.9 = (f32[96,128]{1,0:T(8,128)S(1)}, f32[96,128]{1,0:T(8,128)S(1)}, u32[]{:S(2)}, u32[]{:S(2)}) collective-permute-start(f32[96,128]{1,0:T(8,128)S(1)} %add.31), channel_id=1, source_target_pairs={{0,16},{8,24},{16,0},{24,8},{32,48},{40,56},{48,32},{56,40},{64,80... | collective-permute-start | bytes 147464 | tf_op jit(solution)/shard_map/ppermute | solution.py:319
  89.2 3.6 %collective-permute-done.9 = f32[96,128]{1,0:T(8,128)S(1)} collective-permute-done((f32[96,128]{1,0:T(8,128)S(1)}, f32[96,128]{1,0:T(8,128)S(1)}, u32[]{:S(2)}, u32[]{:S(2)}) %collective-permute-start.9) | collective-permute-done | bytes 49184 | tf_op jit(solution)/shard_map/ppermute | solution.py:319
  92.8 0.1 collective-permute-start.10
  92.9 0.0 all-to-all-done.before_ref.even_ref
  92.9 0.0 collective-permute-done.3.got_one_ref
  93.0 0.0 collective-permute-done.7.got_three_ref
  93.0 0.0 copy-start
  93.0 1.9 %copy-done = bf16[256,6144]{1,0:T(8,128)(2,1)S(1)} copy-done((bf16[256,6144]{1,0:T(8,128)(2,1)S(1)}, bf16[256,6144]{1,0:T(8,128)(2,1)}, u32[]{:S(2)}) %copy-start) | copy-done | bytes 3145752
  94.9 0.0 copy-start.2
  94.9 2.0 %project_high.1 = (f32[128,6144]{1,0:T(8,128)S(1)}, bf16[128,6144]{1,0:T(8,128)(2,1)S(1)}, f32[256,256]{1,0:T(8,128)S(1)}) custom-call(s32[3]{0:T(128)S(1)} %pad_add_fusion.place_ref, f32[16,4,6144]{2,1,0:T(4,128)S(1)} %all-to-all-done.before_ref.even_ref, f32[2,2,4,6144]{3,2,1,0:T(4,128)S(1)} %get-tuple-element.31.kept_one_ref, ...), custom_call_target="tpu_custom_call" | custom-call | tf_op jit(solution)/shard_map/project_high/pallas_call | solution.py:265
  96.9 0.1 collective-permute-done.10.more_ref
  97.0 0.0 copy-done.2
  97.0 0.0 copy-start.1
  97.0 0.0 copy-start.3
  97.0 1.0 project_low.1
  98.0 0.1 collective-permute-start.11
  98.1 1.2 collective-permute-done.11
  99.4 2.5 %collective-permute-start.12 = (f32[128,128]{1,0:T(8,128)S(1)}, f32[128,128]{1,0:T(8,128)S(1)}, u32[]{:S(2)}, u32[]{:S(2)}) collective-permute-start(f32[128,128]{1,0:T(8,128)S(1)} %add.33), channel_id=1, source_target_pairs={{0,16},{8,24},{16,0},{24,8},{32,48},{40,56},{48,32},{56,40},{64,80... | collective-permute-start | bytes 196616 | tf_op jit(solution)/shard_map/ppermute | solution.py:319
  101.9 3.4 %collective-permute-done.12 = f32[128,128]{1,0:T(8,128)S(1)} collective-permute-done((f32[128,128]{1,0:T(8,128)S(1)}, f32[128,128]{1,0:T(8,128)S(1)}, u32[]{:S(2)}, u32[]{:S(2)}) %collective-permute-start.12) | collective-permute-done | bytes 65568 | tf_op jit(solution)/shard_map/ppermute | solution.py:319
  105.2 0.3 collective-permute-start.14
  105.5 4.3 %collective-permute-start.15 = (f32[128,128]{1,0:T(8,128)S(1)}, f32[128,128]{1,0:T(8,128)S(1)}, u32[]{:S(2)}, u32[]{:S(2)}) collective-permute-start(f32[128,128]{1,0:T(8,128)S(1)} %add.34), channel_id=1, source_target_pairs={{0,96},{8,104},{16,112},{24,120},{32,64},{40,72},{48,80},{56,88},{... | collective-permute-start | bytes 196616 | tf_op jit(solution)/shard_map/ppermute | solution.py:319
  109.8 0.0 collective-permute-start.13
  109.8 5.3 %collective-permute-done.14 = f32[224,128]{1,0:T(8,128)S(1)} collective-permute-done((f32[224,128]{1,0:T(8,128)S(1)}, f32[224,128]{1,0:T(8,128)S(1)}, u32[]{:S(2)}, u32[]{:S(2)}) %collective-permute-start.14) | collective-permute-done | bytes 114720 | tf_op jit(solution)/shard_map/ppermute | solution.py:319
  115.1 0.0 collective-permute-done.15
  115.1 0.5 collective-permute-done.13
  115.7 1.4 %collective-permute-start.16 = (f32[224,128]{1,0:T(8,128)S(1)}, f32[224,128]{1,0:T(8,128)S(1)}, u32[]{:S(2)}, u32[]{:S(2)}) collective-permute-start(f32[224,128]{1,0:T(8,128)S(1)} %pad_maximum_fusion.1), channel_id=1, source_target_pairs={{0,192},{8,200},{16,208},{24,216},{32,224},{40,232},{48,240},{56,2... | collective-permute-start | bytes 344072 | tf_op jit(solution)/shard_map/ppermute | solution.py:319
  117.1 5.7 %collective-permute-done.16 = f32[224,128]{1,0:T(8,128)S(1)} collective-permute-done((f32[224,128]{1,0:T(8,128)S(1)}, f32[224,128]{1,0:T(8,128)S(1)}, u32[]{:S(2)}, u32[]{:S(2)}) %collective-permute-start.16) | collective-permute-done | bytes 114720 | tf_op jit(solution)/shard_map/ppermute | solution.py:319
  122.8 0.1 collective-permute-start.17
  122.9 1.3 %collective-permute-done.17.other_ref = f32[224,128]{1,0:T(8,128)S(1)} collective-permute-done((f32[224,128]{1,0:T(8,128)S(1)}, f32[224,128]{1,0:T(8,128)S(1)}, u32[]{:S(2)}, u32[]{:S(2)}) %collective-permute-start.17) | collective-permute-done | bytes 114720 | tf_op jit(solution)/shard_map/ppermute | solution.py:319
  124.2 0.0 copy-done.1
  124.2 0.0 copy-done.3
  124.2 3.4 %finish.1 = f32[128,6144]{1,0:T(8,128)} custom-call(s32[1]{0:T(128)} %bitcast.core_ref, f32[224,128]{1,0:T(8,128)S(1)} %fusion.1.own_ref, f32[224,128]{1,0:T(8,128)S(1)} %collective-permute-done.17.other_ref, f32[4,64,64]{2,1,0:T(8,128)S(1)} %copy-done.3, f32[128,6144]{1,0:T(8,128)S(1)} %get-tuple-element.48.current_ref, bf16[256,6144]{1,0:T(8,128)(2,1)S(1)} %copy-done.1, ...), custom_call_target="tpu_custom_call" | custom-call | tf_op jit(solution)/shard_map/finish/pallas_call | solution.py:296
  (10 shorter events, 0.1 us)
Async XLA Ops:
  2.9 16.7 %collective-permute-start = (f32[4,24576]{1,0:T(4,128)S(1)}, f32[4,24576]{1,0:T(4,128)S(1)}, u32[]{:S(2)}, u32[]{:S(2)}) collective-permute-start(f32[4,24576]{1,0:T(4,128)S(1)} %get-tuple-element.27), channel_id=1, source_target_pairs={{0,32},{32,64},{64,96},{96,128},{128,160},{160,192},{192,224},{224... | collective-permute-start | bytes 1179656 | tf_op jit(solution)/shard_map/ppermute | solution.py:330
  4.9 19.1 %collective-permute-start.1 = (f32[4,24576]{1,0:T(4,128)S(1)}, f32[4,24576]{1,0:T(4,128)S(1)}, u32[]{:S(2)}, u32[]{:S(2)}) collective-permute-start(f32[4,24576]{1,0:T(4,128)S(1)} %get-tuple-element.28), channel_id=1, source_target_pairs={{0,224},{32,0},{64,32},{96,64},{128,96},{160,128},{192,160},{224,1... | collective-permute-start | bytes 1179656 | tf_op jit(solution)/shard_map/ppermute | solution.py:330
  9.0 40.2 %collective-permute-start.4 = (f32[4,24576]{1,0:T(4,128)}, f32[4,24576]{1,0:T(4,128)S(1)}, u32[]{:S(2)}, u32[]{:S(2)}) collective-permute-start(f32[4,24576]{1,0:T(4,128)} %get-tuple-element.33), channel_id=1, source_target_pairs={{0,96},{32,128},{64,160},{96,192},{128,224},{160,0},{192,32},{224,... | collective-permute-start | bytes 1179656 | tf_op jit(solution)/shard_map/ppermute | solution.py:330
  10.8 51.4 %collective-permute-start.5 = (f32[4,24576]{1,0:T(4,128)}, f32[4,24576]{1,0:T(4,128)S(1)}, u32[]{:S(2)}, u32[]{:S(2)}) collective-permute-start(f32[4,24576]{1,0:T(4,128)} %get-tuple-element.34), channel_id=1, source_target_pairs={{0,160},{32,192},{64,224},{96,0},{128,32},{160,64},{192,96},{224,1... | collective-permute-start | bytes 1179656 | tf_op jit(solution)/shard_map/ppermute | solution.py:330
  25.3 47.6 %collective-permute-start.2 = (f32[2,4,12288]{2,1,0:T(4,128)}, f32[2,4,12288]{2,1,0:T(4,128)S(1)}, u32[]{:S(2)}, u32[]{:S(2)}) collective-permute-start(f32[2,4,12288]{2,1,0:T(4,128)} %get-tuple-element.30), channel_id=1, source_target_pairs={{0,16},{8,24},{16,0},{24,8},{32,48},{40,56},{48,32},{56,40},{64,80... | collective-permute-start | bytes 1179656 | tf_op jit(solution)/shard_map/ppermute | solution.py:319
  32.7 60.3 %all-to-all-start = ((f32[16,4,6144]{2,1,0:T(4,128)}), f32[16,4,6144]{2,1,0:T(4,128)S(1)}, u32[]{:S(2)}, u32[]{:S(2)}) async-start(f32[16,4,6144]{2,1,0:T(4,128)} %even.1), calls=%async_computation | async-start | bytes 3145728 | tf_op jit(solution)/shard_map/all_to_all | solution.py:345
  62.8 21.6 %collective-permute-start.6 = (f32[2,4,12288]{2,1,0:T(4,128)S(1)}, f32[2,4,12288]{2,1,0:T(4,128)S(1)}, u32[]{:S(2)}, u32[]{:S(2)}) collective-permute-start(f32[2,4,12288]{2,1,0:T(4,128)S(1)} %get-tuple-element.37), channel_id=1, source_target_pairs={{0,16},{8,24},{16,0},{24,8},{32,48},{40,56},{48,32},{56,40},{64,80... | collective-permute-start | bytes 1179656 | tf_op jit(solution)/shard_map/ppermute | solution.py:319
  74.2 18.7 %collective-permute-start.3 = (f32[2,2,4,6144]{3,2,1,0:T(4,128)}, f32[2,2,4,6144]{3,2,1,0:T(4,128)S(1)}, u32[]{:S(2)}, u32[]{:S(2)}) collective-permute-start(f32[2,2,4,6144]{3,2,1,0:T(4,128)} %get-tuple-element.32), channel_id=1, source_target_pairs={{0,8},{8,0},{16,24},{24,16},{32,40},{40,32},{48,56},{56,48},{64,72... | collective-permute-start | bytes 1179656 | tf_op jit(solution)/shard_map/ppermute | solution.py:319
  85.8 7.2 %collective-permute-start.7 = (f32[2,2,4,6144]{3,2,1,0:T(4,128)}, f32[2,2,4,6144]{3,2,1,0:T(4,128)S(1)}, u32[]{:S(2)}, u32[]{:S(2)}) collective-permute-start(f32[2,2,4,6144]{3,2,1,0:T(4,128)} %get-tuple-element.39), channel_id=1, source_target_pairs={{0,8},{8,0},{16,24},{24,16},{32,40},{40,32},{48,56},{56,48},{64,72... | collective-permute-start | bytes 1179656 | tf_op jit(solution)/shard_map/ppermute | solution.py:319
  85.8 1.4 %collective-permute-start.8 = (f32[96,128]{1,0:T(8,128)S(1)}, f32[96,128]{1,0:T(8,128)S(1)}, u32[]{:S(2)}, u32[]{:S(2)}) collective-permute-start(f32[96,128]{1,0:T(8,128)S(1)} %get-tuple-element.44), channel_id=1, source_target_pairs={{0,8},{8,0},{16,24},{24,16},{32,40},{40,32},{48,56},{56,48},{64,72... | collective-permute-start | bytes 147464 | tf_op jit(solution)/shard_map/ppermute | solution.py:319
  87.2 5.6 %collective-permute-start.9 = (f32[96,128]{1,0:T(8,128)S(1)}, f32[96,128]{1,0:T(8,128)S(1)}, u32[]{:S(2)}, u32[]{:S(2)}) collective-permute-start(f32[96,128]{1,0:T(8,128)S(1)} %add.31), channel_id=1, source_target_pairs={{0,16},{8,24},{16,0},{24,8},{32,48},{40,56},{48,32},{56,40},{64,80... | collective-permute-start | bytes 147464 | tf_op jit(solution)/shard_map/ppermute | solution.py:319
  92.8 4.2 %collective-permute-start.10 = (f32[96,128]{1,0:T(8,128)S(1)}, f32[96,128]{1,0:T(8,128)S(1)}, u32[]{:S(2)}, u32[]{:S(2)}) collective-permute-start(f32[96,128]{1,0:T(8,128)S(1)} %add.32.gram_ref), channel_id=1, source_target_pairs={{0,32},{8,40},{16,48},{24,56},{32,0},{40,8},{48,16},{56,24},{64,96... | collective-permute-start | bytes 147464 | tf_op jit(solution)/shard_map/ppermute | solution.py:319
  93.0 1.9 %copy-start = (bf16[256,6144]{1,0:T(8,128)(2,1)S(1)}, bf16[256,6144]{1,0:T(8,128)(2,1)}, u32[]{:S(2)}) copy-start(bf16[256,6144]{1,0:T(8,128)(2,1)} %after.1.high_ref) | copy-start | bytes 9437188
  94.9 2.1 %copy-start.2 = (bf16[256,6144]{1,0:T(8,128)(2,1)S(1)}, bf16[256,6144]{1,0:T(8,128)(2,1)}, u32[]{:S(2)}) copy-start(bf16[256,6144]{1,0:T(8,128)(2,1)} %get-tuple-element.43.low_ref) | copy-start | bytes 9437188
  97.0 27.2 %copy-start.1 = (bf16[256,6144]{1,0:T(8,128)(2,1)S(1)}, bf16[256,6144]{1,0:T(8,128)(2,1)}, u32[]{:S(2)}) copy-start(bf16[256,6144]{1,0:T(8,128)(2,1)} %after.1.high_ref) | copy-start | bytes 9437188
  97.0 27.2 %copy-start.3 = (f32[4,64,64]{2,1,0:T(8,128)S(1)}, f32[4,64,64]{2,1,0:T(8,128)}, u32[]{:S(2)}) copy-start(f32[4,64,64]{2,1,0:T(8,128)} %tfactors_ref.1) | copy-start | bytes 196612
  98.0 1.3 %collective-permute-start.11 = (f32[128,128]{1,0:T(8,128)S(1)}, f32[128,128]{1,0:T(8,128)S(1)}, u32[]{:S(2)}, u32[]{:S(2)}) collective-permute-start(f32[128,128]{1,0:T(8,128)S(1)} %get-tuple-element.46), channel_id=1, source_target_pairs={{0,8},{8,0},{16,24},{24,16},{32,40},{40,32},{48,56},{56,48},{64,72... | collective-permute-start | bytes 196616 | tf_op jit(solution)/shard_map/ppermute | solution.py:319
  99.4 5.9 %collective-permute-start.12 = (f32[128,128]{1,0:T(8,128)S(1)}, f32[128,128]{1,0:T(8,128)S(1)}, u32[]{:S(2)}, u32[]{:S(2)}) collective-permute-start(f32[128,128]{1,0:T(8,128)S(1)} %add.33), channel_id=1, source_target_pairs={{0,16},{8,24},{16,0},{24,8},{32,48},{40,56},{48,32},{56,40},{64,80... | collective-permute-start | bytes 196616 | tf_op jit(solution)/shard_map/ppermute | solution.py:319
  105.2 9.9 %collective-permute-start.14 = (f32[224,128]{1,0:T(8,128)S(1)}, f32[224,128]{1,0:T(8,128)S(1)}, u32[]{:S(2)}, u32[]{:S(2)}) collective-permute-start(f32[224,128]{1,0:T(8,128)S(1)} %pad_maximum_fusion), channel_id=1, source_target_pairs={{0,64},{8,72},{16,80},{24,88},{32,96},{40,104},{48,112},{56,120},{... | collective-permute-start | bytes 344072 | tf_op jit(solution)/shard_map/ppermute | solution.py:319
  105.5 9.6 %collective-permute-start.15 = (f32[128,128]{1,0:T(8,128)S(1)}, f32[128,128]{1,0:T(8,128)S(1)}, u32[]{:S(2)}, u32[]{:S(2)}) collective-permute-start(f32[128,128]{1,0:T(8,128)S(1)} %add.34), channel_id=1, source_target_pairs={{0,96},{8,104},{16,112},{24,120},{32,64},{40,72},{48,80},{56,88},{... | collective-permute-start | bytes 196616 | tf_op jit(solution)/shard_map/ppermute | solution.py:319
  109.8 5.8 %collective-permute-start.13 = (f32[128,128]{1,0:T(8,128)S(1)}, f32[128,128]{1,0:T(8,128)S(1)}, u32[]{:S(2)}, u32[]{:S(2)}) collective-permute-start(f32[128,128]{1,0:T(8,128)S(1)} %add.34), channel_id=1, source_target_pairs={{0,32},{8,40},{16,48},{24,56},{32,0},{40,8},{48,16},{56,24},{64,96... | collective-permute-start | bytes 196616 | tf_op jit(solution)/shard_map/ppermute | solution.py:319
  115.7 7.1 %collective-permute-start.16 = (f32[224,128]{1,0:T(8,128)S(1)}, f32[224,128]{1,0:T(8,128)S(1)}, u32[]{:S(2)}, u32[]{:S(2)}) collective-permute-start(f32[224,128]{1,0:T(8,128)S(1)} %pad_maximum_fusion.1), channel_id=1, source_target_pairs={{0,192},{8,200},{16,208},{24,216},{32,224},{40,232},{48,240},{56,2... | collective-permute-start | bytes 344072 | tf_op jit(solution)/shard_map/ppermute | solution.py:319
  122.8 1.4 %collective-permute-start.17 = (f32[224,128]{1,0:T(8,128)S(1)}, f32[224,128]{1,0:T(8,128)S(1)}, u32[]{:S(2)}, u32[]{:S(2)}) collective-permute-start(f32[224,128]{1,0:T(8,128)S(1)} %fusion.1.own_ref), channel_id=1, source_target_pairs={{0,8},{8,0},{16,24},{24,16},{32,40},{40,32},{48,56},{56,48},{64,72... | collective-permute-start | bytes 344072 | tf_op jit(solution)/shard_map/ppermute | solution.py:319

commit v10 on v9

--- a/solution.py
+++ b/solution.py
@@ -331,7 +331,7 @@
 
         def sides(up, down, before):
             block = pltpu.VMEM((2, each, wide // 2), jnp.float32)
-            return local_call(side_kernel, (block, block), [IN_VMEM, IN_VMEM, IN_ANY], (place, up, down, before))
+            return local_call(side_kernel, (block, block), [IN_VMEM, IN_VMEM, IN_HBM], (place, up, down, in_hbm(before)))
 
         def spread(kept, got):
             block = pltpu.VMEM((2, 2, each, wide // 4), jnp.float32)
@@ -343,12 +343,12 @@
         came = [moved(part, shift) for part, shift in zip(cut, SHIFTS)]
         packed = even_call(place, vectors_in, came[0], planes)
         even = lax.all_to_all(packed, ("half", "y", "core"), split_axis=0, concat_axis=0, tiled=True)
-        one_kept, one_sent = sides(came[0], came[1], came[0])
+        one_kept, one_sent = sides(came[0], came[1], packed)
         one_got = swap(one_sent, 2)
-        high, low, kept, sent = gram_call(core, householder, came[0])
+        high, low, kept, sent = gram_call(core, householder, one_sent)
         gram = kept + swap(sent, 1)
         gram = gram + swap(gram, 2)
-        three_kept, three_sent = sides(came[2], came[3], kept)
+        three_kept, three_sent = sides(came[2], came[3], high)
         three_got = swap(three_sent, 2)
         scattered = spread(one_kept, one_got) + spread(three_kept, three_got)
         high = after(high, even)

time: 129 us -> 130 us (level); the launches traced: 128 us -> 127 us
  starting transfers between devices: 43.3 us -> 52 us
  waiting for transfers between devices: 55.2 us -> 46.8 us
    ppermute x4, waiting for transfers between devices: 23 us -> 11.4 us  [moved(): lax.ppermute(part, ('half', 'odd'), [(i, (i + shift) % planes) for i in r...]
    ppermute x14, starting transfers between devices: 24.6 us -> 30.3 us  [swap(): return lax.ppermute(value, row, [(i, i ^ flip) for i in range(devices)])]
    ppermute x14, waiting for transfers between devices: 32.2 us -> 35.3 us  [swap(): return lax.ppermute(value, row, [(i, i ^ flip) for i in range(devices)])]
    all_to_all x1, starting transfers between devices: 7.66 us -> 10.7 us  [shards(): lax.all_to_all(packed, ('half', 'y', 'core'), split_axis=0, concat_axis=0...]
  transfers between devices with their start and end apart: 19 -> 19, of which waited for: 13 -> 12; matrix products, arithmetic and copies ran while one was open for 0% -> 0% of each run, Pallas kernels for 15% -> 15%
where the time goes in v10:
time: 130 us; the launch traced here: 127 us
  starting transfers between devices  52 us (40%)
  waiting for transfers between devices  46.8 us (36%)
  Pallas kernels  26.1 us (20%)
  local copies, waits for them, and re-layouts  1.9 us (1%)
    ppermute x14, waiting for transfers between devices, swap(): return lax.ppermute(value, row, [(i, i ^ flip) for i in range(devices)])  35.3 us
    ppermute x14, starting transfers between devices, swap(): return lax.ppermute(value, row, [(i, i ^ flip) for i in range(devices)])  30.3 us
    ppermute x4, waiting for transfers between devices, moved(): lax.ppermute(part, ('half', 'odd'), [(i, (i + shift) % planes) for i in r...  11.4 us
    ppermute x4, starting transfers between devices, moved(): lax.ppermute(part, ('half', 'odd'), [(i, (i + shift) % planes) for i in r...  11.1 us
    all_to_all x1, starting transfers between devices, shards(): lax.all_to_all(packed, ('half', 'y', 'core'), split_axis=0, concat_axis=0...  10.7 us
    pallas_call x1, Pallas kernels, gram_call(): pl.pallas_call(gram_kernel, out_shape=(pltpu.HBM((size, rows), jnp.bfloat...  8.77 us
    pallas_call x5, Pallas kernels, local_call(): pl.pallas_call(kernel, out_shape=outs, in_specs=[IN_SMEM] + specs, out_sp...  6.85 us
    pallas_call x1, Pallas kernels, even_call(): pl.pallas_call(even_kernel, out_shape=pltpu.HBM((planes * 2, each, wide /...  4.14 us
  transfers between devices with their start and end apart: 19, of which 12 were waited for; matrix products, arithmetic and copies ran while one was open for 0% of the time, Pallas kernels for 15%

profile of v10, /device:TPU:4, one launch (start us, length us, event | category | flops | bytes accessed | tf_op | source)
XLA Modules:
  0.0 127.3 jit_solution(11369482171032233787)
XLA Ops:
  0.0 0.1 pad_add_fusion.place_ref
  0.1 3.0 %cut_kernel.1 = (f32[4,24576]{1,0:T(4,128)S(1)}, f32[4,24576]{1,0:T(4,128)}, f32[4,24576]{1,0:T(4,128)}, f32[4,24576]{1,0:T(4,128)}) custom-call(s32[3]{0:T(128)S(1)} %pad_add_fusion.place_ref, f32[4,196608]{1,0:T(4,128)} %block_ref.1), custom_call_target="tpu_custom_call" | custom-call | tf_op jit(solution)/shard_map/cut_kernel/pallas_call | solution.py:221
  3.0 2.0 %collective-permute-start = (f32[4,24576]{1,0:T(4,128)S(1)}, f32[4,24576]{1,0:T(4,128)S(1)}, u32[]{:S(2)}, u32[]{:S(2)}) collective-permute-start(f32[4,24576]{1,0:T(4,128)S(1)} %get-tuple-element.27), channel_id=1, source_target_pairs={{0,32},{32,64},{64,96},{96,128},{128,160},{160,192},{192,224},{224... | collective-permute-start | bytes 1179656 | tf_op jit(solution)/shard_map/ppermute | solution.py:330
  5.0 4.0 %collective-permute-start.1 = (f32[4,24576]{1,0:T(4,128)}, f32[4,24576]{1,0:T(4,128)S(1)}, u32[]{:S(2)}, u32[]{:S(2)}) collective-permute-start(f32[4,24576]{1,0:T(4,128)} %get-tuple-element.28), channel_id=1, source_target_pairs={{0,224},{32,0},{64,32},{96,64},{128,96},{160,128},{192,160},{224,1... | collective-permute-start | bytes 1179656 | tf_op jit(solution)/shard_map/ppermute | solution.py:330
  9.1 1.8 %collective-permute-start.4 = (f32[4,24576]{1,0:T(4,128)}, f32[4,24576]{1,0:T(4,128)S(1)}, u32[]{:S(2)}, u32[]{:S(2)}) collective-permute-start(f32[4,24576]{1,0:T(4,128)} %get-tuple-element.33), channel_id=1, source_target_pairs={{0,96},{32,128},{64,160},{96,192},{128,224},{160,0},{192,32},{224,... | collective-permute-start | bytes 1179656 | tf_op jit(solution)/shard_map/ppermute | solution.py:330
  10.9 3.2 %collective-permute-start.5 = (f32[4,24576]{1,0:T(4,128)}, f32[4,24576]{1,0:T(4,128)S(1)}, u32[]{:S(2)}, u32[]{:S(2)}) collective-permute-start(f32[4,24576]{1,0:T(4,128)} %get-tuple-element.34), channel_id=1, source_target_pairs={{0,160},{32,192},{64,224},{96,0},{128,32},{160,64},{192,96},{224,1... | collective-permute-start | bytes 1179656 | tf_op jit(solution)/shard_map/ppermute | solution.py:330
  14.1 5.7 %collective-permute-done.before_ref.up_ref = f32[4,24576]{1,0:T(4,128)S(1)} collective-permute-done((f32[4,24576]{1,0:T(4,128)S(1)}, f32[4,24576]{1,0:T(4,128)S(1)}, u32[]{:S(2)}, u32[]{:S(2)}) %collective-permute-start) | collective-permute-done | bytes 393248 | tf_op jit(solution)/shard_map/ppermute | solution.py:330
  19.8 4.1 %even.1.before_ref = f32[16,4,6144]{2,1,0:T(4,128)} custom-call(s32[3]{0:T(128)S(1)} %pad_add_fusion.place_ref, f32[4,196608]{1,0:T(4,128)} %block_ref.1, f32[4,24576]{1,0:T(4,128)S(1)} %collective-permute-done.before_ref.up_ref), custom_call_target="tpu_custom_call" | custom-call | tf_op jit(solution)/shard_map/even/pallas_call | solution.py:235
  23.9 10.7 %all-to-all-start = ((f32[16,4,6144]{2,1,0:T(4,128)}), f32[16,4,6144]{2,1,0:T(4,128)S(1)}, u32[]{:S(2)}, u32[]{:S(2)}) async-start(f32[16,4,6144]{2,1,0:T(4,128)} %even.1.before_ref), calls=%async_computation | async-start | bytes 3145728 | tf_op jit(solution)/shard_map/all_to_all | solution.py:345
  34.6 0.0 collective-permute-done.1.down_ref
  34.6 0.6 side_kernel.2
  35.2 3.5 %collective-permute-start.2 = (f32[2,4,12288]{2,1,0:T(4,128)S(1)}, f32[2,4,12288]{2,1,0:T(4,128)S(1)}, u32[]{:S(2)}, u32[]{:S(2)}) collective-permute-start(f32[2,4,12288]{2,1,0:T(4,128)S(1)} %get-tuple-element.30.before_ref), channel_id=1, source_target_pairs={{0,16},{8,24},{16,0},{24,8},{32,48},{40,56},{48,32},{56,40},{64,80... | collective-permute-start | bytes 1179656 | tf_op jit(solution)/shard_map/ppermute | solution.py:319
  38.7 8.8 %gram.1 = (bf16[256,6144]{1,0:T(8,128)(2,1)}, bf16[256,6144]{1,0:T(8,128)(2,1)}, f32[96,128]{1,0:T(8,128)S(1)}, f32[96,128]{1,0:T(8,128)S(1)}) custom-call(s32[1]{0:T(128)} %bitcast.core_ref, f32[4,64,6144]{2,1,0:T(8,128)} %householder_ref.1, f32[2,4,12288]{2,1,0:T(4,128)S(1)} %get-tuple-element.30.before_ref), custom_call_target="tpu_custom_call" | custom-call | flops 32212254720 | bytes 12582912 | tf_op jit(solution)/shard_map/gram/pallas_call | solution.py:197
  47.5 2.6 %collective-permute-done.4.up_ref = f32[4,24576]{1,0:T(4,128)S(1)} collective-permute-done((f32[4,24576]{1,0:T(4,128)}, f32[4,24576]{1,0:T(4,128)S(1)}, u32[]{:S(2)}, u32[]{:S(2)}) %collective-permute-start.4) | collective-permute-done | bytes 393248 | tf_op jit(solution)/shard_map/ppermute | solution.py:330
  50.0 3.2 %collective-permute-done.5.down_ref = f32[4,24576]{1,0:T(4,128)S(1)} collective-permute-done((f32[4,24576]{1,0:T(4,128)}, f32[4,24576]{1,0:T(4,128)S(1)}, u32[]{:S(2)}, u32[]{:S(2)}) %collective-permute-start.5) | collective-permute-done | bytes 393248 | tf_op jit(solution)/shard_map/ppermute | solution.py:330
  53.2 0.6 side_kernel.3
  53.8 3.2 %collective-permute-start.6 = (f32[2,4,12288]{2,1,0:T(4,128)S(1)}, f32[2,4,12288]{2,1,0:T(4,128)S(1)}, u32[]{:S(2)}, u32[]{:S(2)}) collective-permute-start(f32[2,4,12288]{2,1,0:T(4,128)S(1)} %get-tuple-element.37), channel_id=1, source_target_pairs={{0,16},{8,24},{16,0},{24,8},{32,48},{40,56},{48,32},{56,40},{64,80... | collective-permute-start | bytes 1179656 | tf_op jit(solution)/shard_map/ppermute | solution.py:319
  57.1 0.0 collective-permute-done.2.got_ref
  57.1 1.3 %core_kernel.2 = (f32[2,2,4,6144]{3,2,1,0:T(4,128)S(1)}, f32[2,2,4,6144]{3,2,1,0:T(4,128)}) custom-call(s32[3]{0:T(128)S(1)} %pad_add_fusion.place_ref, f32[2,4,12288]{2,1,0:T(4,128)S(1)} %get-tuple-element.29.own_ref, f32[2,4,12288]{2,1,0:T(4,128)S(1)} %collective-permute-done.2.got_ref), custom_call_target="tpu_custom_call" | custom-call | tf_op jit(solution)/shard_map/core_kernel/pallas_call | solution.py:221
  58.4 0.0 collective-permute-start.3
  58.4 10.5 %collective-permute-done.6.got_ref = f32[2,4,12288]{2,1,0:T(4,128)S(1)} collective-permute-done((f32[2,4,12288]{2,1,0:T(4,128)S(1)}, f32[2,4,12288]{2,1,0:T(4,128)S(1)}, u32[]{:S(2)}, u32[]{:S(2)}) %collective-permute-start.6) | collective-permute-done | bytes 393248 | tf_op jit(solution)/shard_map/ppermute | solution.py:319
  68.9 1.4 %core_kernel.3 = (f32[2,2,4,6144]{3,2,1,0:T(4,128)S(1)}, f32[2,2,4,6144]{3,2,1,0:T(4,128)}) custom-call(s32[3]{0:T(128)S(1)} %pad_add_fusion.place_ref, f32[2,4,12288]{2,1,0:T(4,128)S(1)} %get-tuple-element.36.own_ref, f32[2,4,12288]{2,1,0:T(4,128)S(1)} %collective-permute-done.6.got_ref), custom_call_target="tpu_custom_call" | custom-call | tf_op jit(solution)/shard_map/core_kernel/pallas_call | solution.py:221
  70.2 0.0 collective-permute-start.7
  70.2 0.5 collective-permute-start.8
  70.7 0.9 collective-permute-done.8
  71.7 0.0 collective-permute-start.9
  71.7 6.8 %collective-permute-done.9 = f32[96,128]{1,0:T(8,128)S(1)} collective-permute-done((f32[96,128]{1,0:T(8,128)S(1)}, f32[96,128]{1,0:T(8,128)S(1)}, u32[]{:S(2)}, u32[]{:S(2)}) %collective-permute-start.9) | collective-permute-done | bytes 49184 | tf_op jit(solution)/shard_map/ppermute | solution.py:319
  78.5 15.4 %collective-permute-start.10 = (f32[96,128]{1,0:T(8,128)S(1)}, f32[96,128]{1,0:T(8,128)S(1)}, u32[]{:S(2)}, u32[]{:S(2)}) collective-permute-start(f32[96,128]{1,0:T(8,128)S(1)} %add.32.gram_ref), channel_id=1, source_target_pairs={{0,32},{8,40},{16,48},{24,56},{32,0},{40,8},{48,16},{56,24},{64,96... | collective-permute-start | bytes 147464 | tf_op jit(solution)/shard_map/ppermute | solution.py:319
  93.9 0.0 all-to-all-done.before_ref.even_ref
  93.9 0.0 collective-permute-done.3.got_one_ref
  93.9 0.0 collective-permute-done.7.got_three_ref
  93.9 0.0 copy-start
  93.9 1.9 %copy-done = bf16[256,6144]{1,0:T(8,128)(2,1)S(1)} copy-done((bf16[256,6144]{1,0:T(8,128)(2,1)S(1)}, bf16[256,6144]{1,0:T(8,128)(2,1)}, u32[]{:S(2)}) %copy-start) | copy-done | bytes 3145752
  95.8 0.0 copy-start.2
  95.8 2.0 %project_high.1 = (f32[128,6144]{1,0:T(8,128)S(1)}, bf16[128,6144]{1,0:T(8,128)(2,1)S(1)}, f32[256,256]{1,0:T(8,128)S(1)}) custom-call(s32[3]{0:T(128)S(1)} %pad_add_fusion.place_ref, f32[16,4,6144]{2,1,0:T(4,128)S(1)} %all-to-all-done.before_ref.even_ref, f32[2,2,4,6144]{3,2,1,0:T(4,128)S(1)} %get-tuple-element.31.kept_one_ref, ...), custom_call_target="tpu_custom_call" | custom-call | tf_op jit(solution)/shard_map/project_high/pallas_call | solution.py:265
  97.8 0.0 collective-permute-done.10.more_ref
  97.8 0.0 copy-done.2
  97.8 0.0 copy-start.1
  97.9 0.0 copy-start.3
  97.9 1.0 project_low.1
  98.9 0.1 collective-permute-start.11
  99.0 1.2 collective-permute-done.11
  100.2 2.8 %collective-permute-start.12 = (f32[128,128]{1,0:T(8,128)S(1)}, f32[128,128]{1,0:T(8,128)S(1)}, u32[]{:S(2)}, u32[]{:S(2)}) collective-permute-start(f32[128,128]{1,0:T(8,128)S(1)} %add.33), channel_id=1, source_target_pairs={{0,16},{8,24},{16,0},{24,8},{32,48},{40,56},{48,32},{56,40},{64,80... | collective-permute-start | bytes 196616 | tf_op jit(solution)/shard_map/ppermute | solution.py:319
  103.0 3.1 %collective-permute-done.12 = f32[128,128]{1,0:T(8,128)S(1)} collective-permute-done((f32[128,128]{1,0:T(8,128)S(1)}, f32[128,128]{1,0:T(8,128)S(1)}, u32[]{:S(2)}, u32[]{:S(2)}) %collective-permute-start.12) | collective-permute-done | bytes 65568 | tf_op jit(solution)/shard_map/ppermute | solution.py:319
  106.1 0.3 collective-permute-start.14
  106.4 2.5 %collective-permute-start.15 = (f32[128,128]{1,0:T(8,128)S(1)}, f32[128,128]{1,0:T(8,128)S(1)}, u32[]{:S(2)}, u32[]{:S(2)}) collective-permute-start(f32[128,128]{1,0:T(8,128)S(1)} %add.34), channel_id=1, source_target_pairs={{0,96},{8,104},{16,112},{24,120},{32,64},{40,72},{48,80},{56,88},{... | collective-permute-start | bytes 196616 | tf_op jit(solution)/shard_map/ppermute | solution.py:319
  108.9 1.0 collective-permute-start.13
  109.9 5.1 %collective-permute-done.14 = f32[224,128]{1,0:T(8,128)S(1)} collective-permute-done((f32[224,128]{1,0:T(8,128)S(1)}, f32[224,128]{1,0:T(8,128)S(1)}, u32[]{:S(2)}, u32[]{:S(2)}) %collective-permute-start.14) | collective-permute-done | bytes 114720 | tf_op jit(solution)/shard_map/ppermute | solution.py:319
  115.0 0.0 collective-permute-done.15
  115.0 0.4 collective-permute-done.13
  115.4 0.9 collective-permute-start.16
  116.3 6.1 %collective-permute-done.16 = f32[224,128]{1,0:T(8,128)S(1)} collective-permute-done((f32[224,128]{1,0:T(8,128)S(1)}, f32[224,128]{1,0:T(8,128)S(1)}, u32[]{:S(2)}, u32[]{:S(2)}) %collective-permute-start.16) | collective-permute-done | bytes 114720 | tf_op jit(solution)/shard_map/ppermute | solution.py:319
  122.4 0.1 collective-permute-start.17
  122.5 1.3 %collective-permute-done.17.other_ref = f32[224,128]{1,0:T(8,128)S(1)} collective-permute-done((f32[224,128]{1,0:T(8,128)S(1)}, f32[224,128]{1,0:T(8,128)S(1)}, u32[]{:S(2)}, u32[]{:S(2)}) %collective-permute-start.17) | collective-permute-done | bytes 114720 | tf_op jit(solution)/shard_map/ppermute | solution.py:319
  123.8 0.0 copy-done.1
  123.8 0.0 copy-done.3
  123.8 3.4 %finish.1 = f32[128,6144]{1,0:T(8,128)} custom-call(s32[1]{0:T(128)} %bitcast.core_ref, f32[224,128]{1,0:T(8,128)S(1)} %fusion.1.own_ref, f32[224,128]{1,0:T(8,128)S(1)} %collective-permute-done.17.other_ref, f32[4,64,64]{2,1,0:T(8,128)S(1)} %copy-done.3, f32[128,6144]{1,0:T(8,128)S(1)} %get-tuple-element.48.current_ref, bf16[256,6144]{1,0:T(8,128)(2,1)S(1)} %copy-done.1, ...), custom_call_target="tpu_custom_call" | custom-call | tf_op jit(solution)/shard_map/finish/pallas_call | solution.py:296
  (10 shorter events, 0.1 us)
Async XLA Ops:
  3.0 16.7 %collective-permute-start = (f32[4,24576]{1,0:T(4,128)S(1)}, f32[4,24576]{1,0:T(4,128)S(1)}, u32[]{:S(2)}, u32[]{:S(2)}) collective-permute-start(f32[4,24576]{1,0:T(4,128)S(1)} %get-tuple-element.27), channel_id=1, source_target_pairs={{0,32},{32,64},{64,96},{96,128},{128,160},{160,192},{192,224},{224... | collective-permute-start | bytes 1179656 | tf_op jit(solution)/shard_map/ppermute | solution.py:330
  5.0 29.5 %collective-permute-start.1 = (f32[4,24576]{1,0:T(4,128)}, f32[4,24576]{1,0:T(4,128)S(1)}, u32[]{:S(2)}, u32[]{:S(2)}) collective-permute-start(f32[4,24576]{1,0:T(4,128)} %get-tuple-element.28), channel_id=1, source_target_pairs={{0,224},{32,0},{64,32},{96,64},{128,96},{160,128},{192,160},{224,1... | collective-permute-start | bytes 1179656 | tf_op jit(solution)/shard_map/ppermute | solution.py:330
  9.1 41.0 %collective-permute-start.4 = (f32[4,24576]{1,0:T(4,128)}, f32[4,24576]{1,0:T(4,128)S(1)}, u32[]{:S(2)}, u32[]{:S(2)}) collective-permute-start(f32[4,24576]{1,0:T(4,128)} %get-tuple-element.33), channel_id=1, source_target_pairs={{0,96},{32,128},{64,160},{96,192},{128,224},{160,0},{192,32},{224,... | collective-permute-start | bytes 1179656 | tf_op jit(solution)/shard_map/ppermute | solution.py:330
  10.9 42.4 %collective-permute-start.5 = (f32[4,24576]{1,0:T(4,128)}, f32[4,24576]{1,0:T(4,128)S(1)}, u32[]{:S(2)}, u32[]{:S(2)}) collective-permute-start(f32[4,24576]{1,0:T(4,128)} %get-tuple-element.34), channel_id=1, source_target_pairs={{0,160},{32,192},{64,224},{96,0},{128,32},{160,64},{192,96},{224,1... | collective-permute-start | bytes 1179656 | tf_op jit(solution)/shard_map/ppermute | solution.py:330
  23.9 70.0 %all-to-all-start = ((f32[16,4,6144]{2,1,0:T(4,128)}), f32[16,4,6144]{2,1,0:T(4,128)S(1)}, u32[]{:S(2)}, u32[]{:S(2)}) async-start(f32[16,4,6144]{2,1,0:T(4,128)} %even.1.before_ref), calls=%async_computation | async-start | bytes 3145728 | tf_op jit(solution)/shard_map/all_to_all | solution.py:345
  35.2 21.9 %collective-permute-start.2 = (f32[2,4,12288]{2,1,0:T(4,128)S(1)}, f32[2,4,12288]{2,1,0:T(4,128)S(1)}, u32[]{:S(2)}, u32[]{:S(2)}) collective-permute-start(f32[2,4,12288]{2,1,0:T(4,128)S(1)} %get-tuple-element.30.before_ref), channel_id=1, source_target_pairs={{0,16},{8,24},{16,0},{24,8},{32,48},{40,56},{48,32},{56,40},{64,80... | collective-permute-start | bytes 1179656 | tf_op jit(solution)/shard_map/ppermute | solution.py:319
  53.8 15.0 %collective-permute-start.6 = (f32[2,4,12288]{2,1,0:T(4,128)S(1)}, f32[2,4,12288]{2,1,0:T(4,128)S(1)}, u32[]{:S(2)}, u32[]{:S(2)}) collective-permute-start(f32[2,4,12288]{2,1,0:T(4,128)S(1)} %get-tuple-element.37), channel_id=1, source_target_pairs={{0,16},{8,24},{16,0},{24,8},{32,48},{40,56},{48,32},{56,40},{64,80... | collective-permute-start | bytes 1179656 | tf_op jit(solution)/shard_map/ppermute | solution.py:319
  58.4 35.5 %collective-permute-start.3 = (f32[2,2,4,6144]{3,2,1,0:T(4,128)}, f32[2,2,4,6144]{3,2,1,0:T(4,128)S(1)}, u32[]{:S(2)}, u32[]{:S(2)}) collective-permute-start(f32[2,2,4,6144]{3,2,1,0:T(4,128)} %get-tuple-element.32), channel_id=1, source_target_pairs={{0,8},{8,0},{16,24},{24,16},{32,40},{40,32},{48,56},{56,48},{64,72... | collective-permute-start | bytes 1179656 | tf_op jit(solution)/shard_map/ppermute | solution.py:319
  70.2 23.7 %collective-permute-start.7 = (f32[2,2,4,6144]{3,2,1,0:T(4,128)}, f32[2,2,4,6144]{3,2,1,0:T(4,128)S(1)}, u32[]{:S(2)}, u32[]{:S(2)}) collective-permute-start(f32[2,2,4,6144]{3,2,1,0:T(4,128)} %get-tuple-element.39), channel_id=1, source_target_pairs={{0,8},{8,0},{16,24},{24,16},{32,40},{40,32},{48,56},{56,48},{64,72... | collective-permute-start | bytes 1179656 | tf_op jit(solution)/shard_map/ppermute | solution.py:319
  70.2 1.4 %collective-permute-start.8 = (f32[96,128]{1,0:T(8,128)S(1)}, f32[96,128]{1,0:T(8,128)S(1)}, u32[]{:S(2)}, u32[]{:S(2)}) collective-permute-start(f32[96,128]{1,0:T(8,128)S(1)} %get-tuple-element.44), channel_id=1, source_target_pairs={{0,8},{8,0},{16,24},{24,16},{32,40},{40,32},{48,56},{56,48},{64,72... | collective-permute-start | bytes 147464 | tf_op jit(solution)/shard_map/ppermute | solution.py:319
  71.7 6.8 %collective-permute-start.9 = (f32[96,128]{1,0:T(8,128)S(1)}, f32[96,128]{1,0:T(8,128)S(1)}, u32[]{:S(2)}, u32[]{:S(2)}) collective-permute-start(f32[96,128]{1,0:T(8,128)S(1)} %add.31), channel_id=1, source_target_pairs={{0,16},{8,24},{16,0},{24,8},{32,48},{40,56},{48,32},{56,40},{64,80... | collective-permute-start | bytes 147464 | tf_op jit(solution)/shard_map/ppermute | solution.py:319
  78.5 19.3 %collective-permute-start.10 = (f32[96,128]{1,0:T(8,128)S(1)}, f32[96,128]{1,0:T(8,128)S(1)}, u32[]{:S(2)}, u32[]{:S(2)}) collective-permute-start(f32[96,128]{1,0:T(8,128)S(1)} %add.32.gram_ref), channel_id=1, source_target_pairs={{0,32},{8,40},{16,48},{24,56},{32,0},{40,8},{48,16},{56,24},{64,96... | collective-permute-start | bytes 147464 | tf_op jit(solution)/shard_map/ppermute | solution.py:319
  93.9 1.9 %copy-start = (bf16[256,6144]{1,0:T(8,128)(2,1)S(1)}, bf16[256,6144]{1,0:T(8,128)(2,1)}, u32[]{:S(2)}) copy-start(bf16[256,6144]{1,0:T(8,128)(2,1)} %after.1.high_ref) | copy-start | bytes 9437188
  95.8 2.0 %copy-start.2 = (bf16[256,6144]{1,0:T(8,128)(2,1)S(1)}, bf16[256,6144]{1,0:T(8,128)(2,1)}, u32[]{:S(2)}) copy-start(bf16[256,6144]{1,0:T(8,128)(2,1)} %get-tuple-element.42.low_ref) | copy-start | bytes 9437188
  97.8 26.0 %copy-start.1 = (bf16[256,6144]{1,0:T(8,128)(2,1)S(1)}, bf16[256,6144]{1,0:T(8,128)(2,1)}, u32[]{:S(2)}) copy-start(bf16[256,6144]{1,0:T(8,128)(2,1)} %after.1.high_ref) | copy-start | bytes 9437188
  97.9 26.0 %copy-start.3 = (f32[4,64,64]{2,1,0:T(8,128)S(1)}, f32[4,64,64]{2,1,0:T(8,128)}, u32[]{:S(2)}) copy-start(f32[4,64,64]{2,1,0:T(8,128)} %tfactors_ref.1) | copy-start | bytes 196612
  98.9 1.3 %collective-permute-start.11 = (f32[128,128]{1,0:T(8,128)S(1)}, f32[128,128]{1,0:T(8,128)S(1)}, u32[]{:S(2)}, u32[]{:S(2)}) collective-permute-start(f32[128,128]{1,0:T(8,128)S(1)} %get-tuple-element.46), channel_id=1, source_target_pairs={{0,8},{8,0},{16,24},{24,16},{32,40},{40,32},{48,56},{56,48},{64,72... | collective-permute-start | bytes 196616 | tf_op jit(solution)/shard_map/ppermute | solution.py:319
  100.2 5.9 %collective-permute-start.12 = (f32[128,128]{1,0:T(8,128)S(1)}, f32[128,128]{1,0:T(8,128)S(1)}, u32[]{:S(2)}, u32[]{:S(2)}) collective-permute-start(f32[128,128]{1,0:T(8,128)S(1)} %add.33), channel_id=1, source_target_pairs={{0,16},{8,24},{16,0},{24,8},{32,48},{40,56},{48,32},{56,40},{64,80... | collective-permute-start | bytes 196616 | tf_op jit(solution)/shard_map/ppermute | solution.py:319
  106.1 8.9 %collective-permute-start.14 = (f32[224,128]{1,0:T(8,128)S(1)}, f32[224,128]{1,0:T(8,128)S(1)}, u32[]{:S(2)}, u32[]{:S(2)}) collective-permute-start(f32[224,128]{1,0:T(8,128)S(1)} %pad_maximum_fusion), channel_id=1, source_target_pairs={{0,64},{8,72},{16,80},{24,88},{32,96},{40,104},{48,112},{56,120},{... | collective-permute-start | bytes 344072 | tf_op jit(solution)/shard_map/ppermute | solution.py:319
  106.4 8.6 %collective-permute-start.15 = (f32[128,128]{1,0:T(8,128)S(1)}, f32[128,128]{1,0:T(8,128)S(1)}, u32[]{:S(2)}, u32[]{:S(2)}) collective-permute-start(f32[128,128]{1,0:T(8,128)S(1)} %add.34), channel_id=1, source_target_pairs={{0,96},{8,104},{16,112},{24,120},{32,64},{40,72},{48,80},{56,88},{... | collective-permute-start | bytes 196616 | tf_op jit(solution)/shard_map/ppermute | solution.py:319
  108.9 6.5 %collective-permute-start.13 = (f32[128,128]{1,0:T(8,128)S(1)}, f32[128,128]{1,0:T(8,128)S(1)}, u32[]{:S(2)}, u32[]{:S(2)}) collective-permute-start(f32[128,128]{1,0:T(8,128)S(1)} %add.34), channel_id=1, source_target_pairs={{0,32},{8,40},{16,48},{24,56},{32,0},{40,8},{48,16},{56,24},{64,96... | collective-permute-start | bytes 196616 | tf_op jit(solution)/shard_map/ppermute | solution.py:319
  115.4 7.0 %collective-permute-start.16 = (f32[224,128]{1,0:T(8,128)S(1)}, f32[224,128]{1,0:T(8,128)S(1)}, u32[]{:S(2)}, u32[]{:S(2)}) collective-permute-start(f32[224,128]{1,0:T(8,128)S(1)} %pad_maximum_fusion.1), channel_id=1, source_target_pairs={{0,192},{8,200},{16,208},{24,216},{32,224},{40,232},{48,240},{56,2... | collective-permute-start | bytes 344072 | tf_op jit(solution)/shard_map/ppermute | solution.py:319
  122.4 1.4 %collective-permute-start.17 = (f32[224,128]{1,0:T(8,128)S(1)}, f32[224,128]{1,0:T(8,128)S(1)}, u32[]{:S(2)}, u32[]{:S(2)}) collective-permute-start(f32[224,128]{1,0:T(8,128)S(1)} %fusion.1.own_ref), channel_id=1, source_target_pairs={{0,8},{8,0},{16,24},{24,16},{32,40},{40,32},{48,56},{56,48},{64,72... | collective-permute-start | bytes 344072 | tf_op jit(solution)/shard_map/ppermute | solution.py:319

commit v11 on v8

--- a/solution.py
+++ b/solution.py
@@ -339,12 +339,12 @@
         block = pltpu.VMEM((each, wide), jnp.float32)
         cut = local_call(cut_kernel, (block,) * len(SHIFTS), [IN_HBM], (place, in_hbm(vectors_in)), len(SHIFTS))
         came = [moved(part, shift) for part, shift in zip(cut, SHIFTS)]
-        even = even_call(place, vectors_in, came[0], planes)
+        even = even_call(place, vectors_in, place, planes)
         even = lax.all_to_all(even, ("half", "y", "core"), split_axis=0, concat_axis=0, tiled=True)
-        high, low, kept, sent = gram_call(core, householder, came[0])
+        high, low, kept, sent = gram_call(core, householder, place)
         gram = kept + swap(sent, 1)
         gram = gram + swap(gram, 2)
-        scattered = spread(came[0], came[1], came[0]) + spread(came[2], came[3], gram)
+        scattered = spread(came[0], came[1], kept) + spread(came[2], came[3], gram)
         high = after(high, even)
         current, value, sent, gram = project_call(core, place, even, scattered, high, low, gram, swap(gram, 4))
         value = value + swap(sent, 1)

time: 119 us -> 117 us (0.983)
  waiting for transfers between devices: 50.3 us -> 47.8 us
    ppermute x4, waiting for transfers between devices: 9.16 us -> 2.58 us  [moved(): lax.ppermute(part, ('half', 'odd'), [(i, (i + shift) % planes) for i in r...]
    all_to_all x1, waiting for transfers between devices: 0.01 us -> 6.13 us  [shards(): lax.all_to_all(even, ('half', 'y', 'core'), split_axis=0, concat_axis=0,...]
    ppermute x14, waiting for transfers between devices: 41.1 us -> 39 us  [swap(): return lax.ppermute(value, row, [(i, i ^ flip) for i in range(devices)])]
    ppermute x14, starting transfers between devices: 18.5 us -> 19.9 us  [swap(): return lax.ppermute(value, row, [(i, i ^ flip) for i in range(devices)])]
    all_to_all x1, starting transfers between devices: 10.7 us -> 9.4 us  [shards(): lax.all_to_all(even, ('half', 'y', 'core'), split_axis=0, concat_axis=0,...]
where the time goes in v11:
time: 117 us; the launch traced here: 116 us
  waiting for transfers between devices  47.8 us (41%)
  starting transfers between devices  39.5 us (34%)
  Pallas kernels  26.3 us (22%)
  local copies, waits for them, and re-layouts  1.9 us (2%)
    ppermute x14, waiting for transfers between devices, swap(): return lax.ppermute(value, row, [(i, i ^ flip) for i in range(devices)])  39 us
    ppermute x14, starting transfers between devices, swap(): return lax.ppermute(value, row, [(i, i ^ flip) for i in range(devices)])  19.9 us
    ppermute x4, starting transfers between devices, moved(): lax.ppermute(part, ('half', 'odd'), [(i, (i + shift) % planes) for i in r...  10.1 us
    all_to_all x1, starting transfers between devices, shards(): lax.all_to_all(even, ('half', 'y', 'core'), split_axis=0, concat_axis=0,...  9.4 us
    pallas_call x1, Pallas kernels, gram_call(): pl.pallas_call(gram_kernel, out_shape=(pltpu.HBM((size, rows), jnp.bfloat...  8.78 us
    pallas_call x5, Pallas kernels, local_call(): pl.pallas_call(kernel, out_shape=outs, in_specs=[IN_SMEM] + specs, out_sp...  7.01 us
    all_to_all x1, waiting for transfers between devices, shards(): lax.all_to_all(even, ('half', 'y', 'core'), split_axis=0, concat_axis=0,...  6.13 us
    pallas_call x1, Pallas kernels, even_call(): pl.pallas_call(even_kernel, out_shape=pltpu.HBM((planes * 2, each, wide /...  4.14 us
  transfers between devices with their start and end apart: 19, of which 12 were waited for; matrix products, arithmetic and copies ran while one was open for 0% of the time, Pallas kernels for 16%

profile of v11, /device:TPU:4, one launch (start us, length us, event | category | flops | bytes accessed | tf_op | source)
XLA Modules:
  0.0 115.9 jit_solution(18136758723555065438)
XLA Ops:
  0.0 0.1 pad_add_fusion.place_ref.before_ref
  0.1 3.1 %cut_kernel.1 = (f32[4,24576]{1,0:T(4,128)}, f32[4,24576]{1,0:T(4,128)}, f32[4,24576]{1,0:T(4,128)}, f32[4,24576]{1,0:T(4,128)}) custom-call(s32[3]{0:T(128)S(1)} %pad_add_fusion.place_ref.before_ref, f32[4,196608]{1,0:T(4,128)} %vectors_ref.1), custom_call_target="tpu_custom_call" | custom-call | tf_op jit(solution)/shard_map/cut_kernel/pallas_call | solution.py:221
  3.2 4.7 %collective-permute-start.4 = (f32[4,24576]{1,0:T(4,128)}, f32[4,24576]{1,0:T(4,128)S(1)}, u32[]{:S(2)}, u32[]{:S(2)}) collective-permute-start(f32[4,24576]{1,0:T(4,128)} %get-tuple-element.34), channel_id=1, source_target_pairs={{0,96},{32,128},{64,160},{96,192},{128,224},{160,0},{192,32},{224,... | collective-permute-start | bytes 1179656 | tf_op jit(solution)/shard_map/ppermute | solution.py:330
  7.9 2.2 %collective-permute-start.5 = (f32[4,24576]{1,0:T(4,128)}, f32[4,24576]{1,0:T(4,128)S(1)}, u32[]{:S(2)}, u32[]{:S(2)}) collective-permute-start(f32[4,24576]{1,0:T(4,128)} %get-tuple-element.35), channel_id=1, source_target_pairs={{0,160},{32,192},{64,224},{96,0},{128,32},{160,64},{192,96},{224,1... | collective-permute-start | bytes 1179656 | tf_op jit(solution)/shard_map/ppermute | solution.py:330
  10.1 1.0 collective-permute-start
  11.1 2.2 %collective-permute-start.1 = (f32[4,24576]{1,0:T(4,128)}, f32[4,24576]{1,0:T(4,128)S(1)}, u32[]{:S(2)}, u32[]{:S(2)}) collective-permute-start(f32[4,24576]{1,0:T(4,128)} %get-tuple-element.28), channel_id=1, source_target_pairs={{0,224},{32,0},{64,32},{96,64},{128,96},{160,128},{192,160},{224,1... | collective-permute-start | bytes 1179656 | tf_op jit(solution)/shard_map/ppermute | solution.py:330
  13.3 4.1 %even.1 = f32[16,4,6144]{2,1,0:T(4,128)} custom-call(s32[3]{0:T(128)S(1)} %pad_add_fusion.place_ref.before_ref, f32[4,196608]{1,0:T(4,128)} %vectors_ref.1, s32[3]{0:T(128)S(1)} %pad_add_fusion.place_ref.before_ref), custom_call_target="tpu_custom_call" | custom-call | tf_op jit(solution)/shard_map/even/pallas_call | solution.py:235
  17.5 9.4 %all-to-all-start = ((f32[16,4,6144]{2,1,0:T(4,128)}), f32[16,4,6144]{2,1,0:T(4,128)S(1)}, u32[]{:S(2)}, u32[]{:S(2)}) async-start(f32[16,4,6144]{2,1,0:T(4,128)} %even.1), calls=%async_computation | async-start | bytes 3145728 | tf_op jit(solution)/shard_map/all_to_all | solution.py:343
  26.9 8.8 %gram.1 = (bf16[256,6144]{1,0:T(8,128)(2,1)}, bf16[256,6144]{1,0:T(8,128)(2,1)}, f32[96,128]{1,0:T(8,128)S(1)}, f32[96,128]{1,0:T(8,128)S(1)}) custom-call(s32[1]{0:T(128)} %bitcast.core_ref, f32[4,64,6144]{2,1,0:T(8,128)} %householder_ref.1, s32[3]{0:T(128)S(1)} %pad_add_fusion.place_ref.before_ref), custom_call_target="tpu_custom_call" | custom-call | flops 32212254720 | bytes 12582912 | tf_op jit(solution)/shard_map/gram/pallas_call | solution.py:197
  35.7 0.4 collective-permute-start.6
  36.1 0.9 collective-permute-done.6
  37.0 3.4 %collective-permute-start.7 = (f32[96,128]{1,0:T(8,128)S(1)}, f32[96,128]{1,0:T(8,128)S(1)}, u32[]{:S(2)}, u32[]{:S(2)}) collective-permute-start(f32[96,128]{1,0:T(8,128)S(1)} %add.31), channel_id=1, source_target_pairs={{0,16},{8,24},{16,0},{24,8},{32,48},{40,56},{48,32},{56,40},{64,80... | collective-permute-start | bytes 147464 | tf_op jit(solution)/shard_map/ppermute | solution.py:319
  40.4 2.2 %collective-permute-done.7 = f32[96,128]{1,0:T(8,128)S(1)} collective-permute-done((f32[96,128]{1,0:T(8,128)S(1)}, f32[96,128]{1,0:T(8,128)S(1)}, u32[]{:S(2)}, u32[]{:S(2)}) %collective-permute-start.7) | collective-permute-done | bytes 49184 | tf_op jit(solution)/shard_map/ppermute | solution.py:319
  42.6 0.0 collective-permute-done.4.up_ref
  42.7 0.0 collective-permute-done.5.down_ref
  42.7 0.6 side_kernel.3
  43.3 3.5 %collective-permute-start.8 = (f32[2,4,12288]{2,1,0:T(4,128)S(1)}, f32[2,4,12288]{2,1,0:T(4,128)S(1)}, u32[]{:S(2)}, u32[]{:S(2)}) collective-permute-start(f32[2,4,12288]{2,1,0:T(4,128)S(1)} %get-tuple-element.38), channel_id=1, source_target_pairs={{0,16},{8,24},{16,0},{24,8},{32,48},{40,56},{48,32},{56,40},{64,80... | collective-permute-start | bytes 1179656 | tf_op jit(solution)/shard_map/ppermute | solution.py:319
  46.7 0.0 collective-permute-done.up_ref
  46.7 2.6 %collective-permute-done.1.down_ref = f32[4,24576]{1,0:T(4,128)S(1)} collective-permute-done((f32[4,24576]{1,0:T(4,128)}, f32[4,24576]{1,0:T(4,128)S(1)}, u32[]{:S(2)}, u32[]{:S(2)}) %collective-permute-start.1) | collective-permute-done | bytes 393248 | tf_op jit(solution)/shard_map/ppermute | solution.py:330
  49.3 0.6 side_kernel.2
  49.9 3.3 %collective-permute-start.2 = (f32[2,4,12288]{2,1,0:T(4,128)S(1)}, f32[2,4,12288]{2,1,0:T(4,128)S(1)}, u32[]{:S(2)}, u32[]{:S(2)}) collective-permute-start(f32[2,4,12288]{2,1,0:T(4,128)S(1)} %get-tuple-element.31), channel_id=1, source_target_pairs={{0,16},{8,24},{16,0},{24,8},{32,48},{40,56},{48,32},{56,40},{64,80... | collective-permute-start | bytes 1179656 | tf_op jit(solution)/shard_map/ppermute | solution.py:319
  53.2 8.4 %collective-permute-done.8.got_ref = f32[2,4,12288]{2,1,0:T(4,128)S(1)} collective-permute-done((f32[2,4,12288]{2,1,0:T(4,128)S(1)}, f32[2,4,12288]{2,1,0:T(4,128)S(1)}, u32[]{:S(2)}, u32[]{:S(2)}) %collective-permute-start.8) | collective-permute-done | bytes 393248 | tf_op jit(solution)/shard_map/ppermute | solution.py:319
  61.6 1.4 %core_kernel.3 = (f32[2,2,4,6144]{3,2,1,0:T(4,128)S(1)}, f32[2,2,4,6144]{3,2,1,0:T(4,128)}) custom-call(s32[3]{0:T(128)S(1)} %pad_add_fusion.place_ref.before_ref, f32[2,4,12288]{2,1,0:T(4,128)S(1)} %get-tuple-element.37.own_ref, f32[2,4,12288]{2,1,0:T(4,128)S(1)} %collective-permute-done.8.got_ref), custom_call_target="tpu_custom_call" | custom-call | tf_op jit(solution)/shard_map/core_kernel/pallas_call | solution.py:221
  62.9 0.0 collective-permute-start.9
  62.9 9.5 %collective-permute-done.2.got_ref = f32[2,4,12288]{2,1,0:T(4,128)S(1)} collective-permute-done((f32[2,4,12288]{2,1,0:T(4,128)S(1)}, f32[2,4,12288]{2,1,0:T(4,128)S(1)}, u32[]{:S(2)}, u32[]{:S(2)}) %collective-permute-start.2) | collective-permute-done | bytes 393248 | tf_op jit(solution)/shard_map/ppermute | solution.py:319
  72.5 1.3 %core_kernel.2 = (f32[2,2,4,6144]{3,2,1,0:T(4,128)S(1)}, f32[2,2,4,6144]{3,2,1,0:T(4,128)}) custom-call(s32[3]{0:T(128)S(1)} %pad_add_fusion.place_ref.before_ref, f32[2,4,12288]{2,1,0:T(4,128)S(1)} %get-tuple-element.30.own_ref, f32[2,4,12288]{2,1,0:T(4,128)S(1)} %collective-permute-done.2.got_ref), custom_call_target="tpu_custom_call" | custom-call | tf_op jit(solution)/shard_map/core_kernel/pallas_call | solution.py:221
  73.8 0.0 collective-permute-start.3
  73.8 0.7 collective-permute-start.10
  74.5 6.1 %all-to-all-done.before_ref.even_ref = f32[16,4,6144]{2,1,0:T(4,128)S(1)} async-done(((f32[16,4,6144]{2,1,0:T(4,128)}), f32[16,4,6144]{2,1,0:T(4,128)S(1)}, u32[]{:S(2)}, u32[]{:S(2)}) %all-to-all-start) | async-done | bytes 1572896 | tf_op jit(solution)/shard_map/all_to_all | solution.py:343
  80.7 0.0 collective-permute-done.9.got_three_ref
  80.7 0.0 collective-permute-done.3.got_one_ref
  80.7 0.0 copy-start
  80.7 1.9 %copy-done = bf16[256,6144]{1,0:T(8,128)(2,1)S(1)} copy-done((bf16[256,6144]{1,0:T(8,128)(2,1)S(1)}, bf16[256,6144]{1,0:T(8,128)(2,1)}, u32[]{:S(2)}) %copy-start) | copy-done | bytes 3145752
  82.6 0.0 copy-start.2
  82.6 2.0 %project_high.1 = (f32[128,6144]{1,0:T(8,128)S(1)}, bf16[128,6144]{1,0:T(8,128)(2,1)S(1)}, f32[256,256]{1,0:T(8,128)S(1)}) custom-call(s32[3]{0:T(128)S(1)} %pad_add_fusion.place_ref.before_ref, f32[16,4,6144]{2,1,0:T(4,128)S(1)} %all-to-all-done.before_ref.even_ref, f32[2,2,4,6144]{3,2,1,0:T(4,128)S(1)} %get-tuple-element.32.kept_one_ref, ...), custom_call_target="tpu_custom_call" | custom-call | tf_op jit(solution)/shard_map/project_high/pallas_call | solution.py:265
  84.6 0.0 collective-permute-done.10.more_ref
  84.6 0.0 copy-done.2
  84.6 0.0 copy-start.1
  84.6 0.0 copy-start.3
  84.6 1.0 project_low.1
  85.7 0.1 collective-permute-start.11
  85.8 1.2 %collective-permute-done.11 = f32[128,128]{1,0:T(8,128)S(1)} collective-permute-done((f32[128,128]{1,0:T(8,128)S(1)}, f32[128,128]{1,0:T(8,128)S(1)}, u32[]{:S(2)}, u32[]{:S(2)}) %collective-permute-start.11) | collective-permute-done | bytes 65568 | tf_op jit(solution)/shard_map/ppermute | solution.py:319
  87.0 1.5 %collective-permute-start.12 = (f32[128,128]{1,0:T(8,128)S(1)}, f32[128,128]{1,0:T(8,128)S(1)}, u32[]{:S(2)}, u32[]{:S(2)}) collective-permute-start(f32[128,128]{1,0:T(8,128)S(1)} %add.33), channel_id=1, source_target_pairs={{0,16},{8,24},{16,0},{24,8},{32,48},{40,56},{48,32},{56,40},{64,80... | collective-permute-start | bytes 196616 | tf_op jit(solution)/shard_map/ppermute | solution.py:319
  88.5 4.4 %collective-permute-done.12 = f32[128,128]{1,0:T(8,128)S(1)} collective-permute-done((f32[128,128]{1,0:T(8,128)S(1)}, f32[128,128]{1,0:T(8,128)S(1)}, u32[]{:S(2)}, u32[]{:S(2)}) %collective-permute-start.12) | collective-permute-done | bytes 65568 | tf_op jit(solution)/shard_map/ppermute | solution.py:319
  92.9 1.9 %collective-permute-start.14 = (f32[224,128]{1,0:T(8,128)S(1)}, f32[224,128]{1,0:T(8,128)S(1)}, u32[]{:S(2)}, u32[]{:S(2)}) collective-permute-start(f32[224,128]{1,0:T(8,128)S(1)} %pad_maximum_fusion), channel_id=1, source_target_pairs={{0,64},{8,72},{16,80},{24,88},{32,96},{40,104},{48,112},{56,120},{... | collective-permute-start | bytes 344072 | tf_op jit(solution)/shard_map/ppermute | solution.py:319
  94.8 2.9 %collective-permute-start.13 = (f32[128,128]{1,0:T(8,128)S(1)}, f32[128,128]{1,0:T(8,128)S(1)}, u32[]{:S(2)}, u32[]{:S(2)}) collective-permute-start(f32[128,128]{1,0:T(8,128)S(1)} %add.34), channel_id=1, source_target_pairs={{0,32},{8,40},{16,48},{24,56},{32,0},{40,8},{48,16},{56,24},{64,96... | collective-permute-start | bytes 196616 | tf_op jit(solution)/shard_map/ppermute | solution.py:319
  97.7 0.0 collective-permute-start.15
  97.7 4.9 %collective-permute-done.14 = f32[224,128]{1,0:T(8,128)S(1)} collective-permute-done((f32[224,128]{1,0:T(8,128)S(1)}, f32[224,128]{1,0:T(8,128)S(1)}, u32[]{:S(2)}, u32[]{:S(2)}) %collective-permute-start.14) | collective-permute-done | bytes 114720 | tf_op jit(solution)/shard_map/ppermute | solution.py:319
  102.6 0.0 collective-permute-done.13
  102.6 1.2 %collective-permute-done.15 = f32[128,128]{1,0:T(8,128)S(1)} collective-permute-done((f32[128,128]{1,0:T(8,128)S(1)}, f32[128,128]{1,0:T(8,128)S(1)}, u32[]{:S(2)}, u32[]{:S(2)}) %collective-permute-start.15) | collective-permute-done | bytes 65568 | tf_op jit(solution)/shard_map/ppermute | solution.py:319
  103.9 2.1 %collective-permute-start.16 = (f32[224,128]{1,0:T(8,128)S(1)}, f32[224,128]{1,0:T(8,128)S(1)}, u32[]{:S(2)}, u32[]{:S(2)}) collective-permute-start(f32[224,128]{1,0:T(8,128)S(1)} %pad_maximum_fusion.1), channel_id=1, source_target_pairs={{0,192},{8,200},{16,208},{24,216},{32,224},{40,232},{48,240},{56,2... | collective-permute-start | bytes 344072 | tf_op jit(solution)/shard_map/ppermute | solution.py:319
  106.0 5.0 %collective-permute-done.16 = f32[224,128]{1,0:T(8,128)S(1)} collective-permute-done((f32[224,128]{1,0:T(8,128)S(1)}, f32[224,128]{1,0:T(8,128)S(1)}, u32[]{:S(2)}, u32[]{:S(2)}) %collective-permute-start.16) | collective-permute-done | bytes 114720 | tf_op jit(solution)/shard_map/ppermute | solution.py:319
  111.0 0.1 collective-permute-start.17
  111.1 1.3 %collective-permute-done.17.other_ref = f32[224,128]{1,0:T(8,128)S(1)} collective-permute-done((f32[224,128]{1,0:T(8,128)S(1)}, f32[224,128]{1,0:T(8,128)S(1)}, u32[]{:S(2)}, u32[]{:S(2)}) %collective-permute-start.17) | collective-permute-done | bytes 114720 | tf_op jit(solution)/shard_map/ppermute | solution.py:319
  112.4 0.0 copy-done.1
  112.4 0.0 copy-done.3
  112.4 3.4 %finish.1 = f32[128,6144]{1,0:T(8,128)} custom-call(s32[1]{0:T(128)} %bitcast.core_ref, f32[224,128]{1,0:T(8,128)S(1)} %fusion.1.own_ref, f32[224,128]{1,0:T(8,128)S(1)} %collective-permute-done.17.other_ref, f32[4,64,64]{2,1,0:T(8,128)S(1)} %copy-done.3, f32[128,6144]{1,0:T(8,128)S(1)} %get-tuple-element.48.current_ref, bf16[256,6144]{1,0:T(8,128)(2,1)S(1)} %copy-done.1, ...), custom_call_target="tpu_custom_call" | custom-call | tf_op jit(solution)/shard_map/finish/pallas_call | solution.py:296
  (10 shorter events, 0.1 us)
Async XLA Ops:
  3.2 39.5 %collective-permute-start.4 = (f32[4,24576]{1,0:T(4,128)}, f32[4,24576]{1,0:T(4,128)S(1)}, u32[]{:S(2)}, u32[]{:S(2)}) collective-permute-start(f32[4,24576]{1,0:T(4,128)} %get-tuple-element.34), channel_id=1, source_target_pairs={{0,96},{32,128},{64,160},{96,192},{128,224},{160,0},{192,32},{224,... | collective-permute-start | bytes 1179656 | tf_op jit(solution)/shard_map/ppermute | solution.py:330
  7.9 34.8 %collective-permute-start.5 = (f32[4,24576]{1,0:T(4,128)}, f32[4,24576]{1,0:T(4,128)S(1)}, u32[]{:S(2)}, u32[]{:S(2)}) collective-permute-start(f32[4,24576]{1,0:T(4,128)} %get-tuple-element.35), channel_id=1, source_target_pairs={{0,160},{32,192},{64,224},{96,0},{128,32},{160,64},{192,96},{224,1... | collective-permute-start | bytes 1179656 | tf_op jit(solution)/shard_map/ppermute | solution.py:330
  10.1 36.6 %collective-permute-start = (f32[4,24576]{1,0:T(4,128)}, f32[4,24576]{1,0:T(4,128)S(1)}, u32[]{:S(2)}, u32[]{:S(2)}) collective-permute-start(f32[4,24576]{1,0:T(4,128)} %get-tuple-element.27), channel_id=1, source_target_pairs={{0,32},{32,64},{64,96},{96,128},{128,160},{160,192},{192,224},{224... | collective-permute-start | bytes 1179656 | tf_op jit(solution)/shard_map/ppermute | solution.py:330
  11.1 38.2 %collective-permute-start.1 = (f32[4,24576]{1,0:T(4,128)}, f32[4,24576]{1,0:T(4,128)S(1)}, u32[]{:S(2)}, u32[]{:S(2)}) collective-permute-start(f32[4,24576]{1,0:T(4,128)} %get-tuple-element.28), channel_id=1, source_target_pairs={{0,224},{32,0},{64,32},{96,64},{128,96},{160,128},{192,160},{224,1... | collective-permute-start | bytes 1179656 | tf_op jit(solution)/shard_map/ppermute | solution.py:330
  17.5 63.2 %all-to-all-start = ((f32[16,4,6144]{2,1,0:T(4,128)}), f32[16,4,6144]{2,1,0:T(4,128)S(1)}, u32[]{:S(2)}, u32[]{:S(2)}) async-start(f32[16,4,6144]{2,1,0:T(4,128)} %even.1), calls=%async_computation | async-start | bytes 3145728 | tf_op jit(solution)/shard_map/all_to_all | solution.py:343
  35.7 1.3 %collective-permute-start.6 = (f32[96,128]{1,0:T(8,128)S(1)}, f32[96,128]{1,0:T(8,128)S(1)}, u32[]{:S(2)}, u32[]{:S(2)}) collective-permute-start(f32[96,128]{1,0:T(8,128)S(1)} %get-tuple-element.36), channel_id=1, source_target_pairs={{0,8},{8,0},{16,24},{24,16},{32,40},{40,32},{48,56},{56,48},{64,72... | collective-permute-start | bytes 147464 | tf_op jit(solution)/shard_map/ppermute | solution.py:319
  37.0 5.7 %collective-permute-start.7 = (f32[96,128]{1,0:T(8,128)S(1)}, f32[96,128]{1,0:T(8,128)S(1)}, u32[]{:S(2)}, u32[]{:S(2)}) collective-permute-start(f32[96,128]{1,0:T(8,128)S(1)} %add.31), channel_id=1, source_target_pairs={{0,16},{8,24},{16,0},{24,8},{32,48},{40,56},{48,32},{56,40},{64,80... | collective-permute-start | bytes 147464 | tf_op jit(solution)/shard_map/ppermute | solution.py:319
  43.3 18.3 %collective-permute-start.8 = (f32[2,4,12288]{2,1,0:T(4,128)S(1)}, f32[2,4,12288]{2,1,0:T(4,128)S(1)}, u32[]{:S(2)}, u32[]{:S(2)}) collective-permute-start(f32[2,4,12288]{2,1,0:T(4,128)S(1)} %get-tuple-element.38), channel_id=1, source_target_pairs={{0,16},{8,24},{16,0},{24,8},{32,48},{40,56},{48,32},{56,40},{64,80... | collective-permute-start | bytes 1179656 | tf_op jit(solution)/shard_map/ppermute | solution.py:319
  49.9 22.6 %collective-permute-start.2 = (f32[2,4,12288]{2,1,0:T(4,128)S(1)}, f32[2,4,12288]{2,1,0:T(4,128)S(1)}, u32[]{:S(2)}, u32[]{:S(2)}) collective-permute-start(f32[2,4,12288]{2,1,0:T(4,128)S(1)} %get-tuple-element.31), channel_id=1, source_target_pairs={{0,16},{8,24},{16,0},{24,8},{32,48},{40,56},{48,32},{56,40},{64,80... | collective-permute-start | bytes 1179656 | tf_op jit(solution)/shard_map/ppermute | solution.py:319
  62.9 17.7 %collective-permute-start.9 = (f32[2,2,4,6144]{3,2,1,0:T(4,128)}, f32[2,2,4,6144]{3,2,1,0:T(4,128)S(1)}, u32[]{:S(2)}, u32[]{:S(2)}) collective-permute-start(f32[2,2,4,6144]{3,2,1,0:T(4,128)} %get-tuple-element.40), channel_id=1, source_target_pairs={{0,8},{8,0},{16,24},{24,16},{32,40},{40,32},{48,56},{56,48},{64,72... | collective-permute-start | bytes 1179656 | tf_op jit(solution)/shard_map/ppermute | solution.py:319
  73.8 6.9 %collective-permute-start.3 = (f32[2,2,4,6144]{3,2,1,0:T(4,128)}, f32[2,2,4,6144]{3,2,1,0:T(4,128)S(1)}, u32[]{:S(2)}, u32[]{:S(2)}) collective-permute-start(f32[2,2,4,6144]{3,2,1,0:T(4,128)} %get-tuple-element.33), channel_id=1, source_target_pairs={{0,8},{8,0},{16,24},{24,16},{32,40},{40,32},{48,56},{56,48},{64,72... | collective-permute-start | bytes 1179656 | tf_op jit(solution)/shard_map/ppermute | solution.py:319
  73.8 10.8 %collective-permute-start.10 = (f32[96,128]{1,0:T(8,128)S(1)}, f32[96,128]{1,0:T(8,128)S(1)}, u32[]{:S(2)}, u32[]{:S(2)}) collective-permute-start(f32[96,128]{1,0:T(8,128)S(1)} %add.32.before_ref.gram_ref), channel_id=1, source_target_pairs={{0,32},{8,40},{16,48},{24,56},{32,0},{40,8},{48,16},{56,24},{64,96... | collective-permute-start | bytes 147464 | tf_op jit(solution)/shard_map/ppermute | solution.py:319
  80.7 1.9 %copy-start = (bf16[256,6144]{1,0:T(8,128)(2,1)S(1)}, bf16[256,6144]{1,0:T(8,128)(2,1)}, u32[]{:S(2)}) copy-start(bf16[256,6144]{1,0:T(8,128)(2,1)} %after.1.high_ref) | copy-start | bytes 9437188
  82.6 2.0 %copy-start.2 = (bf16[256,6144]{1,0:T(8,128)(2,1)S(1)}, bf16[256,6144]{1,0:T(8,128)(2,1)}, u32[]{:S(2)}) copy-start(bf16[256,6144]{1,0:T(8,128)(2,1)} %get-tuple-element.44.low_ref) | copy-start | bytes 9437188
  84.6 27.8 %copy-start.1 = (bf16[256,6144]{1,0:T(8,128)(2,1)S(1)}, bf16[256,6144]{1,0:T(8,128)(2,1)}, u32[]{:S(2)}) copy-start(bf16[256,6144]{1,0:T(8,128)(2,1)} %after.1.high_ref) | copy-start | bytes 9437188
  84.6 27.8 %copy-start.3 = (f32[4,64,64]{2,1,0:T(8,128)S(1)}, f32[4,64,64]{2,1,0:T(8,128)}, u32[]{:S(2)}) copy-start(f32[4,64,64]{2,1,0:T(8,128)} %tfactors_ref.1) | copy-start | bytes 196612
  85.7 1.3 %collective-permute-start.11 = (f32[128,128]{1,0:T(8,128)S(1)}, f32[128,128]{1,0:T(8,128)S(1)}, u32[]{:S(2)}, u32[]{:S(2)}) collective-permute-start(f32[128,128]{1,0:T(8,128)S(1)} %get-tuple-element.46), channel_id=1, source_target_pairs={{0,8},{8,0},{16,24},{24,16},{32,40},{40,32},{48,56},{56,48},{64,72... | collective-permute-start | bytes 196616 | tf_op jit(solution)/shard_map/ppermute | solution.py:319
  87.0 5.9 %collective-permute-start.12 = (f32[128,128]{1,0:T(8,128)S(1)}, f32[128,128]{1,0:T(8,128)S(1)}, u32[]{:S(2)}, u32[]{:S(2)}) collective-permute-start(f32[128,128]{1,0:T(8,128)S(1)} %add.33), channel_id=1, source_target_pairs={{0,16},{8,24},{16,0},{24,8},{32,48},{40,56},{48,32},{56,40},{64,80... | collective-permute-start | bytes 196616 | tf_op jit(solution)/shard_map/ppermute | solution.py:319
  92.9 9.7 %collective-permute-start.14 = (f32[224,128]{1,0:T(8,128)S(1)}, f32[224,128]{1,0:T(8,128)S(1)}, u32[]{:S(2)}, u32[]{:S(2)}) collective-permute-start(f32[224,128]{1,0:T(8,128)S(1)} %pad_maximum_fusion), channel_id=1, source_target_pairs={{0,64},{8,72},{16,80},{24,88},{32,96},{40,104},{48,112},{56,120},{... | collective-permute-start | bytes 344072 | tf_op jit(solution)/shard_map/ppermute | solution.py:319
  94.8 7.8 %collective-permute-start.13 = (f32[128,128]{1,0:T(8,128)S(1)}, f32[128,128]{1,0:T(8,128)S(1)}, u32[]{:S(2)}, u32[]{:S(2)}) collective-permute-start(f32[128,128]{1,0:T(8,128)S(1)} %add.34), channel_id=1, source_target_pairs={{0,32},{8,40},{16,48},{24,56},{32,0},{40,8},{48,16},{56,24},{64,96... | collective-permute-start | bytes 196616 | tf_op jit(solution)/shard_map/ppermute | solution.py:319
  97.7 6.2 %collective-permute-start.15 = (f32[128,128]{1,0:T(8,128)S(1)}, f32[128,128]{1,0:T(8,128)S(1)}, u32[]{:S(2)}, u32[]{:S(2)}) collective-permute-start(f32[128,128]{1,0:T(8,128)S(1)} %add.34), channel_id=1, source_target_pairs={{0,96},{8,104},{16,112},{24,120},{32,64},{40,72},{48,80},{56,88},{... | collective-permute-start | bytes 196616 | tf_op jit(solution)/shard_map/ppermute | solution.py:319
  103.9 7.1 %collective-permute-start.16 = (f32[224,128]{1,0:T(8,128)S(1)}, f32[224,128]{1,0:T(8,128)S(1)}, u32[]{:S(2)}, u32[]{:S(2)}) collective-permute-start(f32[224,128]{1,0:T(8,128)S(1)} %pad_maximum_fusion.1), channel_id=1, source_target_pairs={{0,192},{8,200},{16,208},{24,216},{32,224},{40,232},{48,240},{56,2... | collective-permute-start | bytes 344072 | tf_op jit(solution)/shard_map/ppermute | solution.py:319
  111.0 1.4 %collective-permute-start.17 = (f32[224,128]{1,0:T(8,128)S(1)}, f32[224,128]{1,0:T(8,128)S(1)}, u32[]{:S(2)}, u32[]{:S(2)}) collective-permute-start(f32[224,128]{1,0:T(8,128)S(1)} %fusion.1.own_ref), channel_id=1, source_target_pairs={{0,8},{8,0},{16,24},{24,16},{32,40},{40,32},{48,56},{56,48},{64,72... | collective-permute-start | bytes 344072 | tf_op jit(solution)/shard_map/ppermute | solution.py:319

commit v12 on v11

--- a/solution.py
+++ b/solution.py
@@ -10,7 +10,7 @@
 
 COLUMNS = 1024
 OUT_COLUMNS = 2048
-SHIFTS = (1, -1, 3, -3)
+NEAR, FAR = (1, -1), (3, -3)
 LIMIT = 40 * 1024 * 1024
 IN_VMEM = pl.BlockSpec(memory_space=pltpu.VMEM)
 IN_SMEM = pl.BlockSpec(memory_space=pltpu.SMEM)
@@ -69,12 +69,12 @@
         halves(core_ref[0], packed, kept_ref, sent_ref)
 
 
-def cut_kernel(place_ref, vectors_ref, *refs):
+def cut_kernel(shifts, place_ref, vectors_ref, *refs):
     outs, sems = refs[:-1], refs[-1]
     wide = outs[0].shape[1]
     planes = vectors_ref.shape[1] // wide
     copies = []
-    for i, shift in enumerate(SHIFTS):
+    for i, shift in enumerate(shifts):
         plane = (place_ref[0] + shift + planes) % planes
         columns = pl.ds(pl.multiple_of(plane * wide, 128), wide)
         copies.append(pltpu.make_async_copy(vectors_ref.at[:, columns], outs[i], sems.at[i]))
@@ -157,16 +157,22 @@
     for side, part_ref in ((core, own_ref), (1 - core, other_ref)):
         joint[pl.ds(pl.multiple_of(side * half, 8), half), :] = part_ref[:half, :]
         packed[pl.ds(pl.multiple_of(side * rest, 8), rest), :] = part_ref[half:, :]
-    gram = {}
-    for i, pair in enumerate(pairs_of(panels)):
-        at = i // 2 * width
-        gram[pair] = packed[at : at + width, i % 2 * width : (i % 2 + 1) * width]
+    pairs = pairs_of(panels)
     exact = functools.partial(product, contract=((1,), (0,)), precision=lax.Precision.HIGHEST)
-    scaled = [exact(tfactors_ref[p], joint[p * width : (p + 1) * width, :]) for p in range(panels)]
-    links = {(p, q): exact(tfactors_ref[p], gram[p, q]) for p, q in gram}
+    scaled, links = [], {}
+    for p in range(panels):
+        tiles = sorted({i // 2 for i, pair in enumerate(pairs) if pair[0] == p})
+        right = [joint[p * width : (p + 1) * width, :]] + [packed[i * width : (i + 1) * width, :] for i in tiles]
+        whole = exact(tfactors_ref[p], jnp.concatenate(right, axis=1))
+        scaled.append(whole[:, :count])
+        for i, pair in enumerate(pairs):
+            if pair[0] == p:
+                at = count + tiles.index(i // 2) * 2 * width + i % 2 * width
+                links[pair] = whole[:, at : at + width]
     for q in range(panels - 1, 0, -1):
+        less = exact(jnp.concatenate([links[p, q] for p in range(q)], axis=0), scaled[q])
         for p in range(q):
-            scaled[p] = scaled[p] - exact(links[p, q], scaled[q])
+            scaled[p] = scaled[p] - less[p * width : (p + 1) * width]
     high, low = split(jnp.concatenate(scaled, axis=0).T)
     both = jnp.concatenate([high, low], axis=0)
     copies = []
@@ -225,7 +231,7 @@
         out_specs=tuple(IN_HBM if out.memory_space == pltpu.HBM else IN_VMEM for out in outs),
         scratch_shapes=[pltpu.SemaphoreType.DMA((copies,))] if copies else [],
         compiler_params=pltpu.CompilerParams(vmem_limit_bytes=LIMIT),
-        name=kernel.__name__,
+        name=getattr(kernel, "__name__", "cut"),
     )(*operands)
 
 
@@ -337,8 +343,11 @@
             return kept, swap(sent, 1)
 
         block = pltpu.VMEM((each, wide), jnp.float32)
-        cut = local_call(cut_kernel, (block,) * len(SHIFTS), [IN_HBM], (place, in_hbm(vectors_in)), len(SHIFTS))
-        came = [moved(part, shift) for part, shift in zip(cut, SHIFTS)]
+        came = []
+        for shifts in (NEAR, FAR):
+            kernel = functools.partial(cut_kernel, shifts)
+            cut = local_call(kernel, (block,) * len(shifts), [IN_HBM], (place, in_hbm(vectors_in)), len(shifts))
+            came += [moved(part, shift) for part, shift in zip(cut, shifts)]
         even = even_call(place, vectors_in, place, planes)
         even = lax.all_to_all(even, ("half", "y", "core"), split_axis=0, concat_axis=0, tiled=True)
         high, low, kept, sent = gram_call(core, householder, place)

time: 117 us -> 117 us (level)
  waiting for transfers between devices: 47.8 us -> 42.7 us
  starting transfers between devices: 39.5 us -> 41.9 us
  Pallas kernels: 26.3 us -> 28.6 us
    all_to_all x1, waiting for transfers between devices: 6.13 us -> 1.3 us  [shards(): lax.all_to_all(even, ('half', 'y', 'core'), split_axis=0, concat_axis=0,...]
    ppermute x4, waiting for transfers between devices: 2.58 us -> 0.01 us  [moved(): lax.ppermute(part, ('half', 'odd'), [(i, (i + shift) % planes) for i in r...]
    ppermute x14, starting transfers between devices: 19.9 us -> 22.3 us  [swap(): return lax.ppermute(value, row, [(i, i ^ flip) for i in range(devices)])]
    ppermute x14, waiting for transfers between devices: 39 us -> 41.3 us  [swap(): return lax.ppermute(value, row, [(i, i ^ flip) for i in range(devices)])]
    pallas_call x5 -> x6, Pallas kernels: 7.01 us -> 9.08 us  [local_call(): pl.pallas_call(kernel, out_shape=outs, in_specs=[IN_SMEM] + specs, out_sp...]
  transfers between devices with their start and end apart: 19 -> 19, of which waited for: 12 -> 11; matrix products, arithmetic and copies ran while one was open for 0% -> 0% of each run, Pallas kernels for 16% -> 19%
where the time goes in v12:
time: 117 us; the launch traced here: 116 us
  waiting for transfers between devices  42.7 us (36%)
  starting transfers between devices  41.9 us (36%)
  Pallas kernels  28.6 us (24%)
  local copies, waits for them, and re-layouts  1.9 us (2%)
    ppermute x14, waiting for transfers between devices, swap(): return lax.ppermute(value, row, [(i, i ^ flip) for i in range(devices)])  41.3 us
    ppermute x14, starting transfers between devices, swap(): return lax.ppermute(value, row, [(i, i ^ flip) for i in range(devices)])  22.3 us
    ppermute x4, starting transfers between devices, moved(): lax.ppermute(part, ('half', 'odd'), [(i, (i + shift) % planes) for i in r...  10.2 us
    all_to_all x1, starting transfers between devices, shards(): lax.all_to_all(even, ('half', 'y', 'core'), split_axis=0, concat_axis=0,...  9.4 us
    pallas_call x6, Pallas kernels, local_call(): pl.pallas_call(kernel, out_shape=outs, in_specs=[IN_SMEM] + specs, out_sp...  9.08 us
    pallas_call x1, Pallas kernels, gram_call(): pl.pallas_call(gram_kernel, out_shape=(pltpu.HBM((size, rows), jnp.bfloat...  8.8 us
    pallas_call x1, Pallas kernels, even_call(): pl.pallas_call(even_kernel, out_shape=pltpu.HBM((planes * 2, each, wide /...  4.14 us
    pallas_call x1, Pallas kernels, finish_call(): pl.pallas_call(finish_kernel, out_shape=jax.ShapeDtypeStruct((count, rows...  3.58 us
  transfers between devices with their start and end apart: 19, of which 11 were waited for; matrix products, arithmetic and copies ran while one was open for 0% of the time, Pallas kernels for 19%

profile of v12, /device:TPU:4, one launch (start us, length us, event | category | flops | bytes accessed | tf_op | source)
XLA Modules:
  0.0 115.6 jit_solution(5123399545661342930)
XLA Ops:
  0.0 0.1 pad_add_fusion.place_ref.before_ref
  0.1 2.6 %cut.3 = (f32[4,24576]{1,0:T(4,128)}, f32[4,24576]{1,0:T(4,128)}) custom-call(s32[3]{0:T(128)S(1)} %pad_add_fusion.place_ref.before_ref, f32[4,196608]{1,0:T(4,128)} %vectors_ref.3), custom_call_target="tpu_custom_call" | custom-call | tf_op jit(solution)/shard_map/cut/pallas_call | solution.py:227
  2.7 4.7 %collective-permute-start.4 = (f32[4,24576]{1,0:T(4,128)}, f32[4,24576]{1,0:T(4,128)S(1)}, u32[]{:S(2)}, u32[]{:S(2)}) collective-permute-start(f32[4,24576]{1,0:T(4,128)} %get-tuple-element.34), channel_id=1, source_target_pairs={{0,96},{32,128},{64,160},{96,192},{128,224},{160,0},{192,32},{224,... | collective-permute-start | bytes 1179656 | tf_op jit(solution)/shard_map/ppermute | solution.py:336
  7.4 2.2 %collective-permute-start.5 = (f32[4,24576]{1,0:T(4,128)}, f32[4,24576]{1,0:T(4,128)S(1)}, u32[]{:S(2)}, u32[]{:S(2)}) collective-permute-start(f32[4,24576]{1,0:T(4,128)} %get-tuple-element.35), channel_id=1, source_target_pairs={{0,160},{32,192},{64,224},{96,0},{128,32},{160,64},{192,96},{224,1... | collective-permute-start | bytes 1179656 | tf_op jit(solution)/shard_map/ppermute | solution.py:336
  9.6 2.6 %cut.2 = (f32[4,24576]{1,0:T(4,128)}, f32[4,24576]{1,0:T(4,128)}) custom-call(s32[3]{0:T(128)S(1)} %pad_add_fusion.place_ref.before_ref, f32[4,196608]{1,0:T(4,128)} %vectors_ref.3), custom_call_target="tpu_custom_call" | custom-call | tf_op jit(solution)/shard_map/cut/pallas_call | solution.py:227
  12.2 1.1 collective-permute-start
  13.3 2.2 %collective-permute-start.1 = (f32[4,24576]{1,0:T(4,128)}, f32[4,24576]{1,0:T(4,128)S(1)}, u32[]{:S(2)}, u32[]{:S(2)}) collective-permute-start(f32[4,24576]{1,0:T(4,128)} %get-tuple-element.28), channel_id=1, source_target_pairs={{0,224},{32,0},{64,32},{96,64},{128,96},{160,128},{192,160},{224,1... | collective-permute-start | bytes 1179656 | tf_op jit(solution)/shard_map/ppermute | solution.py:336
  15.5 4.1 %even.1 = f32[16,4,6144]{2,1,0:T(4,128)} custom-call(s32[3]{0:T(128)S(1)} %pad_add_fusion.place_ref.before_ref, f32[4,196608]{1,0:T(4,128)} %vectors_ref.3, s32[3]{0:T(128)S(1)} %pad_add_fusion.place_ref.before_ref), custom_call_target="tpu_custom_call" | custom-call | tf_op jit(solution)/shard_map/even/pallas_call | solution.py:241
  19.6 9.4 %all-to-all-start = ((f32[16,4,6144]{2,1,0:T(4,128)}), f32[16,4,6144]{2,1,0:T(4,128)S(1)}, u32[]{:S(2)}, u32[]{:S(2)}) async-start(f32[16,4,6144]{2,1,0:T(4,128)} %even.1), calls=%async_computation | async-start | bytes 3145728 | tf_op jit(solution)/shard_map/all_to_all | solution.py:352
  29.0 8.8 %gram.1 = (bf16[256,6144]{1,0:T(8,128)(2,1)}, bf16[256,6144]{1,0:T(8,128)(2,1)}, f32[96,128]{1,0:T(8,128)S(1)}, f32[96,128]{1,0:T(8,128)S(1)}) custom-call(s32[1]{0:T(128)} %bitcast.core_ref, f32[4,64,6144]{2,1,0:T(8,128)} %householder_ref.1, s32[3]{0:T(128)S(1)} %pad_add_fusion.place_ref.before_ref), custom_call_target="tpu_custom_call" | custom-call | flops 32212254720 | bytes 12582912 | tf_op jit(solution)/shard_map/gram/pallas_call | solution.py:203
  37.8 0.4 collective-permute-start.6
  38.2 0.9 collective-permute-done.6
  39.1 3.4 %collective-permute-start.7 = (f32[96,128]{1,0:T(8,128)S(1)}, f32[96,128]{1,0:T(8,128)S(1)}, u32[]{:S(2)}, u32[]{:S(2)}) collective-permute-start(f32[96,128]{1,0:T(8,128)S(1)} %add.31), channel_id=1, source_target_pairs={{0,16},{8,24},{16,0},{24,8},{32,48},{40,56},{48,32},{56,40},{64,80... | collective-permute-start | bytes 147464 | tf_op jit(solution)/shard_map/ppermute | solution.py:325
  42.6 2.2 %collective-permute-done.7 = f32[96,128]{1,0:T(8,128)S(1)} collective-permute-done((f32[96,128]{1,0:T(8,128)S(1)}, f32[96,128]{1,0:T(8,128)S(1)}, u32[]{:S(2)}, u32[]{:S(2)}) %collective-permute-start.7) | collective-permute-done | bytes 49184 | tf_op jit(solution)/shard_map/ppermute | solution.py:325
  44.8 0.0 collective-permute-done.4.up_ref
  44.8 0.0 collective-permute-done.5.down_ref
  44.8 0.6 side_kernel.3
  45.4 3.5 %collective-permute-start.8 = (f32[2,4,12288]{2,1,0:T(4,128)S(1)}, f32[2,4,12288]{2,1,0:T(4,128)S(1)}, u32[]{:S(2)}, u32[]{:S(2)}) collective-permute-start(f32[2,4,12288]{2,1,0:T(4,128)S(1)} %get-tuple-element.38), channel_id=1, source_target_pairs={{0,16},{8,24},{16,0},{24,8},{32,48},{40,56},{48,32},{56,40},{64,80... | collective-permute-start | bytes 1179656 | tf_op jit(solution)/shard_map/ppermute | solution.py:325
  48.9 0.0 collective-permute-done.up_ref
  48.9 0.0 collective-permute-done.1.down_ref
  48.9 0.6 side_kernel.2
  49.5 3.2 %collective-permute-start.2 = (f32[2,4,12288]{2,1,0:T(4,128)S(1)}, f32[2,4,12288]{2,1,0:T(4,128)S(1)}, u32[]{:S(2)}, u32[]{:S(2)}) collective-permute-start(f32[2,4,12288]{2,1,0:T(4,128)S(1)} %get-tuple-element.31), channel_id=1, source_target_pairs={{0,16},{8,24},{16,0},{24,8},{32,48},{40,56},{48,32},{56,40},{64,80... | collective-permute-start | bytes 1179656 | tf_op jit(solution)/shard_map/ppermute | solution.py:325
  52.7 10.2 %collective-permute-done.8.got_ref = f32[2,4,12288]{2,1,0:T(4,128)S(1)} collective-permute-done((f32[2,4,12288]{2,1,0:T(4,128)S(1)}, f32[2,4,12288]{2,1,0:T(4,128)S(1)}, u32[]{:S(2)}, u32[]{:S(2)}) %collective-permute-start.8) | collective-permute-done | bytes 393248 | tf_op jit(solution)/shard_map/ppermute | solution.py:325
  62.9 1.4 %core_kernel.3 = (f32[2,2,4,6144]{3,2,1,0:T(4,128)S(1)}, f32[2,2,4,6144]{3,2,1,0:T(4,128)}) custom-call(s32[3]{0:T(128)S(1)} %pad_add_fusion.place_ref.before_ref, f32[2,4,12288]{2,1,0:T(4,128)S(1)} %get-tuple-element.37.own_ref, f32[2,4,12288]{2,1,0:T(4,128)S(1)} %collective-permute-done.8.got_ref), custom_call_target="tpu_custom_call" | custom-call | tf_op jit(solution)/shard_map/core_kernel/pallas_call | solution.py:227
  64.2 0.0 collective-permute-start.9
  64.2 11.8 %collective-permute-done.2.got_ref = f32[2,4,12288]{2,1,0:T(4,128)S(1)} collective-permute-done((f32[2,4,12288]{2,1,0:T(4,128)S(1)}, f32[2,4,12288]{2,1,0:T(4,128)S(1)}, u32[]{:S(2)}, u32[]{:S(2)}) %collective-permute-start.2) | collective-permute-done | bytes 393248 | tf_op jit(solution)/shard_map/ppermute | solution.py:325
  76.1 1.4 %core_kernel.2 = (f32[2,2,4,6144]{3,2,1,0:T(4,128)S(1)}, f32[2,2,4,6144]{3,2,1,0:T(4,128)}) custom-call(s32[3]{0:T(128)S(1)} %pad_add_fusion.place_ref.before_ref, f32[2,4,12288]{2,1,0:T(4,128)S(1)} %get-tuple-element.30.own_ref, f32[2,4,12288]{2,1,0:T(4,128)S(1)} %collective-permute-done.2.got_ref), custom_call_target="tpu_custom_call" | custom-call | tf_op jit(solution)/shard_map/core_kernel/pallas_call | solution.py:227
  77.5 0.0 collective-permute-start.3
  77.5 1.4 %collective-permute-start.10 = (f32[96,128]{1,0:T(8,128)S(1)}, f32[96,128]{1,0:T(8,128)S(1)}, u32[]{:S(2)}, u32[]{:S(2)}) collective-permute-start(f32[96,128]{1,0:T(8,128)S(1)} %add.32.before_ref.gram_ref), channel_id=1, source_target_pairs={{0,32},{8,40},{16,48},{24,56},{32,0},{40,8},{48,16},{56,24},{64,96... | collective-permute-start | bytes 147464 | tf_op jit(solution)/shard_map/ppermute | solution.py:325
  78.8 1.3 %all-to-all-done.before_ref.even_ref = f32[16,4,6144]{2,1,0:T(4,128)S(1)} async-done(((f32[16,4,6144]{2,1,0:T(4,128)}), f32[16,4,6144]{2,1,0:T(4,128)S(1)}, u32[]{:S(2)}, u32[]{:S(2)}) %all-to-all-start) | async-done | bytes 1572896 | tf_op jit(solution)/shard_map/all_to_all | solution.py:352
  80.1 0.0 collective-permute-done.9.got_three_ref
  80.1 0.0 collective-permute-done.3.got_one_ref
  80.1 0.0 copy-start
  80.2 1.9 %copy-done = bf16[256,6144]{1,0:T(8,128)(2,1)S(1)} copy-done((bf16[256,6144]{1,0:T(8,128)(2,1)S(1)}, bf16[256,6144]{1,0:T(8,128)(2,1)}, u32[]{:S(2)}) %copy-start) | copy-done | bytes 3145752
  82.0 0.0 copy-start.2
  82.0 2.0 %project_high.1 = (f32[128,6144]{1,0:T(8,128)S(1)}, bf16[128,6144]{1,0:T(8,128)(2,1)S(1)}, f32[256,256]{1,0:T(8,128)S(1)}) custom-call(s32[3]{0:T(128)S(1)} %pad_add_fusion.place_ref.before_ref, f32[16,4,6144]{2,1,0:T(4,128)S(1)} %all-to-all-done.before_ref.even_ref, f32[2,2,4,6144]{3,2,1,0:T(4,128)S(1)} %get-tuple-element.32.kept_one_ref, ...), custom_call_target="tpu_custom_call" | custom-call | tf_op jit(solution)/shard_map/project_high/pallas_call | solution.py:271
  84.1 0.0 collective-permute-done.10.more_ref
  84.1 0.0 copy-done.2
  84.1 0.0 copy-start.1
  84.1 0.0 copy-start.3
  84.1 1.0 project_low.1
  85.1 0.1 collective-permute-start.11
  85.2 1.2 %collective-permute-done.11 = f32[128,128]{1,0:T(8,128)S(1)} collective-permute-done((f32[128,128]{1,0:T(8,128)S(1)}, f32[128,128]{1,0:T(8,128)S(1)}, u32[]{:S(2)}, u32[]{:S(2)}) %collective-permute-start.11) | collective-permute-done | bytes 65568 | tf_op jit(solution)/shard_map/ppermute | solution.py:325
  86.5 3.1 %collective-permute-start.12 = (f32[128,128]{1,0:T(8,128)S(1)}, f32[128,128]{1,0:T(8,128)S(1)}, u32[]{:S(2)}, u32[]{:S(2)}) collective-permute-start(f32[128,128]{1,0:T(8,128)S(1)} %add.33), channel_id=1, source_target_pairs={{0,16},{8,24},{16,0},{24,8},{32,48},{40,56},{48,32},{56,40},{64,80... | collective-permute-start | bytes 196616 | tf_op jit(solution)/shard_map/ppermute | solution.py:325
  89.6 2.8 %collective-permute-done.12 = f32[128,128]{1,0:T(8,128)S(1)} collective-permute-done((f32[128,128]{1,0:T(8,128)S(1)}, f32[128,128]{1,0:T(8,128)S(1)}, u32[]{:S(2)}, u32[]{:S(2)}) %collective-permute-start.12) | collective-permute-done | bytes 65568 | tf_op jit(solution)/shard_map/ppermute | solution.py:325
  92.4 3.2 %collective-permute-start.14 = (f32[224,128]{1,0:T(8,128)S(1)}, f32[224,128]{1,0:T(8,128)S(1)}, u32[]{:S(2)}, u32[]{:S(2)}) collective-permute-start(f32[224,128]{1,0:T(8,128)S(1)} %pad_maximum_fusion), channel_id=1, source_target_pairs={{0,64},{8,72},{16,80},{24,88},{32,96},{40,104},{48,112},{56,120},{... | collective-permute-start | bytes 344072 | tf_op jit(solution)/shard_map/ppermute | solution.py:325
  95.6 1.6 %collective-permute-start.13 = (f32[128,128]{1,0:T(8,128)S(1)}, f32[128,128]{1,0:T(8,128)S(1)}, u32[]{:S(2)}, u32[]{:S(2)}) collective-permute-start(f32[128,128]{1,0:T(8,128)S(1)} %add.34), channel_id=1, source_target_pairs={{0,32},{8,40},{16,48},{24,56},{32,0},{40,8},{48,16},{56,24},{64,96... | collective-permute-start | bytes 196616 | tf_op jit(solution)/shard_map/ppermute | solution.py:325
  97.1 0.0 collective-permute-start.15
  97.1 4.9 %collective-permute-done.14 = f32[224,128]{1,0:T(8,128)S(1)} collective-permute-done((f32[224,128]{1,0:T(8,128)S(1)}, f32[224,128]{1,0:T(8,128)S(1)}, u32[]{:S(2)}, u32[]{:S(2)}) %collective-permute-start.14) | collective-permute-done | bytes 114720 | tf_op jit(solution)/shard_map/ppermute | solution.py:325
  102.1 0.0 collective-permute-done.13
  102.1 1.2 %collective-permute-done.15 = f32[128,128]{1,0:T(8,128)S(1)} collective-permute-done((f32[128,128]{1,0:T(8,128)S(1)}, f32[128,128]{1,0:T(8,128)S(1)}, u32[]{:S(2)}, u32[]{:S(2)}) %collective-permute-start.15) | collective-permute-done | bytes 65568 | tf_op jit(solution)/shard_map/ppermute | solution.py:325
  103.3 2.4 %collective-permute-start.16 = (f32[224,128]{1,0:T(8,128)S(1)}, f32[224,128]{1,0:T(8,128)S(1)}, u32[]{:S(2)}, u32[]{:S(2)}) collective-permute-start(f32[224,128]{1,0:T(8,128)S(1)} %pad_maximum_fusion.1), channel_id=1, source_target_pairs={{0,192},{8,200},{16,208},{24,216},{32,224},{40,232},{48,240},{56,2... | collective-permute-start | bytes 344072 | tf_op jit(solution)/shard_map/ppermute | solution.py:325
  105.7 4.7 %collective-permute-done.16 = f32[224,128]{1,0:T(8,128)S(1)} collective-permute-done((f32[224,128]{1,0:T(8,128)S(1)}, f32[224,128]{1,0:T(8,128)S(1)}, u32[]{:S(2)}, u32[]{:S(2)}) %collective-permute-start.16) | collective-permute-done | bytes 114720 | tf_op jit(solution)/shard_map/ppermute | solution.py:325
  110.4 0.1 collective-permute-start.17
  110.5 1.3 %collective-permute-done.17.other_ref = f32[224,128]{1,0:T(8,128)S(1)} collective-permute-done((f32[224,128]{1,0:T(8,128)S(1)}, f32[224,128]{1,0:T(8,128)S(1)}, u32[]{:S(2)}, u32[]{:S(2)}) %collective-permute-start.17) | collective-permute-done | bytes 114720 | tf_op jit(solution)/shard_map/ppermute | solution.py:325
  111.9 0.0 copy-done.1
  111.9 0.0 copy-done.3
  111.9 3.6 %finish.1 = f32[128,6144]{1,0:T(8,128)} custom-call(s32[1]{0:T(128)} %bitcast.core_ref, f32[224,128]{1,0:T(8,128)S(1)} %fusion.1.own_ref, f32[224,128]{1,0:T(8,128)S(1)} %collective-permute-done.17.other_ref, f32[4,64,64]{2,1,0:T(8,128)S(1)} %copy-done.3, f32[128,6144]{1,0:T(8,128)S(1)} %get-tuple-element.48.current_ref, bf16[256,6144]{1,0:T(8,128)(2,1)S(1)} %copy-done.1, ...), custom_call_target="tpu_custom_call" | custom-call | tf_op jit(solution)/shard_map/finish/pallas_call | solution.py:302
  (10 shorter events, 0.1 us)
Async XLA Ops:
  2.7 42.1 %collective-permute-start.4 = (f32[4,24576]{1,0:T(4,128)}, f32[4,24576]{1,0:T(4,128)S(1)}, u32[]{:S(2)}, u32[]{:S(2)}) collective-permute-start(f32[4,24576]{1,0:T(4,128)} %get-tuple-element.34), channel_id=1, source_target_pairs={{0,96},{32,128},{64,160},{96,192},{128,224},{160,0},{192,32},{224,... | collective-permute-start | bytes 1179656 | tf_op jit(solution)/shard_map/ppermute | solution.py:336
  7.4 37.4 %collective-permute-start.5 = (f32[4,24576]{1,0:T(4,128)}, f32[4,24576]{1,0:T(4,128)S(1)}, u32[]{:S(2)}, u32[]{:S(2)}) collective-permute-start(f32[4,24576]{1,0:T(4,128)} %get-tuple-element.35), channel_id=1, source_target_pairs={{0,160},{32,192},{64,224},{96,0},{128,32},{160,64},{192,96},{224,1... | collective-permute-start | bytes 1179656 | tf_op jit(solution)/shard_map/ppermute | solution.py:336
  12.2 36.7 %collective-permute-start = (f32[4,24576]{1,0:T(4,128)}, f32[4,24576]{1,0:T(4,128)S(1)}, u32[]{:S(2)}, u32[]{:S(2)}) collective-permute-start(f32[4,24576]{1,0:T(4,128)} %get-tuple-element.27), channel_id=1, source_target_pairs={{0,32},{32,64},{64,96},{96,128},{128,160},{160,192},{192,224},{224... | collective-permute-start | bytes 1179656 | tf_op jit(solution)/shard_map/ppermute | solution.py:336
  13.3 35.6 %collective-permute-start.1 = (f32[4,24576]{1,0:T(4,128)}, f32[4,24576]{1,0:T(4,128)S(1)}, u32[]{:S(2)}, u32[]{:S(2)}) collective-permute-start(f32[4,24576]{1,0:T(4,128)} %get-tuple-element.28), channel_id=1, source_target_pairs={{0,224},{32,0},{64,32},{96,64},{128,96},{160,128},{192,160},{224,1... | collective-permute-start | bytes 1179656 | tf_op jit(solution)/shard_map/ppermute | solution.py:336
  19.6 60.5 %all-to-all-start = ((f32[16,4,6144]{2,1,0:T(4,128)}), f32[16,4,6144]{2,1,0:T(4,128)S(1)}, u32[]{:S(2)}, u32[]{:S(2)}) async-start(f32[16,4,6144]{2,1,0:T(4,128)} %even.1), calls=%async_computation | async-start | bytes 3145728 | tf_op jit(solution)/shard_map/all_to_all | solution.py:352
  37.8 1.3 %collective-permute-start.6 = (f32[96,128]{1,0:T(8,128)S(1)}, f32[96,128]{1,0:T(8,128)S(1)}, u32[]{:S(2)}, u32[]{:S(2)}) collective-permute-start(f32[96,128]{1,0:T(8,128)S(1)} %get-tuple-element.36), channel_id=1, source_target_pairs={{0,8},{8,0},{16,24},{24,16},{32,40},{40,32},{48,56},{56,48},{64,72... | collective-permute-start | bytes 147464 | tf_op jit(solution)/shard_map/ppermute | solution.py:325
  39.1 5.7 %collective-permute-start.7 = (f32[96,128]{1,0:T(8,128)S(1)}, f32[96,128]{1,0:T(8,128)S(1)}, u32[]{:S(2)}, u32[]{:S(2)}) collective-permute-start(f32[96,128]{1,0:T(8,128)S(1)} %add.31), channel_id=1, source_target_pairs={{0,16},{8,24},{16,0},{24,8},{32,48},{40,56},{48,32},{56,40},{64,80... | collective-permute-start | bytes 147464 | tf_op jit(solution)/shard_map/ppermute | solution.py:325
  45.4 17.5 %collective-permute-start.8 = (f32[2,4,12288]{2,1,0:T(4,128)S(1)}, f32[2,4,12288]{2,1,0:T(4,128)S(1)}, u32[]{:S(2)}, u32[]{:S(2)}) collective-permute-start(f32[2,4,12288]{2,1,0:T(4,128)S(1)} %get-tuple-element.38), channel_id=1, source_target_pairs={{0,16},{8,24},{16,0},{24,8},{32,48},{40,56},{48,32},{56,40},{64,80... | collective-permute-start | bytes 1179656 | tf_op jit(solution)/shard_map/ppermute | solution.py:325
  49.5 26.6 %collective-permute-start.2 = (f32[2,4,12288]{2,1,0:T(4,128)S(1)}, f32[2,4,12288]{2,1,0:T(4,128)S(1)}, u32[]{:S(2)}, u32[]{:S(2)}) collective-permute-start(f32[2,4,12288]{2,1,0:T(4,128)S(1)} %get-tuple-element.31), channel_id=1, source_target_pairs={{0,16},{8,24},{16,0},{24,8},{32,48},{40,56},{48,32},{56,40},{64,80... | collective-permute-start | bytes 1179656 | tf_op jit(solution)/shard_map/ppermute | solution.py:325
  64.2 15.9 %collective-permute-start.9 = (f32[2,2,4,6144]{3,2,1,0:T(4,128)}, f32[2,2,4,6144]{3,2,1,0:T(4,128)S(1)}, u32[]{:S(2)}, u32[]{:S(2)}) collective-permute-start(f32[2,2,4,6144]{3,2,1,0:T(4,128)} %get-tuple-element.40), channel_id=1, source_target_pairs={{0,8},{8,0},{16,24},{24,16},{32,40},{40,32},{48,56},{56,48},{64,72... | collective-permute-start | bytes 1179656 | tf_op jit(solution)/shard_map/ppermute | solution.py:325
  77.5 2.7 %collective-permute-start.3 = (f32[2,2,4,6144]{3,2,1,0:T(4,128)}, f32[2,2,4,6144]{3,2,1,0:T(4,128)S(1)}, u32[]{:S(2)}, u32[]{:S(2)}) collective-permute-start(f32[2,2,4,6144]{3,2,1,0:T(4,128)} %get-tuple-element.33), channel_id=1, source_target_pairs={{0,8},{8,0},{16,24},{24,16},{32,40},{40,32},{48,56},{56,48},{64,72... | collective-permute-start | bytes 1179656 | tf_op jit(solution)/shard_map/ppermute | solution.py:325
  77.5 6.6 %collective-permute-start.10 = (f32[96,128]{1,0:T(8,128)S(1)}, f32[96,128]{1,0:T(8,128)S(1)}, u32[]{:S(2)}, u32[]{:S(2)}) collective-permute-start(f32[96,128]{1,0:T(8,128)S(1)} %add.32.before_ref.gram_ref), channel_id=1, source_target_pairs={{0,32},{8,40},{16,48},{24,56},{32,0},{40,8},{48,16},{56,24},{64,96... | collective-permute-start | bytes 147464 | tf_op jit(solution)/shard_map/ppermute | solution.py:325
  80.1 1.9 %copy-start = (bf16[256,6144]{1,0:T(8,128)(2,1)S(1)}, bf16[256,6144]{1,0:T(8,128)(2,1)}, u32[]{:S(2)}) copy-start(bf16[256,6144]{1,0:T(8,128)(2,1)} %after.1.high_ref) | copy-start | bytes 9437188
  82.0 2.0 %copy-start.2 = (bf16[256,6144]{1,0:T(8,128)(2,1)S(1)}, bf16[256,6144]{1,0:T(8,128)(2,1)}, u32[]{:S(2)}) copy-start(bf16[256,6144]{1,0:T(8,128)(2,1)} %get-tuple-element.44.low_ref) | copy-start | bytes 9437188
  84.1 27.8 %copy-start.1 = (bf16[256,6144]{1,0:T(8,128)(2,1)S(1)}, bf16[256,6144]{1,0:T(8,128)(2,1)}, u32[]{:S(2)}) copy-start(bf16[256,6144]{1,0:T(8,128)(2,1)} %after.1.high_ref) | copy-start | bytes 9437188
  84.1 27.8 %copy-start.3 = (f32[4,64,64]{2,1,0:T(8,128)S(1)}, f32[4,64,64]{2,1,0:T(8,128)}, u32[]{:S(2)}) copy-start(f32[4,64,64]{2,1,0:T(8,128)} %tfactors_ref.1) | copy-start | bytes 196612
  85.1 1.3 %collective-permute-start.11 = (f32[128,128]{1,0:T(8,128)S(1)}, f32[128,128]{1,0:T(8,128)S(1)}, u32[]{:S(2)}, u32[]{:S(2)}) collective-permute-start(f32[128,128]{1,0:T(8,128)S(1)} %get-tuple-element.46), channel_id=1, source_target_pairs={{0,8},{8,0},{16,24},{24,16},{32,40},{40,32},{48,56},{56,48},{64,72... | collective-permute-start | bytes 196616 | tf_op jit(solution)/shard_map/ppermute | solution.py:325
  86.5 5.9 %collective-permute-start.12 = (f32[128,128]{1,0:T(8,128)S(1)}, f32[128,128]{1,0:T(8,128)S(1)}, u32[]{:S(2)}, u32[]{:S(2)}) collective-permute-start(f32[128,128]{1,0:T(8,128)S(1)} %add.33), channel_id=1, source_target_pairs={{0,16},{8,24},{16,0},{24,8},{32,48},{40,56},{48,32},{56,40},{64,80... | collective-permute-start | bytes 196616 | tf_op jit(solution)/shard_map/ppermute | solution.py:325
  92.4 9.7 %collective-permute-start.14 = (f32[224,128]{1,0:T(8,128)S(1)}, f32[224,128]{1,0:T(8,128)S(1)}, u32[]{:S(2)}, u32[]{:S(2)}) collective-permute-start(f32[224,128]{1,0:T(8,128)S(1)} %pad_maximum_fusion), channel_id=1, source_target_pairs={{0,64},{8,72},{16,80},{24,88},{32,96},{40,104},{48,112},{56,120},{... | collective-permute-start | bytes 344072 | tf_op jit(solution)/shard_map/ppermute | solution.py:325
  95.6 6.5 %collective-permute-start.13 = (f32[128,128]{1,0:T(8,128)S(1)}, f32[128,128]{1,0:T(8,128)S(1)}, u32[]{:S(2)}, u32[]{:S(2)}) collective-permute-start(f32[128,128]{1,0:T(8,128)S(1)} %add.34), channel_id=1, source_target_pairs={{0,32},{8,40},{16,48},{24,56},{32,0},{40,8},{48,16},{56,24},{64,96... | collective-permute-start | bytes 196616 | tf_op jit(solution)/shard_map/ppermute | solution.py:325
  97.1 6.2 %collective-permute-start.15 = (f32[128,128]{1,0:T(8,128)S(1)}, f32[128,128]{1,0:T(8,128)S(1)}, u32[]{:S(2)}, u32[]{:S(2)}) collective-permute-start(f32[128,128]{1,0:T(8,128)S(1)} %add.34), channel_id=1, source_target_pairs={{0,96},{8,104},{16,112},{24,120},{32,64},{40,72},{48,80},{56,88},{... | collective-permute-start | bytes 196616 | tf_op jit(solution)/shard_map/ppermute | solution.py:325
  103.3 7.1 %collective-permute-start.16 = (f32[224,128]{1,0:T(8,128)S(1)}, f32[224,128]{1,0:T(8,128)S(1)}, u32[]{:S(2)}, u32[]{:S(2)}) collective-permute-start(f32[224,128]{1,0:T(8,128)S(1)} %pad_maximum_fusion.1), channel_id=1, source_target_pairs={{0,192},{8,200},{16,208},{24,216},{32,224},{40,232},{48,240},{56,2... | collective-permute-start | bytes 344072 | tf_op jit(solution)/shard_map/ppermute | solution.py:325
  110.4 1.4 %collective-permute-start.17 = (f32[224,128]{1,0:T(8,128)S(1)}, f32[224,128]{1,0:T(8,128)S(1)}, u32[]{:S(2)}, u32[]{:S(2)}) collective-permute-start(f32[224,128]{1,0:T(8,128)S(1)} %fusion.1.own_ref), channel_id=1, source_target_pairs={{0,8},{8,0},{16,24},{24,16},{32,40},{40,32},{48,56},{56,48},{64,72... | collective-permute-start | bytes 344072 | tf_op jit(solution)/shard_map/ppermute | solution.py:325

commit v13 on v11

--- a/solution.py
+++ b/solution.py
@@ -9,8 +9,9 @@
 from jax.sharding import PartitionSpec as P
 
 COLUMNS = 1024
-OUT_COLUMNS = 2048
-SHIFTS = (1, -1, 3, -3)
+OUT_COLUMNS = 1024
+WIDE_COLUMNS = 2048
+NEAR, FAR = (1, -1), (3, -3)
 LIMIT = 40 * 1024 * 1024
 IN_VMEM = pl.BlockSpec(memory_space=pltpu.VMEM)
 IN_SMEM = pl.BlockSpec(memory_space=pltpu.SMEM)
@@ -69,12 +70,12 @@
         halves(core_ref[0], packed, kept_ref, sent_ref)
 
 
-def cut_kernel(place_ref, vectors_ref, *refs):
+def cut_kernel(shifts, place_ref, vectors_ref, *refs):
     outs, sems = refs[:-1], refs[-1]
     wide = outs[0].shape[1]
     planes = vectors_ref.shape[1] // wide
     copies = []
-    for i, shift in enumerate(SHIFTS):
+    for i, shift in enumerate(shifts):
         plane = (place_ref[0] + shift + planes) % planes
         columns = pl.ds(pl.multiple_of(plane * wide, 128), wide)
         copies.append(pltpu.make_async_copy(vectors_ref.at[:, columns], outs[i], sems.at[i]))
@@ -113,8 +114,8 @@
     z, y, core = place_ref[0], place_ref[1], place_ref[2]
     pair = 2 * even_ref.shape[1]
     total_ref[...] = jnp.zeros_like(total_ref)
-    for step in range(rows // COLUMNS):
-        columns = pl.ds(step * COLUMNS, COLUMNS)
+    for step in range(rows // WIDE_COLUMNS):
+        columns = pl.ds(step * WIDE_COLUMNS, WIDE_COLUMNS)
 
         def put(plane, side, block):
             at = pl.multiple_of((plane * 2 + side) * pair, 8)
@@ -123,7 +124,7 @@
         for k in range(planes // 2):
             for side in range(2):
                 at = (2 * k + side) * 2
-                put(2 * k + z % 2, side, even_ref[at : at + 2, :, columns].reshape(pair, COLUMNS))
+                put(2 * k + z % 2, side, even_ref[at : at + 2, :, columns].reshape(pair, WIDE_COLUMNS))
         for shift, kept_ref, got_ref in ((1, kept_one_ref, got_one_ref), (3, kept_three_ref, got_three_ref)):
             for other in range(2):
                 for i, by in enumerate((shift, -shift)):
@@ -225,7 +226,7 @@
         out_specs=tuple(IN_HBM if out.memory_space == pltpu.HBM else IN_VMEM for out in outs),
         scratch_shapes=[pltpu.SemaphoreType.DMA((copies,))] if copies else [],
         compiler_params=pltpu.CompilerParams(vmem_limit_bytes=LIMIT),
-        name=kernel.__name__,
+        name=getattr(kernel, "__name__", "cut"),
     )(*operands)
 
 
@@ -337,8 +338,11 @@
             return kept, swap(sent, 1)
 
         block = pltpu.VMEM((each, wide), jnp.float32)
-        cut = local_call(cut_kernel, (block,) * len(SHIFTS), [IN_HBM], (place, in_hbm(vectors_in)), len(SHIFTS))
-        came = [moved(part, shift) for part, shift in zip(cut, SHIFTS)]
+        came = []
+        for shifts in (NEAR, FAR):
+            kernel = functools.partial(cut_kernel, shifts)
+            cut = local_call(kernel, (block,) * len(shifts), [IN_HBM], (place, in_hbm(vectors_in)), len(shifts))
+            came += [moved(part, shift) for part, shift in zip(cut, shifts)]
         even = even_call(place, vectors_in, place, planes)
         even = lax.all_to_all(even, ("half", "y", "core"), split_axis=0, concat_axis=0, tiled=True)
         high, low, kept, sent = gram_call(core, householder, place)

time: 117 us -> 117 us (level)
  waiting for transfers between devices: 47.8 us -> 42.7 us
  starting transfers between devices: 39.5 us -> 41.9 us
  Pallas kernels: 26.3 us -> 28.3 us
    all_to_all x1, waiting for transfers between devices: 6.13 us -> 1.3 us  [shards(): lax.all_to_all(even, ('half', 'y', 'core'), split_axis=0, concat_axis=0,...]
    ppermute x4, waiting for transfers between devices: 2.58 us -> 0.01 us  [moved(): lax.ppermute(part, ('half', 'odd'), [(i, (i + shift) % planes) for i in r...]
    ppermute x14, starting transfers between devices: 19.9 us -> 22.3 us  [swap(): return lax.ppermute(value, row, [(i, i ^ flip) for i in range(devices)])]
    ppermute x14, waiting for transfers between devices: 39 us -> 41.4 us  [swap(): return lax.ppermute(value, row, [(i, i ^ flip) for i in range(devices)])]
    pallas_call x5 -> x6, Pallas kernels: 7.01 us -> 9.08 us  [local_call(): pl.pallas_call(kernel, out_shape=outs, in_specs=[IN_SMEM] + specs, out_sp...]
  transfers between devices with their start and end apart: 19 -> 19, of which waited for: 12 -> 11; matrix products, arithmetic and copies ran while one was open for 0% -> 0% of each run, Pallas kernels for 16% -> 19%
where the time goes in v13:
time: 117 us; the launch traced here: 115 us
  waiting for transfers between devices  42.7 us (36%)
  starting transfers between devices  41.9 us (36%)
  Pallas kernels  28.3 us (24%)
  local copies, waits for them, and re-layouts  1.9 us (2%)
    ppermute x14, waiting for transfers between devices, swap(): return lax.ppermute(value, row, [(i, i ^ flip) for i in range(devices)])  41.4 us
    ppermute x14, starting transfers between devices, swap(): return lax.ppermute(value, row, [(i, i ^ flip) for i in range(devices)])  22.3 us
    ppermute x4, starting transfers between devices, moved(): lax.ppermute(part, ('half', 'odd'), [(i, (i + shift) % planes) for i in r...  10.2 us
    all_to_all x1, starting transfers between devices, shards(): lax.all_to_all(even, ('half', 'y', 'core'), split_axis=0, concat_axis=0,...  9.4 us
    pallas_call x6, Pallas kernels, local_call(): pl.pallas_call(kernel, out_shape=outs, in_specs=[IN_SMEM] + specs, out_sp...  9.08 us
    pallas_call x1, Pallas kernels, gram_call(): pl.pallas_call(gram_kernel, out_shape=(pltpu.HBM((size, rows), jnp.bfloat...  8.8 us
    pallas_call x1, Pallas kernels, even_call(): pl.pallas_call(even_kernel, out_shape=pltpu.HBM((planes * 2, each, wide /...  4.14 us
    pallas_call x1, Pallas kernels, finish_call(): pl.pallas_call(finish_kernel, out_shape=jax.ShapeDtypeStruct((count, rows...  3.21 us
  transfers between devices with their start and end apart: 19, of which 11 were waited for; matrix products, arithmetic and copies ran while one was open for 0% of the time, Pallas kernels for 19%

profile of v13, /device:TPU:4, one launch (start us, length us, event | category | flops | bytes accessed | tf_op | source)
XLA Modules:
  0.0 115.2 jit_solution(11439950546054192985)
XLA Ops:
  0.0 0.1 pad_add_fusion.place_ref.before_ref
  0.1 2.6 %cut.3 = (f32[4,24576]{1,0:T(4,128)}, f32[4,24576]{1,0:T(4,128)}) custom-call(s32[3]{0:T(128)S(1)} %pad_add_fusion.place_ref.before_ref, f32[4,196608]{1,0:T(4,128)} %vectors_ref.3), custom_call_target="tpu_custom_call" | custom-call | tf_op jit(solution)/shard_map/cut/pallas_call | solution.py:222
  2.7 4.7 %collective-permute-start.4 = (f32[4,24576]{1,0:T(4,128)}, f32[4,24576]{1,0:T(4,128)S(1)}, u32[]{:S(2)}, u32[]{:S(2)}) collective-permute-start(f32[4,24576]{1,0:T(4,128)} %get-tuple-element.34), channel_id=1, source_target_pairs={{0,96},{32,128},{64,160},{96,192},{128,224},{160,0},{192,32},{224,... | collective-permute-start | bytes 1179656 | tf_op jit(solution)/shard_map/ppermute | solution.py:331
  7.4 2.2 %collective-permute-start.5 = (f32[4,24576]{1,0:T(4,128)}, f32[4,24576]{1,0:T(4,128)S(1)}, u32[]{:S(2)}, u32[]{:S(2)}) collective-permute-start(f32[4,24576]{1,0:T(4,128)} %get-tuple-element.35), channel_id=1, source_target_pairs={{0,160},{32,192},{64,224},{96,0},{128,32},{160,64},{192,96},{224,1... | collective-permute-start | bytes 1179656 | tf_op jit(solution)/shard_map/ppermute | solution.py:331
  9.6 2.6 %cut.2 = (f32[4,24576]{1,0:T(4,128)}, f32[4,24576]{1,0:T(4,128)}) custom-call(s32[3]{0:T(128)S(1)} %pad_add_fusion.place_ref.before_ref, f32[4,196608]{1,0:T(4,128)} %vectors_ref.3), custom_call_target="tpu_custom_call" | custom-call | tf_op jit(solution)/shard_map/cut/pallas_call | solution.py:222
  12.2 1.1 collective-permute-start
  13.3 2.2 %collective-permute-start.1 = (f32[4,24576]{1,0:T(4,128)}, f32[4,24576]{1,0:T(4,128)S(1)}, u32[]{:S(2)}, u32[]{:S(2)}) collective-permute-start(f32[4,24576]{1,0:T(4,128)} %get-tuple-element.28), channel_id=1, source_target_pairs={{0,224},{32,0},{64,32},{96,64},{128,96},{160,128},{192,160},{224,1... | collective-permute-start | bytes 1179656 | tf_op jit(solution)/shard_map/ppermute | solution.py:331
  15.5 4.1 %even.1 = f32[16,4,6144]{2,1,0:T(4,128)} custom-call(s32[3]{0:T(128)S(1)} %pad_add_fusion.place_ref.before_ref, f32[4,196608]{1,0:T(4,128)} %vectors_ref.3, s32[3]{0:T(128)S(1)} %pad_add_fusion.place_ref.before_ref), custom_call_target="tpu_custom_call" | custom-call | tf_op jit(solution)/shard_map/even/pallas_call | solution.py:236
  19.6 9.4 %all-to-all-start = ((f32[16,4,6144]{2,1,0:T(4,128)}), f32[16,4,6144]{2,1,0:T(4,128)S(1)}, u32[]{:S(2)}, u32[]{:S(2)}) async-start(f32[16,4,6144]{2,1,0:T(4,128)} %even.1), calls=%async_computation | async-start | bytes 3145728 | tf_op jit(solution)/shard_map/all_to_all | solution.py:347
  29.0 8.8 %gram.1 = (bf16[256,6144]{1,0:T(8,128)(2,1)}, bf16[256,6144]{1,0:T(8,128)(2,1)}, f32[96,128]{1,0:T(8,128)S(1)}, f32[96,128]{1,0:T(8,128)S(1)}) custom-call(s32[1]{0:T(128)} %bitcast.core_ref, f32[4,64,6144]{2,1,0:T(8,128)} %householder_ref.1, s32[3]{0:T(128)S(1)} %pad_add_fusion.place_ref.before_ref), custom_call_target="tpu_custom_call" | custom-call | flops 32212254720 | bytes 12582912 | tf_op jit(solution)/shard_map/gram/pallas_call | solution.py:198
  37.8 0.4 collective-permute-start.6
  38.2 0.9 collective-permute-done.6
  39.1 3.4 %collective-permute-start.7 = (f32[96,128]{1,0:T(8,128)S(1)}, f32[96,128]{1,0:T(8,128)S(1)}, u32[]{:S(2)}, u32[]{:S(2)}) collective-permute-start(f32[96,128]{1,0:T(8,128)S(1)} %add.31), channel_id=1, source_target_pairs={{0,16},{8,24},{16,0},{24,8},{32,48},{40,56},{48,32},{56,40},{64,80... | collective-permute-start | bytes 147464 | tf_op jit(solution)/shard_map/ppermute | solution.py:320
  42.6 2.2 %collective-permute-done.7 = f32[96,128]{1,0:T(8,128)S(1)} collective-permute-done((f32[96,128]{1,0:T(8,128)S(1)}, f32[96,128]{1,0:T(8,128)S(1)}, u32[]{:S(2)}, u32[]{:S(2)}) %collective-permute-start.7) | collective-permute-done | bytes 49184 | tf_op jit(solution)/shard_map/ppermute | solution.py:320
  44.8 0.0 collective-permute-done.4.up_ref
  44.8 0.0 collective-permute-done.5.down_ref
  44.8 0.6 side_kernel.3
  45.4 3.5 %collective-permute-start.8 = (f32[2,4,12288]{2,1,0:T(4,128)S(1)}, f32[2,4,12288]{2,1,0:T(4,128)S(1)}, u32[]{:S(2)}, u32[]{:S(2)}) collective-permute-start(f32[2,4,12288]{2,1,0:T(4,128)S(1)} %get-tuple-element.38), channel_id=1, source_target_pairs={{0,16},{8,24},{16,0},{24,8},{32,48},{40,56},{48,32},{56,40},{64,80... | collective-permute-start | bytes 1179656 | tf_op jit(solution)/shard_map/ppermute | solution.py:320
  48.9 0.0 collective-permute-done.up_ref
  48.9 0.0 collective-permute-done.1.down_ref
  48.9 0.6 side_kernel.2
  49.5 3.2 %collective-permute-start.2 = (f32[2,4,12288]{2,1,0:T(4,128)S(1)}, f32[2,4,12288]{2,1,0:T(4,128)S(1)}, u32[]{:S(2)}, u32[]{:S(2)}) collective-permute-start(f32[2,4,12288]{2,1,0:T(4,128)S(1)} %get-tuple-element.31), channel_id=1, source_target_pairs={{0,16},{8,24},{16,0},{24,8},{32,48},{40,56},{48,32},{56,40},{64,80... | collective-permute-start | bytes 1179656 | tf_op jit(solution)/shard_map/ppermute | solution.py:320
  52.7 10.2 %collective-permute-done.8.got_ref = f32[2,4,12288]{2,1,0:T(4,128)S(1)} collective-permute-done((f32[2,4,12288]{2,1,0:T(4,128)S(1)}, f32[2,4,12288]{2,1,0:T(4,128)S(1)}, u32[]{:S(2)}, u32[]{:S(2)}) %collective-permute-start.8) | collective-permute-done | bytes 393248 | tf_op jit(solution)/shard_map/ppermute | solution.py:320
  62.9 1.4 %core_kernel.3 = (f32[2,2,4,6144]{3,2,1,0:T(4,128)S(1)}, f32[2,2,4,6144]{3,2,1,0:T(4,128)}) custom-call(s32[3]{0:T(128)S(1)} %pad_add_fusion.place_ref.before_ref, f32[2,4,12288]{2,1,0:T(4,128)S(1)} %get-tuple-element.37.own_ref, f32[2,4,12288]{2,1,0:T(4,128)S(1)} %collective-permute-done.8.got_ref), custom_call_target="tpu_custom_call" | custom-call | tf_op jit(solution)/shard_map/core_kernel/pallas_call | solution.py:222
  64.2 0.0 collective-permute-start.9
  64.2 11.8 %collective-permute-done.2.got_ref = f32[2,4,12288]{2,1,0:T(4,128)S(1)} collective-permute-done((f32[2,4,12288]{2,1,0:T(4,128)S(1)}, f32[2,4,12288]{2,1,0:T(4,128)S(1)}, u32[]{:S(2)}, u32[]{:S(2)}) %collective-permute-start.2) | collective-permute-done | bytes 393248 | tf_op jit(solution)/shard_map/ppermute | solution.py:320
  76.1 1.4 %core_kernel.2 = (f32[2,2,4,6144]{3,2,1,0:T(4,128)S(1)}, f32[2,2,4,6144]{3,2,1,0:T(4,128)}) custom-call(s32[3]{0:T(128)S(1)} %pad_add_fusion.place_ref.before_ref, f32[2,4,12288]{2,1,0:T(4,128)S(1)} %get-tuple-element.30.own_ref, f32[2,4,12288]{2,1,0:T(4,128)S(1)} %collective-permute-done.2.got_ref), custom_call_target="tpu_custom_call" | custom-call | tf_op jit(solution)/shard_map/core_kernel/pallas_call | solution.py:222
  77.5 0.0 collective-permute-start.3
  77.5 1.4 %collective-permute-start.10 = (f32[96,128]{1,0:T(8,128)S(1)}, f32[96,128]{1,0:T(8,128)S(1)}, u32[]{:S(2)}, u32[]{:S(2)}) collective-permute-start(f32[96,128]{1,0:T(8,128)S(1)} %add.32.before_ref.gram_ref), channel_id=1, source_target_pairs={{0,32},{8,40},{16,48},{24,56},{32,0},{40,8},{48,16},{56,24},{64,96... | collective-permute-start | bytes 147464 | tf_op jit(solution)/shard_map/ppermute | solution.py:320
  78.8 1.3 %all-to-all-done.before_ref.even_ref = f32[16,4,6144]{2,1,0:T(4,128)S(1)} async-done(((f32[16,4,6144]{2,1,0:T(4,128)}), f32[16,4,6144]{2,1,0:T(4,128)S(1)}, u32[]{:S(2)}, u32[]{:S(2)}) %all-to-all-start) | async-done | bytes 1572896 | tf_op jit(solution)/shard_map/all_to_all | solution.py:347
  80.1 0.0 collective-permute-done.9.got_three_ref
  80.1 0.0 collective-permute-done.3.got_one_ref
  80.1 0.0 copy-start
  80.2 1.9 %copy-done = bf16[256,6144]{1,0:T(8,128)(2,1)S(1)} copy-done((bf16[256,6144]{1,0:T(8,128)(2,1)S(1)}, bf16[256,6144]{1,0:T(8,128)(2,1)}, u32[]{:S(2)}) %copy-start) | copy-done | bytes 3145752
  82.0 0.0 copy-start.2
  82.0 2.0 %project_high.1 = (f32[128,6144]{1,0:T(8,128)S(1)}, bf16[128,6144]{1,0:T(8,128)(2,1)S(1)}, f32[256,256]{1,0:T(8,128)S(1)}) custom-call(s32[3]{0:T(128)S(1)} %pad_add_fusion.place_ref.before_ref, f32[16,4,6144]{2,1,0:T(4,128)S(1)} %all-to-all-done.before_ref.even_ref, f32[2,2,4,6144]{3,2,1,0:T(4,128)S(1)} %get-tuple-element.32.kept_one_ref, ...), custom_call_target="tpu_custom_call" | custom-call | tf_op jit(solution)/shard_map/project_high/pallas_call | solution.py:266
  84.1 0.0 collective-permute-done.10.more_ref
  84.1 0.0 copy-done.2
  84.1 0.0 copy-start.1
  84.1 0.0 copy-start.3
  84.1 1.0 project_low.1
  85.1 0.1 collective-permute-start.11
  85.2 1.2 %collective-permute-done.11 = f32[128,128]{1,0:T(8,128)S(1)} collective-permute-done((f32[128,128]{1,0:T(8,128)S(1)}, f32[128,128]{1,0:T(8,128)S(1)}, u32[]{:S(2)}, u32[]{:S(2)}) %collective-permute-start.11) | collective-permute-done | bytes 65568 | tf_op jit(solution)/shard_map/ppermute | solution.py:320
  86.5 3.1 %collective-permute-start.12 = (f32[128,128]{1,0:T(8,128)S(1)}, f32[128,128]{1,0:T(8,128)S(1)}, u32[]{:S(2)}, u32[]{:S(2)}) collective-permute-start(f32[128,128]{1,0:T(8,128)S(1)} %add.33), channel_id=1, source_target_pairs={{0,16},{8,24},{16,0},{24,8},{32,48},{40,56},{48,32},{56,40},{64,80... | collective-permute-start | bytes 196616 | tf_op jit(solution)/shard_map/ppermute | solution.py:320
  89.6 2.8 %collective-permute-done.12 = f32[128,128]{1,0:T(8,128)S(1)} collective-permute-done((f32[128,128]{1,0:T(8,128)S(1)}, f32[128,128]{1,0:T(8,128)S(1)}, u32[]{:S(2)}, u32[]{:S(2)}) %collective-permute-start.12) | collective-permute-done | bytes 65568 | tf_op jit(solution)/shard_map/ppermute | solution.py:320
  92.4 3.2 %collective-permute-start.14 = (f32[224,128]{1,0:T(8,128)S(1)}, f32[224,128]{1,0:T(8,128)S(1)}, u32[]{:S(2)}, u32[]{:S(2)}) collective-permute-start(f32[224,128]{1,0:T(8,128)S(1)} %pad_maximum_fusion), channel_id=1, source_target_pairs={{0,64},{8,72},{16,80},{24,88},{32,96},{40,104},{48,112},{56,120},{... | collective-permute-start | bytes 344072 | tf_op jit(solution)/shard_map/ppermute | solution.py:320
  95.6 1.6 %collective-permute-start.13 = (f32[128,128]{1,0:T(8,128)S(1)}, f32[128,128]{1,0:T(8,128)S(1)}, u32[]{:S(2)}, u32[]{:S(2)}) collective-permute-start(f32[128,128]{1,0:T(8,128)S(1)} %add.34), channel_id=1, source_target_pairs={{0,32},{8,40},{16,48},{24,56},{32,0},{40,8},{48,16},{56,24},{64,96... | collective-permute-start | bytes 196616 | tf_op jit(solution)/shard_map/ppermute | solution.py:320
  97.1 0.0 collective-permute-start.15
  97.1 4.9 %collective-permute-done.14 = f32[224,128]{1,0:T(8,128)S(1)} collective-permute-done((f32[224,128]{1,0:T(8,128)S(1)}, f32[224,128]{1,0:T(8,128)S(1)}, u32[]{:S(2)}, u32[]{:S(2)}) %collective-permute-start.14) | collective-permute-done | bytes 114720 | tf_op jit(solution)/shard_map/ppermute | solution.py:320
  102.1 0.0 collective-permute-done.13
  102.1 1.2 %collective-permute-done.15 = f32[128,128]{1,0:T(8,128)S(1)} collective-permute-done((f32[128,128]{1,0:T(8,128)S(1)}, f32[128,128]{1,0:T(8,128)S(1)}, u32[]{:S(2)}, u32[]{:S(2)}) %collective-permute-start.15) | collective-permute-done | bytes 65568 | tf_op jit(solution)/shard_map/ppermute | solution.py:320
  103.3 2.4 %collective-permute-start.16 = (f32[224,128]{1,0:T(8,128)S(1)}, f32[224,128]{1,0:T(8,128)S(1)}, u32[]{:S(2)}, u32[]{:S(2)}) collective-permute-start(f32[224,128]{1,0:T(8,128)S(1)} %pad_maximum_fusion.1), channel_id=1, source_target_pairs={{0,192},{8,200},{16,208},{24,216},{32,224},{40,232},{48,240},{56,2... | collective-permute-start | bytes 344072 | tf_op jit(solution)/shard_map/ppermute | solution.py:320
  105.7 4.7 %collective-permute-done.16 = f32[224,128]{1,0:T(8,128)S(1)} collective-permute-done((f32[224,128]{1,0:T(8,128)S(1)}, f32[224,128]{1,0:T(8,128)S(1)}, u32[]{:S(2)}, u32[]{:S(2)}) %collective-permute-start.16) | collective-permute-done | bytes 114720 | tf_op jit(solution)/shard_map/ppermute | solution.py:320
  110.5 0.1 collective-permute-start.17
  110.6 1.3 %collective-permute-done.17.other_ref = f32[224,128]{1,0:T(8,128)S(1)} collective-permute-done((f32[224,128]{1,0:T(8,128)S(1)}, f32[224,128]{1,0:T(8,128)S(1)}, u32[]{:S(2)}, u32[]{:S(2)}) %collective-permute-start.17) | collective-permute-done | bytes 114720 | tf_op jit(solution)/shard_map/ppermute | solution.py:320
  111.9 0.0 copy-done.1
  111.9 0.0 copy-done.3
  111.9 3.2 %finish.1 = f32[128,6144]{1,0:T(8,128)} custom-call(s32[1]{0:T(128)} %bitcast.core_ref, f32[224,128]{1,0:T(8,128)S(1)} %fusion.1.own_ref, f32[224,128]{1,0:T(8,128)S(1)} %collective-permute-done.17.other_ref, f32[4,64,64]{2,1,0:T(8,128)S(1)} %copy-done.3, f32[128,6144]{1,0:T(8,128)S(1)} %get-tuple-element.48.current_ref, bf16[256,6144]{1,0:T(8,128)(2,1)S(1)} %copy-done.1, ...), custom_call_target="tpu_custom_call" | custom-call | tf_op jit(solution)/shard_map/finish/pallas_call | solution.py:297
  (10 shorter events, 0.1 us)
Async XLA Ops:
  2.7 42.1 %collective-permute-start.4 = (f32[4,24576]{1,0:T(4,128)}, f32[4,24576]{1,0:T(4,128)S(1)}, u32[]{:S(2)}, u32[]{:S(2)}) collective-permute-start(f32[4,24576]{1,0:T(4,128)} %get-tuple-element.34), channel_id=1, source_target_pairs={{0,96},{32,128},{64,160},{96,192},{128,224},{160,0},{192,32},{224,... | collective-permute-start | bytes 1179656 | tf_op jit(solution)/shard_map/ppermute | solution.py:331
  7.4 37.4 %collective-permute-start.5 = (f32[4,24576]{1,0:T(4,128)}, f32[4,24576]{1,0:T(4,128)S(1)}, u32[]{:S(2)}, u32[]{:S(2)}) collective-permute-start(f32[4,24576]{1,0:T(4,128)} %get-tuple-element.35), channel_id=1, source_target_pairs={{0,160},{32,192},{64,224},{96,0},{128,32},{160,64},{192,96},{224,1... | collective-permute-start | bytes 1179656 | tf_op jit(solution)/shard_map/ppermute | solution.py:331
  12.2 36.7 %collective-permute-start = (f32[4,24576]{1,0:T(4,128)}, f32[4,24576]{1,0:T(4,128)S(1)}, u32[]{:S(2)}, u32[]{:S(2)}) collective-permute-start(f32[4,24576]{1,0:T(4,128)} %get-tuple-element.27), channel_id=1, source_target_pairs={{0,32},{32,64},{64,96},{96,128},{128,160},{160,192},{192,224},{224... | collective-permute-start | bytes 1179656 | tf_op jit(solution)/shard_map/ppermute | solution.py:331
  13.3 35.6 %collective-permute-start.1 = (f32[4,24576]{1,0:T(4,128)}, f32[4,24576]{1,0:T(4,128)S(1)}, u32[]{:S(2)}, u32[]{:S(2)}) collective-permute-start(f32[4,24576]{1,0:T(4,128)} %get-tuple-element.28), channel_id=1, source_target_pairs={{0,224},{32,0},{64,32},{96,64},{128,96},{160,128},{192,160},{224,1... | collective-permute-start | bytes 1179656 | tf_op jit(solution)/shard_map/ppermute | solution.py:331
  19.6 60.5 %all-to-all-start = ((f32[16,4,6144]{2,1,0:T(4,128)}), f32[16,4,6144]{2,1,0:T(4,128)S(1)}, u32[]{:S(2)}, u32[]{:S(2)}) async-start(f32[16,4,6144]{2,1,0:T(4,128)} %even.1), calls=%async_computation | async-start | bytes 3145728 | tf_op jit(solution)/shard_map/all_to_all | solution.py:347
  37.8 1.3 %collective-permute-start.6 = (f32[96,128]{1,0:T(8,128)S(1)}, f32[96,128]{1,0:T(8,128)S(1)}, u32[]{:S(2)}, u32[]{:S(2)}) collective-permute-start(f32[96,128]{1,0:T(8,128)S(1)} %get-tuple-element.36), channel_id=1, source_target_pairs={{0,8},{8,0},{16,24},{24,16},{32,40},{40,32},{48,56},{56,48},{64,72... | collective-permute-start | bytes 147464 | tf_op jit(solution)/shard_map/ppermute | solution.py:320
  39.1 5.7 %collective-permute-start.7 = (f32[96,128]{1,0:T(8,128)S(1)}, f32[96,128]{1,0:T(8,128)S(1)}, u32[]{:S(2)}, u32[]{:S(2)}) collective-permute-start(f32[96,128]{1,0:T(8,128)S(1)} %add.31), channel_id=1, source_target_pairs={{0,16},{8,24},{16,0},{24,8},{32,48},{40,56},{48,32},{56,40},{64,80... | collective-permute-start | bytes 147464 | tf_op jit(solution)/shard_map/ppermute | solution.py:320
  45.4 17.5 %collective-permute-start.8 = (f32[2,4,12288]{2,1,0:T(4,128)S(1)}, f32[2,4,12288]{2,1,0:T(4,128)S(1)}, u32[]{:S(2)}, u32[]{:S(2)}) collective-permute-start(f32[2,4,12288]{2,1,0:T(4,128)S(1)} %get-tuple-element.38), channel_id=1, source_target_pairs={{0,16},{8,24},{16,0},{24,8},{32,48},{40,56},{48,32},{56,40},{64,80... | collective-permute-start | bytes 1179656 | tf_op jit(solution)/shard_map/ppermute | solution.py:320
  49.5 26.6 %collective-permute-start.2 = (f32[2,4,12288]{2,1,0:T(4,128)S(1)}, f32[2,4,12288]{2,1,0:T(4,128)S(1)}, u32[]{:S(2)}, u32[]{:S(2)}) collective-permute-start(f32[2,4,12288]{2,1,0:T(4,128)S(1)} %get-tuple-element.31), channel_id=1, source_target_pairs={{0,16},{8,24},{16,0},{24,8},{32,48},{40,56},{48,32},{56,40},{64,80... | collective-permute-start | bytes 1179656 | tf_op jit(solution)/shard_map/ppermute | solution.py:320
  64.2 15.9 %collective-permute-start.9 = (f32[2,2,4,6144]{3,2,1,0:T(4,128)}, f32[2,2,4,6144]{3,2,1,0:T(4,128)S(1)}, u32[]{:S(2)}, u32[]{:S(2)}) collective-permute-start(f32[2,2,4,6144]{3,2,1,0:T(4,128)} %get-tuple-element.40), channel_id=1, source_target_pairs={{0,8},{8,0},{16,24},{24,16},{32,40},{40,32},{48,56},{56,48},{64,72... | collective-permute-start | bytes 1179656 | tf_op jit(solution)/shard_map/ppermute | solution.py:320
  77.5 2.7 %collective-permute-start.3 = (f32[2,2,4,6144]{3,2,1,0:T(4,128)}, f32[2,2,4,6144]{3,2,1,0:T(4,128)S(1)}, u32[]{:S(2)}, u32[]{:S(2)}) collective-permute-start(f32[2,2,4,6144]{3,2,1,0:T(4,128)} %get-tuple-element.33), channel_id=1, source_target_pairs={{0,8},{8,0},{16,24},{24,16},{32,40},{40,32},{48,56},{56,48},{64,72... | collective-permute-start | bytes 1179656 | tf_op jit(solution)/shard_map/ppermute | solution.py:320
  77.5 6.6 %collective-permute-start.10 = (f32[96,128]{1,0:T(8,128)S(1)}, f32[96,128]{1,0:T(8,128)S(1)}, u32[]{:S(2)}, u32[]{:S(2)}) collective-permute-start(f32[96,128]{1,0:T(8,128)S(1)} %add.32.before_ref.gram_ref), channel_id=1, source_target_pairs={{0,32},{8,40},{16,48},{24,56},{32,0},{40,8},{48,16},{56,24},{64,96... | collective-permute-start | bytes 147464 | tf_op jit(solution)/shard_map/ppermute | solution.py:320
  80.1 1.9 %copy-start = (bf16[256,6144]{1,0:T(8,128)(2,1)S(1)}, bf16[256,6144]{1,0:T(8,128)(2,1)}, u32[]{:S(2)}) copy-start(bf16[256,6144]{1,0:T(8,128)(2,1)} %after.1.high_ref) | copy-start | bytes 9437188
  82.0 2.0 %copy-start.2 = (bf16[256,6144]{1,0:T(8,128)(2,1)S(1)}, bf16[256,6144]{1,0:T(8,128)(2,1)}, u32[]{:S(2)}) copy-start(bf16[256,6144]{1,0:T(8,128)(2,1)} %get-tuple-element.44.low_ref) | copy-start | bytes 9437188
  84.1 27.8 %copy-start.1 = (bf16[256,6144]{1,0:T(8,128)(2,1)S(1)}, bf16[256,6144]{1,0:T(8,128)(2,1)}, u32[]{:S(2)}) copy-start(bf16[256,6144]{1,0:T(8,128)(2,1)} %after.1.high_ref) | copy-start | bytes 9437188
  84.1 27.8 %copy-start.3 = (f32[4,64,64]{2,1,0:T(8,128)S(1)}, f32[4,64,64]{2,1,0:T(8,128)}, u32[]{:S(2)}) copy-start(f32[4,64,64]{2,1,0:T(8,128)} %tfactors_ref.1) | copy-start | bytes 196612
  85.1 1.3 %collective-permute-start.11 = (f32[128,128]{1,0:T(8,128)S(1)}, f32[128,128]{1,0:T(8,128)S(1)}, u32[]{:S(2)}, u32[]{:S(2)}) collective-permute-start(f32[128,128]{1,0:T(8,128)S(1)} %get-tuple-element.46), channel_id=1, source_target_pairs={{0,8},{8,0},{16,24},{24,16},{32,40},{40,32},{48,56},{56,48},{64,72... | collective-permute-start | bytes 196616 | tf_op jit(solution)/shard_map/ppermute | solution.py:320
  86.5 5.9 %collective-permute-start.12 = (f32[128,128]{1,0:T(8,128)S(1)}, f32[128,128]{1,0:T(8,128)S(1)}, u32[]{:S(2)}, u32[]{:S(2)}) collective-permute-start(f32[128,128]{1,0:T(8,128)S(1)} %add.33), channel_id=1, source_target_pairs={{0,16},{8,24},{16,0},{24,8},{32,48},{40,56},{48,32},{56,40},{64,80... | collective-permute-start | bytes 196616 | tf_op jit(solution)/shard_map/ppermute | solution.py:320
  92.4 9.7 %collective-permute-start.14 = (f32[224,128]{1,0:T(8,128)S(1)}, f32[224,128]{1,0:T(8,128)S(1)}, u32[]{:S(2)}, u32[]{:S(2)}) collective-permute-start(f32[224,128]{1,0:T(8,128)S(1)} %pad_maximum_fusion), channel_id=1, source_target_pairs={{0,64},{8,72},{16,80},{24,88},{32,96},{40,104},{48,112},{56,120},{... | collective-permute-start | bytes 344072 | tf_op jit(solution)/shard_map/ppermute | solution.py:320
  95.6 6.5 %collective-permute-start.13 = (f32[128,128]{1,0:T(8,128)S(1)}, f32[128,128]{1,0:T(8,128)S(1)}, u32[]{:S(2)}, u32[]{:S(2)}) collective-permute-start(f32[128,128]{1,0:T(8,128)S(1)} %add.34), channel_id=1, source_target_pairs={{0,32},{8,40},{16,48},{24,56},{32,0},{40,8},{48,16},{56,24},{64,96... | collective-permute-start | bytes 196616 | tf_op jit(solution)/shard_map/ppermute | solution.py:320
  97.1 6.2 %collective-permute-start.15 = (f32[128,128]{1,0:T(8,128)S(1)}, f32[128,128]{1,0:T(8,128)S(1)}, u32[]{:S(2)}, u32[]{:S(2)}) collective-permute-start(f32[128,128]{1,0:T(8,128)S(1)} %add.34), channel_id=1, source_target_pairs={{0,96},{8,104},{16,112},{24,120},{32,64},{40,72},{48,80},{56,88},{... | collective-permute-start | bytes 196616 | tf_op jit(solution)/shard_map/ppermute | solution.py:320
  103.3 7.1 %collective-permute-start.16 = (f32[224,128]{1,0:T(8,128)S(1)}, f32[224,128]{1,0:T(8,128)S(1)}, u32[]{:S(2)}, u32[]{:S(2)}) collective-permute-start(f32[224,128]{1,0:T(8,128)S(1)} %pad_maximum_fusion.1), channel_id=1, source_target_pairs={{0,192},{8,200},{16,208},{24,216},{32,224},{40,232},{48,240},{56,2... | collective-permute-start | bytes 344072 | tf_op jit(solution)/shard_map/ppermute | solution.py:320
  110.5 1.4 %collective-permute-start.17 = (f32[224,128]{1,0:T(8,128)S(1)}, f32[224,128]{1,0:T(8,128)S(1)}, u32[]{:S(2)}, u32[]{:S(2)}) collective-permute-start(f32[224,128]{1,0:T(8,128)S(1)} %fusion.1.own_ref), channel_id=1, source_target_pairs={{0,8},{8,0},{16,24},{24,16},{32,40},{40,32},{48,56},{56,48},{64,72... | collective-permute-start | bytes 344072 | tf_op jit(solution)/shard_map/ppermute | solution.py:320

commit v14 on v12

--- a/solution.py
+++ b/solution.py
@@ -355,13 +355,13 @@
         gram = gram + swap(gram, 2)
         scattered = spread(came[0], came[1], kept) + spread(came[2], came[3], gram)
         high = after(high, even)
-        current, value, sent, gram = project_call(core, place, even, scattered, high, low, gram, swap(gram, 4))
+        current, value, sent, gram = project_call(core, place, even, scattered, high, low, gram, swap(gram, 8))
         value = value + swap(sent, 1)
         value = value + swap(value, 2)
         half = value.shape[0]
-        first, third = swap(value, 4), swap(value, 12)
-        second = swap(jnp.concatenate([value, gram], axis=0), 8)
-        own = jnp.concatenate([(value + first) + (second[:half] + third), gram + second[half:]], axis=0)
+        second, third = swap(value, 8), swap(value, 12)
+        first = swap(jnp.concatenate([value, gram], axis=0), 4)
+        own = jnp.concatenate([(value + first[:half]) + (second + third), gram + first[half:]], axis=0)
         own = own + swap(own, 24)
         other = swap(own, 1)
         return finish_call(core, own, other, tfactors, current, high, low)

time: 117 us -> 117 us (level)
  waiting for transfers between devices: 42.7 us -> 40.8 us
  starting transfers between devices: 41.9 us -> 43.7 us
    ppermute x14, starting transfers between devices: 22.3 us -> 24.1 us  [swap(): return lax.ppermute(value, row, [(i, i ^ flip) for i in range(devices)])]
    all_to_all x1, waiting for transfers between devices: 1.3 us -> 0.01 us  [shards(): lax.all_to_all(even, ('half', 'y', 'core'), split_axis=0, concat_axis=0,...]
where the time goes in v14:
time: 117 us; the launch traced here: 116 us
  starting transfers between devices  43.7 us (37%)
  waiting for transfers between devices  40.8 us (35%)
  Pallas kernels  28.6 us (24%)
  local copies, waits for them, and re-layouts  1.9 us (2%)
    ppermute x14, waiting for transfers between devices, swap(): return lax.ppermute(value, row, [(i, i ^ flip) for i in range(devices)])  40.8 us
    ppermute x14, starting transfers between devices, swap(): return lax.ppermute(value, row, [(i, i ^ flip) for i in range(devices)])  24.1 us
    ppermute x4, starting transfers between devices, moved(): lax.ppermute(part, ('half', 'odd'), [(i, (i + shift) % planes) for i in r...  10.2 us
    all_to_all x1, starting transfers between devices, shards(): lax.all_to_all(even, ('half', 'y', 'core'), split_axis=0, concat_axis=0,...  9.4 us
    pallas_call x6, Pallas kernels, local_call(): pl.pallas_call(kernel, out_shape=outs, in_specs=[IN_SMEM] + specs, out_sp...  9.08 us
    pallas_call x1, Pallas kernels, gram_call(): pl.pallas_call(gram_kernel, out_shape=(pltpu.HBM((size, rows), jnp.bfloat...  8.8 us
    pallas_call x1, Pallas kernels, even_call(): pl.pallas_call(even_kernel, out_shape=pltpu.HBM((planes * 2, each, wide /...  4.14 us
    pallas_call x1, Pallas kernels, finish_call(): pl.pallas_call(finish_kernel, out_shape=jax.ShapeDtypeStruct((count, rows...  3.59 us
  transfers between devices with their start and end apart: 19, of which 11 were waited for; matrix products, arithmetic and copies ran while one was open for 0% of the time, Pallas kernels for 19%

profile of v14, /device:TPU:4, one launch (start us, length us, event | category | flops | bytes accessed | tf_op | source)
XLA Modules:
  0.0 115.5 jit_solution(2859944787392847370)
XLA Ops:
  0.0 0.1 pad_add_fusion.place_ref.before_ref
  0.1 2.6 %cut.3 = (f32[4,24576]{1,0:T(4,128)}, f32[4,24576]{1,0:T(4,128)}) custom-call(s32[3]{0:T(128)S(1)} %pad_add_fusion.place_ref.before_ref, f32[4,196608]{1,0:T(4,128)} %vectors_ref.3), custom_call_target="tpu_custom_call" | custom-call | tf_op jit(solution)/shard_map/cut/pallas_call | solution.py:227
  2.7 4.7 %collective-permute-start.4 = (f32[4,24576]{1,0:T(4,128)}, f32[4,24576]{1,0:T(4,128)S(1)}, u32[]{:S(2)}, u32[]{:S(2)}) collective-permute-start(f32[4,24576]{1,0:T(4,128)} %get-tuple-element.34), channel_id=1, source_target_pairs={{0,96},{32,128},{64,160},{96,192},{128,224},{160,0},{192,32},{224,... | collective-permute-start | bytes 1179656 | tf_op jit(solution)/shard_map/ppermute | solution.py:336
  7.4 2.2 %collective-permute-start.5 = (f32[4,24576]{1,0:T(4,128)}, f32[4,24576]{1,0:T(4,128)S(1)}, u32[]{:S(2)}, u32[]{:S(2)}) collective-permute-start(f32[4,24576]{1,0:T(4,128)} %get-tuple-element.35), channel_id=1, source_target_pairs={{0,160},{32,192},{64,224},{96,0},{128,32},{160,64},{192,96},{224,1... | collective-permute-start | bytes 1179656 | tf_op jit(solution)/shard_map/ppermute | solution.py:336
  9.6 2.6 %cut.2 = (f32[4,24576]{1,0:T(4,128)}, f32[4,24576]{1,0:T(4,128)}) custom-call(s32[3]{0:T(128)S(1)} %pad_add_fusion.place_ref.before_ref, f32[4,196608]{1,0:T(4,128)} %vectors_ref.3), custom_call_target="tpu_custom_call" | custom-call | tf_op jit(solution)/shard_map/cut/pallas_call | solution.py:227
  12.2 1.1 collective-permute-start
  13.3 2.2 %collective-permute-start.1 = (f32[4,24576]{1,0:T(4,128)}, f32[4,24576]{1,0:T(4,128)S(1)}, u32[]{:S(2)}, u32[]{:S(2)}) collective-permute-start(f32[4,24576]{1,0:T(4,128)} %get-tuple-element.28), channel_id=1, source_target_pairs={{0,224},{32,0},{64,32},{96,64},{128,96},{160,128},{192,160},{224,1... | collective-permute-start | bytes 1179656 | tf_op jit(solution)/shard_map/ppermute | solution.py:336
  15.5 4.1 %even.1 = f32[16,4,6144]{2,1,0:T(4,128)} custom-call(s32[3]{0:T(128)S(1)} %pad_add_fusion.place_ref.before_ref, f32[4,196608]{1,0:T(4,128)} %vectors_ref.3, s32[3]{0:T(128)S(1)} %pad_add_fusion.place_ref.before_ref), custom_call_target="tpu_custom_call" | custom-call | tf_op jit(solution)/shard_map/even/pallas_call | solution.py:241
  19.6 9.4 %all-to-all-start = ((f32[16,4,6144]{2,1,0:T(4,128)}), f32[16,4,6144]{2,1,0:T(4,128)S(1)}, u32[]{:S(2)}, u32[]{:S(2)}) async-start(f32[16,4,6144]{2,1,0:T(4,128)} %even.1), calls=%async_computation | async-start | bytes 3145728 | tf_op jit(solution)/shard_map/all_to_all | solution.py:352
  29.0 8.8 %gram.1 = (bf16[256,6144]{1,0:T(8,128)(2,1)}, bf16[256,6144]{1,0:T(8,128)(2,1)}, f32[96,128]{1,0:T(8,128)S(1)}, f32[96,128]{1,0:T(8,128)S(1)}) custom-call(s32[1]{0:T(128)} %bitcast.core_ref, f32[4,64,6144]{2,1,0:T(8,128)} %householder_ref.1, s32[3]{0:T(128)S(1)} %pad_add_fusion.place_ref.before_ref), custom_call_target="tpu_custom_call" | custom-call | flops 32212254720 | bytes 12582912 | tf_op jit(solution)/shard_map/gram/pallas_call | solution.py:203
  37.8 0.4 collective-permute-start.6
  38.2 0.9 collective-permute-done.6
  39.1 3.4 %collective-permute-start.7 = (f32[96,128]{1,0:T(8,128)S(1)}, f32[96,128]{1,0:T(8,128)S(1)}, u32[]{:S(2)}, u32[]{:S(2)}) collective-permute-start(f32[96,128]{1,0:T(8,128)S(1)} %add.31), channel_id=1, source_target_pairs={{0,16},{8,24},{16,0},{24,8},{32,48},{40,56},{48,32},{56,40},{64,80... | collective-permute-start | bytes 147464 | tf_op jit(solution)/shard_map/ppermute | solution.py:325
  42.6 2.2 %collective-permute-done.7 = f32[96,128]{1,0:T(8,128)S(1)} collective-permute-done((f32[96,128]{1,0:T(8,128)S(1)}, f32[96,128]{1,0:T(8,128)S(1)}, u32[]{:S(2)}, u32[]{:S(2)}) %collective-permute-start.7) | collective-permute-done | bytes 49184 | tf_op jit(solution)/shard_map/ppermute | solution.py:325
  44.8 0.0 collective-permute-done.4.up_ref
  44.8 0.0 collective-permute-done.5.down_ref
  44.8 0.6 side_kernel.3
  45.4 3.5 %collective-permute-start.8 = (f32[2,4,12288]{2,1,0:T(4,128)S(1)}, f32[2,4,12288]{2,1,0:T(4,128)S(1)}, u32[]{:S(2)}, u32[]{:S(2)}) collective-permute-start(f32[2,4,12288]{2,1,0:T(4,128)S(1)} %get-tuple-element.38), channel_id=1, source_target_pairs={{0,16},{8,24},{16,0},{24,8},{32,48},{40,56},{48,32},{56,40},{64,80... | collective-permute-start | bytes 1179656 | tf_op jit(solution)/shard_map/ppermute | solution.py:325
  48.9 0.0 collective-permute-done.up_ref
  48.9 0.0 collective-permute-done.1.down_ref
  48.9 0.6 side_kernel.2
  49.5 3.2 %collective-permute-start.2 = (f32[2,4,12288]{2,1,0:T(4,128)S(1)}, f32[2,4,12288]{2,1,0:T(4,128)S(1)}, u32[]{:S(2)}, u32[]{:S(2)}) collective-permute-start(f32[2,4,12288]{2,1,0:T(4,128)S(1)} %get-tuple-element.31), channel_id=1, source_target_pairs={{0,16},{8,24},{16,0},{24,8},{32,48},{40,56},{48,32},{56,40},{64,80... | collective-permute-start | bytes 1179656 | tf_op jit(solution)/shard_map/ppermute | solution.py:325
  52.7 10.2 %collective-permute-done.8.got_ref = f32[2,4,12288]{2,1,0:T(4,128)S(1)} collective-permute-done((f32[2,4,12288]{2,1,0:T(4,128)S(1)}, f32[2,4,12288]{2,1,0:T(4,128)S(1)}, u32[]{:S(2)}, u32[]{:S(2)}) %collective-permute-start.8) | collective-permute-done | bytes 393248 | tf_op jit(solution)/shard_map/ppermute | solution.py:325
  62.9 1.4 %core_kernel.3 = (f32[2,2,4,6144]{3,2,1,0:T(4,128)S(1)}, f32[2,2,4,6144]{3,2,1,0:T(4,128)}) custom-call(s32[3]{0:T(128)S(1)} %pad_add_fusion.place_ref.before_ref, f32[2,4,12288]{2,1,0:T(4,128)S(1)} %get-tuple-element.37.own_ref, f32[2,4,12288]{2,1,0:T(4,128)S(1)} %collective-permute-done.8.got_ref), custom_call_target="tpu_custom_call" | custom-call | tf_op jit(solution)/shard_map/core_kernel/pallas_call | solution.py:227
  64.2 0.0 collective-permute-start.9
  64.2 11.8 %collective-permute-done.2.got_ref = f32[2,4,12288]{2,1,0:T(4,128)S(1)} collective-permute-done((f32[2,4,12288]{2,1,0:T(4,128)S(1)}, f32[2,4,12288]{2,1,0:T(4,128)S(1)}, u32[]{:S(2)}, u32[]{:S(2)}) %collective-permute-start.2) | collective-permute-done | bytes 393248 | tf_op jit(solution)/shard_map/ppermute | solution.py:325
  76.1 1.4 %core_kernel.2 = (f32[2,2,4,6144]{3,2,1,0:T(4,128)S(1)}, f32[2,2,4,6144]{3,2,1,0:T(4,128)}) custom-call(s32[3]{0:T(128)S(1)} %pad_add_fusion.place_ref.before_ref, f32[2,4,12288]{2,1,0:T(4,128)S(1)} %get-tuple-element.30.own_ref, f32[2,4,12288]{2,1,0:T(4,128)S(1)} %collective-permute-done.2.got_ref), custom_call_target="tpu_custom_call" | custom-call | tf_op jit(solution)/shard_map/core_kernel/pallas_call | solution.py:227
  77.5 0.0 collective-permute-start.3
  77.5 3.7 %collective-permute-start.10 = (f32[96,128]{1,0:T(8,128)S(1)}, f32[96,128]{1,0:T(8,128)S(1)}, u32[]{:S(2)}, u32[]{:S(2)}) collective-permute-start(f32[96,128]{1,0:T(8,128)S(1)} %add.32.before_ref.gram_ref), channel_id=1, source_target_pairs={{0,64},{8,72},{16,80},{24,88},{32,96},{40,104},{48,112},{56,120},{... | collective-permute-start | bytes 147464 | tf_op jit(solution)/shard_map/ppermute | solution.py:325
  81.2 0.0 all-to-all-done.before_ref.even_ref
  81.2 0.0 collective-permute-done.9.got_three_ref
  81.2 0.0 collective-permute-done.3.got_one_ref
  81.2 0.0 copy-start
  81.2 1.9 %copy-done = bf16[256,6144]{1,0:T(8,128)(2,1)S(1)} copy-done((bf16[256,6144]{1,0:T(8,128)(2,1)S(1)}, bf16[256,6144]{1,0:T(8,128)(2,1)}, u32[]{:S(2)}) %copy-start) | copy-done | bytes 3145752
  83.1 0.0 copy-start.2
  83.1 2.0 %project_high.1 = (f32[128,6144]{1,0:T(8,128)S(1)}, bf16[128,6144]{1,0:T(8,128)(2,1)S(1)}, f32[256,256]{1,0:T(8,128)S(1)}) custom-call(s32[3]{0:T(128)S(1)} %pad_add_fusion.place_ref.before_ref, f32[16,4,6144]{2,1,0:T(4,128)S(1)} %all-to-all-done.before_ref.even_ref, f32[2,2,4,6144]{3,2,1,0:T(4,128)S(1)} %get-tuple-element.32.kept_one_ref, ...), custom_call_target="tpu_custom_call" | custom-call | tf_op jit(solution)/shard_map/project_high/pallas_call | solution.py:271
  85.1 0.0 collective-permute-done.10.more_ref
  85.1 0.0 copy-done.2
  85.1 0.0 copy-start.1
  85.1 0.0 copy-start.3
  85.1 1.0 project_low.1
  86.1 0.3 collective-permute-start.11
  86.5 1.0 collective-permute-done.11
  87.5 2.1 %collective-permute-start.12 = (f32[128,128]{1,0:T(8,128)S(1)}, f32[128,128]{1,0:T(8,128)S(1)}, u32[]{:S(2)}, u32[]{:S(2)}) collective-permute-start(f32[128,128]{1,0:T(8,128)S(1)} %add.33), channel_id=1, source_target_pairs={{0,16},{8,24},{16,0},{24,8},{32,48},{40,56},{48,32},{56,40},{64,80... | collective-permute-start | bytes 196616 | tf_op jit(solution)/shard_map/ppermute | solution.py:325
  89.6 3.8 %collective-permute-done.12 = f32[128,128]{1,0:T(8,128)S(1)} collective-permute-done((f32[128,128]{1,0:T(8,128)S(1)}, f32[128,128]{1,0:T(8,128)S(1)}, u32[]{:S(2)}, u32[]{:S(2)}) %collective-permute-start.12) | collective-permute-done | bytes 65568 | tf_op jit(solution)/shard_map/ppermute | solution.py:325
  93.4 0.3 collective-permute-start.13
  93.7 3.5 %collective-permute-start.14 = (f32[128,128]{1,0:T(8,128)S(1)}, f32[128,128]{1,0:T(8,128)S(1)}, u32[]{:S(2)}, u32[]{:S(2)}) collective-permute-start(f32[128,128]{1,0:T(8,128)S(1)} %add.34), channel_id=1, source_target_pairs={{0,64},{8,72},{16,80},{24,88},{32,96},{40,104},{48,112},{56,120},{... | collective-permute-start | bytes 196616 | tf_op jit(solution)/shard_map/ppermute | solution.py:325
  97.1 0.9 collective-permute-start.15
  98.0 1.3 %collective-permute-done.13 = f32[224,128]{1,0:T(8,128)S(1)} collective-permute-done((f32[224,128]{1,0:T(8,128)S(1)}, f32[224,128]{1,0:T(8,128)S(1)}, u32[]{:S(2)}, u32[]{:S(2)}) %collective-permute-start.13) | collective-permute-done | bytes 114720 | tf_op jit(solution)/shard_map/ppermute | solution.py:325
  99.4 2.3 %collective-permute-done.14 = f32[128,128]{1,0:T(8,128)S(1)} collective-permute-done((f32[128,128]{1,0:T(8,128)S(1)}, f32[128,128]{1,0:T(8,128)S(1)}, u32[]{:S(2)}, u32[]{:S(2)}) %collective-permute-start.14) | collective-permute-done | bytes 65568 | tf_op jit(solution)/shard_map/ppermute | solution.py:325
  101.7 1.5 %collective-permute-done.15 = f32[128,128]{1,0:T(8,128)S(1)} collective-permute-done((f32[128,128]{1,0:T(8,128)S(1)}, f32[128,128]{1,0:T(8,128)S(1)}, u32[]{:S(2)}, u32[]{:S(2)}) %collective-permute-start.15) | collective-permute-done | bytes 65568 | tf_op jit(solution)/shard_map/ppermute | solution.py:325
  103.2 2.8 %collective-permute-start.16 = (f32[224,128]{1,0:T(8,128)S(1)}, f32[224,128]{1,0:T(8,128)S(1)}, u32[]{:S(2)}, u32[]{:S(2)}) collective-permute-start(f32[224,128]{1,0:T(8,128)S(1)} %pad_maximum_fusion.1), channel_id=1, source_target_pairs={{0,192},{8,200},{16,208},{24,216},{32,224},{40,232},{48,240},{56,2... | collective-permute-start | bytes 344072 | tf_op jit(solution)/shard_map/ppermute | solution.py:325
  106.0 4.3 %collective-permute-done.16 = f32[224,128]{1,0:T(8,128)S(1)} collective-permute-done((f32[224,128]{1,0:T(8,128)S(1)}, f32[224,128]{1,0:T(8,128)S(1)}, u32[]{:S(2)}, u32[]{:S(2)}) %collective-permute-start.16) | collective-permute-done | bytes 114720 | tf_op jit(solution)/shard_map/ppermute | solution.py:325
  110.3 0.1 collective-permute-start.17
  110.4 1.3 %collective-permute-done.17.other_ref = f32[224,128]{1,0:T(8,128)S(1)} collective-permute-done((f32[224,128]{1,0:T(8,128)S(1)}, f32[224,128]{1,0:T(8,128)S(1)}, u32[]{:S(2)}, u32[]{:S(2)}) %collective-permute-start.17) | collective-permute-done | bytes 114720 | tf_op jit(solution)/shard_map/ppermute | solution.py:325
  111.8 0.0 copy-done.1
  111.8 0.0 copy-done.3
  111.8 3.6 %finish.1 = f32[128,6144]{1,0:T(8,128)} custom-call(s32[1]{0:T(128)} %bitcast.core_ref, f32[224,128]{1,0:T(8,128)S(1)} %fusion.1.own_ref, f32[224,128]{1,0:T(8,128)S(1)} %collective-permute-done.17.other_ref, f32[4,64,64]{2,1,0:T(8,128)S(1)} %copy-done.3, f32[128,6144]{1,0:T(8,128)S(1)} %get-tuple-element.48.current_ref, bf16[256,6144]{1,0:T(8,128)(2,1)S(1)} %copy-done.1, ...), custom_call_target="tpu_custom_call" | custom-call | tf_op jit(solution)/shard_map/finish/pallas_call | solution.py:302
  (10 shorter events, 0.1 us)
Async XLA Ops:
  2.7 42.1 %collective-permute-start.4 = (f32[4,24576]{1,0:T(4,128)}, f32[4,24576]{1,0:T(4,128)S(1)}, u32[]{:S(2)}, u32[]{:S(2)}) collective-permute-start(f32[4,24576]{1,0:T(4,128)} %get-tuple-element.34), channel_id=1, source_target_pairs={{0,96},{32,128},{64,160},{96,192},{128,224},{160,0},{192,32},{224,... | collective-permute-start | bytes 1179656 | tf_op jit(solution)/shard_map/ppermute | solution.py:336
  7.4 37.4 %collective-permute-start.5 = (f32[4,24576]{1,0:T(4,128)}, f32[4,24576]{1,0:T(4,128)S(1)}, u32[]{:S(2)}, u32[]{:S(2)}) collective-permute-start(f32[4,24576]{1,0:T(4,128)} %get-tuple-element.35), channel_id=1, source_target_pairs={{0,160},{32,192},{64,224},{96,0},{128,32},{160,64},{192,96},{224,1... | collective-permute-start | bytes 1179656 | tf_op jit(solution)/shard_map/ppermute | solution.py:336
  12.2 36.7 %collective-permute-start = (f32[4,24576]{1,0:T(4,128)}, f32[4,24576]{1,0:T(4,128)S(1)}, u32[]{:S(2)}, u32[]{:S(2)}) collective-permute-start(f32[4,24576]{1,0:T(4,128)} %get-tuple-element.27), channel_id=1, source_target_pairs={{0,32},{32,64},{64,96},{96,128},{128,160},{160,192},{192,224},{224... | collective-permute-start | bytes 1179656 | tf_op jit(solution)/shard_map/ppermute | solution.py:336
  13.3 35.6 %collective-permute-start.1 = (f32[4,24576]{1,0:T(4,128)}, f32[4,24576]{1,0:T(4,128)S(1)}, u32[]{:S(2)}, u32[]{:S(2)}) collective-permute-start(f32[4,24576]{1,0:T(4,128)} %get-tuple-element.28), channel_id=1, source_target_pairs={{0,224},{32,0},{64,32},{96,64},{128,96},{160,128},{192,160},{224,1... | collective-permute-start | bytes 1179656 | tf_op jit(solution)/shard_map/ppermute | solution.py:336
  19.6 61.5 %all-to-all-start = ((f32[16,4,6144]{2,1,0:T(4,128)}), f32[16,4,6144]{2,1,0:T(4,128)S(1)}, u32[]{:S(2)}, u32[]{:S(2)}) async-start(f32[16,4,6144]{2,1,0:T(4,128)} %even.1), calls=%async_computation | async-start | bytes 3145728 | tf_op jit(solution)/shard_map/all_to_all | solution.py:352
  37.8 1.3 %collective-permute-start.6 = (f32[96,128]{1,0:T(8,128)S(1)}, f32[96,128]{1,0:T(8,128)S(1)}, u32[]{:S(2)}, u32[]{:S(2)}) collective-permute-start(f32[96,128]{1,0:T(8,128)S(1)} %get-tuple-element.36), channel_id=1, source_target_pairs={{0,8},{8,0},{16,24},{24,16},{32,40},{40,32},{48,56},{56,48},{64,72... | collective-permute-start | bytes 147464 | tf_op jit(solution)/shard_map/ppermute | solution.py:325
  39.1 5.7 %collective-permute-start.7 = (f32[96,128]{1,0:T(8,128)S(1)}, f32[96,128]{1,0:T(8,128)S(1)}, u32[]{:S(2)}, u32[]{:S(2)}) collective-permute-start(f32[96,128]{1,0:T(8,128)S(1)} %add.31), channel_id=1, source_target_pairs={{0,16},{8,24},{16,0},{24,8},{32,48},{40,56},{48,32},{56,40},{64,80... | collective-permute-start | bytes 147464 | tf_op jit(solution)/shard_map/ppermute | solution.py:325
  45.4 17.5 %collective-permute-start.8 = (f32[2,4,12288]{2,1,0:T(4,128)S(1)}, f32[2,4,12288]{2,1,0:T(4,128)S(1)}, u32[]{:S(2)}, u32[]{:S(2)}) collective-permute-start(f32[2,4,12288]{2,1,0:T(4,128)S(1)} %get-tuple-element.38), channel_id=1, source_target_pairs={{0,16},{8,24},{16,0},{24,8},{32,48},{40,56},{48,32},{56,40},{64,80... | collective-permute-start | bytes 1179656 | tf_op jit(solution)/shard_map/ppermute | solution.py:325
  49.5 26.6 %collective-permute-start.2 = (f32[2,4,12288]{2,1,0:T(4,128)S(1)}, f32[2,4,12288]{2,1,0:T(4,128)S(1)}, u32[]{:S(2)}, u32[]{:S(2)}) collective-permute-start(f32[2,4,12288]{2,1,0:T(4,128)S(1)} %get-tuple-element.31), channel_id=1, source_target_pairs={{0,16},{8,24},{16,0},{24,8},{32,48},{40,56},{48,32},{56,40},{64,80... | collective-permute-start | bytes 1179656 | tf_op jit(solution)/shard_map/ppermute | solution.py:325
  64.2 16.9 %collective-permute-start.9 = (f32[2,2,4,6144]{3,2,1,0:T(4,128)}, f32[2,2,4,6144]{3,2,1,0:T(4,128)S(1)}, u32[]{:S(2)}, u32[]{:S(2)}) collective-permute-start(f32[2,2,4,6144]{3,2,1,0:T(4,128)} %get-tuple-element.40), channel_id=1, source_target_pairs={{0,8},{8,0},{16,24},{24,16},{32,40},{40,32},{48,56},{56,48},{64,72... | collective-permute-start | bytes 1179656 | tf_op jit(solution)/shard_map/ppermute | solution.py:325
  77.5 3.7 %collective-permute-start.3 = (f32[2,2,4,6144]{3,2,1,0:T(4,128)}, f32[2,2,4,6144]{3,2,1,0:T(4,128)S(1)}, u32[]{:S(2)}, u32[]{:S(2)}) collective-permute-start(f32[2,2,4,6144]{3,2,1,0:T(4,128)} %get-tuple-element.33), channel_id=1, source_target_pairs={{0,8},{8,0},{16,24},{24,16},{32,40},{40,32},{48,56},{56,48},{64,72... | collective-permute-start | bytes 1179656 | tf_op jit(solution)/shard_map/ppermute | solution.py:325
  77.5 7.6 %collective-permute-start.10 = (f32[96,128]{1,0:T(8,128)S(1)}, f32[96,128]{1,0:T(8,128)S(1)}, u32[]{:S(2)}, u32[]{:S(2)}) collective-permute-start(f32[96,128]{1,0:T(8,128)S(1)} %add.32.before_ref.gram_ref), channel_id=1, source_target_pairs={{0,64},{8,72},{16,80},{24,88},{32,96},{40,104},{48,112},{56,120},{... | collective-permute-start | bytes 147464 | tf_op jit(solution)/shard_map/ppermute | solution.py:325
  81.2 1.9 %copy-start = (bf16[256,6144]{1,0:T(8,128)(2,1)S(1)}, bf16[256,6144]{1,0:T(8,128)(2,1)}, u32[]{:S(2)}) copy-start(bf16[256,6144]{1,0:T(8,128)(2,1)} %after.1.high_ref) | copy-start | bytes 9437188
  83.1 2.0 %copy-start.2 = (bf16[256,6144]{1,0:T(8,128)(2,1)S(1)}, bf16[256,6144]{1,0:T(8,128)(2,1)}, u32[]{:S(2)}) copy-start(bf16[256,6144]{1,0:T(8,128)(2,1)} %get-tuple-element.44.low_ref) | copy-start | bytes 9437188
  85.1 26.6 %copy-start.1 = (bf16[256,6144]{1,0:T(8,128)(2,1)S(1)}, bf16[256,6144]{1,0:T(8,128)(2,1)}, u32[]{:S(2)}) copy-start(bf16[256,6144]{1,0:T(8,128)(2,1)} %after.1.high_ref) | copy-start | bytes 9437188
  85.1 26.6 %copy-start.3 = (f32[4,64,64]{2,1,0:T(8,128)S(1)}, f32[4,64,64]{2,1,0:T(8,128)}, u32[]{:S(2)}) copy-start(f32[4,64,64]{2,1,0:T(8,128)} %tfactors_ref.1) | copy-start | bytes 196612
  86.1 1.3 %collective-permute-start.11 = (f32[128,128]{1,0:T(8,128)S(1)}, f32[128,128]{1,0:T(8,128)S(1)}, u32[]{:S(2)}, u32[]{:S(2)}) collective-permute-start(f32[128,128]{1,0:T(8,128)S(1)} %get-tuple-element.46), channel_id=1, source_target_pairs={{0,8},{8,0},{16,24},{24,16},{32,40},{40,32},{48,56},{56,48},{64,72... | collective-permute-start | bytes 196616 | tf_op jit(solution)/shard_map/ppermute | solution.py:325
  87.5 5.9 %collective-permute-start.12 = (f32[128,128]{1,0:T(8,128)S(1)}, f32[128,128]{1,0:T(8,128)S(1)}, u32[]{:S(2)}, u32[]{:S(2)}) collective-permute-start(f32[128,128]{1,0:T(8,128)S(1)} %add.33), channel_id=1, source_target_pairs={{0,16},{8,24},{16,0},{24,8},{32,48},{40,56},{48,32},{56,40},{64,80... | collective-permute-start | bytes 196616 | tf_op jit(solution)/shard_map/ppermute | solution.py:325
  93.4 6.0 %collective-permute-start.13 = (f32[224,128]{1,0:T(8,128)S(1)}, f32[224,128]{1,0:T(8,128)S(1)}, u32[]{:S(2)}, u32[]{:S(2)}) collective-permute-start(f32[224,128]{1,0:T(8,128)S(1)} %pad_maximum_fusion), channel_id=1, source_target_pairs={{0,32},{8,40},{16,48},{24,56},{32,0},{40,8},{48,16},{56,24},{64,96... | collective-permute-start | bytes 344072 | tf_op jit(solution)/shard_map/ppermute | solution.py:325
  93.7 8.0 %collective-permute-start.14 = (f32[128,128]{1,0:T(8,128)S(1)}, f32[128,128]{1,0:T(8,128)S(1)}, u32[]{:S(2)}, u32[]{:S(2)}) collective-permute-start(f32[128,128]{1,0:T(8,128)S(1)} %add.34), channel_id=1, source_target_pairs={{0,64},{8,72},{16,80},{24,88},{32,96},{40,104},{48,112},{56,120},{... | collective-permute-start | bytes 196616 | tf_op jit(solution)/shard_map/ppermute | solution.py:325
  97.1 6.1 %collective-permute-start.15 = (f32[128,128]{1,0:T(8,128)S(1)}, f32[128,128]{1,0:T(8,128)S(1)}, u32[]{:S(2)}, u32[]{:S(2)}) collective-permute-start(f32[128,128]{1,0:T(8,128)S(1)} %add.34), channel_id=1, source_target_pairs={{0,96},{8,104},{16,112},{24,120},{32,64},{40,72},{48,80},{56,88},{... | collective-permute-start | bytes 196616 | tf_op jit(solution)/shard_map/ppermute | solution.py:325
  103.2 7.1 %collective-permute-start.16 = (f32[224,128]{1,0:T(8,128)S(1)}, f32[224,128]{1,0:T(8,128)S(1)}, u32[]{:S(2)}, u32[]{:S(2)}) collective-permute-start(f32[224,128]{1,0:T(8,128)S(1)} %pad_maximum_fusion.1), channel_id=1, source_target_pairs={{0,192},{8,200},{16,208},{24,216},{32,224},{40,232},{48,240},{56,2... | collective-permute-start | bytes 344072 | tf_op jit(solution)/shard_map/ppermute | solution.py:325
  110.3 1.4 %collective-permute-start.17 = (f32[224,128]{1,0:T(8,128)S(1)}, f32[224,128]{1,0:T(8,128)S(1)}, u32[]{:S(2)}, u32[]{:S(2)}) collective-permute-start(f32[224,128]{1,0:T(8,128)S(1)} %fusion.1.own_ref), channel_id=1, source_target_pairs={{0,8},{8,0},{16,24},{24,16},{32,40},{40,32},{48,56},{56,48},{64,72... | collective-permute-start | bytes 344072 | tf_op jit(solution)/shard_map/ppermute | solution.py:325
